TPU v7x, 256 devices: a whole 4x4x8 slice. The times are simulated.
256 devices in a mesh: gy: 64 (over x, y_lo, z), gx: 4 (over y_hi, core).
Axes of the slice: x: 4, y: 4 (y_hi: 2, y_lo: 2; y = y_hi * 2 + y_lo), z: 8, core: 2. Of those that a mesh axis runs over, the one named last changes fastest.
Arguments:
- cell_index: int32 [3, 98304], P(None, ('gy', 'gx')), may hold values from 0 to 383, as said below
- offsets: float32 [3, 98304], P(None, ('gy', 'gx')), may hold values from 0 to 1
- charges: float32 [98304], P(('gy', 'gx')), may hold values from -6 to 6
- dipoles: float32 [3, 98304], P(None, ('gy', 'gx')), may hold values from -6 to 6
- block_count: int32 [1536], P(('gy', 'gx')), may hold values from 32 to 64, as said below
- shear_cells: int32 [1], replicated, may hold values from 1 to 383
Outputs:
- charge_grad: float32 [98304], P(('gy', 'gx'))
- dipole_grad: float32 [3, 98304], P(None, ('gy', 'gx'))
- position_grad: float32 [3, 98304], P(None, ('gy', 'gx'))
- energy: float32 [1], replicated
Inputs may be any that keep to these rules, and one draw needn't show every extreme that they name: `cell_index`: slot s lies in block k = s // 64; block k lies on the device d = k // 6 at gy index d // 4 and gx index d % 4; its atoms have x cells from (d % 4) * 96 + (k % 6) * 16 up to 15 beyond, y cells from (d // 4) * 6 up to 5 beyond, and z cells below 360. The first slot of each block sits at the largest x, y and z cells of that range. Row 0 holds x, row 1 y, row 2 z. The live atoms of a block are its first block_count slots; every device holds a full block.
All inputs are finite; a program needn't handle non-finite values.
Results may differ from a plain program's by a relative error of at most 0.0003.
Values sent between devices are 32-bit elements; how exact they have to be, the bound alone decides.
No kernel may reach another device: no remote copies, remote signals or barrier semaphores. Data moves between devices by JAX's collectives and lax.ppermute only.
A program may use at most 128 MiB of HBM per device.

v0:
```python
import math

import jax
import jax.numpy as jnp
from jax import lax
from jax.sharding import PartitionSpec as P

NX = 384
NZ = 360
CY = 6
BX = 16


screening = 0.9
combos = (
    (0, 0, 0),
    (1, 0, 0),
    (0, 1, 0),
    (0, 0, 1),
    (2, 0, 0),
    (0, 2, 0),
    (0, 0, 2),
    (1, 1, 0),
    (1, 0, 1),
    (0, 1, 1),
)
planar_orders = ((0, 0), (1, 0), (0, 1), (2, 0), (0, 2), (1, 1))


def spline_tables(fraction):
    levels = {2: [1.0 - fraction, fraction]}
    current = levels[2]
    for n in range(3, 7):
        inverse_n = 1.0 / (n - 1)
        updated = [None] * n
        updated[n - 1] = inverse_n * fraction * current[n - 2]
        for j in range(1, n - 1):
            updated[n - 1 - j] = inverse_n * (
                (fraction + j) * current[n - 2 - j] + (n - j - fraction) * current[n - 1 - j]
            )
        updated[0] = inverse_n * (1.0 - fraction) * current[0]
        current = updated
        levels[n] = current
    zero_row = jnp.zeros_like(fraction)

    def entry_at(values_list, k):
        return values_list[k] if 0 <= k < len(values_list) else zero_row

    values_w = jnp.stack(levels[6])
    first_w = jnp.stack([entry_at(levels[5], t - 1) - entry_at(levels[5], t) for t in range(6)])
    second_w = jnp.stack(
        [
            entry_at(levels[4], t - 2) - 2.0 * entry_at(levels[4], t - 1) + entry_at(levels[4], t)
            for t in range(6)
        ]
    )
    return jnp.stack([values_w, first_w, second_w])


def spline_modulus(angles):
    return (66.0 + 52.0 * jnp.cos(angles) + 2.0 * jnp.cos(2.0 * angles)) / 120.0


def green_values(index_x, index_y, index_z, shear_step, size_x, size_y, size_z):
    fold_x = (index_x + size_x // 2) % size_x - size_x // 2
    fold_y = (index_y + size_y // 2) % size_y - size_y // 2
    fold_z = (index_z + size_z // 2) % size_z - size_z // 2
    float_x = fold_x.astype(jnp.float32)
    float_z = fold_z.astype(jnp.float32)
    wave_y = fold_y.astype(jnp.float32) + float_x * shear_step.astype(jnp.float32) / size_x
    square_norm = (float_x / size_x) ** 2 + (wave_y / size_y) ** 2 + (float_z / size_z) ** 2
    is_zero = (fold_x == 0) & (fold_y == 0) & (fold_z == 0)
    at_edge = (fold_x == -(size_x // 2)) | (fold_y == -(size_y // 2)) | (fold_z == -(size_z // 2))
    safe_norm = jnp.where(is_zero, 1.0, square_norm)
    moduli = (
        spline_modulus(2.0 * math.pi * float_x / size_x)
        * spline_modulus(2.0 * math.pi * wave_y / size_y)
        * spline_modulus(2.0 * math.pi * float_z / size_z)
    )
    kernel = jnp.exp(-((math.pi / screening) ** 2) * safe_norm) / (
        math.pi * safe_norm * moduli * moduli
    )
    return jnp.where(is_zero | at_edge, 0.0, kernel)


def dense_weights(tables, base_cell, length, period):
    columns = jnp.arange(length, dtype=jnp.int32)
    summed = jnp.zeros((3, base_cell.shape[0], length), jnp.float32)
    for t in range(6):
        position = base_cell + t
        if period > 0:
            position = position % period
        matches = (position[:, None] == columns[None, :]).astype(jnp.float32)
        summed = summed + tables[:, t, :, None] * matches[None, :, :]
    return summed


def twiddle(rows_index, cols_index, period):
    tick_count = rows_index[:, None] * cols_index[None, :] % period
    angles = 2.0 * math.pi / period * tick_count.astype(jnp.float32)
    return (jnp.cos(angles), jnp.sin(angles))


def contract(pattern, operand, matrix):
    return jnp.einsum(pattern, operand, matrix, precision=lax.Precision.HIGHEST)


def forward_pair(pattern, real_in, imag_in, cos_table, sin_table):
    real_out = contract(pattern, real_in, cos_table) + contract(pattern, imag_in, sin_table)
    imag_out = contract(pattern, imag_in, cos_table) - contract(pattern, real_in, sin_table)
    return (real_out, imag_out)


def inverse_pair(pattern, real_in, imag_in, cos_table, sin_table):
    real_out = contract(pattern, real_in, cos_table) - contract(pattern, imag_in, sin_table)
    imag_out = contract(pattern, imag_in, cos_table) + contract(pattern, real_in, sin_table)
    return (real_out, imag_out)


def on_device(cell_index, offsets, charges, dipoles, block_count, shear_cells):
    groups_x = lax.axis_size("gx")
    groups_y = lax.axis_size("gy")
    pencil_index = lax.axis_index("gx")
    slab_index = lax.axis_index("gy")
    width_x = NX // groups_x
    window_x = width_x + 5
    depth_y = CY + 5
    block_x = BX + 5
    total_y = CY * groups_y
    part_x = NX // groups_y
    blocks = block_count.shape[0]
    per_block = charges.shape[0] // blocks
    shear_step = shear_cells[0]
    slot_rank = jnp.arange(per_block, dtype=jnp.int32)
    spread_grid = jnp.zeros((depth_y, window_x, NZ), jnp.float32)
    block_store = []
    for b in range(blocks):
        first_slot = b * per_block
        last_slot = first_slot + per_block
        live_slots = (slot_rank < block_count[b]).astype(jnp.float32)
        charge_live = charges[first_slot:last_slot] * live_slots
        dipole_live = dipoles[:, first_slot:last_slot] * live_slots[None, :]
        local_x = cell_index[0, first_slot:last_slot] - pencil_index * width_x - b * BX
        local_y = cell_index[1, first_slot:last_slot] - slab_index * CY
        dense_x = dense_weights(
            spline_tables(offsets[0, first_slot:last_slot]), local_x, block_x, 0
        )
        dense_y = dense_weights(
            spline_tables(offsets[1, first_slot:last_slot]), local_y, depth_y, 0
        )
        dense_z = dense_weights(
            spline_tables(offsets[2, first_slot:last_slot]),
            cell_index[2, first_slot:last_slot],
            NZ,
            NZ,
        )
        planar = {}
        for p, r in planar_orders:
            planar[p, r] = (dense_y[r][:, :, None] * dense_x[p][:, None, :]).reshape(
                per_block, depth_y * block_x
            )
        left_side = jnp.concatenate(
            [
                planar[0, 0],
                dipole_live[0][:, None] * planar[1, 0] + dipole_live[1][:, None] * planar[0, 1],
            ],
            axis=0,
        )
        right_side = jnp.concatenate(
            [charge_live[:, None] * dense_z[0] + dipole_live[2][:, None] * dense_z[1], dense_z[0]],
            axis=0,
        )
        block_grid = contract("ac,az->cz", left_side, right_side).reshape(depth_y, block_x, NZ)
        spread_grid = spread_grid.at[:, b * BX : b * BX + block_x, :].add(block_grid)
        block_store.append((planar, dense_z, live_slots, charge_live, dipole_live))
    rows_z = jnp.arange(NZ, dtype=jnp.int32)
    kept_z = NZ
    modes_z = jnp.arange(kept_z, dtype=jnp.int32)
    fold_weight = jnp.ones((kept_z,), jnp.float32)
    part_z = kept_z // groups_x
    cos_z, sin_z = twiddle(rows_z, modes_z, NZ)
    back_cos = cos_z * fold_weight[None, :]
    back_sin = sin_z * fold_weight[None, :]
    real_part = contract("yxz,zk->ykx", spread_grid, cos_z)
    imag_part = -contract("yxz,zk->ykx", spread_grid, sin_z)
    pencils = lax.all_to_all(
        jnp.stack([real_part, imag_part]), "gx", split_axis=2, concat_axis=3, tiled=True
    )
    extended = jnp.arange(groups_x * window_x, dtype=jnp.int32)
    place_x = extended // window_x * width_x + extended % window_x
    modes_x = jnp.arange(NX, dtype=jnp.int32)
    cos_x, sin_x = twiddle(place_x, modes_x, NX)
    real_part, imag_part = forward_pair("ykx,xm->ykm", pencils[0], pencils[1], cos_x, sin_x)
    fold_x = (modes_x + NX // 2) % NX - NX // 2
    rows_y = slab_index * CY + jnp.arange(depth_y, dtype=jnp.int32)
    tick_count = rows_y[:, None] * shear_step * fold_x[None, :] % (NX * total_y)
    angles = 2.0 * math.pi / (NX * total_y) * tick_count.astype(jnp.float32)
    cos_t = jnp.cos(angles)[:, None, :]
    sin_t = jnp.sin(angles)[:, None, :]
    twisted = jnp.stack(
        [real_part * cos_t + imag_part * sin_t, imag_part * cos_t - real_part * sin_t]
    )
    gathered = lax.all_to_all(twisted, "gy", split_axis=3, concat_axis=1, tiled=True)
    ext_y = jnp.arange(groups_y * depth_y, dtype=jnp.int32)
    place_y = ext_y // depth_y * CY + ext_y % depth_y
    modes_y = jnp.arange(total_y, dtype=jnp.int32)
    cos_y, sin_y = twiddle(place_y, modes_y, total_y)
    spectrum_real, spectrum_imag = forward_pair(
        "yzm,yn->nzm", gathered[0], gathered[1], cos_y, sin_y
    )
    index_z = pencil_index * part_z + jnp.arange(part_z, dtype=jnp.int32)
    index_x = slab_index * part_x + jnp.arange(part_x, dtype=jnp.int32)
    green_k = green_values(
        index_x[None, None, :],
        modes_y[:, None, None],
        index_z[None, :, None],
        shear_step,
        NX,
        total_y,
        NZ,
    )
    own_weight = lax.dynamic_slice_in_dim(fold_weight, pencil_index * part_z, part_z)
    local_energy = (
        0.5
        / (NX * total_y * NZ)
        * jnp.sum(
            green_k
            * own_weight[None, :, None]
            * (spectrum_real * spectrum_real + spectrum_imag * spectrum_imag)
        )
    )
    energy = lax.psum(local_energy, ("gy", "gx"))
    scaled = green_k / (NX * total_y * NZ)
    back_real, back_imag = inverse_pair(
        "nzm,yn->yzm", scaled * spectrum_real, scaled * spectrum_imag, cos_y, sin_y
    )
    returned = lax.all_to_all(
        jnp.stack([back_real, back_imag]), "gy", split_axis=1, concat_axis=3, tiled=True
    )
    plain_real = returned[0] * cos_t - returned[1] * sin_t
    plain_imag = returned[1] * cos_t + returned[0] * sin_t
    line_real, line_imag = inverse_pair("ykm,xm->ykx", plain_real, plain_imag, cos_x, sin_x)
    arrived_x = lax.all_to_all(
        jnp.stack([line_real, line_imag]), "gx", split_axis=3, concat_axis=2, tiled=True
    )
    potential = contract("ykx,zk->yxz", arrived_x[0], back_cos) - contract(
        "ykx,zk->yxz", arrived_x[1], back_sin
    )
    charge_parts = []
    dipole_parts = []
    position_parts = []
    atom_energy = jnp.zeros((), jnp.float32)
    for b in range(blocks):
        planar, dense_z, live_slots, charge_live, dipole_live = block_store[b]
        window_cells = potential[:, b * BX : b * BX + block_x, :].reshape(depth_y * block_x, NZ)
        projected = contract("cz,daz->dac", window_cells, dense_z)
        sampled = [jnp.sum(planar[p, r] * projected[s], axis=1) for p, r, s in combos]
        field = jnp.stack(sampled[1:4])
        charge_parts.append(live_slots * sampled[0])
        dipole_parts.append(live_slots[None, :] * field)
        force_x = (
            charge_live * sampled[1]
            + dipole_live[0] * sampled[4]
            + dipole_live[1] * sampled[7]
            + dipole_live[2] * sampled[8]
        )
        force_y = (
            charge_live * sampled[2]
            + dipole_live[0] * sampled[7]
            + dipole_live[1] * sampled[5]
            + dipole_live[2] * sampled[9]
        )
        force_z = (
            charge_live * sampled[3]
            + dipole_live[0] * sampled[8]
            + dipole_live[1] * sampled[9]
            + dipole_live[2] * sampled[6]
        )
        position_parts.append(live_slots[None, :] * jnp.stack([force_x, force_y, force_z]))
        atom_energy = atom_energy + 0.5 * jnp.sum(
            charge_live * sampled[0] + jnp.sum(dipole_live * field, axis=0)
        )
    charge_grad = jnp.concatenate(charge_parts, axis=0)
    dipole_grad = jnp.concatenate(dipole_parts, axis=1)
    position_grad = jnp.concatenate(position_parts, axis=1)
    return (charge_grad, dipole_grad, position_grad, jnp.reshape(energy, (1,)))


def solution(mesh):
    placed = (
        P(None, ("gy", "gx")),
        P(None, ("gy", "gx")),
        P(("gy", "gx")),
        P(None, ("gy", "gx")),
        P(("gy", "gx")),
        P(),
    )
    return jax.shard_map(
        on_device,
        mesh=mesh,
        in_specs=placed,
        out_specs=(P(("gy", "gx")), P(None, ("gy", "gx")), P(None, ("gy", "gx")), P()),
        check_vma=False,
    )
```

profile of v0, /device:TPU:1, one launch (start us, length us, event | category | flops | bytes accessed | tf_op | source)
XLA Modules:
  0.0 754.3 jit_solution(6017972487313349901)
XLA Ops:
  25.7 5.4 slice_select_fusion
  60.5 5.2 scatter-add.21
  65.7 4.8 scatter-add.24
  70.6 4.8 scatter-add.25
  75.4 4.3 scatter-add.26
  79.8 5.9 negate_bitcast_fusion
  85.7 6.2 convolution_bitcast_fusion
  92.4 5.7 copy.180
  98.1 8.0 %all-to-all-start = ((f32[2,11,360,101]{3,0,1,2:T(2,128)}), f32[2,11,360,101]{3,0,1,2:T(2,128)}, u32[]{:S(2)}, u32[]{:S(2)}) async-start(f32[2,11,360,101]{3,0,1,2:T(2,128)} %copy.180), calls=%async_computation | async-start | bytes 8110080 | tf_op jit(solution)/shard_map/all_to_all | solution.py:186
  107.0 46.5 %all-to-all-done = f32[2,11,360,101]{3,0,1,2:T(2,128)} async-done(((f32[2,11,360,101]{3,0,1,2:T(2,128)}), f32[2,11,360,101]{3,0,1,2:T(2,128)}, u32[]{:S(2)}, u32[]{:S(2)}) %all-to-all-start) | async-done | bytes 3199712 | tf_op jit(solution)/shard_map/all_to_all | solution.py:186
  153.5 9.0 %copy.267 = f32[2,11,4,90,101]{3,2,4,1,0:T(4,128)} copy(f32[2,11,4,90,101]{4,0,1,3,2:T(2,128)} %bitcast.195) | data formatting | bytes 6399360 | tf_op jit(solution)/shard_map/all_to_all | solution.py:186
  162.5 4.0 fusion.481
  171.8 4.1 copy.182
  179.2 6.0 fusion.39
  185.2 6.0 fusion.41
  191.2 6.2 convolution_subtract_fusion.1
  197.4 6.3 add_bitcast_fusion.2
  203.9 5.6 copy.184
  209.5 11.4 %all-to-all-start.1 = ((f32[2,11,90,384]{2,0,1,3:T(2,128)}), f32[2,11,90,384]{2,0,1,3:T(2,128)}, u32[]{:S(2)}, u32[]{:S(2)}) async-start(f32[2,11,90,384]{2,0,1,3:T(2,128)} %copy.184), calls=%async_computation.1 | async-start | bytes 8650752 | tf_op jit(solution)/shard_map/all_to_all | solution.py:203
  221.5 93.2 %all-to-all-done.1 = f32[2,11,90,384]{2,0,1,3:T(2,128)} async-done(((f32[2,11,90,384]{2,0,1,3:T(2,128)}), f32[2,11,90,384]{2,0,1,3:T(2,128)}, u32[]{:S(2)}, u32[]{:S(2)}) %all-to-all-start.1) | async-done | bytes 3041312 | tf_op jit(solution)/shard_map/all_to_all | solution.py:203
  314.7 4.2 copy.185
  318.9 5.7 fusion.483
  332.2 9.8 %fusion.12 = f32[384,90,6]{0,1,2:T(8,128)S(1)} fusion(f32[704,90,6]{1,0,2:T(8,128)} %squeeze.111, s32[704]{0:T(1024)S(1)} %fusion.347), kind=kOutput, calls=%fused_computation.35 | convolution fusion | flops 1754210304 | bytes 2352896 | tf_op jit(solution)/shard_map/yzm,yn->nzm/dot_general | solution.py:105
  342.0 8.2 %fusion.8 = f32[384,90,6]{0,1,2:T(8,128)S(1)} fusion(f32[704,90,6]{1,0,2:T(8,128)S(1)} %copy-done.1, s32[704]{0:T(1024)S(1)} %fusion.347), kind=kOutput, calls=%fused_computation.31 | convolution fusion | flops 1754210304 | bytes 2352896 | tf_op jit(solution)/shard_map/yzm,yn->nzm/dot_general | solution.py:105
  350.2 8.1 %convolution_add_fusion.1 = f32[384,90,6]{0,1,2:T(8,128)S(1)} fusion(f32[384,90,6]{0,1,2:T(8,128)S(1)} %fusion.12, f32[704,90,6]{1,0,2:T(8,128)S(1)} %copy-done.1, s32[704]{0:T(1024)S(1)} %fusion.347), kind=kOutput, calls=%fused_computation.20 | convolution fusion | flops 1754417664 | bytes 3182336 | tf_op jit(solution)/shard_map/yzm,yn->nzm/dot_general | solution.py:105
  358.3 7.7 %fusion.10 = f32[704,90,6]{0,1,2:T(8,128)S(1)} fusion(s32[704]{0:T(1024)S(1)} %fusion.347, f32[384,90,6]{0,1,2:T(8,128)S(1)} %convolution_add_fusion.1, f32[90]{0:T(128)S(1)} %get-tuple-element.1314, f32[384,6]{0,1:T(8,128)S(1)} %get-tuple-element.979, f32[90]{0:T(128)S(1)} %get-tuple-element.1315, f32[384,6]{0,1:T(8,128)S(1)} %get-tuple-element.978, ...), kind=kOutput, calls=%fused_computation.33 | convolution fusion | flops 1757113344 | bytes 2376836 | tf_op jit(solution)/shard_map/nzm,yn->yzm/dot_general | solution.py:105
  366.1 9.7 %multiply_reduce_fusion = (f32[]{:T(128)}, f32[384,90,6]{0,1,2:T(8,128)S(1)}) fusion(f32[384,90,6]{0,1,2:T(8,128)S(1)} %convolution_add_fusion.1, f32[90]{0:T(128)S(1)} %get-tuple-element.1314, f32[384,6]{0,1:T(8,128)S(1)} %get-tuple-element.979, f32[90]{0:T(128)S(1)} %get-tuple-element.1315, f32[384,6]{0,1:T(8,128)S(1)} %get-tuple-element.978, ...), kind=kOutput, calls=%fused_computation.46 | convolution fusion | flops 1757942784 | bytes 4035720 | tf_op jit(solution)/shard_map/yzm,yn->nzm/dot_general | solution.py:105
  375.8 7.5 fusion.6
  383.3 7.8 %add_bitcast_fusion.1 = f32[1,704,90,6]{1,2,3,0:T(8,128)S(1)} fusion(f32[704,90,6]{0,1,2:T(8,128)S(1)} %fusion.6, s32[704]{0:T(1024)S(1)} %fusion.347, f32[384,90,6]{0,1,2:T(8,128)S(1)} %convolution_add_fusion.1, f32[90]{0:T(128)S(1)} %get-tuple-element.1314, f32[384,6]{0,1:T(8,128)S(1)} %get-tuple-element.979, f32[90]{0:T(128)S(1)} %get-tuple-element.1315, ...), kind=kOutput, calls=%fused_computation.6 | convolution fusion | flops 1757493504 | bytes 3897476 | tf_op jit(solution)/shard_map/nzm,yn->yzm/dot_general | solution.py:105
  391.1 7.9 %subtract_bitcast_fusion.1 = f32[1,704,90,6]{1,2,3,0:T(8,128)S(1)} fusion(f32[704,90,6]{0,1,2:T(8,128)S(1)} %fusion.10, s32[704]{0:T(1024)S(1)} %fusion.347, f32[384,90,6]{0,1,2:T(8,128)S(1)} %get-tuple-element.1215, f32[90]{0:T(128)S(1)} %get-tuple-element.1314, f32[384,6]{0,1:T(8,128)S(1)} %get-tuple-element.979, f32[90]{0:T(128)S(1)} %get-tuple-element.1315, ...), kind=kOutput, calls=%fused_computation.7 | convolution fusion | flops 1757493504 | bytes 3897476 | tf_op jit(solution)/shard_map/nzm,yn->yzm/dot_general | solution.py:105
  399.3 5.3 copy.192
  404.6 110.9 %all_to_all.60 = f32[2,704,90,6]{2,0,3,1:T(2,128)S(1)} all-to-all(f32[2,704,90,6]{2,0,3,1:T(2,128)} %copy.192), channel_id=1, replica_groups=mesh['gy'=64,'gx'=4] {'gy'}, dimensions={1} | all-to-all | bytes 6082560 | tf_op jit(solution)/shard_map/all_to_all | solution.py:237
  515.5 4.7 fusion.482
  524.3 3.5 copy.193
  527.7 3.6 squeeze.113
  534.2 6.0 fusion.35
  540.2 6.4 fusion.37
  546.6 6.0 add_bitcast_fusion
  552.6 6.0 subtract_bitcast_fusion
  561.4 9.1 %copy.199 = f32[2,11,90,404]{2,0,1,3:T(2,128)} copy(f32[2,11,90,404]{3,2,1,0:T(8,128)} %pad_maximum_fusion) | data formatting | bytes 6399360 | tf_op jit(solution)/shard_map/stack | solution.py:244
  570.6 7.4 all-to-all-start.3
  603.3 92.1 %psum.7 = f32[1]{0:T(128)} all-reduce(f32[1]{0:T(128)} %bitcast.280), channel_id=1, replica_groups=mesh['gy'=64,'gx'=4] {'gy','gx'}, use_global_device_ids=true, to_apply=%region_61.62 | all-reduce | flops 1 | bytes 8 | tf_op jit(solution)/shard_map/psum | solution.py:232
  695.4 8.9 %copy.268 = f32[2,11,90,4,101]{4,3,0,2,1:T(4,128)} copy(f32[2,11,90,4,101]{2,0,1,4,3:T(2,128)} %bitcast.212) | data formatting | bytes 6399360 | tf_op jit(solution)/shard_map/all_to_all | solution.py:243
  704.3 4.4 fusion.484
  708.7 3.5 copy.202
  715.0 3.9 copy.201
  721.7 7.5 fusion.60
  729.2 6.2 convolution_subtract_fusion
  (889 shorter events, 126.7 us)
Async XLA Ops:
  0.6 32.9 %copy-start.77 = (f32[3,384]{1,0:T(4,128)S(1)}, f32[3,384]{1,0:T(4,128)}, u32[]{:S(2)}) copy-start(f32[3,384]{1,0:T(4,128)} %param.19) | copy-start | bytes 13828
  22.5 22.6 %copy-start.162 = (f32[64]{0:T(128)}, f32[64]{0:T(128)S(1)}, u32[]{:S(2)}) copy-start(f32[64]{0:T(128)S(1)} %fusion.366) | copy-start | bytes 772
  23.2 21.9 %copy-start.158 = (f32[64]{0:T(128)}, f32[64]{0:T(128)S(1)}, u32[]{:S(2)}) copy-start(f32[64]{0:T(128)S(1)} %fusion.370) | copy-start | bytes 772
  23.9 21.2 %copy-start.156 = (f32[64]{0:T(128)}, f32[64]{0:T(128)S(1)}, u32[]{:S(2)}) copy-start(f32[64]{0:T(128)S(1)} %fusion.372) | copy-start | bytes 772
  24.5 20.6 %copy-start.154 = (f32[64]{0:T(128)}, f32[64]{0:T(128)S(1)}, u32[]{:S(2)}) copy-start(f32[64]{0:T(128)S(1)} %fusion.374) | copy-start | bytes 772
  25.2 20.0 %copy-start.152 = (f32[64]{0:T(128)}, f32[64]{0:T(128)S(1)}, u32[]{:S(2)}) copy-start(f32[64]{0:T(128)S(1)} %fusion.376) | copy-start | bytes 772
  25.7 19.4 %copy-start.160 = (f32[64]{0:T(128)}, f32[64]{0:T(128)S(1)}, u32[]{:S(2)}) copy-start(f32[64]{0:T(128)S(1)} %fusion.368) | copy-start | bytes 772
  31.1 15.3 %copy-start.133 = (f32[64]{0:T(128)}, f32[64]{0:T(128)S(1)}, u32[]{:S(2)}) copy-start(f32[64]{0:T(128)S(1)} %get-tuple-element.990) | copy-start | bytes 772
  40.3 6.2 copy-start.3
  40.8 16.7 %copy-start.9 = (f32[3,64,360]{2,1,0:T(8,128)}, f32[3,64,360]{2,1,0:T(8,128)S(1)}, u32[]{:S(2)}) copy-start(f32[3,64,360]{2,1,0:T(8,128)S(1)} %multiply_add_fusion.3) | copy-start | bytes 829444
  41.3 9.1 %copy-start.5 = (f32[3,64,360]{2,1,0:T(8,128)}, f32[3,64,360]{2,1,0:T(8,128)S(1)}, u32[]{:S(2)}) copy-start(f32[3,64,360]{2,1,0:T(8,128)S(1)} %multiply_add_fusion.6) | copy-start | bytes 829444
  41.8 6.4 copy-start.11
  42.4 12.8 %copy-start.7 = (f32[3,64,360]{2,1,0:T(8,128)}, f32[3,64,360]{2,1,0:T(8,128)S(1)}, u32[]{:S(2)}) copy-start(f32[3,64,360]{2,1,0:T(8,128)S(1)} %multiply_add_fusion.8) | copy-start | bytes 829444
  43.5 9.5 %copy-start.13 = (f32[3,64,360]{2,1,0:T(8,128)}, f32[3,64,360]{2,1,0:T(8,128)S(1)}, u32[]{:S(2)}) copy-start(f32[3,64,360]{2,1,0:T(8,128)S(1)} %multiply_add_fusion.7) | copy-start | bytes 829444
  70.6 9.1 %copy-start.16 = (f32[11,21,360]{2,1,0:T(8,128)S(1)}, f32[11,21,360]{2,1,0:T(8,128)}, u32[]{:S(2)}) copy-start(f32[11,21,360]{2,1,0:T(8,128)} %reshape.4064) | copy-start | bytes 997924
  98.1 55.4 %all-to-all-start = ((f32[2,11,360,101]{3,0,1,2:T(2,128)}), f32[2,11,360,101]{3,0,1,2:T(2,128)}, u32[]{:S(2)}, u32[]{:S(2)}) async-start(f32[2,11,360,101]{3,0,1,2:T(2,128)} %copy.180), calls=%async_computation | async-start | bytes 8110080 | tf_op jit(solution)/shard_map/all_to_all | solution.py:186
  107.0 90.4 %copy-start.53 = (f32[11,384]{1,0:T(8,128)}, f32[11,384]{1,0:T(8,128)S(1)}, u32[]{:S(2)}) copy-start(f32[11,384]{1,0:T(8,128)S(1)} %get-tuple-element.980) | copy-start | bytes 50692
  107.0 90.4 %copy-start.55 = (f32[11,384]{1,0:T(8,128)}, f32[11,384]{1,0:T(8,128)S(1)}, u32[]{:S(2)}) copy-start(f32[11,384]{1,0:T(8,128)S(1)} %get-tuple-element.981) | copy-start | bytes 50692
  209.5 105.2 %all-to-all-start.1 = ((f32[2,11,90,384]{2,0,1,3:T(2,128)}), f32[2,11,90,384]{2,0,1,3:T(2,128)}, u32[]{:S(2)}, u32[]{:S(2)}) async-start(f32[2,11,90,384]{2,0,1,3:T(2,128)} %copy.184), calls=%async_computation.1 | async-start | bytes 8650752 | tf_op jit(solution)/shard_map/all_to_all | solution.py:203
  332.2 9.8 %copy-start.1 = (f32[704,90,6]{1,0,2:T(8,128)S(1)}, f32[704,90,6]{1,0,2:T(8,128)}, u32[]{:S(2)}) copy-start(f32[704,90,6]{1,0,2:T(8,128)} %squeeze.112) | copy-start | bytes 4561924
  358.3 7.8 %copy-start.15 = (f32[704,90,6]{1,0,2:T(8,128)S(1)}, f32[704,90,6]{1,0,2:T(8,128)}, u32[]{:S(2)}) copy-start(f32[704,90,6]{1,0,2:T(8,128)} %squeeze.111) | copy-start | bytes 4561924
  570.5 7.5 copy-start.30
  570.5 8.3 %copy-start.18 = (f32[64,231]{0,1:T(8,128)S(1)}, f32[64,231]{0,1:T(8,128)}, u32[]{:S(2)}) copy-start(f32[64,231]{0,1:T(8,128)} %copy-done.17) | copy-start | bytes 177412
  570.5 9.0 %copy-start.32 = (f32[64,231]{0,1:T(8,128)S(1)}, f32[64,231]{0,1:T(8,128)}, u32[]{:S(2)}) copy-start(f32[64,231]{0,1:T(8,128)} %copy-done.31) | copy-start | bytes 177412
  570.5 9.7 %copy-start.34 = (f32[64,231]{0,1:T(8,128)S(1)}, f32[64,231]{0,1:T(8,128)}, u32[]{:S(2)}) copy-start(f32[64,231]{0,1:T(8,128)} %copy-done.33) | copy-start | bytes 177412
  570.5 10.4 %copy-start.20 = (f32[64,231]{0,1:T(8,128)S(1)}, f32[64,231]{0,1:T(8,128)}, u32[]{:S(2)}) copy-start(f32[64,231]{0,1:T(8,128)} %copy-done.19) | copy-start | bytes 177412
  570.5 11.1 %copy-start.36 = (f32[64,231]{0,1:T(8,128)S(1)}, f32[64,231]{0,1:T(8,128)}, u32[]{:S(2)}) copy-start(f32[64,231]{0,1:T(8,128)} %copy-done.35) | copy-start | bytes 177412
  570.5 11.8 %copy-start.38 = (f32[64,231]{0,1:T(8,128)S(1)}, f32[64,231]{0,1:T(8,128)}, u32[]{:S(2)}) copy-start(f32[64,231]{0,1:T(8,128)} %copy-done.37) | copy-start | bytes 177412
  570.5 12.5 %copy-start.22 = (f32[64,231]{0,1:T(8,128)S(1)}, f32[64,231]{0,1:T(8,128)}, u32[]{:S(2)}) copy-start(f32[64,231]{0,1:T(8,128)} %copy-done.21) | copy-start | bytes 177412
  570.5 13.2 %copy-start.40 = (f32[64,231]{0,1:T(8,128)S(1)}, f32[64,231]{0,1:T(8,128)}, u32[]{:S(2)}) copy-start(f32[64,231]{0,1:T(8,128)} %copy-done.39) | copy-start | bytes 177412
  570.6 124.9 %all-to-all-start.3 = ((f32[2,11,90,404]{2,0,1,3:T(2,128)}), f32[2,11,90,404]{2,0,1,3:T(2,128)}, u32[]{:S(2)}, u32[]{:S(2)}) async-start(f32[2,11,90,404]{2,0,1,3:T(2,128)} %copy.199), calls=%async_computation.3 | async-start | bytes 9101312 | tf_op jit(solution)/shard_map/all_to_all | solution.py:243
  578.0 6.4 copy-start.42
  578.0 7.1 copy-start.24
  578.0 7.8 %copy-start.44 = (f32[64,231]{0,1:T(8,128)S(1)}, f32[64,231]{0,1:T(8,128)}, u32[]{:S(2)}) copy-start(f32[64,231]{0,1:T(8,128)} %copy-done.43) | copy-start | bytes 177412
  578.0 8.5 %copy-start.46 = (f32[64,231]{0,1:T(8,128)S(1)}, f32[64,231]{0,1:T(8,128)}, u32[]{:S(2)}) copy-start(f32[64,231]{0,1:T(8,128)} %copy-done.45) | copy-start | bytes 177412
  578.0 8.6 %copy-start.26 = (f32[64,231]{0,1:T(8,128)S(1)}, f32[64,231]{0,1:T(8,128)}, u32[]{:S(2)}) copy-start(f32[64,231]{0,1:T(8,128)} %copy-done.25) | copy-start | bytes 177412
  578.0 8.7 %copy-start.48 = (f32[64,231]{0,1:T(8,128)S(1)}, f32[64,231]{0,1:T(8,128)}, u32[]{:S(2)}) copy-start(f32[64,231]{0,1:T(8,128)} %copy-done.47) | copy-start | bytes 177412
  578.0 9.4 %copy-start.50 = (f32[64,231]{0,1:T(8,128)S(1)}, f32[64,231]{0,1:T(8,128)}, u32[]{:S(2)}) copy-start(f32[64,231]{0,1:T(8,128)} %copy-done.49) | copy-start | bytes 177412
  578.0 10.1 %copy-start.28 = (f32[64,231]{0,1:T(8,128)S(1)}, f32[64,231]{0,1:T(8,128)}, u32[]{:S(2)}) copy-start(f32[64,231]{0,1:T(8,128)} %copy-done.27) | copy-start | bytes 177412
  578.1 10.8 %copy-start.52 = (f32[64,231]{0,1:T(8,128)S(1)}, f32[64,231]{0,1:T(8,128)}, u32[]{:S(2)}) copy-start(f32[64,231]{0,1:T(8,128)} %copy-done.51) | copy-start | bytes 177412
  578.1 11.5 %copy-start.59 = (f32[64,11,21]{0,2,1:T(8,128)S(1)}, f32[64,11,21]{0,2,1:T(8,128)}, u32[]{:S(2)}) copy-start(f32[64,11,21]{0,2,1:T(8,128)} %get-tuple-element.475) | copy-start | bytes 177412
  580.2 10.1 %copy-start.58 = (f32[64,11,21]{0,2,1:T(8,128)S(1)}, f32[64,11,21]{0,2,1:T(8,128)}, u32[]{:S(2)}) copy-start(f32[64,11,21]{0,2,1:T(8,128)} %get-tuple-element.625) | copy-start | bytes 177412
  581.6 9.4 %copy-start.57 = (f32[64,11,21]{0,2,1:T(8,128)S(1)}, f32[64,11,21]{0,2,1:T(8,128)}, u32[]{:S(2)}) copy-start(f32[64,11,21]{0,2,1:T(8,128)} %get-tuple-element.627) | copy-start | bytes 177412
  583.7 8.0 %copy-start.62 = (f32[64,11,21]{0,2,1:T(8,128)S(1)}, f32[64,11,21]{0,2,1:T(8,128)}, u32[]{:S(2)}) copy-start(f32[64,11,21]{0,2,1:T(8,128)} %get-tuple-element.480) | copy-start | bytes 177412
  585.1 7.4 copy-start.61
  586.5 6.7 copy-start.60
  587.4 6.5 copy-start.65
  721.7 7.5 copy-start.2
  (120 other events, 331.8 us)
where the time goes:
time: 766 us; the launch traced here: 754 us
  blocking collectives  203 us (27%)
  local copies, waits for them, and re-layouts  173 us (23%)
  matrix products  148 us (19%)
  waiting for transfers between devices  140 us (18%)
  other arithmetic  55.8 us (7%)
  starting transfers between devices  26.8 us (3%)
    dot_general x32, matrix products, contract(): return jnp.einsum(pattern, operand, matrix, precision=lax.Precision.HIGHEST)  148 us
    all_to_all x1, blocking collectives, on_device(): lax.all_to_all(jnp.stack([back_real, back_imag]), 'gy', split_axis=1, con...  111 us
    all_to_all x1, waiting for transfers between devices, on_device(): lax.all_to_all(twisted, 'gy', split_axis=3, concat_axis=1, tiled=True)  93.2 us
    psum x1, blocking collectives, on_device(): energy = lax.psum(local_energy, ('gy', 'gx'))  92.1 us
    all_to_all x1, waiting for transfers between devices, on_device(): lax.all_to_all(jnp.stack([real_part, imag_part]), 'gx', split_axis=2, con...  46.5 us
    mul x84, local copies, waits for them, and re-layouts, on_device(): dense_y[r][:, :, None] * dense_x[p][:, None, :]  28.2 us
    scatter-add x5, local copies, waits for them, and re-layouts, on_device(): spread_grid = spread_grid.at[:, b * BX:b * BX + block_x, :].add(block_grid)  19.1 us
  transfers between devices with their start and end apart: 3, of which 2 were waited for; matrix products, arithmetic and copies ran while one was open for 3% of the time, Pallas kernels for 0%

commit v1 on v0

v1 whole, which is shorter than its diff:
```python
import math

import jax
import jax.numpy as jnp
import ml_dtypes
import numpy as np
from jax import lax
from jax.experimental import pallas as pl
from jax.experimental.pallas import tpu as pltpu
from jax.sharding import PartitionSpec as P

NX = 384
NY = 384
NZ = 360
CY = 6
CX = 96
PENCILS = 4
SLABS = 64
PART_X = 6
PART_Z = 45
ATOM_BLK = 64
ATOM_DEV = 384
PAIRS = 3
WINDOW = 40
ROWS = 11
HALF = 64
LANES = 128
PADDED_Z = 48
screening = 0.9
f32 = jnp.float32
bf16 = jnp.bfloat16


def split_table(table):
    high = table.astype(ml_dtypes.bfloat16)
    low = (table - high.astype(np.float64)).astype(ml_dtypes.bfloat16)
    return high, low


def wave_tables():
    natural = np.arange(NX)
    angle_x = 2.0 * np.pi / NX * (natural[:, None] * natural[None, :] % NX)
    table_x = np.concatenate([np.cos(angle_x), np.sin(angle_x)], axis=1)
    place_y = np.arange(NY) % SLABS * CY + np.arange(NY) // SLABS
    angle_y = 2.0 * np.pi / NY * (natural[:, None] * place_y[None, :] % NY)
    forward_y = np.concatenate([np.cos(angle_y), np.sin(angle_y)], axis=1)
    inverse_y = np.concatenate([np.cos(angle_y.T), np.sin(angle_y.T)], axis=1)
    return split_table(table_x), split_table(forward_y), split_table(inverse_y)


def spline_rows(fraction):
    levels = {2: [1.0 - fraction, fraction]}
    current = levels[2]
    for n in range(3, 7):
        inverse_n = 1.0 / (n - 1)
        updated = [None] * n
        updated[n - 1] = inverse_n * fraction * current[n - 2]
        for j in range(1, n - 1):
            updated[n - 1 - j] = inverse_n * (
                (fraction + j) * current[n - 2 - j] + (n - j - fraction) * current[n - 1 - j]
            )
        updated[0] = inverse_n * (1.0 - fraction) * current[0]
        current = updated
        levels[n] = current
    zero_row = jnp.zeros_like(fraction)

    def entry_at(values_list, k):
        return values_list[k] if 0 <= k < len(values_list) else zero_row

    first = [entry_at(levels[5], t - 1) - entry_at(levels[5], t) for t in range(6)]
    second = [
        entry_at(levels[4], t - 2) - 2.0 * entry_at(levels[4], t - 1) + entry_at(levels[4], t)
        for t in range(6)
    ]
    return levels[6], first, second


def dense_rows(tables, cell, length):
    away = lax.broadcasted_iota(jnp.int32, (length, cell.shape[1]), 0).astype(f32) - cell
    summed = [jnp.zeros(away.shape, f32) for _ in tables]
    for t in range(6):
        here = away == float(t)
        summed = [jnp.where(here, table[t], so_far) for table, so_far in zip(tables, summed)]
    return summed


def unit_phase(turns):
    turns = turns - jnp.floor(turns + 0.5)
    quarter = jnp.floor(4.0 * turns + 0.5)
    rest = turns - 0.25 * quarter
    theta = (2.0 * math.pi) * rest
    square = theta * theta
    sine = theta * (
        1.0
        + square
        * (-1.0 / 6 + square * (1.0 / 120 + square * (-1.0 / 5040 + square * (1.0 / 362880))))
    )
    cosine = 1.0 + square * (
        -0.5
        + square
        * (1.0 / 24 + square * (-1.0 / 720 + square * (1.0 / 40320 - square * (1.0 / 3628800))))
    )
    odd = jnp.abs(quarter) == 1.0
    cos_out = jnp.where(odd, sine, cosine)
    sin_out = jnp.where(odd, cosine, sine)
    cos_out = jnp.where((quarter == 1.0) | (jnp.abs(quarter) == 2.0), -cos_out, cos_out)
    sin_out = jnp.where((quarter == -1.0) | (jnp.abs(quarter) == 2.0), -sin_out, sin_out)
    return cos_out, sin_out


def halves(value):
    high = value.astype(bf16)
    return high, (value - high.astype(f32)).astype(bf16)


def product(left, right, dims=((1,), (0,))):
    def one(a, b):
        return lax.dot_general(a, b, (dims, ((), ())), preferred_element_type=f32)

    return one(left[0], right[0]) + (one(left[0], right[1]) + one(left[1], right[0]))


def lane_sign(shape):
    return jnp.where(lax.broadcasted_iota(jnp.int32, shape, 1) < HALF, 1.0, -1.0).astype(f32)


def turned(value, sign):
    return pltpu.roll(value, HALF, 1) * sign


def atom_weights(atoms, lanes):
    offset = [atoms[3 + a : 4 + a, lanes] for a in range(3)]
    return [spline_rows(one) for one in offset]


def spread_kernel(
    atoms_ref, base_ref, taps_ref, high_ref, low_ref, cos_ref, sin_ref, out_ref, waves_ref, grid_ref
):
    grid_ref[...] = jnp.zeros_like(grid_ref)
    part = ROWS * LANES
    gap = jnp.zeros((HALF - PADDED_Z, LANES), f32)
    for own in (True, False):
        rows = list(range(CY)) if own else list(range(CY, ROWS))
        start = 0 if own else PENCILS

        def pencil_body(pencil, carry, rows=rows, start=start):
            for i in range(PAIRS):
                atoms = atoms_ref[start + pencil, :, i * LANES : (i + 1) * LANES]
                row = [atoms[a : a + 1] for a in range(10)]
                weights = [spline_rows(row[3 + a]) for a in range(3)]
                charge, dip_x, dip_y, dip_z = row[6:10]
                window = pencil * CX + i * 32
                dense_x = dense_rows(weights[0][:2], row[0] - window.astype(f32), WINDOW)
                dense_y = dense_rows(weights[1][:2], row[1], 16)
                cell_z = row[2]
                turn = base_ref[...] * cell_z
                turn = turn - 360.0 * jnp.floor(turn * (1.0 / 360.0))
                cos_k, sin_k = unit_phase(turn * (1.0 / 360.0))
                turn = 8.0 * cell_z
                turn = turn - 360.0 * jnp.floor(turn * (1.0 / 360.0))
                cos_8, sin_8 = unit_phase(turn * (1.0 / 360.0))
                pieces = [[], [], []]
                pieces_im = [[], [], []]
                for q in range(PADDED_Z // 8):
                    span = slice(q * 8, q * 8 + 8)
                    for s in range(3):
                        real = sum(weights[2][s][t] * taps_ref[t, span, :] for t in range(6))
                        imag = sum(weights[2][s][t] * taps_ref[6 + t, span, :] for t in range(6))
                        pieces[s].append(real * cos_k - imag * sin_k)
                        pieces_im[s].append(-(real * sin_k + imag * cos_k))
                    cos_k, sin_k = cos_k * cos_8 - sin_k * sin_8, sin_k * cos_8 + cos_k * sin_8
                re = [jnp.concatenate(pieces[s], axis=0) for s in range(3)]
                im = [jnp.concatenate(pieces_im[s], axis=0) for s in range(3)]
                pair = (start + pencil) * PAIRS + i
                for s in range(3):
                    waves_ref[pair, s, :PADDED_Z] = re[s]
                    waves_ref[pair, s, PADDED_Z:] = im[s]
                full = []
                for wave_re, wave_im in (
                    (charge * re[0] + dip_z * re[1], charge * im[0] + dip_z * im[1]),
                    (re[0], im[0]),
                ):
                    full.append(
                        jnp.concatenate(
                            [wave_re, gap, wave_im, gap, wave_im, gap, -wave_re, gap], axis=0
                        )
                    )
                right = jnp.concatenate(full, axis=1)
                left = []
                for r in rows:
                    value = dense_y[0][r : r + 1]
                    first = dense_y[1][r : r + 1]
                    left.append(
                        jnp.concatenate(
                            [
                                value * dense_x[0],
                                (dip_x * value) * dense_x[1] + (dip_y * first) * dense_x[0],
                            ],
                            axis=1,
                        )
                    )
                left = jnp.concatenate(left, axis=0)
                added = product(halves(left), halves(right), ((1,), (1,)))
                at = pl.ds(pl.multiple_of(window, 8), WINDOW)
                for n, r in enumerate(rows):
                    piece = added[n * WINDOW : (n + 1) * WINDOW]
                    grid_ref[at, r * LANES : (r + 1) * LANES] += piece[:, :LANES]
                    grid_ref[at, part + r * LANES : part + (r + 1) * LANES] += piece[:, LANES:]
            return carry

        lax.fori_loop(0, PENCILS, pencil_body, 0)
    grid_ref[0:8] += grid_ref[NX : NX + 8]
    table = (high_ref[...], low_ref[...])
    sign = lane_sign((NX, LANES))
    for y in range(CY):
        rows = [y] if y == CY - 1 else [y, CY + y]
        spans = [slice(r * LANES, (r + 1) * LANES) for r in rows]
        top = jnp.concatenate([grid_ref[:NX, span] for span in spans], axis=1)
        low_spans = [slice(part + r * LANES, part + (r + 1) * LANES) for r in rows]
        bottom = jnp.concatenate([grid_ref[:NX, span] for span in low_spans], axis=1)
        line = product(table, halves(jnp.concatenate([top, bottom], axis=0)))
        total = jnp.zeros((NX, LANES), f32)
        for n, r in enumerate(rows):
            one = line[:, n * LANES : (n + 1) * LANES]
            total = total + one * cos_ref[:, r : r + 1] + turned(one, sign) * sin_ref[:, r : r + 1]
        for j in range(PART_X):
            at = (j * CY + y) * LANES
            out_ref[:, at : at + LANES] = total[j * SLABS : (j + 1) * SLABS]


def filter_kernel(
    in_ref, high_ref, low_ref, back_high_ref, back_low_ref, top_ref, norm_ref, mode_ref, out_ref, energy_ref
):
    forward = (high_ref[...], low_ref[...])
    inverse = (back_high_ref[...], back_low_ref[...])
    sign = lane_sign((NY, LANES))
    energy = jnp.zeros((8, LANES), f32)
    for first in range(0, PART_X, 2):
        lines = []
        for j in (first, first + 1):
            lines.append(
                jnp.concatenate(
                    [in_ref[:, (j * CY + y) * LANES : (j * CY + y + 1) * LANES] for y in range(CY)],
                    axis=0,
                )
            )
        stacked = jnp.concatenate(
            [
                jnp.concatenate([one, turned(one, sign)], axis=0)
                for one in lines
            ],
            axis=1,
        )
        spectrum = product(forward, halves(stacked))
        backs = []
        for n in range(2):
            j = first + n
            one = spectrum[:, n * LANES : (n + 1) * LANES]
            square = norm_ref[:, j : j + 1] + mode_ref[1:2, :]
            green = top_ref[:, j : j + 1] * mode_ref[0:1, :] / jnp.where(square == 0.0, 1.0, square)
            green = jnp.where(square == 0.0, 0.0, green)
            scaled = green * one
            share = scaled * one
            energy = energy + sum(share[8 * i : 8 * i + 8] for i in range(NY // 8))
            backs.append(jnp.concatenate([scaled, -turned(scaled, sign)], axis=0))
        potential = product(inverse, halves(jnp.concatenate(backs, axis=1)))
        for n in range(2):
            j = first + n
            for y in range(CY):
                at = (j * CY + y) * LANES
                out_ref[:, at : at + LANES] = potential[
                    y * SLABS : (y + 1) * SLABS, n * LANES : (n + 1) * LANES
                ]
    energy_ref[...] = energy


def sample_kernel(in_ref, atoms_ref, waves_ref, high_ref, low_ref, cos_ref, sin_ref, out_ref, grid_ref):
    table = (high_ref[...], low_ref[...])
    sign = lane_sign((NX, LANES))
    for y in range(CY):
        rows = [y] if y == CY - 1 else [y, CY + y]
        line = jnp.concatenate(
            [in_ref[:, (j * CY + y) * LANES : (j * CY + y + 1) * LANES] for j in range(PART_X)],
            axis=0,
        )
        swapped = turned(line, sign)
        stacked = []
        for r in rows:
            one = line * cos_ref[:, r : r + 1] - swapped * sin_ref[:, r : r + 1]
            stacked.append(jnp.concatenate([one, -turned(one, sign)], axis=0))
        cells = product(table, halves(jnp.concatenate(stacked, axis=1)))
        for n, r in enumerate(rows):
            piece = cells[:, n * LANES : (n + 1) * LANES]
            grid_ref[:NX, r * LANES : (r + 1) * LANES] = piece
            grid_ref[NX:, r * LANES : (r + 1) * LANES] = piece[:8]
    gap = jnp.zeros((HALF - PADDED_Z, LANES), f32)
    for own in (True, False):
        rows = list(range(CY)) if own else list(range(CY, ROWS))
        start = 0 if own else PENCILS

        def pencil_body(pencil, carry, rows=rows, start=start):
            for i in range(PAIRS):
                lanes = slice(i * LANES, (i + 1) * LANES)
                atoms = atoms_ref[start + pencil, :, lanes]
                row = [atoms[a : a + 1] for a in range(11)]
                weights = [spline_rows(row[3 + a]) for a in range(2)]
                window = pencil * CX + i * 32
                dense_x = dense_rows(weights[0], row[0] - window.astype(f32), WINDOW)
                dense_y = dense_rows(weights[1], row[1], 16)
                pair = (start + pencil) * PAIRS + i
                waves = jnp.concatenate(
                    [
                        jnp.concatenate(
                            [waves_ref[pair, s, :PADDED_Z], gap, waves_ref[pair, s, PADDED_Z:], gap],
                            axis=0,
                        )
                        for s in range(3)
                    ],
                    axis=1,
                )
                at = pl.ds(pl.multiple_of(window, 8), WINDOW)
                cells = jnp.concatenate(
                    [grid_ref[at, r * LANES : (r + 1) * LANES] for r in rows], axis=0
                )
                read = product(halves(cells), halves(waves))
                lined = {}
                for order_y, order_z in ((0, 0), (1, 0), (2, 0), (0, 1), (1, 1), (0, 2)):
                    lined[order_y, order_z] = sum(
                        dense_y[order_y][r : r + 1]
                        * read[
                            n * WINDOW : (n + 1) * WINDOW, order_z * LANES : (order_z + 1) * LANES
                        ]
                        for n, r in enumerate(rows)
                    )

                def sampled(p, r, s):
                    return jnp.sum(dense_x[p] * lined[r, s], axis=0, keepdims=True)

                charge, dip_x, dip_y, dip_z, live = row[6:11]
                s100 = sampled(1, 0, 0)
                s010 = sampled(0, 1, 0)
                s001 = sampled(0, 0, 1)
                s110 = sampled(1, 1, 0)
                s101 = sampled(1, 0, 1)
                s011 = sampled(0, 1, 1)
                out = [
                    live * sampled(0, 0, 0),
                    live * s100,
                    live * s010,
                    live * s001,
                    charge * s100 + dip_x * sampled(2, 0, 0) + dip_y * s110 + dip_z * s101,
                    charge * s010 + dip_x * s110 + dip_y * sampled(0, 2, 0) + dip_z * s011,
                    charge * s001 + dip_x * s101 + dip_y * s011 + dip_z * sampled(0, 0, 2),
                    jnp.zeros_like(live),
                ]
                out_ref[start + pencil, :, lanes] = jnp.concatenate(out, axis=0)
            return carry

        lax.fori_loop(0, PENCILS, pencil_body, 0)


def spline_modulus(angles):
    return (66.0 + 52.0 * jnp.cos(angles) + 2.0 * jnp.cos(2.0 * angles)) / 120.0


def folded(index, size):
    return (index + size // 2) % size - size // 2


def call(kernel, out_shape, scratch=(), **cost):
    return pl.pallas_call(
        kernel,
        out_shape=out_shape,
        scratch_shapes=list(scratch),
        compiler_params=pltpu.CompilerParams(vmem_limit_bytes=50 * 1024 * 1024),
        cost_estimate=pl.CostEstimate(transcendentals=0, **cost),
    )


def next_slab(value, back=False):
    step = -1 if back else 1
    return lax.ppermute(value, "gy", [(i, (i + step) % SLABS) for i in range(SLABS)])


def on_device(cell_index, offsets, charges, dipoles, block_count, shear_cells):
    pencil_index = lax.axis_index("gx")
    slab_index = lax.axis_index("gy")
    shear_step = shear_cells[0]
    (x_high, x_low), (y_high, y_low), (back_high, back_low) = wave_tables()

    slot = jnp.arange(ATOM_DEV, dtype=jnp.int32)
    counts = jnp.repeat(block_count, ATOM_BLK, total_repeat_length=ATOM_DEV)
    live = (slot % ATOM_BLK < counts).astype(f32)
    cells = cell_index - jnp.stack([0, slab_index * CY, 0])[:, None]
    mine = jnp.concatenate(
        [
            cells.astype(f32),
            offsets,
            (charges * live)[None],
            dipoles * live[None],
            live[None],
            jnp.zeros((5, ATOM_DEV), f32),
        ],
        axis=0,
    )
    slab_atoms = lax.all_gather(mine, "gx", axis=0, tiled=False)
    atoms = jnp.concatenate([slab_atoms, next_slab(slab_atoms)], axis=0)

    mode_z = pencil_index * PART_Z + jnp.arange(PADDED_Z, dtype=jnp.int32)
    kept = jnp.arange(PADDED_Z) < PART_Z
    ticks = jnp.arange(6, dtype=jnp.int32)[:, None] * mode_z[None, :] % NZ
    angles = 2.0 * math.pi / NZ * ticks.astype(f32)
    taps = jnp.concatenate([jnp.cos(angles), jnp.sin(angles)], axis=0) * kept[None, :]
    taps = jnp.broadcast_to(taps[:, :, None], (12, PADDED_Z, LANES))
    base = jnp.broadcast_to(mode_z[:8, None].astype(f32), (8, LANES))

    index_x = jnp.arange(NX, dtype=jnp.int32)
    above = (slab_index - 1) % SLABS * CY
    rows = jnp.arange(16, dtype=jnp.int32)
    rows = jnp.where(rows < CY, slab_index * CY + rows, above + rows)
    twist = folded(index_x, NX)[:, None] * shear_step * rows[None, :] % (NX * NY)
    angles = 2.0 * math.pi / (NX * NY) * twist.astype(f32)
    cos_t, sin_t = jnp.cos(angles), jnp.sin(angles)

    own_x = folded(jnp.arange(8, dtype=jnp.int32) * SLABS + slab_index, NX)[None, :]
    own_y = folded(jnp.arange(NY, dtype=jnp.int32), NY)[:, None]
    float_x = own_x.astype(f32)
    wave_y = own_y.astype(f32) + float_x * shear_step.astype(f32) / NX
    norm = (float_x / NX) ** 2 + (wave_y / NY) ** 2
    moduli = spline_modulus(2.0 * math.pi * float_x / NX) * spline_modulus(
        2.0 * math.pi * wave_y / NY
    )
    decay = (math.pi / screening) ** 2
    top = jnp.exp(-decay * norm) / (math.pi * moduli * moduli)
    top = jnp.where((own_x == -(NX // 2)) | (own_y == -(NY // 2)), 0.0, top)
    float_z = mode_z.astype(f32)
    norm_z = (float_z / NZ) ** 2
    modulus_z = spline_modulus(2.0 * math.pi * float_z / NZ)
    twice = jnp.where(mode_z == 0, 1.0, 2.0) / (NX * NY * NZ)
    mode_top = jnp.where(kept, twice * jnp.exp(-decay * norm_z) / (modulus_z * modulus_z), 0.0)
    mode_norm = jnp.where(kept, norm_z, 1.0)
    half_rows = jnp.stack([mode_top, mode_norm])
    half_rows = jnp.pad(half_rows, ((0, 6), (0, HALF - PADDED_Z)), constant_values=1.0)
    half_rows = half_rows.at[0, PADDED_Z:].set(0.0)
    mode = jnp.concatenate([half_rows, half_rows], axis=1)

    shape = jax.ShapeDtypeStruct
    wide = PART_X * CY * LANES
    lines, waves = call(
        spread_kernel,
        (shape((SLABS, wide), f32), shape((24, 3, 2 * PADDED_Z, LANES), f32)),
        [pltpu.VMEM((NX + 8, 2 * ROWS * LANES), f32)],
        flops=4_000_000_000,
        bytes_accessed=8_000_000,
    )(atoms, base, taps, x_high, x_low, cos_t, sin_t)
    lines = lax.all_to_all(lines, "gy", split_axis=0, concat_axis=0, tiled=True)
    filtered, energy_rows = call(
        filter_kernel,
        (shape((SLABS, wide), f32), shape((8, LANES), f32)),
        flops=4_000_000_000,
        bytes_accessed=5_000_000,
    )(lines, y_high, y_low, back_high, back_low, top, norm, mode)
    energy = lax.psum(0.5 * jnp.sum(energy_rows), ("gy", "gx"))
    filtered = lax.all_to_all(filtered, "gy", split_axis=0, concat_axis=0, tiled=True)
    shares = call(
        sample_kernel,
        shape((2 * PENCILS, 8, ATOM_DEV), f32),
        [pltpu.VMEM((NX + 8, ROWS * LANES), f32)],
        flops=4_000_000_000,
        bytes_accessed=8_000_000,
    )(filtered, atoms, waves, x_high, x_low, cos_t, sin_t)
    slab_shares = shares[:PENCILS] + next_slab(shares[PENCILS:], back=True)
    own = lax.psum_scatter(slab_shares, "gx", scatter_dimension=0, tiled=False)
    return own[0], own[1:4], own[4:7], jnp.reshape(energy, (1,))


def solution(mesh):
    placed = (
        P(None, ("gy", "gx")),
        P(None, ("gy", "gx")),
        P(("gy", "gx")),
        P(None, ("gy", "gx")),
        P(("gy", "gx")),
        P(),
    )
    return jax.shard_map(
        on_device,
        mesh=mesh,
        in_specs=placed,
        out_specs=(P(("gy", "gx")), P(None, ("gy", "gx")), P(None, ("gy", "gx")), P()),
        check_vma=False,
    )
```

time: 766 us -> 237 us (0.31); the launches traced: 754 us -> 236 us
  local copies, waits for them, and re-layouts: 173 us -> 13.9 us
  matrix products: 148 us -> 0 us
  waiting for transfers between devices: 140 us -> 30.5 us
  blocking collectives: 203 us -> 135 us
  other arithmetic: 55.8 us -> 13.5 us
  Pallas kernels: 0 us -> 29.3 us
  starting transfers between devices: 26.8 us -> 10.7 us
    dot_general x32 -> x0, matrix products: 148 us -> none  [contract(): return jnp.einsum(pattern, operand, matrix, precision=lax.Precision.HIGHEST)]
    all_to_all x3 -> x1, waiting for transfers between devices: 140 us -> 22.1 us  [on_device(): lines = lax.all_to_all(lines, 'gy', split_axis=0, concat_axis=0, tiled=True)]
    all_to_all x1, blocking collectives: 111 us -> 34.9 us  [on_device(): lax.all_to_all(filtered, 'gy', split_axis=0, concat_axis=0, tiled=True)]
    slice x14 -> x3, local copies, waits for them, and re-layouts: 42.9 us -> 2.32 us  [the longest x2 2.32 us: on_device(): return (own[0], own[1:4], own[4:7], jnp.reshape(energy, (1,)))]
    mul x49 -> x5, other arithmetic: 31.6 us -> 1.48 us  [the longest x1 0.69 us: on_device(): dipoles * live[None]]
    pallas_call x0 -> x3, Pallas kernels: none -> 29.3 us  [the longest x1 12.2 us: on_device(): call(spread_kernel, (shape((SLABS, wide), f32), shape((24, 3, 2 * PADDED_...]
    mul x87 -> x0, local copies, waits for them, and re-layouts: 28.8 us -> none  [the longest x84 28.2 us: on_device(): dense_y[r][:, :, None] * dense_x[p][:, None, :]]
    another operation x63 -> x1, local copies, waits for them, and re-layouts: 28 us -> 0.58 us  [the longest x1 9.1 us: on_device(): jnp.stack([line_real, line_imag])]
  transfers between devices with their start and end apart: 3 -> 3, of which waited for: 2 -> 2; matrix products, arithmetic and copies ran while one was open for 3% -> 4% of each run, Pallas kernels for 0% -> 0%
where the time goes in v1:
time: 237 us; the launch traced here: 236 us
  blocking collectives  135 us (57%)
  waiting for transfers between devices  30.5 us (13%)
  Pallas kernels  29.3 us (12%)
  local copies, waits for them, and re-layouts  13.9 us (6%)
  other arithmetic  13.5 us (6%)
  starting transfers between devices  10.7 us (5%)
    psum x1, blocking collectives, on_device(): energy = lax.psum(0.5 * jnp.sum(energy_rows), ('gy', 'gx'))  76.9 us
    all_to_all x1, blocking collectives, on_device(): lax.all_to_all(filtered, 'gy', split_axis=0, concat_axis=0, tiled=True)  34.9 us
    all_to_all x1, waiting for transfers between devices, on_device(): lines = lax.all_to_all(lines, 'gy', split_axis=0, concat_axis=0, tiled=True)  22.1 us
    unnamed x1, blocking collectives  13.8 us
    pallas_call x1, Pallas kernels, on_device(): call(spread_kernel, (shape((SLABS, wide), f32), shape((24, 3, 2 * PADDED_...  12.2 us
    pallas_call x1, Pallas kernels, on_device(): call(sample_kernel, shape((2 * PENCILS, 8, ATOM_DEV), f32), [pltpu.VMEM((...  11.8 us
    all_gather x1, blocking collectives, on_device(): slab_atoms = lax.all_gather(mine, 'gx', axis=0, tiled=False)  9.91 us
    ppermute x2, waiting for transfers between devices, next_slab(): lax.ppermute(value, 'gy', [(i, (i + step) % SLABS) for i in range(SLABS)])  8.44 us
  transfers between devices with their start and end apart: 3, of which 2 were waited for; matrix products, arithmetic and copies ran while one was open for 4% of the time, Pallas kernels for 0%

profile of v1, /device:TPU:1, one launch (start us, length us, event | category | flops | bytes accessed | tf_op | source)
XLA Modules:
  0.0 235.6 jit_solution(16536420268753887942)
XLA Ops:
  0.6 0.0 copy-start
  0.6 0.0 copy-start.1
  0.7 1.5 fusion.43
  2.2 0.8 fusion.22
  3.0 3.8 %compare_convert_fusion = (f32[1,384]{1,0:T(1,128)S(1)}, s32[384,1]{0,1:T(1,128)S(1)}) fusion(s32[1,1,3,128]{3,2,1,0:T(4,128)S(1)} %get-tuple-element.47, s32[1,1,3,128]{3,2,1,0:T(4,128)S(1)} %get-tuple-element.46, s32[]{:T(128)} %bitcast.8, s32[]{:T(128)} %bitcast.7, s32[]{:T(128)} %bitcast.6, s32[]{:T(128)} %bitcast.5, s32[]{:T(128)} %bitcast.4, s32[]{:T(128)} %bitcast.3), kind=kLoop, calls=%fused_computation.39 | loop fusion | flops 9984 | bytes 6168 | tf_op jit(solution)/shard_map/convert_element_type | solution.py:393
  6.8 0.8 fusion.40
  7.6 0.7 broadcast_select_fusion
  8.3 0.7 broadcast_multiply_fusion
  9.0 0.1 pad_add_fusion
  9.1 0.8 subtract_convert_fusion
  9.8 0.8 concatenate.22
  10.7 9.9 %all-gather = f32[64,384]{1,0:T(8,128)S(1)} all-gather(f32[16,384]{1,0:T(8,128)S(1)} %concatenate.22), channel_id=2, replica_groups=mesh['gy'=64,'gx'=4] {'gx'}, dimensions={0}, use_global_device_ids=true | all-gather | bytes 122880 | tf_op jit(solution)/shard_map/all_gather | solution.py:406
  20.6 0.0 collective-permute-start
  21.3 0.1 fusion.11
  21.3 0.1 copy.18
  21.5 0.7 multiply_sine_fusion
  22.2 0.1 fusion.20
  22.3 8.4 %collective-permute-done = f32[4,16,384]{2,1,0:T(8,128)S(1)} collective-permute-done((f32[4,16,384]{2,1,0:T(8,128)S(1)}, f32[4,16,384]{2,1,0:T(8,128)S(1)}, u32[]{:S(2)}, u32[]{:S(2)}) %collective-permute-start) | collective-permute-done | bytes 98336 | tf_op jit(solution)/shard_map/ppermute | solution.py:382
  30.7 0.1 broadcast_in_dim.60.taps_ref
  30.9 0.1 broadcast_in_dim.59.base_ref
  30.9 12.2 %shard_map.147 = (f32[64,4608]{1,0:T(8,128)S(1)}, f32[24,3,96,128]{3,2,1,0:T(8,128)}) custom-call(f32[8,16,384]{2,1,0:T(8,128)S(1)} %pad_maximum_fusion.atoms_ref, f32[8,128]{1,0:T(8,128)S(1)} %broadcast_in_dim.59.base_ref, f32[12,48,128]{2,1,0:T(8,128)S(1)} %broadcast_in_dim.60.taps_ref, bf16[384,768]{1,0:T(8,128)(2,1)S(1)} %copy-done, ...), custom_call_target="tpu_custom_call" | custom-call | flops 4000000000 | bytes 8000000 | tf_op jit(solution)/shard_map/pallas_call | solution.py:449
  43.1 2.3 copy.19
  45.4 6.8 %all-to-all-start = ((f32[64,1,4608]{2,1,0:T(1,128)}), f32[64,1,4608]{2,1,0:T(1,128)}, u32[]{:S(2)}, u32[]{:S(2)}) async-start(f32[64,1,4608]{2,1,0:T(1,128)} %copy.19), calls=%async_computation | async-start | bytes 2359296 | tf_op jit(solution)/shard_map/all_to_all | solution.py:456
  52.2 0.1 compare_select_fusion.10
  52.3 0.6 fusion.42
  52.9 0.6 and_reduce_fusion
  53.5 2.0 broadcast_select_fusion.1
  55.5 1.6 scatter.4
  57.2 0.1 add_multiply_fusion.3
  57.2 0.1 pad_maximum_fusion.1.mode_ref
  57.3 1.5 fusion.3
  58.8 0.0 copy-start.2
  58.8 0.0 copy-start.3
  58.8 22.1 %all-to-all-done = f32[64,1,4608]{2,1,0:T(1,128)} async-done(((f32[64,1,4608]{2,1,0:T(1,128)}), f32[64,1,4608]{2,1,0:T(1,128)}, u32[]{:S(2)}, u32[]{:S(2)}) %all-to-all-start) | async-done | bytes 1179680 | tf_op jit(solution)/shard_map/all_to_all | solution.py:456
  80.9 2.5 %copy.37 = f32[64,1,4608]{2,0,1:T(8,128)} copy(f32[64,1,4608]{2,1,0:T(1,128)} %all-to-all-done) | data formatting | bytes 2359296
  83.5 5.3 %shard_map.148 = (f32[64,4608]{1,0:T(8,128)S(1)}, f32[8,128]{1,0:T(8,128)S(1)}) custom-call(f32[64,4608]{1,0:T(8,128)} %bitcast.68, bf16[384,768]{1,0:T(8,128)(2,1)S(1)} %copy-done.2, bf16[384,768]{1,0:T(8,128)(2,1)S(1)} %copy-done.3, bf16[384,768]{1,0:T(8,128)(2,1)S(1)} %copy-done.4, bf16[384,768]{1,0:T(8,128)(2,1)S(1)} %copy-done.5, ...), custom_call_target="tpu_custom_call" | custom-call | flops 4000000000 | bytes 5000000 | tf_op jit(solution)/shard_map/pallas_call | solution.py:457
  88.8 1.2 copy.21
  90.0 34.9 %all_to_all.22 = f32[64,1,4608]{2,1,0:T(1,128)S(1)} all-to-all(f32[64,1,4608]{2,1,0:T(1,128)S(1)} %copy.21), channel_id=1, replica_groups=mesh['gy'=64,'gx'=4] {'gy'}, dimensions={0} | all-to-all | bytes 2359296 | tf_op jit(solution)/shard_map/all_to_all | solution.py:464
  125.0 0.1 copy.36
  125.1 0.0 copy-start.6
  125.1 11.8 %shard_map.149 = f32[8,8,384]{2,1,0:T(8,128)S(1)} custom-call(f32[64,4608]{1,0:T(8,128)S(1)} %bitcast.66, f32[8,16,384]{2,1,0:T(8,128)S(1)} %pad_maximum_fusion.atoms_ref, f32[24,3,96,128]{3,2,1,0:T(8,128)} %get-tuple-element.34.waves_ref, bf16[384,768]{1,0:T(8,128)(2,1)S(1)} %copy-done, bf16[384,768]{1,0:T(8,128)(2,1)S(1)} %copy-done.1, ...), custom_call_target="tpu_custom_call" | custom-call | flops 4000000000 | bytes 8000000 | tf_op jit(solution)/shard_map/pallas_call | solution.py:465
  136.9 3.9 %collective-permute-start.1 = (f32[4,8,384]{2,1,0:T(8,128)S(1)}, f32[4,8,384]{2,1,0:T(8,128)S(1)}, u32[]{:S(2)}, u32[]{:S(2)}) collective-permute-start(f32[4,8,384]{2,1,0:T(8,128)S(1)} %slice.81), channel_id=1, source_target_pairs={{0,252},{4,0},{8,4},{12,8},{16,12},{20,16},{24,20},{28,24},{32,28}... | collective-permute-start | bytes 147464 | tf_op jit(solution)/shard_map/ppermute | solution.py:382
  140.8 0.6 dynamic-slice.16
  141.4 0.6 reduce_sum.9
  142.6 76.9 %psum.7 = f32[1]{0:T(128)} all-reduce(f32[1]{0:T(128)} %bitcast.19), channel_id=1, replica_groups=mesh['gy'=64,'gx'=4] {'gy','gx'}, use_global_device_ids=true, to_apply=%region_3.4 | all-reduce | flops 1 | bytes 8 | tf_op jit(solution)/shard_map/psum | solution.py:463
  219.5 13.8 %all-reduce.1 = f32[4,8,384]{2,1,0:T(8,128)S(1)} all-reduce(f32[4,8,384]{2,1,0:T(8,128)S(1)} %slice_add_fusion), channel_id=3, replica_groups=mesh['gy'=64,'gx'=4] {'gx'}, use_global_device_ids=true, to_apply=%region_1.2.clone | all-reduce | flops 12288 | bytes 98304
  233.3 1.2 dynamic-slice_reduce_fusion
  234.4 1.2 dynamic-slice_bitcast_fusion
  (31 shorter events, 0.2 us)
Async XLA Ops:
  0.6 30.3 %copy-start = (bf16[384,768]{1,0:T(8,128)(2,1)S(1)}, bf16[384,768]{1,0:T(8,128)(2,1)}, u32[]{:S(2)}) copy-start(bf16[384,768]{1,0:T(8,128)(2,1)} %constant.291.clone.high_ref) | copy-start | bytes 1769476
  0.6 30.3 %copy-start.1 = (bf16[384,768]{1,0:T(8,128)(2,1)S(1)}, bf16[384,768]{1,0:T(8,128)(2,1)}, u32[]{:S(2)}) copy-start(bf16[384,768]{1,0:T(8,128)(2,1)} %constant.292.clone.low_ref) | copy-start | bytes 1769476
  20.6 10.1 %collective-permute-start = (f32[4,16,384]{2,1,0:T(8,128)S(1)}, f32[4,16,384]{2,1,0:T(8,128)S(1)}, u32[]{:S(2)}, u32[]{:S(2)}) collective-permute-start(f32[4,16,384]{2,1,0:T(8,128)S(1)} %bitcast.69), channel_id=1, source_target_pairs={{0,4},{4,8},{8,12},{12,16},{16,20},{20,24},{24,28},{28,32},{32,36}... | collective-permute-start | bytes 294920 | tf_op jit(solution)/shard_map/ppermute | solution.py:382
  45.4 7.5 %copy-start.7 = (s32[2]{0:T(128)S(1)}, s32[2]{0:T(128)}, u32[]{:S(2)}) copy-start(s32[2]{0:T(128)} %constant.288.clone.1) | copy-start | bytes 28
  45.4 35.5 %all-to-all-start = ((f32[64,1,4608]{2,1,0:T(1,128)}), f32[64,1,4608]{2,1,0:T(1,128)}, u32[]{:S(2)}, u32[]{:S(2)}) async-start(f32[64,1,4608]{2,1,0:T(1,128)} %copy.19), calls=%async_computation | async-start | bytes 2359296 | tf_op jit(solution)/shard_map/all_to_all | solution.py:456
  58.8 24.6 %copy-start.2 = (bf16[384,768]{1,0:T(8,128)(2,1)S(1)}, bf16[384,768]{1,0:T(8,128)(2,1)}, u32[]{:S(2)}) copy-start(bf16[384,768]{1,0:T(8,128)(2,1)} %constant.293.clone.high_ref) | copy-start | bytes 1769476
  58.8 24.6 %copy-start.3 = (bf16[384,768]{1,0:T(8,128)(2,1)S(1)}, bf16[384,768]{1,0:T(8,128)(2,1)}, u32[]{:S(2)}) copy-start(bf16[384,768]{1,0:T(8,128)(2,1)} %constant.294.clone.low_ref) | copy-start | bytes 1769476
  80.9 2.5 %copy-start.4 = (bf16[384,768]{1,0:T(8,128)(2,1)S(1)}, bf16[384,768]{1,0:T(8,128)(2,1)}, u32[]{:S(2)}) copy-start(bf16[384,768]{1,0:T(8,128)(2,1)} %constant.295.clone.back_high_ref) | copy-start | bytes 1769476
  80.9 2.5 %copy-start.5 = (bf16[384,768]{1,0:T(8,128)(2,1)S(1)}, bf16[384,768]{1,0:T(8,128)(2,1)}, u32[]{:S(2)}) copy-start(bf16[384,768]{1,0:T(8,128)(2,1)} %constant.296.clone.back_low_ref) | copy-start | bytes 1769476
  125.1 15.7 %copy-start.6 = (u32[256]{0:T(256)S(1)}, u32[256]{0:T(256)}, u32[]{:S(2)}) copy-start(u32[256]{0:T(256)} %constant.312) | copy-start | bytes 3076
  136.9 82.6 %collective-permute-start.1 = (f32[4,8,384]{2,1,0:T(8,128)S(1)}, f32[4,8,384]{2,1,0:T(8,128)S(1)}, u32[]{:S(2)}, u32[]{:S(2)}) collective-permute-start(f32[4,8,384]{2,1,0:T(8,128)S(1)} %slice.81), channel_id=1, source_target_pairs={{0,252},{4,0},{8,4},{12,8},{16,12},{20,16},{24,20},{28,24},{32,28}... | collective-permute-start | bytes 147464 | tf_op jit(solution)/shard_map/ppermute | solution.py:382

commit v2 on v1

v2 whole, which is shorter than its diff:
```python
import math

import jax
import jax.numpy as jnp
import ml_dtypes
import numpy as np
from jax import lax
from jax.experimental import pallas as pl
from jax.experimental.pallas import tpu as pltpu
from jax.sharding import PartitionSpec as P

NX = 384
NY = 384
NZ = 360
CY = 6
CX = 96
PENCILS = 4
SLABS = 64
PART_X = 6
PART_Z = 45
ATOM_BLK = 64
ATOM_DEV = 384
PAIRS = 3
WINDOW = 40
ROWS = 11
HALF = 64
LANES = 128
PADDED_Z = 48
screening = 0.9
f32 = jnp.float32
bf16 = jnp.bfloat16


def split_table(table):
    high = table.astype(ml_dtypes.bfloat16)
    low = (table - high.astype(np.float64)).astype(ml_dtypes.bfloat16)
    return high, low


def wave_tables():
    natural = np.arange(NX)
    angle_x = 2.0 * np.pi / NX * (natural[:, None] * natural[None, :] % NX)
    table_x = np.concatenate([np.cos(angle_x), np.sin(angle_x)], axis=1)
    place_y = np.arange(NY) % SLABS * CY + np.arange(NY) // SLABS
    angle_y = 2.0 * np.pi / NY * (natural[:, None] * place_y[None, :] % NY)
    forward_y = np.concatenate([np.cos(angle_y), np.sin(angle_y)], axis=1)
    inverse_y = np.concatenate([np.cos(angle_y.T), np.sin(angle_y.T)], axis=1)
    return split_table(table_x), split_table(forward_y), split_table(inverse_y)


def spline_rows(fraction):
    levels = {2: [1.0 - fraction, fraction]}
    current = levels[2]
    for n in range(3, 7):
        inverse_n = 1.0 / (n - 1)
        updated = [None] * n
        updated[n - 1] = inverse_n * fraction * current[n - 2]
        for j in range(1, n - 1):
            updated[n - 1 - j] = inverse_n * (
                (fraction + j) * current[n - 2 - j] + (n - j - fraction) * current[n - 1 - j]
            )
        updated[0] = inverse_n * (1.0 - fraction) * current[0]
        current = updated
        levels[n] = current
    zero_row = jnp.zeros_like(fraction)

    def entry_at(values_list, k):
        return values_list[k] if 0 <= k < len(values_list) else zero_row

    first = [entry_at(levels[5], t - 1) - entry_at(levels[5], t) for t in range(6)]
    second = [
        entry_at(levels[4], t - 2) - 2.0 * entry_at(levels[4], t - 1) + entry_at(levels[4], t)
        for t in range(6)
    ]
    return levels[6], first, second


def dense_rows(tables, cell, length):
    away = lax.broadcasted_iota(jnp.int32, (length, cell.shape[1]), 0).astype(f32) - cell
    summed = [jnp.zeros(away.shape, f32) for _ in tables]
    for t in range(6):
        here = away == float(t)
        summed = [jnp.where(here, table[t], so_far) for table, so_far in zip(tables, summed)]
    return summed


def unit_phase(turns):
    turns = turns - jnp.floor(turns + 0.5)
    quarter = jnp.floor(4.0 * turns + 0.5)
    rest = turns - 0.25 * quarter
    theta = (2.0 * math.pi) * rest
    square = theta * theta
    sine = theta * (
        1.0
        + square
        * (-1.0 / 6 + square * (1.0 / 120 + square * (-1.0 / 5040 + square * (1.0 / 362880))))
    )
    cosine = 1.0 + square * (
        -0.5
        + square
        * (1.0 / 24 + square * (-1.0 / 720 + square * (1.0 / 40320 - square * (1.0 / 3628800))))
    )
    odd = jnp.abs(quarter) == 1.0
    cos_out = jnp.where(odd, sine, cosine)
    sin_out = jnp.where(odd, cosine, sine)
    cos_out = jnp.where((quarter == 1.0) | (jnp.abs(quarter) == 2.0), -cos_out, cos_out)
    sin_out = jnp.where((quarter == -1.0) | (jnp.abs(quarter) == 2.0), -sin_out, sin_out)
    return cos_out, sin_out


def halves(value):
    high = value.astype(bf16)
    return high, (value - high.astype(f32)).astype(bf16)


def product(left, right, dims=((1,), (0,))):
    def one(a, b):
        return lax.dot_general(a, b, (dims, ((), ())), preferred_element_type=f32)

    return one(left[0], right[0]) + (one(left[0], right[1]) + one(left[1], right[0]))


def lane_sign(shape):
    return jnp.where(lax.broadcasted_iota(jnp.int32, shape, 1) < HALF, 1.0, -1.0).astype(f32)


def turned(value, sign):
    return pltpu.roll(value, HALF, 1) * sign


def atom_weights(atoms, lanes):
    offset = [atoms[3 + a : 4 + a, lanes] for a in range(3)]
    return [spline_rows(one) for one in offset]


PIECES = (0, 16, 32, 64, 80, 96)
GROUPS = PART_X * CY // 4
CARRIERS = 3 * GROUPS


def lane_range(first):
    lane = lax.broadcasted_iota(jnp.int32, (SLABS, LANES), 1)
    return (lane >= first) & (lane < first + 16)


def pack_blocks(blocks):
    carriers = []
    for c in range(3):
        value = blocks[c]
        for half in range(2):
            gap = PADDED_Z + half * HALF
            shift = (gap - PIECES[2 * c + half]) % LANES
            value = jnp.where(lane_range(gap), pltpu.roll(blocks[3], shift, 1), value)
        carriers.append(value)
    return carriers


def unpack_block(carriers):
    value = jnp.zeros((SLABS, LANES), f32)
    for p, source in enumerate(PIECES):
        gap = PADDED_Z + p % 2 * HALF
        shift = (source - gap) % LANES
        value = jnp.where(lane_range(source), pltpu.roll(carriers[p // 2], shift, 1), value)
    return value


def rows_of(carrier):
    return pl.ds(carrier, SLABS, stride=CARRIERS)


def block_at(ref, j, y):
    block = j * CY + y
    group, place = block // 4, block % 4
    if place < 3:
        return ref[rows_of(3 * group + place), :]
    return unpack_block([ref[rows_of(3 * group + c), :] for c in range(3)])


def prepare_kernel(
    where_ref, shear_ref, count_ref, cell_ref, offset_ref, charge_ref, dipole_ref,
    atoms_ref, base_ref, taps_ref, cos_ref, sin_ref
):
    slab, pencil = where_ref[0], where_ref[1]
    slot = lax.broadcasted_iota(jnp.int32, (1, ATOM_DEV), 1)
    live = jnp.zeros((1, ATOM_DEV), f32)
    for b in range(ATOM_DEV // ATOM_BLK):
        inside = (slot >= b * ATOM_BLK) & (slot < b * ATOM_BLK + count_ref[b])
        live = jnp.where(inside, 1.0, live)
    atoms_ref[0:1, :] = cell_ref[0:1, :].astype(f32)
    atoms_ref[1:2, :] = (cell_ref[1:2, :] - slab * CY).astype(f32)
    atoms_ref[2:3, :] = cell_ref[2:3, :].astype(f32)
    atoms_ref[3:6, :] = offset_ref[...]
    atoms_ref[6:7, :] = charge_ref[...] * live
    atoms_ref[7:10, :] = dipole_ref[...] * live
    atoms_ref[10:11, :] = live
    atoms_ref[11:16, :] = jnp.zeros((5, ATOM_DEV), f32)
    first = pencil * PART_Z
    row = lax.broadcasted_iota(jnp.int32, (PADDED_Z, LANES), 0)
    mode = (row + first).astype(f32)
    base_ref[...] = mode[:8]
    for t in range(6):
        cos_t, sin_t = unit_phase(mode * float(t) * (1.0 / NZ))
        taps_ref[t] = jnp.where(row < PART_Z, cos_t, 0.0)
        taps_ref[6 + t] = jnp.where(row < PART_Z, sin_t, 0.0)
    column = lax.broadcasted_iota(jnp.int32, (1, LANES), 1)
    above = jnp.where(slab == 0, SLABS - 1, slab - 1) * CY
    rows = jnp.where(column < CY, slab * CY, above) + jnp.minimum(column, ROWS)
    index = lax.broadcasted_iota(jnp.int32, (NX, LANES), 0)
    folds = jnp.where(index < NX // 2, index, index - NX)
    ticks = folds * (shear_ref[0] * rows)
    whole = jnp.floor(ticks.astype(f32) * (1.0 / (NX * NY))).astype(jnp.int32)
    rest = ticks - whole * (NX * NY)
    cos_t, sin_t = unit_phase(rest.astype(f32) * (1.0 / (NX * NY)))
    cos_ref[...] = cos_t
    sin_ref[...] = sin_t


def spread_kernel(own, *refs):
    if own:
        atoms_ref, base_ref, taps_ref, high_ref, low_ref, cos_ref, sin_ref, out_ref, waves_ref, grid_ref = refs
    else:
        (
            atoms_ref, base_ref, taps_ref, high_ref, low_ref, cos_ref, sin_ref, lines_ref,
            out_ref, waves_ref, grid_ref
        ) = refs
    grid_ref[...] = jnp.zeros_like(grid_ref)
    rows = list(range(CY)) if own else list(range(CY, ROWS))
    part = len(rows) * LANES
    gap = jnp.zeros((HALF - PADDED_Z, LANES), f32)

    def pencil_body(pencil, carry):
        for i in range(PAIRS):
            atoms = atoms_ref[pencil, :, i * LANES : (i + 1) * LANES]
            row = [atoms[a : a + 1] for a in range(10)]
            weights = [spline_rows(row[3 + a]) for a in range(3)]
            charge, dip_x, dip_y, dip_z = row[6:10]
            window = pencil * CX + i * 32
            dense_x = dense_rows(weights[0][:2], row[0] - window.astype(f32), WINDOW)
            dense_y = dense_rows(weights[1][:2], row[1], 16)
            cell_z = row[2]
            turn = base_ref[...] * cell_z
            turn = turn - 360.0 * jnp.floor(turn * (1.0 / 360.0))
            cos_k, sin_k = unit_phase(turn * (1.0 / 360.0))
            turn = 8.0 * cell_z
            turn = turn - 360.0 * jnp.floor(turn * (1.0 / 360.0))
            cos_8, sin_8 = unit_phase(turn * (1.0 / 360.0))
            pieces = [[], [], []]
            pieces_im = [[], [], []]
            for q in range(PADDED_Z // 8):
                span = slice(q * 8, q * 8 + 8)
                for s in range(3):
                    real = sum(weights[2][s][t] * taps_ref[t, span, :] for t in range(6))
                    imag = sum(weights[2][s][t] * taps_ref[6 + t, span, :] for t in range(6))
                    pieces[s].append(real * cos_k - imag * sin_k)
                    pieces_im[s].append(-(real * sin_k + imag * cos_k))
                cos_k, sin_k = cos_k * cos_8 - sin_k * sin_8, sin_k * cos_8 + cos_k * sin_8
            re = [jnp.concatenate(pieces[s], axis=0) for s in range(3)]
            im = [jnp.concatenate(pieces_im[s], axis=0) for s in range(3)]
            pair = pencil * PAIRS + i
            for s in range(3):
                waves_ref[pair, s, :PADDED_Z] = re[s]
                waves_ref[pair, s, PADDED_Z:] = im[s]
            full = []
            for wave_re, wave_im in (
                (charge * re[0] + dip_z * re[1], charge * im[0] + dip_z * im[1]),
                (re[0], im[0]),
            ):
                full.append(
                    jnp.concatenate(
                        [wave_re, gap, wave_im, gap, wave_im, gap, -wave_re, gap], axis=0
                    )
                )
            right = jnp.concatenate(full, axis=1)
            left = []
            for r in rows:
                value = dense_y[0][r : r + 1]
                first = dense_y[1][r : r + 1]
                left.append(
                    jnp.concatenate(
                        [
                            value * dense_x[0],
                            (dip_x * value) * dense_x[1] + (dip_y * first) * dense_x[0],
                        ],
                        axis=1,
                    )
                )
            left = jnp.concatenate(left, axis=0)
            added = product(halves(left), halves(right), ((1,), (1,)))
            at = pl.ds(pl.multiple_of(window, 8), WINDOW)
            for n in range(len(rows)):
                piece = added[n * WINDOW : (n + 1) * WINDOW]
                grid_ref[at, n * LANES : (n + 1) * LANES] += piece[:, :LANES]
                grid_ref[at, part + n * LANES : part + (n + 1) * LANES] += piece[:, LANES:]
        return carry

    lax.fori_loop(0, PENCILS, pencil_body, 0)
    grid_ref[0:8] += grid_ref[NX : NX + 8]
    table = (high_ref[...], low_ref[...])
    sign = lane_sign((NX, LANES))
    totals = []
    for first in range(0, len(rows), 2):
        lanes = slice(first * LANES, min(first + 2, len(rows)) * LANES)
        below = slice(part + lanes.start, part + lanes.stop)
        stacked = jnp.concatenate([grid_ref[:NX, lanes], grid_ref[:NX, below]], axis=0)
        line = product(table, halves(stacked))
        for n, r in enumerate(rows[first : first + 2]):
            one = line[:, n * LANES : (n + 1) * LANES]
            total = one * cos_ref[:, r : r + 1] + turned(one, sign) * sin_ref[:, r : r + 1]
            y = first + n
            if own:
                out_ref[:, y * LANES : (y + 1) * LANES] = total
            else:
                totals.append(total + lines_ref[:, y * LANES : (y + 1) * LANES])
    if own:
        return
    totals.append(lines_ref[:, (CY - 1) * LANES :])
    for group in range(GROUPS):
        blocks = []
        for block in range(4 * group, 4 * group + 4):
            j, y = block // CY, block % CY
            blocks.append(totals[y][j * SLABS : (j + 1) * SLABS])
        for c, carrier in enumerate(pack_blocks(blocks)):
            out_ref[rows_of(3 * group + c), :] = carrier


def filter_kernel(
    in_ref, high_ref, low_ref, back_high_ref, back_low_ref, top_ref, norm_ref, mode_ref, out_ref
):
    forward = (high_ref[...], low_ref[...])
    inverse = (back_high_ref[...], back_low_ref[...])
    sign = lane_sign((NY, LANES))
    energy = jnp.zeros((8, LANES), f32)
    blocks = []
    for first in range(0, PART_X, 2):
        lines = []
        for j in (first, first + 1):
            lines.append(jnp.concatenate([block_at(in_ref, j, y) for y in range(CY)], axis=0))
        stacked = jnp.concatenate(
            [jnp.concatenate([one, turned(one, sign)], axis=0) for one in lines], axis=1
        )
        spectrum = product(forward, halves(stacked))
        backs = []
        for n in range(2):
            j = first + n
            one = spectrum[:, n * LANES : (n + 1) * LANES]
            square = norm_ref[:, j : j + 1] + mode_ref[1:2, :]
            green = top_ref[:, j : j + 1] * mode_ref[0:1, :] / jnp.where(square == 0.0, 1.0, square)
            green = jnp.where(square == 0.0, 0.0, green)
            scaled = green * one
            share = scaled * one
            energy = energy + sum(share[8 * i : 8 * i + 8] for i in range(NY // 8))
            backs.append(jnp.concatenate([scaled, -turned(scaled, sign)], axis=0))
        potential = product(inverse, halves(jnp.concatenate(backs, axis=1)))
        for n in range(2):
            for y in range(CY):
                blocks.append(
                    potential[y * SLABS : (y + 1) * SLABS, n * LANES : (n + 1) * LANES]
                )
        for group in range(first * CY // 4, (first + 2) * CY // 4):
            for c, carrier in enumerate(pack_blocks(blocks[4 * group : 4 * group + 4])):
                out_ref[rows_of(3 * group + c), :] = carrier
    lane = lax.broadcasted_iota(jnp.int32, (SLABS, LANES), 1)
    share = 0.5 * jnp.sum(energy)
    out_ref[rows_of(0), :] = jnp.where(lane == PART_Z, share, out_ref[rows_of(0), :])


def sample_kernel(own, in_ref, atoms_ref, waves_ref, high_ref, low_ref, cos_ref, sin_ref, out_ref, grid_ref):
    table = (high_ref[...], low_ref[...])
    sign = lane_sign((NX, LANES))
    rows = list(range(CY)) if own else list(range(CY, ROWS))
    for first in range(0, len(rows), 2):
        stacked = []
        for y in range(first, min(first + 2, len(rows))):
            line = jnp.concatenate([block_at(in_ref, j, y) for j in range(PART_X)], axis=0)
            r = rows[y]
            one = line * cos_ref[:, r : r + 1] - turned(line, sign) * sin_ref[:, r : r + 1]
            stacked.append(jnp.concatenate([one, -turned(one, sign)], axis=0))
        cells = product(table, halves(jnp.concatenate(stacked, axis=1)))
        lanes = slice(first * LANES, (first + len(stacked)) * LANES)
        grid_ref[:NX, lanes] = cells
        grid_ref[NX:, lanes] = cells[:8]
    gap = jnp.zeros((HALF - PADDED_Z, LANES), f32)
    if own:
        lane = lax.broadcasted_iota(jnp.int32, (SLABS, LANES), 1)
        energy = jnp.sum(jnp.where(lane == PART_Z, in_ref[rows_of(0), :], 0.0))
    else:
        energy = 0.0

    def pencil_body(pencil, carry):
        for i in range(PAIRS):
            lanes = slice(i * LANES, (i + 1) * LANES)
            atoms = atoms_ref[pencil, :, lanes]
            row = [atoms[a : a + 1] for a in range(11)]
            weights = [spline_rows(row[3 + a]) for a in range(2)]
            window = pencil * CX + i * 32
            dense_x = dense_rows(weights[0], row[0] - window.astype(f32), WINDOW)
            dense_y = dense_rows(weights[1], row[1], 16)
            pair = pencil * PAIRS + i
            waves = jnp.concatenate(
                [
                    jnp.concatenate(
                        [waves_ref[pair, s, :PADDED_Z], gap, waves_ref[pair, s, PADDED_Z:], gap],
                        axis=0,
                    )
                    for s in range(3)
                ],
                axis=1,
            )
            at = pl.ds(pl.multiple_of(window, 8), WINDOW)
            cells = jnp.concatenate(
                [grid_ref[at, n * LANES : (n + 1) * LANES] for n in range(len(rows))], axis=0
            )
            read = product(halves(cells), halves(waves))
            lined = {}
            for order_y, order_z in ((0, 0), (1, 0), (2, 0), (0, 1), (1, 1), (0, 2)):
                lined[order_y, order_z] = sum(
                    dense_y[order_y][r : r + 1]
                    * read[n * WINDOW : (n + 1) * WINDOW, order_z * LANES : (order_z + 1) * LANES]
                    for n, r in enumerate(rows)
                )

            def sampled(p, r, s):
                return jnp.sum(dense_x[p] * lined[r, s], axis=0, keepdims=True)

            charge, dip_x, dip_y, dip_z, live = row[6:11]
            s100 = sampled(1, 0, 0)
            s010 = sampled(0, 1, 0)
            s001 = sampled(0, 0, 1)
            s110 = sampled(1, 1, 0)
            s101 = sampled(1, 0, 1)
            s011 = sampled(0, 1, 1)
            out = [
                live * sampled(0, 0, 0),
                live * s100,
                live * s010,
                live * s001,
                charge * s100 + dip_x * sampled(2, 0, 0) + dip_y * s110 + dip_z * s101,
                charge * s010 + dip_x * s110 + dip_y * sampled(0, 2, 0) + dip_z * s011,
                charge * s001 + dip_x * s101 + dip_y * s011 + dip_z * sampled(0, 0, 2),
                jnp.full(live.shape, energy, f32),
            ]
            out_ref[pencil, :, lanes] = jnp.concatenate(out, axis=0)
        return carry

    lax.fori_loop(0, PENCILS, pencil_body, 0)


def finish_kernel(in_ref, charge_ref, dipole_ref, position_ref, energy_ref):
    total = (in_ref[0] + in_ref[1]) + (in_ref[2] + in_ref[3])
    charge_ref[...] = total[0:1]
    dipole_ref[...] = total[1:4]
    position_ref[...] = total[4:7]
    energy_ref[...] = total[7:8, 0:1]


def spline_modulus(angles):
    return (66.0 + 52.0 * jnp.cos(angles) + 2.0 * jnp.cos(2.0 * angles)) / 120.0


def folded(index, size):
    return (index + size // 2) % size - size // 2


def call(kernel, out_shape, scratch=(), in_smem=0, inputs=0, flops=0, bytes_accessed=0):
    more = {}
    if in_smem:
        whole = pl.BlockSpec(memory_space=pltpu.VMEM)
        scalars = pl.BlockSpec(memory_space=pltpu.SMEM)
        more["in_specs"] = [scalars] * in_smem + [whole] * (inputs - in_smem)
    return pl.pallas_call(
        kernel,
        out_shape=out_shape,
        scratch_shapes=list(scratch),
        compiler_params=pltpu.CompilerParams(vmem_limit_bytes=32 * 1024 * 1024),
        cost_estimate=pl.CostEstimate(
            transcendentals=0, flops=flops, bytes_accessed=bytes_accessed
        ),
        **more,
    )


def next_slab(value, back=False):
    step = -1 if back else 1
    return lax.ppermute(value, "gy", [(i, (i + step) % SLABS) for i in range(SLABS)])


def swap_slabs(lines):
    lines = lines.reshape(SLABS, CARRIERS, 1, LANES)
    lines = lax.all_to_all(lines, "gy", split_axis=0, concat_axis=0, tiled=True)
    return lines.reshape(SLABS * CARRIERS, LANES)


def on_device(cell_index, offsets, charges, dipoles, block_count, shear_cells):
    pencil_index = lax.axis_index("gx")
    slab_index = lax.axis_index("gy")
    shear_step = shear_cells[0]
    (x_high, x_low), (y_high, y_low), (back_high, back_low) = wave_tables()
    shape = jax.ShapeDtypeStruct
    work = {"flops": 2_000_000_000, "bytes_accessed": 8_000_000}

    mine, base, taps, cos_t, sin_t = call(
        prepare_kernel,
        (
            shape((16, ATOM_DEV), f32),
            shape((8, LANES), f32),
            shape((12, PADDED_Z, LANES), f32),
            shape((NX, LANES), f32),
            shape((NX, LANES), f32),
        ),
        in_smem=3,
        inputs=7,
    )(
        jnp.stack([slab_index, pencil_index]),
        shear_cells,
        block_count,
        cell_index,
        offsets,
        charges[None],
        dipoles,
    )
    atoms = lax.all_gather(mine, "gx", axis=0, tiled=False)
    below_atoms = next_slab(atoms)

    own_x = folded(jnp.arange(8, dtype=jnp.int32) * SLABS + slab_index, NX)[None, :]
    own_y = folded(jnp.arange(NY, dtype=jnp.int32), NY)[:, None]
    float_x = own_x.astype(f32)
    wave_y = own_y.astype(f32) + float_x * shear_step.astype(f32) / NX
    norm = (float_x / NX) ** 2 + (wave_y / NY) ** 2
    moduli = spline_modulus(2.0 * math.pi * float_x / NX) * spline_modulus(
        2.0 * math.pi * wave_y / NY
    )
    decay = (math.pi / screening) ** 2
    top = jnp.exp(-decay * norm) / (math.pi * moduli * moduli)
    top = jnp.where((own_x == -(NX // 2)) | (own_y == -(NY // 2)), 0.0, top)
    lane = jnp.arange(LANES, dtype=jnp.int32) % HALF
    mode_z = pencil_index * PART_Z + lane
    kept = lane < PART_Z
    float_z = mode_z.astype(f32)
    norm_z = (float_z / NZ) ** 2
    modulus_z = spline_modulus(2.0 * math.pi * float_z / NZ)
    twice = jnp.where(mode_z == 0, 1.0, 2.0) / (NX * NY * NZ)
    mode_top = jnp.where(kept, twice * jnp.exp(-decay * norm_z) / (modulus_z * modulus_z), 0.0)
    mode_norm = jnp.where(kept, norm_z, 1.0)
    mode = jnp.stack([mode_top, mode_norm])

    waves_shape = shape((PENCILS * PAIRS, 3, 2 * PADDED_Z, LANES), f32)
    packed = shape((SLABS * CARRIERS, LANES), f32)
    own_lines, waves = call(
        lambda *refs: spread_kernel(True, *refs),
        (shape((NX, CY * LANES), f32), waves_shape),
        [pltpu.VMEM((NX + 8, 2 * CY * LANES), f32)],
        **work,
    )(atoms, base, taps, x_high, x_low, cos_t, sin_t)
    lines, below_waves = call(
        lambda *refs: spread_kernel(False, *refs),
        (packed, waves_shape),
        [pltpu.VMEM((NX + 8, 2 * (ROWS - CY) * LANES), f32)],
        **work,
    )(below_atoms, base, taps, x_high, x_low, cos_t, sin_t, own_lines)
    lines = swap_slabs(lines)
    filtered = call(filter_kernel, packed, **work)(
        lines, y_high, y_low, back_high, back_low, top, norm, mode
    )
    filtered = swap_slabs(filtered)
    below_shares = call(
        lambda *refs: sample_kernel(False, *refs),
        shape((PENCILS, 8, ATOM_DEV), f32),
        [pltpu.VMEM((NX + 8, (ROWS - CY) * LANES), f32)],
        **work,
    )(filtered, below_atoms, below_waves, x_high, x_low, cos_t, sin_t)
    below_shares = next_slab(below_shares, back=True)
    shares = call(
        lambda *refs: sample_kernel(True, *refs),
        shape((PENCILS, 8, ATOM_DEV), f32),
        [pltpu.VMEM((NX + 8, CY * LANES), f32)],
        **work,
    )(filtered, atoms, waves, x_high, x_low, cos_t, sin_t)
    shares = lax.all_to_all(shares + below_shares, "gx", split_axis=0, concat_axis=0, tiled=True)
    charge_grad, dipole_grad, position_grad, energy = call(
        finish_kernel,
        (
            shape((1, ATOM_DEV), f32),
            shape((3, ATOM_DEV), f32),
            shape((3, ATOM_DEV), f32),
            shape((1, 1), f32),
        ),
    )(shares)
    return charge_grad[0], dipole_grad, position_grad, energy[0]


def solution(mesh):
    placed = (
        P(None, ("gy", "gx")),
        P(None, ("gy", "gx")),
        P(("gy", "gx")),
        P(None, ("gy", "gx")),
        P(("gy", "gx")),
        P(),
    )
    return jax.shard_map(
        on_device,
        mesh=mesh,
        in_specs=placed,
        out_specs=(P(("gy", "gx")), P(None, ("gy", "gx")), P(None, ("gy", "gx")), P()),
        check_vma=False,
    )
```

time: 237 us -> 133 us (0.56)
  blocking collectives: 135 us -> 51.7 us
  other arithmetic: 13.5 us -> 2.38 us
  waiting for transfers between devices: 30.5 us -> 22.9 us
  starting transfers between devices: 10.7 us -> 14.4 us
  local copies, waits for them, and re-layouts: 13.9 us -> 11.2 us
    psum x1 -> x0, blocking collectives: 76.9 us -> none  [on_device(): energy = lax.psum(0.5 * jnp.sum(energy_rows), ('gy', 'gx'))]
    unnamed x1 -> x0, blocking collectives: 13.8 us -> none
    unnamed x19 -> x32, local copies, waits for them, and re-layouts: 3.21 us -> 10.5 us
    ppermute x2, waiting for transfers between devices: 8.44 us -> 1.32 us  [next_slab(): lax.ppermute(value, 'gy', [(i, (i + step) % SLABS) for i in range(SLABS)])]
    all_to_all x1 -> x2, blocking collectives: 34.9 us -> 41.7 us  [the longest x1 29 us: swap_slabs(): lines = lax.all_to_all(lines, 'gy', split_axis=0, concat_axis=0, tiled=True)]
    convert_element_type x6 -> x0, other arithmetic: 5.45 us -> none  [the longest x2 4.6 us: on_device(): live = (slot % ATOM_BLK < counts).astype(f32)]
    all_to_all x1, starting transfers between devices: 6.78 us -> 10.7 us  [swap_slabs(): lines = lax.all_to_all(lines, 'gy', split_axis=0, concat_axis=0, tiled=True)]
    all_to_all x2 -> x0, local copies, waits for them, and re-layouts: 3.5 us -> none  [the longest x1 2.28 us: on_device(): lines = lax.all_to_all(lines, 'gy', split_axis=0, concat_axis=0, tiled=True)]
  transfers between devices with their start and end apart: 3 -> 3, of which waited for: 2 -> 2; matrix products, arithmetic and copies ran while one was open for 4% -> 1% of each run, Pallas kernels for 0% -> 9%
where the time goes in v2:
time: 133 us
  blocking collectives  51.7 us (39%)
  Pallas kernels  28.9 us (22%)
  waiting for transfers between devices  22.9 us (17%)
  starting transfers between devices  14.4 us (11%)
  local copies, waits for them, and re-layouts  11.2 us (8%)
  other arithmetic  2.38 us (2%)
  between operations  1.41 us (1%)
    all_to_all x1, blocking collectives, swap_slabs(): lines = lax.all_to_all(lines, 'gy', split_axis=0, concat_axis=0, tiled=True)  29 us
    all_to_all x1, waiting for transfers between devices, swap_slabs(): lines = lax.all_to_all(lines, 'gy', split_axis=0, concat_axis=0, tiled=True)  21.6 us
    all_to_all x1, blocking collectives, on_device(): lax.all_to_all(shares + below_shares, 'gx', split_axis=0, concat_axis=0,...  12.7 us
    all_to_all x1, starting transfers between devices, swap_slabs(): lines = lax.all_to_all(lines, 'gy', split_axis=0, concat_axis=0, tiled=True)  10.7 us
    unnamed x32, local copies, waits for them, and re-layouts  10.5 us
    all_gather x1, blocking collectives, on_device(): atoms = lax.all_gather(mine, 'gx', axis=0, tiled=False)  9.91 us
    pallas_call x1, Pallas kernels, on_device(): call(lambda *refs: spread_kernel(False, *refs), (packed, waves_shape), [p...  6.26 us
    pallas_call x1, Pallas kernels, on_device(): call(lambda *refs: sample_kernel(True, *refs), shape((PENCILS, 8, ATOM_DE...  5.9 us
  transfers between devices with their start and end apart: 3, of which 2 were waited for; matrix products, arithmetic and copies ran while one was open for 1% of the time, Pallas kernels for 9%

profile of v2, /device:TPU:1, one launch (start us, length us, event | category | flops | bytes accessed | tf_op | source)
XLA Modules:
  0.0 132.8 jit_solution(2040659752232987929)
XLA Ops:
  1.3 0.7 broadcast_in_dim.22.charge_ref
  2.0 0.1 pad_add_fusion.where_ref
  2.0 0.0 copy-start
  2.0 0.7 copy-done
  2.7 0.7 copy-done.1
  3.4 0.0 copy-start.2
  3.4 0.7 copy-done.2
  4.1 0.0 copy-start.3
  4.1 0.7 copy-done.3
  4.8 1.1 shard_map.147
  5.9 9.9 %all-gather = f32[64,384]{1,0:T(8,128)S(1)} all-gather(f32[16,384]{1,0:T(8,128)S(1)} %get-tuple-element.17), channel_id=2, replica_groups=mesh['gy'=64,'gx'=4] {'gx'}, dimensions={0}, use_global_device_ids=true | all-gather | bytes 122880 | tf_op jit(solution)/shard_map/all_gather | solution.py:521
  15.8 0.0 collective-permute-start
  15.8 0.0 copy-start.4
  15.8 1.1 copy-done.4
  16.9 0.0 copy-start.6
  16.9 1.1 copy-done.6
  18.0 0.0 copy-start.5
  18.0 5.4 %shard_map.148 = (f32[384,768]{1,0:T(8,128)S(1)}, f32[12,3,96,128]{3,2,1,0:T(8,128)S(1)}) custom-call(f32[4,16,384]{2,1,0:T(8,128)S(1)} %bitcast.14, f32[8,128]{1,0:T(8,128)S(1)} %get-tuple-element.18.refs_1_, f32[12,48,128]{2,1,0:T(8,128)S(1)} %get-tuple-element.19.refs_2_, bf16[384,768]{1,0:T(8,128)(2,1)S(1)} %copy-done.4, bf16[384,768]{1,0:T(8,128)(2,1)S(1)} %copy-done.6, ...), custom_call_target="tpu_custom_call" | custom-call | flops 2000000000 | bytes 8000000 | tf_op jit(solution)/shard_map/pallas_call | solution.py:548
  23.4 0.0 copy-start.12
  23.4 1.2 copy-done.12
  24.6 1.3 collective-permute-done.refs_0_.refs_1_
  26.0 0.0 copy-done.5
  26.0 6.3 %shard_map.149 = (f32[1728,128]{1,0:T(8,128)}, f32[12,3,96,128]{3,2,1,0:T(8,128)S(1)}) custom-call(f32[4,16,384]{2,1,0:T(8,128)S(1)} %collective-permute-done.refs_0_.refs_1_, f32[8,128]{1,0:T(8,128)S(1)} %get-tuple-element.18.refs_1_, f32[12,48,128]{2,1,0:T(8,128)S(1)} %get-tuple-element.19.refs_2_, bf16[384,768]{1,0:T(8,128)(2,1)S(1)} %copy-done.5, ...), custom_call_target="tpu_custom_call" | custom-call | flops 2000000000 | bytes 8000000 | tf_op jit(solution)/shard_map/pallas_call | solution.py:554
  32.2 0.0 copy-start.14
  32.2 1.2 copy-done.14
  33.4 0.0 copy-start.8
  33.5 10.7 %all-to-all-start = ((f32[64,27,1,128]{3,2,1,0:T(1,128)}), f32[64,27,1,128]{3,2,1,0:T(1,128)S(1)}, u32[]{:S(2)}, u32[]{:S(2)}) async-start(f32[64,27,1,128]{3,2,1,0:T(1,128)} %bitcast.3), calls=%async_computation | async-start | bytes 1769472 | tf_op jit(solution)/shard_map/all_to_all | solution.py:489
  44.2 0.1 add_multiply_fusion.3
  44.2 0.1 compare_select_fusion.1
  44.3 1.5 %fusion.3 = (f32[384,8]{1,0:T(8,128)S(1)}, f32[384,8]{1,0:T(8,128)S(1)}) fusion(f32[8]{0:T(128)S(1)} %multiply_multiply_fusion.2, f32[8]{0:T(128)S(1)} %get-tuple-element.33, f32[384]{0:T(512)S(1)} %fusion.15, f32[8]{0:T(128)S(1)} %get-tuple-element.32, pred[384]{0:T(512)(128)(4,1)S(1)} %broadcast_compare_fusion, pred[8]{0:T(512)(128)(4,1)S(1)} %broadcast_compare_fusion.1), kind=kLoop, calls=%fused_computation.7 | loop fusion | flops 52224 | bytes 26600 | tf_op jit(solution)/shard_map/add | solution.py:528
  45.8 21.6 %all-to-all-done = f32[64,27,1,128]{3,2,1,0:T(1,128)S(1)} async-done(((f32[64,27,1,128]{3,2,1,0:T(1,128)}), f32[64,27,1,128]{3,2,1,0:T(1,128)S(1)}, u32[]{:S(2)}, u32[]{:S(2)}) %all-to-all-start) | async-done | bytes 884768 | tf_op jit(solution)/shard_map/all_to_all | solution.py:489
  67.4 0.0 copy-done.8
  67.4 1.1 copy-done.9
  68.5 1.1 copy-done.10
  69.6 1.1 copy-done.11
  70.6 4.2 %shard_map.150 = f32[1728,128]{1,0:T(8,128)S(1)} custom-call(f32[1728,128]{1,0:T(8,128)S(1)} %bitcast.9, bf16[384,768]{1,0:T(8,128)(2,1)S(1)} %copy-done.8, bf16[384,768]{1,0:T(8,128)(2,1)S(1)} %copy-done.9, bf16[384,768]{1,0:T(8,128)(2,1)S(1)} %copy-done.10, bf16[384,768]{1,0:T(8,128)(2,1)S(1)} %copy-done.11, f32[384,8]{1,0:T(8,128)S(1)} %get-tuple-element.31.top_ref, ...), custom_call_target="tpu_custom_call" | custom-call | flops 2000000000 | bytes 8000000 | tf_op jit(solution)/shard_map/pallas_call | solution.py:561
  74.9 0.0 copy-start.7
  74.9 29.0 %all_to_all.15 = f32[64,27,1,128]{3,2,1,0:T(1,128)S(1)} all-to-all(f32[64,27,1,128]{3,2,1,0:T(1,128)S(1)} %bitcast.12), channel_id=1, replica_groups=mesh['gy'=64,'gx'=4] {'gy'}, dimensions={0} | all-to-all | bytes 1769472 | tf_op jit(solution)/shard_map/all_to_all | solution.py:489
  103.9 0.0 copy-done.15
  103.9 0.0 copy-done.7
  103.9 5.3 %shard_map.152 = f32[4,8,384]{2,1,0:T(8,128)S(1)} custom-call(f32[1728,128]{1,0:T(8,128)S(1)} %bitcast.10, f32[4,16,384]{2,1,0:T(8,128)S(1)} %collective-permute-done.refs_0_.refs_1_, f32[12,3,96,128]{3,2,1,0:T(8,128)S(1)} %copy-done.15, bf16[384,768]{1,0:T(8,128)(2,1)S(1)} %copy-done.5, bf16[384,768]{1,0:T(8,128)(2,1)S(1)} %copy-done.7, ...), custom_call_target="tpu_custom_call" | custom-call | flops 2000000000 | bytes 8000000 | tf_op jit(solution)/shard_map/pallas_call | solution.py:565
  109.2 3.7 %collective-permute-start.1 = (f32[4,8,384]{2,1,0:T(8,128)S(1)}, f32[4,8,384]{2,1,0:T(8,128)S(1)}, u32[]{:S(2)}, u32[]{:S(2)}) collective-permute-start(f32[4,8,384]{2,1,0:T(8,128)S(1)} %shard_map.152), channel_id=1, source_target_pairs={{0,252},{4,0},{8,4},{12,8},{16,12},{20,16},{24,20},{28,24},{32,28}... | collective-permute-start | bytes 147464 | tf_op jit(solution)/shard_map/ppermute | solution.py:484
  112.9 0.0 copy-done.13
  112.9 5.9 %shard_map.151 = f32[4,8,384]{2,1,0:T(8,128)S(1)} custom-call(f32[1728,128]{1,0:T(8,128)S(1)} %bitcast.11, f32[4,16,384]{2,1,0:T(8,128)S(1)} %bitcast.15, f32[12,3,96,128]{3,2,1,0:T(8,128)S(1)} %copy-done.13, bf16[384,768]{1,0:T(8,128)(2,1)S(1)} %copy-done.5, bf16[384,768]{1,0:T(8,128)(2,1)S(1)} %copy-done.7, f32[384,128]{1,0:T(8,128)S(1)} %get-tuple-element.20.refs_5_, ...), custom_call_target="tpu_custom_call" | custom-call | flops 2000000000 | bytes 8000000 | tf_op jit(solution)/shard_map/pallas_call | solution.py:572
  118.8 0.0 collective-permute-done.1
  118.9 12.7 %all_to_all.16.in_ref = f32[4,8,384]{2,1,0:T(8,128)S(1)} all-to-all(f32[4,8,384]{2,1,0:T(8,128)S(1)} %add.235), channel_id=1, replica_groups=mesh['gy'=64,'gx'=4] {'gx'}, dimensions={0} | all-to-all | bytes 98304 | tf_op jit(solution)/shard_map/all_to_all | solution.py:578
  131.6 0.6 shard_map.153
  132.2 0.6 reduce
  (12 shorter events, 0.1 us)
Async XLA Ops:
  2.0 0.7 copy-start
  2.7 0.7 copy-start.1
  3.4 0.7 copy-start.2
  4.1 0.7 copy-start.3
  15.8 10.1 %collective-permute-start = (f32[4,16,384]{2,1,0:T(8,128)S(1)}, f32[4,16,384]{2,1,0:T(8,128)S(1)}, u32[]{:S(2)}, u32[]{:S(2)}) collective-permute-start(f32[4,16,384]{2,1,0:T(8,128)S(1)} %bitcast.13), channel_id=1, source_target_pairs={{0,4},{4,8},{8,12},{12,16},{16,20},{20,24},{24,28},{28,32},{32,36}... | collective-permute-start | bytes 294920 | tf_op jit(solution)/shard_map/ppermute | solution.py:484
  15.8 1.1 copy-start.4
  16.9 1.1 copy-start.6
  18.0 8.0 %copy-start.5 = (bf16[384,768]{1,0:T(8,128)(2,1)S(1)}, bf16[384,768]{1,0:T(8,128)(2,1)}, u32[]{:S(2)}) copy-start(bf16[384,768]{1,0:T(8,128)(2,1)} %constant.126.clone.refs_3_) | copy-start | bytes 1769476
  23.4 1.2 copy-start.12
  32.2 1.2 copy-start.14
  33.4 34.0 %copy-start.8 = (bf16[384,768]{1,0:T(8,128)(2,1)S(1)}, bf16[384,768]{1,0:T(8,128)(2,1)}, u32[]{:S(2)}) copy-start(bf16[384,768]{1,0:T(8,128)(2,1)} %constant.128.clone.high_ref) | copy-start | bytes 1769476
  33.5 34.0 %all-to-all-start = ((f32[64,27,1,128]{3,2,1,0:T(1,128)}), f32[64,27,1,128]{3,2,1,0:T(1,128)S(1)}, u32[]{:S(2)}, u32[]{:S(2)}) async-start(f32[64,27,1,128]{3,2,1,0:T(1,128)} %bitcast.3), calls=%async_computation | async-start | bytes 1769472 | tf_op jit(solution)/shard_map/all_to_all | solution.py:489
  67.4 1.1 copy-start.9
  68.5 1.1 copy-start.10
  69.6 1.1 copy-start.11
  70.6 33.3 %copy-start.15 = (f32[12,3,96,128]{3,2,1,0:T(8,128)S(1)}, f32[12,3,96,128]{3,2,1,0:T(8,128)}, u32[]{:S(2)}) copy-start(f32[12,3,96,128]{3,2,1,0:T(8,128)} %copy-done.14) | copy-start | bytes 5308420
  74.9 29.1 %copy-start.7 = (bf16[384,768]{1,0:T(8,128)(2,1)S(1)}, bf16[384,768]{1,0:T(8,128)(2,1)}, u32[]{:S(2)}) copy-start(bf16[384,768]{1,0:T(8,128)(2,1)} %constant.127.clone.refs_4_) | copy-start | bytes 1769476
  103.9 9.0 %copy-start.13 = (f32[12,3,96,128]{3,2,1,0:T(8,128)S(1)}, f32[12,3,96,128]{3,2,1,0:T(8,128)}, u32[]{:S(2)}) copy-start(f32[12,3,96,128]{3,2,1,0:T(8,128)} %copy-done.12) | copy-start | bytes 5308420
  109.2 9.6 %collective-permute-start.1 = (f32[4,8,384]{2,1,0:T(8,128)S(1)}, f32[4,8,384]{2,1,0:T(8,128)S(1)}, u32[]{:S(2)}, u32[]{:S(2)}) collective-permute-start(f32[4,8,384]{2,1,0:T(8,128)S(1)} %shard_map.152), channel_id=1, source_target_pairs={{0,252},{4,0},{8,4},{12,8},{16,12},{20,16},{24,20},{28,24},{32,28}... | collective-permute-start | bytes 147464 | tf_op jit(solution)/shard_map/ppermute | solution.py:484

commit v3 on v2

--- a/solution.py
+++ b/solution.py
@@ -26,6 +26,7 @@
 HALF = 64
 LANES = 128
 PADDED_Z = 48
+QUARTER = 96
 screening = 0.9
 f32 = jnp.float32
 bf16 = jnp.bfloat16
@@ -34,18 +35,20 @@
 def split_table(table):
     high = table.astype(ml_dtypes.bfloat16)
     low = (table - high.astype(np.float64)).astype(ml_dtypes.bfloat16)
-    return high, low
+    return np.stack([high, low])
 
 
 def wave_tables():
-    natural = np.arange(NX)
-    angle_x = 2.0 * np.pi / NX * (natural[:, None] * natural[None, :] % NX)
-    table_x = np.concatenate([np.cos(angle_x), np.sin(angle_x)], axis=1)
-    place_y = np.arange(NY) % SLABS * CY + np.arange(NY) // SLABS
-    angle_y = 2.0 * np.pi / NY * (natural[:, None] * place_y[None, :] % NY)
-    forward_y = np.concatenate([np.cos(angle_y), np.sin(angle_y)], axis=1)
-    inverse_y = np.concatenate([np.cos(angle_y.T), np.sin(angle_y.T)], axis=1)
-    return split_table(table_x), split_table(forward_y), split_table(inverse_y)
+    quarter = np.arange(QUARTER)
+    mode = np.arange(4)[:, None] + 4 * quarter[None, :]
+    row_y = CY * (quarter % 16) + quarter // 16
+    tables = []
+    for place in (quarter, row_y):
+        ticks = mode[:, :, None] * place % NX
+        for table in (ticks, ticks.transpose(0, 2, 1)):
+            angle = 2.0 * np.pi / NX * table.reshape(NX, QUARTER)
+            tables.append(split_table(np.concatenate([np.cos(angle), np.sin(angle)], axis=1)))
+    return tables
 
 
 def spline_rows(fraction):
@@ -128,9 +131,46 @@
     return pltpu.roll(value, HALF, 1) * sign
 
 
-def atom_weights(atoms, lanes):
-    offset = [atoms[3 + a : 4 + a, lanes] for a in range(3)]
-    return [spline_rows(one) for one in offset]
+def fetch(source, target, semaphore):
+    copy = pltpu.make_async_copy(source, target, semaphore)
+    copy.start()
+    return copy
+
+
+def table_rows(table_ref, r):
+    rows = slice(r * QUARTER, (r + 1) * QUARTER)
+    return table_ref[0, rows], table_ref[1, rows]
+
+
+def forward_line(table_ref, quarters, turned_quarters):
+    g, h = quarters, turned_quarters
+    a, b, c, d = g[0] + g[2], g[0] - g[2], g[1] + g[3], g[1] - g[3]
+    ta, tb, tc, td = h[0] + h[2], h[0] - h[2], h[1] + h[3], h[1] - h[3]
+    lines = []
+    for r, (one, other) in enumerate(
+        ((a + c, ta + tc), (b + td, tb - d), (a - c, ta - tc), (b - td, tb + d))
+    ):
+        stacked = jnp.concatenate([one, other], axis=0)
+        lines.append(product(table_rows(table_ref, r), halves(stacked)))
+    return lines
+
+
+def inverse_line(table_ref, modes, turned_modes):
+    z = []
+    for r in range(4):
+        stacked = jnp.concatenate([modes[r], -turned_modes[r]], axis=0)
+        z.append(product(table_rows(table_ref, r), halves(stacked)))
+    a, b, c, d = z[0] + z[2], z[0] - z[2], z[1] + z[3], z[1] - z[3]
+    width = d.shape[1]
+    sign = lane_sign((QUARTER, LANES))
+    td = jnp.concatenate(
+        [turned(d[:, n : n + LANES], sign) for n in range(0, width, LANES)], axis=1
+    )
+    return [a + c, b - td, a - c, b + td]
+
+
+def quarters_of(value):
+    return [value[r * QUARTER : (r + 1) * QUARTER] for r in range(4)]
 
 
 PIECES = (0, 16, 32, 64, 80, 96)
@@ -177,10 +217,50 @@
 
 
 def prepare_kernel(
-    where_ref, shear_ref, count_ref, cell_ref, offset_ref, charge_ref, dipole_ref,
-    atoms_ref, base_ref, taps_ref, cos_ref, sin_ref
+    where_ref, shear_ref, counts_ref, cells_ref, offsets_ref, charges_ref, dipoles_ref,
+    atoms_ref, base_ref, taps_ref, cos_ref, sin_ref,
+    count_ref, cell_ref, offset_ref, charge_ref, dipole_ref, semaphores
 ):
+    copies = [
+        fetch(source, target, semaphores.at[n])
+        for n, (source, target) in enumerate(
+            (
+                (counts_ref, count_ref),
+                (cells_ref, cell_ref),
+                (offsets_ref, offset_ref),
+                (charges_ref, charge_ref),
+                (dipoles_ref, dipole_ref),
+            )
+        )
+    ]
     slab, pencil = where_ref[0], where_ref[1]
+    first = pencil * PART_Z
+    row = lax.broadcasted_iota(jnp.int32, (PADDED_Z, LANES), 0)
+    mode = (row + first).astype(f32)
+    base_ref[...] = mode[:8]
+    for t in range(6):
+        cos_t, sin_t = unit_phase(mode * float(t) * (1.0 / NZ))
+        taps_ref[t] = jnp.where(row < PART_Z, cos_t, 0.0)
+        taps_ref[6 + t] = jnp.where(row < PART_Z, sin_t, 0.0)
+    column = lax.broadcasted_iota(jnp.int32, (1, LANES), 1)
+    above = jnp.where(slab == 0, SLABS - 1, slab - 1) * CY
+    rows = jnp.where(column < CY, slab * CY, above) + jnp.minimum(column, ROWS)
+    index = lax.broadcasted_iota(jnp.int32, (NX, LANES), 0)
+    residue = (
+        (index >= QUARTER).astype(jnp.int32)
+        + (index >= 2 * QUARTER).astype(jnp.int32)
+        + (index >= 3 * QUARTER).astype(jnp.int32)
+    )
+    mode_x = 4 * (index - QUARTER * residue) + residue
+    folds = jnp.where(mode_x < NX // 2, mode_x, mode_x - NX)
+    ticks = folds * (shear_ref[0] * rows)
+    whole = jnp.floor(ticks.astype(f32) * (1.0 / (NX * NY))).astype(jnp.int32)
+    rest = ticks - whole * (NX * NY)
+    cos_t, sin_t = unit_phase(rest.astype(f32) * (1.0 / (NX * NY)))
+    cos_ref[...] = cos_t
+    sin_ref[...] = sin_t
+    for copy in copies:
+        copy.wait()
     slot = lax.broadcasted_iota(jnp.int32, (1, ATOM_DEV), 1)
     live = jnp.zeros((1, ATOM_DEV), f32)
     for b in range(ATOM_DEV // ATOM_BLK):
@@ -194,35 +274,13 @@
     atoms_ref[7:10, :] = dipole_ref[...] * live
     atoms_ref[10:11, :] = live
     atoms_ref[11:16, :] = jnp.zeros((5, ATOM_DEV), f32)
-    first = pencil * PART_Z
-    row = lax.broadcasted_iota(jnp.int32, (PADDED_Z, LANES), 0)
-    mode = (row + first).astype(f32)
-    base_ref[...] = mode[:8]
-    for t in range(6):
-        cos_t, sin_t = unit_phase(mode * float(t) * (1.0 / NZ))
-        taps_ref[t] = jnp.where(row < PART_Z, cos_t, 0.0)
-        taps_ref[6 + t] = jnp.where(row < PART_Z, sin_t, 0.0)
-    column = lax.broadcasted_iota(jnp.int32, (1, LANES), 1)
-    above = jnp.where(slab == 0, SLABS - 1, slab - 1) * CY
-    rows = jnp.where(column < CY, slab * CY, above) + jnp.minimum(column, ROWS)
-    index = lax.broadcasted_iota(jnp.int32, (NX, LANES), 0)
-    folds = jnp.where(index < NX // 2, index, index - NX)
-    ticks = folds * (shear_ref[0] * rows)
-    whole = jnp.floor(ticks.astype(f32) * (1.0 / (NX * NY))).astype(jnp.int32)
-    rest = ticks - whole * (NX * NY)
-    cos_t, sin_t = unit_phase(rest.astype(f32) * (1.0 / (NX * NY)))
-    cos_ref[...] = cos_t
-    sin_ref[...] = sin_t
 
 
 def spread_kernel(own, *refs):
-    if own:
-        atoms_ref, base_ref, taps_ref, high_ref, low_ref, cos_ref, sin_ref, out_ref, waves_ref, grid_ref = refs
-    else:
-        (
-            atoms_ref, base_ref, taps_ref, high_ref, low_ref, cos_ref, sin_ref, lines_ref,
-            out_ref, waves_ref, grid_ref
-        ) = refs
+    atoms_ref, base_ref, taps_ref, tables_ref, cos_ref, sin_ref = refs[:6]
+    out_ref, waves_out_ref, grid_ref, table_ref, waves_ref, semaphores = refs[-6:]
+    lines_ref = None if own else refs[6]
+    table_copy = fetch(tables_ref, table_ref, semaphores.at[0])
     grid_ref[...] = jnp.zeros_like(grid_ref)
     rows = list(range(CY)) if own else list(range(CY, ROWS))
     part = len(rows) * LANES
@@ -295,14 +353,19 @@
 
     lax.fori_loop(0, PENCILS, pencil_body, 0)
     grid_ref[0:8] += grid_ref[NX : NX + 8]
-    table = (high_ref[...], low_ref[...])
+    waves_copy = fetch(waves_ref, waves_out_ref, semaphores.at[1])
+    table_copy.wait()
     sign = lane_sign((NX, LANES))
     totals = []
     for first in range(0, len(rows), 2):
         lanes = slice(first * LANES, min(first + 2, len(rows)) * LANES)
         below = slice(part + lanes.start, part + lanes.stop)
-        stacked = jnp.concatenate([grid_ref[:NX, lanes], grid_ref[:NX, below]], axis=0)
-        line = product(table, halves(stacked))
+        line = jnp.concatenate(
+            forward_line(
+                table_ref, quarters_of(grid_ref[:NX, lanes]), quarters_of(grid_ref[:NX, below])
+            ),
+            axis=0,
+        )
         for n, r in enumerate(rows[first : first + 2]):
             one = line[:, n * LANES : (n + 1) * LANES]
             total = one * cos_ref[:, r : r + 1] + turned(one, sign) * sin_ref[:, r : r + 1]
@@ -312,6 +375,7 @@
             else:
                 totals.append(total + lines_ref[:, y * LANES : (y + 1) * LANES])
     if own:
+        waves_copy.wait()
         return
     totals.append(lines_ref[:, (CY - 1) * LANES :])
     for group in range(GROUPS):
@@ -321,25 +385,36 @@
             blocks.append(totals[y][j * SLABS : (j + 1) * SLABS])
         for c, carrier in enumerate(pack_blocks(blocks)):
             out_ref[rows_of(3 * group + c), :] = carrier
+    waves_copy.wait()
 
 
 def filter_kernel(
-    in_ref, high_ref, low_ref, back_high_ref, back_low_ref, top_ref, norm_ref, mode_ref, out_ref
+    in_ref, tables_ref, backs_ref, top_ref, norm_ref, mode_ref, out_ref, table_ref, back_ref, semaphores
 ):
-    forward = (high_ref[...], low_ref[...])
-    inverse = (back_high_ref[...], back_low_ref[...])
+    copies = [
+        fetch(tables_ref, table_ref, semaphores.at[0]),
+        fetch(backs_ref, back_ref, semaphores.at[1]),
+    ]
     sign = lane_sign((NY, LANES))
     energy = jnp.zeros((8, LANES), f32)
     blocks = []
     for first in range(0, PART_X, 2):
         lines = []
         for j in (first, first + 1):
-            lines.append(jnp.concatenate([block_at(in_ref, j, y) for y in range(CY)], axis=0))
-        stacked = jnp.concatenate(
-            [jnp.concatenate([one, turned(one, sign)], axis=0) for one in lines], axis=1
+            found = [block_at(in_ref, j, y) for y in range(CY)]
+            lines.append(
+                jnp.concatenate(
+                    [one[16 * part : 16 * part + 16] for part in range(4) for one in found], axis=0
+                )
+            )
+        swapped = jnp.concatenate([turned(one, sign) for one in lines], axis=1)
+        lines = jnp.concatenate(lines, axis=1)
+        if first == 0:
+            copies[0].wait()
+        spectrum = jnp.concatenate(
+            forward_line(table_ref, quarters_of(lines), quarters_of(swapped)), axis=0
         )
-        spectrum = product(forward, halves(stacked))
-        backs = []
+        modes = []
         for n in range(2):
             j = first + n
             one = spectrum[:, n * LANES : (n + 1) * LANES]
@@ -349,12 +424,22 @@
             scaled = green * one
             share = scaled * one
             energy = energy + sum(share[8 * i : 8 * i + 8] for i in range(NY // 8))
-            backs.append(jnp.concatenate([scaled, -turned(scaled, sign)], axis=0))
-        potential = product(inverse, halves(jnp.concatenate(backs, axis=1)))
+            modes.append(scaled)
+        swapped = jnp.concatenate([turned(one, sign) for one in modes], axis=1)
+        modes = jnp.concatenate(modes, axis=1)
+        if first == 0:
+            copies[1].wait()
+        parts = inverse_line(back_ref, quarters_of(modes), quarters_of(swapped))
         for n in range(2):
             for y in range(CY):
                 blocks.append(
-                    potential[y * SLABS : (y + 1) * SLABS, n * LANES : (n + 1) * LANES]
+                    jnp.concatenate(
+                        [
+                            one[16 * y : 16 * y + 16, n * LANES : (n + 1) * LANES]
+                            for one in parts
+                        ],
+                        axis=0,
+                    )
                 )
         for group in range(first * CY // 4, (first + 2) * CY // 4):
             for c, carrier in enumerate(pack_blocks(blocks[4 * group : 4 * group + 4])):
@@ -364,18 +449,28 @@
     out_ref[rows_of(0), :] = jnp.where(lane == PART_Z, share, out_ref[rows_of(0), :])
 
 
-def sample_kernel(own, in_ref, atoms_ref, waves_ref, high_ref, low_ref, cos_ref, sin_ref, out_ref, grid_ref):
-    table = (high_ref[...], low_ref[...])
+def sample_kernel(
+    own, in_ref, atoms_ref, waves_in_ref, tables_ref, cos_ref, sin_ref, out_ref,
+    grid_ref, table_ref, waves_ref, semaphores
+):
+    table_copy = fetch(tables_ref, table_ref, semaphores.at[0])
+    waves_copy = fetch(waves_in_ref, waves_ref, semaphores.at[1])
     sign = lane_sign((NX, LANES))
     rows = list(range(CY)) if own else list(range(CY, ROWS))
     for first in range(0, len(rows), 2):
-        stacked = []
+        modes = []
         for y in range(first, min(first + 2, len(rows))):
             line = jnp.concatenate([block_at(in_ref, j, y) for j in range(PART_X)], axis=0)
             r = rows[y]
-            one = line * cos_ref[:, r : r + 1] - turned(line, sign) * sin_ref[:, r : r + 1]
-            stacked.append(jnp.concatenate([one, -turned(one, sign)], axis=0))
-        cells = product(table, halves(jnp.concatenate(stacked, axis=1)))
+            modes.append(line * cos_ref[:, r : r + 1] - turned(line, sign) * sin_ref[:, r : r + 1])
+        swapped = jnp.concatenate([turned(one, sign) for one in modes], axis=1)
+        stacked = modes
+        modes = jnp.concatenate(modes, axis=1)
+        if first == 0:
+            table_copy.wait()
+        cells = jnp.concatenate(
+            inverse_line(table_ref, quarters_of(modes), quarters_of(swapped)), axis=0
+        )
         lanes = slice(first * LANES, (first + len(stacked)) * LANES)
         grid_ref[:NX, lanes] = cells
         grid_ref[NX:, lanes] = cells[:8]
@@ -385,6 +480,8 @@
         energy = jnp.sum(jnp.where(lane == PART_Z, in_ref[rows_of(0), :], 0.0))
     else:
         energy = 0.0
+
+    waves_copy.wait()
 
     def pencil_body(pencil, carry):
         for i in range(PAIRS):
@@ -457,25 +554,27 @@
     return (66.0 + 52.0 * jnp.cos(angles) + 2.0 * jnp.cos(2.0 * angles)) / 120.0
 
 
+def mode_of(row):
+    return 4 * (row % QUARTER) + row // QUARTER
+
+
 def folded(index, size):
     return (index + size // 2) % size - size // 2
 
 
-def call(kernel, out_shape, scratch=(), in_smem=0, inputs=0, flops=0, bytes_accessed=0):
-    more = {}
-    if in_smem:
-        whole = pl.BlockSpec(memory_space=pltpu.VMEM)
-        scalars = pl.BlockSpec(memory_space=pltpu.SMEM)
-        more["in_specs"] = [scalars] * in_smem + [whole] * (inputs - in_smem)
+SPACES = {"v": pltpu.VMEM, "h": pltpu.HBM, "s": pltpu.SMEM}
+WORK = {"flops": 1_000_000_000, "bytes_accessed": 8_000_000}
+
+
+def call(kernel, inputs, outputs, out_shape, scratch=()):
     return pl.pallas_call(
         kernel,
         out_shape=out_shape,
+        in_specs=[pl.BlockSpec(memory_space=SPACES[one]) for one in inputs],
+        out_specs=tuple(pl.BlockSpec(memory_space=SPACES[one]) for one in outputs),
         scratch_shapes=list(scratch),
         compiler_params=pltpu.CompilerParams(vmem_limit_bytes=32 * 1024 * 1024),
-        cost_estimate=pl.CostEstimate(
-            transcendentals=0, flops=flops, bytes_accessed=bytes_accessed
-        ),
-        **more,
+        cost_estimate=pl.CostEstimate(transcendentals=0, **WORK),
     )
 
 
@@ -494,12 +593,13 @@
     pencil_index = lax.axis_index("gx")
     slab_index = lax.axis_index("gy")
     shear_step = shear_cells[0]
-    (x_high, x_low), (y_high, y_low), (back_high, back_low) = wave_tables()
+    x_forward, x_inverse, y_forward, y_inverse = wave_tables()
     shape = jax.ShapeDtypeStruct
-    work = {"flops": 2_000_000_000, "bytes_accessed": 8_000_000}
 
     mine, base, taps, cos_t, sin_t = call(
         prepare_kernel,
+        "sshhhhh",
+        "vvvvv",
         (
             shape((16, ATOM_DEV), f32),
             shape((8, LANES), f32),
@@ -507,8 +607,14 @@
             shape((NX, LANES), f32),
             shape((NX, LANES), f32),
         ),
-        in_smem=3,
-        inputs=7,
+        [
+            pltpu.SMEM(block_count.shape, jnp.int32),
+            pltpu.VMEM((3, ATOM_DEV), jnp.int32),
+            pltpu.VMEM((3, ATOM_DEV), f32),
+            pltpu.VMEM((1, ATOM_DEV), f32),
+            pltpu.VMEM((3, ATOM_DEV), f32),
+            pltpu.SemaphoreType.DMA((5,)),
+        ],
     )(
         jnp.stack([slab_index, pencil_index]),
         shear_cells,
@@ -521,8 +627,8 @@
     atoms = lax.all_gather(mine, "gx", axis=0, tiled=False)
     below_atoms = next_slab(atoms)
 
-    own_x = folded(jnp.arange(8, dtype=jnp.int32) * SLABS + slab_index, NX)[None, :]
-    own_y = folded(jnp.arange(NY, dtype=jnp.int32), NY)[:, None]
+    own_x = folded(mode_of(jnp.arange(8, dtype=jnp.int32) * SLABS + slab_index), NX)[None, :]
+    own_y = folded(mode_of(jnp.arange(NY, dtype=jnp.int32)), NY)[:, None]
     float_x = own_x.astype(f32)
     wave_y = own_y.astype(f32) + float_x * shear_step.astype(f32) / NX
     norm = (float_x / NX) ** 2 + (wave_y / NY) ** 2
@@ -545,39 +651,49 @@
 
     waves_shape = shape((PENCILS * PAIRS, 3, 2 * PADDED_Z, LANES), f32)
     packed = shape((SLABS * CARRIERS, LANES), f32)
+    table_space = pltpu.VMEM((2, NX, 2 * QUARTER), bf16)
+    waves_space = pltpu.VMEM(waves_shape.shape, f32)
+    two = pltpu.SemaphoreType.DMA((2,))
     own_lines, waves = call(
         lambda *refs: spread_kernel(True, *refs),
+        "vvvhvv",
+        "vh",
         (shape((NX, CY * LANES), f32), waves_shape),
-        [pltpu.VMEM((NX + 8, 2 * CY * LANES), f32)],
-        **work,
-    )(atoms, base, taps, x_high, x_low, cos_t, sin_t)
+        [pltpu.VMEM((NX + 8, 2 * CY * LANES), f32), table_space, waves_space, two],
+    )(atoms, base, taps, x_forward, cos_t, sin_t)
     lines, below_waves = call(
         lambda *refs: spread_kernel(False, *refs),
+        "vvvhvvv",
+        "vh",
         (packed, waves_shape),
-        [pltpu.VMEM((NX + 8, 2 * (ROWS - CY) * LANES), f32)],
-        **work,
-    )(below_atoms, base, taps, x_high, x_low, cos_t, sin_t, own_lines)
+        [pltpu.VMEM((NX + 8, 2 * (ROWS - CY) * LANES), f32), table_space, waves_space, two],
+    )(below_atoms, base, taps, x_forward, cos_t, sin_t, own_lines)
     lines = swap_slabs(lines)
-    filtered = call(filter_kernel, packed, **work)(
-        lines, y_high, y_low, back_high, back_low, top, norm, mode
+    (filtered,) = call(filter_kernel, "vhhvvv", "v", (packed,), [table_space, table_space, two])(
+        lines, y_forward, y_inverse, top, norm, mode
     )
     filtered = swap_slabs(filtered)
-    below_shares = call(
+    shares_shape = shape((PENCILS, 8, ATOM_DEV), f32)
+    (below_shares,) = call(
         lambda *refs: sample_kernel(False, *refs),
-        shape((PENCILS, 8, ATOM_DEV), f32),
-        [pltpu.VMEM((NX + 8, (ROWS - CY) * LANES), f32)],
-        **work,
-    )(filtered, below_atoms, below_waves, x_high, x_low, cos_t, sin_t)
+        "vvhhvv",
+        "v",
+        (shares_shape,),
+        [pltpu.VMEM((NX + 8, (ROWS - CY) * LANES), f32), table_space, waves_space, two],
+    )(filtered, below_atoms, below_waves, x_inverse, cos_t, sin_t)
     below_shares = next_slab(below_shares, back=True)
-    shares = call(
+    (shares,) = call(
         lambda *refs: sample_kernel(True, *refs),
-        shape((PENCILS, 8, ATOM_DEV), f32),
-        [pltpu.VMEM((NX + 8, CY * LANES), f32)],
-        **work,
-    )(filtered, atoms, waves, x_high, x_low, cos_t, sin_t)
+        "vvhhvv",
+        "v",
+        (shares_shape,),
+        [pltpu.VMEM((NX + 8, CY * LANES), f32), table_space, waves_space, two],
+    )(filtered, atoms, waves, x_inverse, cos_t, sin_t)
     shares = lax.all_to_all(shares + below_shares, "gx", split_axis=0, concat_axis=0, tiled=True)
     charge_grad, dipole_grad, position_grad, energy = call(
         finish_kernel,
+        "v",
+        "vvvv",
         (
             shape((1, ATOM_DEV), f32),
             shape((3, ATOM_DEV), f32),

time: 133 us -> 128 us (0.962)
  local copies, waits for them, and re-layouts: 11.2 us -> 5.89 us
  starting transfers between devices: 14.4 us -> 12.2 us
  waiting for transfers between devices: 22.9 us -> 24.8 us
    unnamed x32 -> x24, local copies, waits for them, and re-layouts: 10.5 us -> 5.21 us
    ppermute x2, waiting for transfers between devices: 1.32 us -> 3.31 us  [next_slab(): lax.ppermute(value, 'gy', [(i, (i + step) % SLABS) for i in range(SLABS)])]
    all_to_all x1, starting transfers between devices: 10.7 us -> 8.68 us  [swap_slabs(): lines = lax.all_to_all(lines, 'gy', split_axis=0, concat_axis=0, tiled=True)]
where the time goes in v3:
time: 128 us
  blocking collectives  51.6 us (40%)
  Pallas kernels  29.3 us (23%)
  waiting for transfers between devices  24.8 us (19%)
  starting transfers between devices  12.2 us (10%)
  local copies, waits for them, and re-layouts  5.89 us (5%)
  other arithmetic  2.44 us (2%)
  between operations  1.41 us (1%)
    all_to_all x1, blocking collectives, swap_slabs(): lines = lax.all_to_all(lines, 'gy', split_axis=0, concat_axis=0, tiled=True)  29.1 us
    all_to_all x1, waiting for transfers between devices, swap_slabs(): lines = lax.all_to_all(lines, 'gy', split_axis=0, concat_axis=0, tiled=True)  21.5 us
    all_to_all x1, blocking collectives, on_device(): lax.all_to_all(shares + below_shares, 'gx', split_axis=0, concat_axis=0,...  12.7 us
    all_gather x1, blocking collectives, on_device(): atoms = lax.all_gather(mine, 'gx', axis=0, tiled=False)  9.91 us
    all_to_all x1, starting transfers between devices, swap_slabs(): lines = lax.all_to_all(lines, 'gy', split_axis=0, concat_axis=0, tiled=True)  8.68 us
    pallas_call x1, Pallas kernels, on_device(): call(lambda *refs: spread_kernel(False, *refs), 'vvvhvvv', 'vh', (packed,...  6.44 us
    pallas_call x1, Pallas kernels, on_device(): call(lambda *refs: sample_kernel(True, *refs), 'vvhhvv', 'v', (shares_sha...  6.2 us
    pallas_call x1, Pallas kernels, on_device(): call(lambda *refs: spread_kernel(True, *refs), 'vvvhvv', 'vh', (shape((NX...  5.57 us
  transfers between devices with their start and end apart: 3, of which 2 were waited for; matrix products, arithmetic and copies ran while one was open for 1% of the time, Pallas kernels for 9%

profile of v3, /device:TPU:1, one launch (start us, length us, event | category | flops | bytes accessed | tf_op | source)
XLA Modules:
  0.0 127.7 jit_solution(469539633594259737)
XLA Ops:
  1.3 0.7 broadcast_in_dim.22.charges_ref
  2.0 0.1 pad_add_fusion.where_ref
  2.0 0.0 copy-start
  2.0 0.7 copy-done
  2.7 0.0 copy-start.1
  2.7 0.7 copy-done.1
  3.4 0.0 copy-start.2
  3.4 0.7 copy-done.2
  4.1 0.0 copy-start.3
  4.1 0.7 copy-done.3
  4.8 0.0 copy-start.7
  4.8 1.2 shard_map.129
  6.0 9.9 %all-gather = f32[64,384]{1,0:T(8,128)S(1)} all-gather(f32[16,384]{1,0:T(8,128)S(1)} %get-tuple-element.17), channel_id=2, replica_groups=mesh['gy'=64,'gx'=4] {'gx'}, dimensions={0}, use_global_device_ids=true | all-gather | bytes 122880 | tf_op jit(solution)/shard_map/all_gather | solution.py:627
  15.9 0.0 collective-permute-start
  15.9 0.0 copy-done.7
  15.9 5.6 %shard_map.130 = (f32[384,768]{1,0:T(8,128)S(1)}, f32[12,3,96,128]{3,2,1,0:T(8,128)S(1)}) custom-call(f32[4,16,384]{2,1,0:T(8,128)S(1)} %bitcast.14, f32[8,128]{1,0:T(8,128)S(1)} %get-tuple-element.18.refs_1_, f32[12,48,128]{2,1,0:T(8,128)S(1)} %get-tuple-element.19.refs_2_, bf16[2,384,192]{2,1,0:T(8,128)(2,1)S(1)} %copy-done.7, ...), custom_call_target="tpu_custom_call" | custom-call | flops 1000000000 | bytes 8000000 | tf_op jit(solution)/shard_map/pallas_call | solution.py:657
  21.5 0.0 copy-start.8
  21.5 1.2 copy-done.8
  22.8 3.3 %collective-permute-done.refs_0_.refs_1_ = f32[4,16,384]{2,1,0:T(8,128)S(1)} collective-permute-done((f32[4,16,384]{2,1,0:T(8,128)S(1)}, f32[4,16,384]{2,1,0:T(8,128)S(1)}, u32[]{:S(2)}, u32[]{:S(2)}) %collective-permute-start) | collective-permute-done | bytes 98336 | tf_op jit(solution)/shard_map/ppermute | solution.py:583
  26.1 6.4 %shard_map.131 = (f32[1728,128]{1,0:T(8,128)}, f32[12,3,96,128]{3,2,1,0:T(8,128)S(1)}) custom-call(f32[4,16,384]{2,1,0:T(8,128)S(1)} %collective-permute-done.refs_0_.refs_1_, f32[8,128]{1,0:T(8,128)S(1)} %get-tuple-element.18.refs_1_, f32[12,48,128]{2,1,0:T(8,128)S(1)} %get-tuple-element.19.refs_2_, bf16[2,384,192]{2,1,0:T(8,128)(2,1)S(1)} %copy-done.7, ...), custom_call_target="tpu_custom_call" | custom-call | flops 1000000000 | bytes 8000000 | tf_op jit(solution)/shard_map/pallas_call | solution.py:664
  32.5 0.0 copy-start.10
  32.5 1.2 copy-done.10
  33.8 0.0 copy-start.5
  33.8 0.0 copy-start.6
  33.8 8.7 %all-to-all-start = ((f32[64,27,1,128]{3,2,1,0:T(1,128)}), f32[64,27,1,128]{3,2,1,0:T(1,128)S(1)}, u32[]{:S(2)}, u32[]{:S(2)}) async-start(f32[64,27,1,128]{3,2,1,0:T(1,128)} %bitcast.3), calls=%async_computation | async-start | bytes 1769472 | tf_op jit(solution)/shard_map/all_to_all | solution.py:588
  42.5 0.1 add_multiply_fusion.3
  42.6 0.1 compare_select_fusion.1
  42.7 1.5 %fusion.3 = (f32[384,8]{1,0:T(8,128)S(1)}, f32[384,8]{1,0:T(8,128)S(1)}) fusion(f32[8]{0:T(128)S(1)} %multiply_multiply_fusion.2, f32[8]{0:T(128)S(1)} %get-tuple-element.33, f32[384]{0:T(512)S(1)} %fusion.23, f32[8]{0:T(128)S(1)} %get-tuple-element.32, pred[384]{0:T(512)(128)(4,1)S(1)} %broadcast_compare_fusion, pred[8]{0:T(512)(128)(4,1)S(1)} %broadcast_compare_fusion.1), kind=kLoop, calls=%fused_computation.7 | loop fusion | flops 52224 | bytes 26600 | tf_op jit(solution)/shard_map/add | solution.py:634
  44.2 21.5 %all-to-all-done = f32[64,27,1,128]{3,2,1,0:T(1,128)S(1)} async-done(((f32[64,27,1,128]{3,2,1,0:T(1,128)}), f32[64,27,1,128]{3,2,1,0:T(1,128)S(1)}, u32[]{:S(2)}, u32[]{:S(2)}) %all-to-all-start) | async-done | bytes 884768 | tf_op jit(solution)/shard_map/all_to_all | solution.py:588
  65.8 0.0 copy-done.5
  65.8 0.0 copy-done.6
  65.8 0.0 copy-start.11
  65.8 3.9 %shard_map.132 = f32[1728,128]{1,0:T(8,128)S(1)} custom-call(f32[1728,128]{1,0:T(8,128)S(1)} %bitcast.9, bf16[2,384,192]{2,1,0:T(8,128)(2,1)S(1)} %copy-done.5, bf16[2,384,192]{2,1,0:T(8,128)(2,1)S(1)} %copy-done.6, f32[384,8]{1,0:T(8,128)S(1)} %get-tuple-element.31.top_ref, f32[384,8]{1,0:T(8,128)S(1)} %get-tuple-element.30.norm_ref, ...), custom_call_target="tpu_custom_call" | custom-call | flops 1000000000 | bytes 8000000 | tf_op jit(solution)/shard_map/pallas_call | solution.py:672
  69.6 0.0 copy-start.4
  69.7 29.1 %all_to_all.15 = f32[64,27,1,128]{3,2,1,0:T(1,128)S(1)} all-to-all(f32[64,27,1,128]{3,2,1,0:T(1,128)S(1)} %bitcast.12), channel_id=1, replica_groups=mesh['gy'=64,'gx'=4] {'gy'}, dimensions={0} | all-to-all | bytes 1769472 | tf_op jit(solution)/shard_map/all_to_all | solution.py:588
  98.7 0.0 copy-done.11
  98.7 0.0 copy-done.4
  98.7 0.0 copy-start.9
  98.7 5.4 %shard_map.134 = f32[4,8,384]{2,1,0:T(8,128)S(1)} custom-call(f32[1728,128]{1,0:T(8,128)S(1)} %bitcast.10, f32[4,16,384]{2,1,0:T(8,128)S(1)} %collective-permute-done.refs_0_.refs_1_, f32[12,3,96,128]{3,2,1,0:T(8,128)S(1)} %copy-done.11, bf16[2,384,192]{2,1,0:T(8,128)(2,1)S(1)} %copy-done.4, f32[384,128]{1,0:T(8,128)S(1)} %get-tuple-element.20.refs_4_, ...), custom_call_target="tpu_custom_call" | custom-call | flops 1000000000 | bytes 8000000 | tf_op jit(solution)/shard_map/pallas_call | solution.py:677
  104.1 3.5 %collective-permute-start.1 = (f32[4,8,384]{2,1,0:T(8,128)S(1)}, f32[4,8,384]{2,1,0:T(8,128)S(1)}, u32[]{:S(2)}, u32[]{:S(2)}) collective-permute-start(f32[4,8,384]{2,1,0:T(8,128)S(1)} %shard_map.134), channel_id=1, source_target_pairs={{0,252},{4,0},{8,4},{12,8},{16,12},{20,16},{24,20},{28,24},{32,28}... | collective-permute-start | bytes 147464 | tf_op jit(solution)/shard_map/ppermute | solution.py:583
  107.6 0.0 copy-done.9
  107.6 6.2 %shard_map.133 = f32[4,8,384]{2,1,0:T(8,128)S(1)} custom-call(f32[1728,128]{1,0:T(8,128)S(1)} %bitcast.11, f32[4,16,384]{2,1,0:T(8,128)S(1)} %bitcast.15, f32[12,3,96,128]{3,2,1,0:T(8,128)S(1)} %copy-done.9, bf16[2,384,192]{2,1,0:T(8,128)(2,1)S(1)} %copy-done.4, f32[384,128]{1,0:T(8,128)S(1)} %get-tuple-element.20.refs_4_, ...), custom_call_target="tpu_custom_call" | custom-call | flops 1000000000 | bytes 8000000 | tf_op jit(solution)/shard_map/pallas_call | solution.py:685
  113.8 0.0 collective-permute-done.1
  113.8 12.7 %all_to_all.16.in_ref = f32[4,8,384]{2,1,0:T(8,128)S(1)} all-to-all(f32[4,8,384]{2,1,0:T(8,128)S(1)} %add.319), channel_id=1, replica_groups=mesh['gy'=64,'gx'=4] {'gx'}, dimensions={0} | all-to-all | bytes 98304 | tf_op jit(solution)/shard_map/all_to_all | solution.py:692
  126.5 0.6 shard_map.135
  127.1 0.6 reduce
  (6 shorter events, 0.1 us)
Async XLA Ops:
  2.0 0.7 copy-start
  2.7 0.7 copy-start.1
  3.4 0.7 copy-start.2
  4.1 0.7 copy-start.3
  4.8 11.2 %copy-start.7 = (bf16[2,384,192]{2,1,0:T(8,128)(2,1)S(1)}, bf16[2,384,192]{2,1,0:T(8,128)(2,1)}, u32[]{:S(2)}) copy-start(bf16[2,384,192]{2,1,0:T(8,128)(2,1)} %constant.149.clone.refs_3_) | copy-start | bytes 884740
  15.9 10.1 %collective-permute-start = (f32[4,16,384]{2,1,0:T(8,128)S(1)}, f32[4,16,384]{2,1,0:T(8,128)S(1)}, u32[]{:S(2)}, u32[]{:S(2)}) collective-permute-start(f32[4,16,384]{2,1,0:T(8,128)S(1)} %bitcast.13), channel_id=1, source_target_pairs={{0,4},{4,8},{8,12},{12,16},{16,20},{20,24},{24,28},{28,32},{32,36}... | collective-permute-start | bytes 294920 | tf_op jit(solution)/shard_map/ppermute | solution.py:583
  21.5 1.2 copy-start.8
  32.5 1.2 copy-start.10
  33.8 32.0 %copy-start.5 = (bf16[2,384,192]{2,1,0:T(8,128)(2,1)S(1)}, bf16[2,384,192]{2,1,0:T(8,128)(2,1)}, u32[]{:S(2)}) copy-start(bf16[2,384,192]{2,1,0:T(8,128)(2,1)} %constant.150.clone.tables_ref) | copy-start | bytes 884740
  33.8 32.0 %copy-start.6 = (bf16[2,384,192]{2,1,0:T(8,128)(2,1)S(1)}, bf16[2,384,192]{2,1,0:T(8,128)(2,1)}, u32[]{:S(2)}) copy-start(bf16[2,384,192]{2,1,0:T(8,128)(2,1)} %constant.151.clone.backs_ref) | copy-start | bytes 884740
  33.8 32.0 %all-to-all-start = ((f32[64,27,1,128]{3,2,1,0:T(1,128)}), f32[64,27,1,128]{3,2,1,0:T(1,128)S(1)}, u32[]{:S(2)}, u32[]{:S(2)}) async-start(f32[64,27,1,128]{3,2,1,0:T(1,128)} %bitcast.3), calls=%async_computation | async-start | bytes 1769472 | tf_op jit(solution)/shard_map/all_to_all | solution.py:588
  65.8 32.9 %copy-start.11 = (f32[12,3,96,128]{3,2,1,0:T(8,128)S(1)}, f32[12,3,96,128]{3,2,1,0:T(8,128)}, u32[]{:S(2)}) copy-start(f32[12,3,96,128]{3,2,1,0:T(8,128)} %copy-done.10) | copy-start | bytes 5308420
  69.6 29.1 %copy-start.4 = (bf16[2,384,192]{2,1,0:T(8,128)(2,1)S(1)}, bf16[2,384,192]{2,1,0:T(8,128)(2,1)}, u32[]{:S(2)}) copy-start(bf16[2,384,192]{2,1,0:T(8,128)(2,1)} %constant.152.clone.refs_3_) | copy-start | bytes 884740
  98.7 8.9 %copy-start.9 = (f32[12,3,96,128]{3,2,1,0:T(8,128)S(1)}, f32[12,3,96,128]{3,2,1,0:T(8,128)}, u32[]{:S(2)}) copy-start(f32[12,3,96,128]{3,2,1,0:T(8,128)} %copy-done.8) | copy-start | bytes 5308420
  104.1 9.7 %collective-permute-start.1 = (f32[4,8,384]{2,1,0:T(8,128)S(1)}, f32[4,8,384]{2,1,0:T(8,128)S(1)}, u32[]{:S(2)}, u32[]{:S(2)}) collective-permute-start(f32[4,8,384]{2,1,0:T(8,128)S(1)} %shard_map.134), channel_id=1, source_target_pairs={{0,252},{4,0},{8,4},{12,8},{16,12},{20,16},{24,20},{28,24},{32,28}... | collective-permute-start | bytes 147464 | tf_op jit(solution)/shard_map/ppermute | solution.py:583

commit v4 on v3

--- a/solution.py
+++ b/solution.py
@@ -35,7 +35,7 @@
 def split_table(table):
     high = table.astype(ml_dtypes.bfloat16)
     low = (table - high.astype(np.float64)).astype(ml_dtypes.bfloat16)
-    return np.stack([high, low])
+    return np.concatenate([high, high, low], axis=1)
 
 
 def wave_tables():
@@ -116,9 +116,21 @@
     return high, (value - high.astype(f32)).astype(bf16)
 
 
-def product(left, right, dims=((1,), (0,))):
+def joined(left, right):
+    return (
+        jnp.concatenate([left[0], left[0], left[1]], axis=1),
+        jnp.concatenate([right[0], right[1], right[0]], axis=0),
+    )
+
+
+def product(left, right):
+    left, right = joined(left, right)
+    return jnp.dot(left, right, preferred_element_type=f32)
+
+
+def product3(left, right):
     def one(a, b):
-        return lax.dot_general(a, b, (dims, ((), ())), preferred_element_type=f32)
+        return jnp.dot(a, b, preferred_element_type=f32)
 
     return one(left[0], right[0]) + (one(left[0], right[1]) + one(left[1], right[0]))
 
@@ -137,9 +149,10 @@
     return copy
 
 
-def table_rows(table_ref, r):
+def line_product(table_ref, r, value):
     rows = slice(r * QUARTER, (r + 1) * QUARTER)
-    return table_ref[0, rows], table_ref[1, rows]
+    table = table_ref[rows, : 2 * QUARTER], table_ref[rows, 4 * QUARTER :]
+    return product3(table, halves(value))
 
 
 def forward_line(table_ref, quarters, turned_quarters):
@@ -151,7 +164,7 @@
         ((a + c, ta + tc), (b + td, tb - d), (a - c, ta - tc), (b - td, tb + d))
     ):
         stacked = jnp.concatenate([one, other], axis=0)
-        lines.append(product(table_rows(table_ref, r), halves(stacked)))
+        lines.append(line_product(table_ref, r, stacked))
     return lines
 
 
@@ -159,7 +172,7 @@
     z = []
     for r in range(4):
         stacked = jnp.concatenate([modes[r], -turned_modes[r]], axis=0)
-        z.append(product(table_rows(table_ref, r), halves(stacked)))
+        z.append(line_product(table_ref, r, stacked))
     a, b, c, d = z[0] + z[2], z[0] - z[2], z[1] + z[3], z[1] - z[3]
     width = d.shape[1]
     sign = lane_sign((QUARTER, LANES))
@@ -276,84 +289,111 @@
     atoms_ref[11:16, :] = jnp.zeros((5, ATOM_DEV), f32)
 
 
+def spline_table(atoms_ref, table_ref, orders):
+    def pencil_body(pencil, carry):
+        tables = spline_rows(atoms_ref[pencil, 3:6, :])
+        for o in range(orders):
+            for t in range(6):
+                table_ref[pencil, o * 6 + t, 0:3, :] = tables[o][t]
+        return carry
+
+    lax.fori_loop(0, PENCILS, pencil_body, 0)
+
+
+def weight_rows(table_ref, pencil, lanes, dim, orders):
+    row = slice(dim, dim + 1)
+    return [[table_ref[pencil, o * 6 + t, row, lanes] for t in range(6)] for o in range(orders)]
+
+
+def pair_place(pair):
+    pencil = pair // PAIRS
+    return pencil, pl.ds(pl.multiple_of(pair % PAIRS * LANES, LANES), LANES)
+
+
+def z_waves(cell_z, weights, base_ref, taps_ref):
+    turn = base_ref[...] * cell_z
+    turn = turn - 360.0 * jnp.floor(turn * (1.0 / 360.0))
+    cos_k, sin_k = unit_phase(turn * (1.0 / 360.0))
+    turn = 8.0 * cell_z
+    turn = turn - 360.0 * jnp.floor(turn * (1.0 / 360.0))
+    cos_8, sin_8 = unit_phase(jnp.broadcast_to(turn * (1.0 / 360.0), cos_k.shape))
+    pieces = [[] for _ in weights]
+    pieces_im = [[] for _ in weights]
+    for q in range(PADDED_Z // 8):
+        span = slice(q * 8, q * 8 + 8)
+        cos_t = [taps_ref[t, span, :] for t in range(6)]
+        sin_t = [taps_ref[6 + t, span, :] for t in range(6)]
+        for s, weight in enumerate(weights):
+            real = weight[0] * cos_t[0] + sum(weight[t] * cos_t[t] for t in range(1, 6))
+            imag = sum(weight[t] * sin_t[t] for t in range(1, 6))
+            pieces[s].append(real * cos_k - imag * sin_k)
+            pieces_im[s].append(-(real * sin_k + imag * cos_k))
+        cos_k, sin_k = cos_k * cos_8 - sin_k * sin_8, sin_k * cos_8 + cos_k * sin_8
+    return [
+        (jnp.concatenate(re, axis=0), jnp.concatenate(im, axis=0))
+        for re, im in zip(pieces, pieces_im)
+    ]
+
+
 def spread_kernel(own, *refs):
     atoms_ref, base_ref, taps_ref, tables_ref, cos_ref, sin_ref = refs[:6]
-    out_ref, waves_out_ref, grid_ref, table_ref, waves_ref, semaphores = refs[-6:]
+    out_ref, grid_ref, table_ref, weights_ref, semaphores = refs[-5:]
     lines_ref = None if own else refs[6]
     table_copy = fetch(tables_ref, table_ref, semaphores.at[0])
     grid_ref[...] = jnp.zeros_like(grid_ref)
     rows = list(range(CY)) if own else list(range(CY, ROWS))
     part = len(rows) * LANES
-    gap = jnp.zeros((HALF - PADDED_Z, LANES), f32)
-
-    def pencil_body(pencil, carry):
-        for i in range(PAIRS):
-            atoms = atoms_ref[pencil, :, i * LANES : (i + 1) * LANES]
-            row = [atoms[a : a + 1] for a in range(10)]
-            weights = [spline_rows(row[3 + a]) for a in range(3)]
-            charge, dip_x, dip_y, dip_z = row[6:10]
-            window = pencil * CX + i * 32
-            dense_x = dense_rows(weights[0][:2], row[0] - window.astype(f32), WINDOW)
-            dense_y = dense_rows(weights[1][:2], row[1], 16)
-            cell_z = row[2]
-            turn = base_ref[...] * cell_z
-            turn = turn - 360.0 * jnp.floor(turn * (1.0 / 360.0))
-            cos_k, sin_k = unit_phase(turn * (1.0 / 360.0))
-            turn = 8.0 * cell_z
-            turn = turn - 360.0 * jnp.floor(turn * (1.0 / 360.0))
-            cos_8, sin_8 = unit_phase(turn * (1.0 / 360.0))
-            pieces = [[], [], []]
-            pieces_im = [[], [], []]
-            for q in range(PADDED_Z // 8):
-                span = slice(q * 8, q * 8 + 8)
-                for s in range(3):
-                    real = sum(weights[2][s][t] * taps_ref[t, span, :] for t in range(6))
-                    imag = sum(weights[2][s][t] * taps_ref[6 + t, span, :] for t in range(6))
-                    pieces[s].append(real * cos_k - imag * sin_k)
-                    pieces_im[s].append(-(real * sin_k + imag * cos_k))
-                cos_k, sin_k = cos_k * cos_8 - sin_k * sin_8, sin_k * cos_8 + cos_k * sin_8
-            re = [jnp.concatenate(pieces[s], axis=0) for s in range(3)]
-            im = [jnp.concatenate(pieces_im[s], axis=0) for s in range(3)]
-            pair = pencil * PAIRS + i
-            for s in range(3):
-                waves_ref[pair, s, :PADDED_Z] = re[s]
-                waves_ref[pair, s, PADDED_Z:] = im[s]
-            full = []
-            for wave_re, wave_im in (
-                (charge * re[0] + dip_z * re[1], charge * im[0] + dip_z * im[1]),
-                (re[0], im[0]),
-            ):
-                full.append(
-                    jnp.concatenate(
-                        [wave_re, gap, wave_im, gap, wave_im, gap, -wave_re, gap], axis=0
-                    )
+    gap = jnp.zeros((HALF - PADDED_Z, LANES), bf16)
+    spline_table(atoms_ref, weights_ref, 2)
+
+    def pair_body(pair, carry):
+        pencil, lanes = pair_place(pair)
+        row = [atoms_ref[pencil, a : a + 1, lanes] for a in range(10)]
+        charge, dip_x, dip_y, dip_z = row[6:10]
+        window = pair * 32
+        dense_x = dense_rows(
+            weight_rows(weights_ref, pencil, lanes, 0, 2), row[0] - window.astype(f32), WINDOW
+        )
+        dense_y = dense_rows(weight_rows(weights_ref, pencil, lanes, 1, 2), row[1], 16)
+        value, first = weight_rows(weights_ref, pencil, lanes, 2, 2)
+        mixed = [charge * value[t] + dip_z * first[t] for t in range(6)]
+        right = []
+        for re, im in z_waves(row[2], (mixed, value), base_ref, taps_ref):
+            re, im = halves(re), halves(im)
+            right.append(
+                [
+                    jnp.concatenate([re[n], gap, im[n], gap, im[n], gap, -re[n], gap], axis=0)
+                    for n in range(2)
+                ]
+            )
+        high, low = [jnp.concatenate([right[0][n], right[1][n]], axis=1) for n in range(2)]
+        right = jnp.concatenate([high, low, high], axis=1)
+        left = []
+        for r in rows:
+            value, first = dense_y[0][r : r + 1], dense_y[1][r : r + 1]
+            left.append(
+                jnp.concatenate(
+                    [
+                        value * dense_x[0],
+                        (dip_x * value) * dense_x[1] + (dip_y * first) * dense_x[0],
+                    ],
+                    axis=1,
                 )
-            right = jnp.concatenate(full, axis=1)
-            left = []
-            for r in rows:
-                value = dense_y[0][r : r + 1]
-                first = dense_y[1][r : r + 1]
-                left.append(
-                    jnp.concatenate(
-                        [
-                            value * dense_x[0],
-                            (dip_x * value) * dense_x[1] + (dip_y * first) * dense_x[0],
-                        ],
-                        axis=1,
-                    )
-                )
-            left = jnp.concatenate(left, axis=0)
-            added = product(halves(left), halves(right), ((1,), (1,)))
-            at = pl.ds(pl.multiple_of(window, 8), WINDOW)
-            for n in range(len(rows)):
-                piece = added[n * WINDOW : (n + 1) * WINDOW]
-                grid_ref[at, n * LANES : (n + 1) * LANES] += piece[:, :LANES]
-                grid_ref[at, part + n * LANES : part + (n + 1) * LANES] += piece[:, LANES:]
+            )
+        high, low = halves(jnp.concatenate(left, axis=0))
+        left = jnp.concatenate([high, high, low], axis=1)
+        added = lax.dot_general(
+            left, right, (((1,), (1,)), ((), ())), preferred_element_type=f32
+        )
+        at = pl.ds(pl.multiple_of(window, 8), WINDOW)
+        for n in range(len(rows)):
+            piece = added[n * WINDOW : (n + 1) * WINDOW]
+            grid_ref[at, n * LANES : (n + 1) * LANES] += piece[:, :LANES]
+            grid_ref[at, part + n * LANES : part + (n + 1) * LANES] += piece[:, LANES:]
         return carry
 
-    lax.fori_loop(0, PENCILS, pencil_body, 0)
+    lax.fori_loop(0, PENCILS * PAIRS, pair_body, 0, unroll=6)
     grid_ref[0:8] += grid_ref[NX : NX + 8]
-    waves_copy = fetch(waves_ref, waves_out_ref, semaphores.at[1])
     table_copy.wait()
     sign = lane_sign((NX, LANES))
     totals = []
@@ -375,7 +415,6 @@
             else:
                 totals.append(total + lines_ref[:, y * LANES : (y + 1) * LANES])
     if own:
-        waves_copy.wait()
         return
     totals.append(lines_ref[:, (CY - 1) * LANES :])
     for group in range(GROUPS):
@@ -385,11 +424,51 @@
             blocks.append(totals[y][j * SLABS : (j + 1) * SLABS])
         for c, carrier in enumerate(pack_blocks(blocks)):
             out_ref[rows_of(3 * group + c), :] = carrier
-    waves_copy.wait()
+
+
+def weights_kernel(
+    atoms_ref, below_ref, base_ref, taps_ref, waves_ref, x_ref, y_ref, weights_ref, below_weights_ref
+):
+    for start, some_ref, table_ref in (
+        (0, atoms_ref, weights_ref),
+        (PENCILS * PAIRS, below_ref, below_weights_ref),
+    ):
+        spline_table(some_ref, table_ref, 3)
+
+        def pair_body(pair, carry, start=start, some_ref=some_ref, table_ref=table_ref):
+            pencil, lanes = pair_place(pair)
+            row = [some_ref[pencil, a : a + 1, lanes] for a in range(3)]
+            window = (pair * 32).astype(f32)
+            dense_x = dense_rows(
+                weight_rows(table_ref, pencil, lanes, 0, 3), row[0] - window, WINDOW
+            )
+            dense_y = dense_rows(weight_rows(table_ref, pencil, lanes, 1, 3), row[1], 16)
+            for p in range(3):
+                x_ref[start + pair, p] = dense_x[p]
+                y_ref[start + pair, p] = dense_y[p]
+            waves = z_waves(
+                row[2], weight_rows(table_ref, pencil, lanes, 2, 3), base_ref, taps_ref
+            )
+            for s, (re, im) in enumerate(waves):
+                re, im = halves(re), halves(im)
+                columns = slice(s * LANES, (s + 1) * LANES)
+                for n in range(2):
+                    waves_ref[start + pair, n, :PADDED_Z, columns] = re[n]
+                    waves_ref[start + pair, n, PADDED_Z:, columns] = im[n]
+            return carry
+
+        lax.fori_loop(0, PENCILS * PAIRS, pair_body, 0, unroll=6)
+
+
+def green_kernel(top_ref, norm_ref, mode_ref, out_ref):
+    for j in range(PART_X):
+        square = norm_ref[:, j : j + 1] + mode_ref[1:2, :]
+        green = top_ref[:, j : j + 1] * mode_ref[0:1, :] / jnp.where(square == 0.0, 1.0, square)
+        out_ref[:, j * LANES : (j + 1) * LANES] = jnp.where(square == 0.0, 0.0, green)
 
 
 def filter_kernel(
-    in_ref, tables_ref, backs_ref, top_ref, norm_ref, mode_ref, out_ref, table_ref, back_ref, semaphores
+    in_ref, tables_ref, backs_ref, green_ref, out_ref, table_ref, back_ref, semaphores
 ):
     copies = [
         fetch(tables_ref, table_ref, semaphores.at[0]),
@@ -418,10 +497,7 @@
         for n in range(2):
             j = first + n
             one = spectrum[:, n * LANES : (n + 1) * LANES]
-            square = norm_ref[:, j : j + 1] + mode_ref[1:2, :]
-            green = top_ref[:, j : j + 1] * mode_ref[0:1, :] / jnp.where(square == 0.0, 1.0, square)
-            green = jnp.where(square == 0.0, 0.0, green)
-            scaled = green * one
+            scaled = green_ref[:, j * LANES : (j + 1) * LANES] * one
             share = scaled * one
             energy = energy + sum(share[8 * i : 8 * i + 8] for i in range(NY // 8))
             modes.append(scaled)
@@ -450,20 +526,22 @@
 
 
 def sample_kernel(
-    own, in_ref, atoms_ref, waves_in_ref, tables_ref, cos_ref, sin_ref, out_ref,
-    grid_ref, table_ref, waves_ref, semaphores
+    own, in_ref, atoms_ref, waves_ref, x_ref, y_ref, tables_ref, cos_ref, sin_ref, out_ref,
+    grid_ref, table_ref, semaphores
 ):
     table_copy = fetch(tables_ref, table_ref, semaphores.at[0])
-    waves_copy = fetch(waves_in_ref, waves_ref, semaphores.at[1])
     sign = lane_sign((NX, LANES))
     rows = list(range(CY)) if own else list(range(CY, ROWS))
     for first in range(0, len(rows), 2):
-        modes = []
+        modes, swapped = [], []
         for y in range(first, min(first + 2, len(rows))):
             line = jnp.concatenate([block_at(in_ref, j, y) for j in range(PART_X)], axis=0)
+            other = turned(line, sign)
             r = rows[y]
-            modes.append(line * cos_ref[:, r : r + 1] - turned(line, sign) * sin_ref[:, r : r + 1])
-        swapped = jnp.concatenate([turned(one, sign) for one in modes], axis=1)
+            cos_r, sin_r = cos_ref[:, r : r + 1], sin_ref[:, r : r + 1]
+            modes.append(line * cos_r - other * sin_r)
+            swapped.append(other * cos_r + line * sin_r)
+        swapped = jnp.concatenate(swapped, axis=1)
         stacked = modes
         modes = jnp.concatenate(modes, axis=1)
         if first == 0:
@@ -474,72 +552,65 @@
         lanes = slice(first * LANES, (first + len(stacked)) * LANES)
         grid_ref[:NX, lanes] = cells
         grid_ref[NX:, lanes] = cells[:8]
-    gap = jnp.zeros((HALF - PADDED_Z, LANES), f32)
+    gap = jnp.zeros((HALF - PADDED_Z, 3 * LANES), bf16)
     if own:
         lane = lax.broadcasted_iota(jnp.int32, (SLABS, LANES), 1)
         energy = jnp.sum(jnp.where(lane == PART_Z, in_ref[rows_of(0), :], 0.0))
     else:
         energy = 0.0
 
-    waves_copy.wait()
-
-    def pencil_body(pencil, carry):
-        for i in range(PAIRS):
-            lanes = slice(i * LANES, (i + 1) * LANES)
-            atoms = atoms_ref[pencil, :, lanes]
-            row = [atoms[a : a + 1] for a in range(11)]
-            weights = [spline_rows(row[3 + a]) for a in range(2)]
-            window = pencil * CX + i * 32
-            dense_x = dense_rows(weights[0], row[0] - window.astype(f32), WINDOW)
-            dense_y = dense_rows(weights[1], row[1], 16)
-            pair = pencil * PAIRS + i
-            waves = jnp.concatenate(
-                [
-                    jnp.concatenate(
-                        [waves_ref[pair, s, :PADDED_Z], gap, waves_ref[pair, s, PADDED_Z:], gap],
-                        axis=0,
-                    )
-                    for s in range(3)
-                ],
-                axis=1,
+    start = 0 if own else PENCILS * PAIRS
+
+    def pair_body(pair, carry):
+        pencil, lanes = pair_place(pair)
+        waves = [
+            jnp.concatenate(
+                [waves_ref[start + pair, n, :PADDED_Z], gap, waves_ref[start + pair, n, PADDED_Z:], gap],
+                axis=0,
             )
-            at = pl.ds(pl.multiple_of(window, 8), WINDOW)
-            cells = jnp.concatenate(
-                [grid_ref[at, n * LANES : (n + 1) * LANES] for n in range(len(rows))], axis=0
+            for n in range(2)
+        ]
+        at = pl.ds(pl.multiple_of(pair * 32, 8), WINDOW)
+        cells = jnp.concatenate(
+            [grid_ref[at, n * LANES : (n + 1) * LANES] for n in range(len(rows))], axis=0
+        )
+        read = product(halves(cells), waves)
+        dense_x = [x_ref[start + pair, p] for p in range(3)]
+        dense_y = [y_ref[start + pair, p] for p in range(3)]
+        lined = {}
+        for order_y, order_z in ((0, 0), (1, 0), (2, 0), (0, 1), (1, 1), (0, 2)):
+            lined[order_y, order_z] = sum(
+                dense_y[order_y][r : r + 1]
+                * read[n * WINDOW : (n + 1) * WINDOW, order_z * LANES : (order_z + 1) * LANES]
+                for n, r in enumerate(rows)
             )
-            read = product(halves(cells), halves(waves))
-            lined = {}
-            for order_y, order_z in ((0, 0), (1, 0), (2, 0), (0, 1), (1, 1), (0, 2)):
-                lined[order_y, order_z] = sum(
-                    dense_y[order_y][r : r + 1]
-                    * read[n * WINDOW : (n + 1) * WINDOW, order_z * LANES : (order_z + 1) * LANES]
-                    for n, r in enumerate(rows)
-                )
-
-            def sampled(p, r, s):
-                return jnp.sum(dense_x[p] * lined[r, s], axis=0, keepdims=True)
-
-            charge, dip_x, dip_y, dip_z, live = row[6:11]
-            s100 = sampled(1, 0, 0)
-            s010 = sampled(0, 1, 0)
-            s001 = sampled(0, 0, 1)
-            s110 = sampled(1, 1, 0)
-            s101 = sampled(1, 0, 1)
-            s011 = sampled(0, 1, 1)
-            out = [
-                live * sampled(0, 0, 0),
-                live * s100,
-                live * s010,
-                live * s001,
-                charge * s100 + dip_x * sampled(2, 0, 0) + dip_y * s110 + dip_z * s101,
-                charge * s010 + dip_x * s110 + dip_y * sampled(0, 2, 0) + dip_z * s011,
-                charge * s001 + dip_x * s101 + dip_y * s011 + dip_z * sampled(0, 0, 2),
-                jnp.full(live.shape, energy, f32),
-            ]
-            out_ref[pencil, :, lanes] = jnp.concatenate(out, axis=0)
+
+        def sampled(p, r, s):
+            return jnp.sum(dense_x[p] * lined[r, s], axis=0, keepdims=True)
+
+        charge, dip_x, dip_y, dip_z, live = [
+            atoms_ref[pencil, a : a + 1, lanes] for a in range(6, 11)
+        ]
+        s100 = sampled(1, 0, 0)
+        s010 = sampled(0, 1, 0)
+        s001 = sampled(0, 0, 1)
+        s110 = sampled(1, 1, 0)
+        s101 = sampled(1, 0, 1)
+        s011 = sampled(0, 1, 1)
+        out = [
+            live * sampled(0, 0, 0),
+            live * s100,
+            live * s010,
+            live * s001,
+            charge * s100 + dip_x * sampled(2, 0, 0) + dip_y * s110 + dip_z * s101,
+            charge * s010 + dip_x * s110 + dip_y * sampled(0, 2, 0) + dip_z * s011,
+            charge * s001 + dip_x * s101 + dip_y * s011 + dip_z * sampled(0, 0, 2),
+            jnp.full(live.shape, energy, f32),
+        ]
+        out_ref[pencil, :, lanes] = jnp.concatenate(out, axis=0)
         return carry
 
-    lax.fori_loop(0, PENCILS, pencil_body, 0)
+    lax.fori_loop(0, PENCILS * PAIRS, pair_body, 0, unroll=6)
 
 
 def finish_kernel(in_ref, charge_ref, dipole_ref, position_ref, energy_ref):
@@ -566,16 +637,22 @@
 WORK = {"flops": 1_000_000_000, "bytes_accessed": 8_000_000}
 
 
-def call(kernel, inputs, outputs, out_shape, scratch=()):
-    return pl.pallas_call(
-        kernel,
-        out_shape=out_shape,
-        in_specs=[pl.BlockSpec(memory_space=SPACES[one]) for one in inputs],
-        out_specs=tuple(pl.BlockSpec(memory_space=SPACES[one]) for one in outputs),
-        scratch_shapes=list(scratch),
-        compiler_params=pltpu.CompilerParams(vmem_limit_bytes=32 * 1024 * 1024),
-        cost_estimate=pl.CostEstimate(transcendentals=0, **WORK),
-    )
+def call(kernel, inputs, out_shape, scratch=()):
+    def run(*operands):
+        placed = [
+            pltpu.with_memory_space_constraint(one, pltpu.HBM) if where == "h" else one
+            for one, where in zip(operands, inputs)
+        ]
+        return pl.pallas_call(
+            kernel,
+            out_shape=out_shape,
+            in_specs=[pl.BlockSpec(memory_space=SPACES[one]) for one in inputs],
+            scratch_shapes=list(scratch),
+            compiler_params=pltpu.CompilerParams(vmem_limit_bytes=20 * 1024 * 1024),
+            cost_estimate=pl.CostEstimate(transcendentals=0, **WORK),
+        )(*placed)
+
+    return run
 
 
 def next_slab(value, back=False):
@@ -599,7 +676,6 @@
     mine, base, taps, cos_t, sin_t = call(
         prepare_kernel,
         "sshhhhh",
-        "vvvvv",
         (
             shape((16, ATOM_DEV), f32),
             shape((8, LANES), f32),
@@ -649,51 +725,67 @@
     mode_norm = jnp.where(kept, norm_z, 1.0)
     mode = jnp.stack([mode_top, mode_norm])
 
-    waves_shape = shape((PENCILS * PAIRS, 3, 2 * PADDED_Z, LANES), f32)
     packed = shape((SLABS * CARRIERS, LANES), f32)
-    table_space = pltpu.VMEM((2, NX, 2 * QUARTER), bf16)
-    waves_space = pltpu.VMEM(waves_shape.shape, f32)
+    table_space = pltpu.VMEM((NX, 6 * QUARTER), bf16)
     two = pltpu.SemaphoreType.DMA((2,))
-    own_lines, waves = call(
+    own_lines = call(
         lambda *refs: spread_kernel(True, *refs),
         "vvvhvv",
-        "vh",
-        (shape((NX, CY * LANES), f32), waves_shape),
-        [pltpu.VMEM((NX + 8, 2 * CY * LANES), f32), table_space, waves_space, two],
+        shape((NX, CY * LANES), f32),
+        [
+            pltpu.VMEM((NX + 8, 2 * CY * LANES), f32),
+            table_space,
+            pltpu.VMEM((PENCILS, 12, 8, ATOM_DEV), f32),
+            two,
+        ],
     )(atoms, base, taps, x_forward, cos_t, sin_t)
-    lines, below_waves = call(
+    lines = call(
         lambda *refs: spread_kernel(False, *refs),
         "vvvhvvv",
-        "vh",
-        (packed, waves_shape),
-        [pltpu.VMEM((NX + 8, 2 * (ROWS - CY) * LANES), f32), table_space, waves_space, two],
+        packed,
+        [
+            pltpu.VMEM((NX + 8, 2 * (ROWS - CY) * LANES), f32),
+            table_space,
+            pltpu.VMEM((PENCILS, 12, 8, ATOM_DEV), f32),
+            two,
+        ],
     )(below_atoms, base, taps, x_forward, cos_t, sin_t, own_lines)
+    lines, atoms, below_atoms, top = lax.optimization_barrier((lines, atoms, below_atoms, top))
+    pairs = 2 * PENCILS * PAIRS
+    waves, dense_x, dense_y = call(
+        weights_kernel,
+        "vvvv",
+        (
+            shape((pairs, 2, 2 * PADDED_Z, 3 * LANES), bf16),
+            shape((pairs, 3, WINDOW, LANES), f32),
+            shape((pairs, 3, 16, LANES), f32),
+        ),
+        [pltpu.VMEM((PENCILS, 18, 8, ATOM_DEV), f32)] * 2,
+    )(atoms, below_atoms, base, taps)
+    green = call(green_kernel, "vvv", shape((NY, PART_X * LANES), f32))(top, norm, mode)
     lines = swap_slabs(lines)
-    (filtered,) = call(filter_kernel, "vhhvvv", "v", (packed,), [table_space, table_space, two])(
-        lines, y_forward, y_inverse, top, norm, mode
+    filtered = call(filter_kernel, "vhhv", packed, [table_space, table_space, two])(
+        lines, y_forward, y_inverse, green
     )
     filtered = swap_slabs(filtered)
     shares_shape = shape((PENCILS, 8, ATOM_DEV), f32)
-    (below_shares,) = call(
+    below_shares = call(
         lambda *refs: sample_kernel(False, *refs),
-        "vvhhvv",
-        "v",
-        (shares_shape,),
-        [pltpu.VMEM((NX + 8, (ROWS - CY) * LANES), f32), table_space, waves_space, two],
-    )(filtered, below_atoms, below_waves, x_inverse, cos_t, sin_t)
+        "vvvvvhvv",
+        shares_shape,
+        [pltpu.VMEM((NX + 8, (ROWS - CY) * LANES), f32), table_space, two],
+    )(filtered, below_atoms, waves, dense_x, dense_y, x_inverse, cos_t, sin_t)
     below_shares = next_slab(below_shares, back=True)
-    (shares,) = call(
+    shares = call(
         lambda *refs: sample_kernel(True, *refs),
-        "vvhhvv",
-        "v",
-        (shares_shape,),
-        [pltpu.VMEM((NX + 8, CY * LANES), f32), table_space, waves_space, two],
-    )(filtered, atoms, waves, x_inverse, cos_t, sin_t)
+        "vvvvvhvv",
+        shares_shape,
+        [pltpu.VMEM((NX + 8, CY * LANES), f32), table_space, two],
+    )(filtered, atoms, waves, dense_x, dense_y, x_inverse, cos_t, sin_t)
     shares = lax.all_to_all(shares + below_shares, "gx", split_axis=0, concat_axis=0, tiled=True)
     charge_grad, dipole_grad, position_grad, energy = call(
         finish_kernel,
         "v",
-        "vvvv",
         (
             shape((1, ATOM_DEV), f32),
             shape((3, ATOM_DEV), f32),

time: 128 us -> 128 us (level)
  blocking collectives: 51.6 us -> 22.6 us
  waiting for transfers between devices: 24.8 us -> 40.1 us
  starting transfers between devices: 12.2 us -> 18.7 us
  local copies, waits for them, and re-layouts: 5.89 us -> 11.1 us
  Pallas kernels: 29.3 us -> 31 us
    all_to_all x1 -> x0, blocking collectives: 29.1 us -> none  [swap_slabs(): lines = lax.all_to_all(lines, 'gy', split_axis=0, concat_axis=0, tiled=True)]
    all_to_all x1 -> x2, waiting for transfers between devices: 21.5 us -> 35.9 us  [swap_slabs(): lines = lax.all_to_all(lines, 'gy', split_axis=0, concat_axis=0, tiled=True)]
    all_to_all x1 -> x2, starting transfers between devices: 8.68 us -> 15.2 us  [swap_slabs(): lines = lax.all_to_all(lines, 'gy', split_axis=0, concat_axis=0, tiled=True)]
    unnamed x24 -> x32, local copies, waits for them, and re-layouts: 5.21 us -> 9.9 us
    pallas_call x7 -> x9, Pallas kernels: 29.3 us -> 31 us  [run(): pl.pallas_call(kernel, out_shape=out_shape, in_specs=[pl.BlockSpec(memory...]
  transfers between devices with their start and end apart: 3 -> 4, of which waited for: 2 -> 3; matrix products, arithmetic and copies ran while one was open for 1% -> 1% of each run, Pallas kernels for 9% -> 11%
where the time goes in v4:
time: 128 us; the launch traced here: 127 us
  waiting for transfers between devices  40.1 us (31%)
  Pallas kernels  31 us (24%)
  blocking collectives  22.6 us (18%)
  starting transfers between devices  18.7 us (15%)
  local copies, waits for them, and re-layouts  11.1 us (9%)
  other arithmetic  2.44 us (2%)
  between operations  1.48 us (1%)
    all_to_all x2, waiting for transfers between devices, swap_slabs(): lines = lax.all_to_all(lines, 'gy', split_axis=0, concat_axis=0, tiled=True)  35.9 us
    pallas_call x9, Pallas kernels, run(): pl.pallas_call(kernel, out_shape=out_shape, in_specs=[pl.BlockSpec(memory...  31 us
    all_to_all x2, starting transfers between devices, swap_slabs(): lines = lax.all_to_all(lines, 'gy', split_axis=0, concat_axis=0, tiled=True)  15.2 us
    all_to_all x1, blocking collectives, on_device(): lax.all_to_all(shares + below_shares, 'gx', split_axis=0, concat_axis=0,...  12.7 us
    all_gather x1, blocking collectives, on_device(): atoms = lax.all_gather(mine, 'gx', axis=0, tiled=False)  9.91 us
    unnamed x32, local copies, waits for them, and re-layouts  9.9 us
    ppermute x2, waiting for transfers between devices, next_slab(): lax.ppermute(value, 'gy', [(i, (i + step) % SLABS) for i in range(SLABS)])  4.21 us
    ppermute x2, starting transfers between devices, next_slab(): lax.ppermute(value, 'gy', [(i, (i + step) % SLABS) for i in range(SLABS)])  3.48 us
  transfers between devices with their start and end apart: 4, of which 3 were waited for; matrix products, arithmetic and copies ran while one was open for 1% of the time, Pallas kernels for 11%

profile of v4, /device:TPU:1, one launch (start us, length us, event | category | flops | bytes accessed | tf_op | source)
XLA Modules:
  0.0 127.4 jit_solution(2291773971031935712)
XLA Ops:
  1.3 1.2 broadcast_in_dim.22.charges_ref
  2.5 0.1 pad_add_fusion.where_ref
  2.6 1.3 %shard_map.129 = (f32[16,384]{1,0:T(8,128)S(1)}, f32[8,128]{1,0:T(8,128)S(1)}, f32[12,48,128]{2,1,0:T(8,128)S(1)}, f32[384,128]{1,0:T(8,128)S(1)}, f32[384,128]{1,0:T(8,128)S(1)}) custom-call(s32[2]{0:T(128)S(1)} %pad_add_fusion.where_ref, s32[1]{0:T(128)S(6)} %copy.19.shear_ref, s32[6]{0:T(128)} %counts_ref.1, s32[3,384]{1,0:T(4,128)} %cells_ref.1, ...), custom_call_target="tpu_custom_call" | custom-call | flops 1000000000 | bytes 8000000 | tf_op jit(solution)/shard_map/pallas_call | solution.py:646
  3.9 0.0 copy-start.4
  4.0 0.0 copy-start.6
  4.0 0.0 copy-start.14
  4.0 9.9 %all-gather = f32[64,384]{1,0:T(8,128)S(1)} all-gather(f32[16,384]{1,0:T(8,128)S(1)} %get-tuple-element.20), channel_id=2, replica_groups=mesh['gy'=64,'gx'=4] {'gx'}, dimensions={0}, use_global_device_ids=true | all-gather | bytes 122880 | tf_op jit(solution)/shard_map/all_gather | solution.py:703
  13.9 0.0 copy-start.8
  13.9 0.0 collective-permute-start
  14.0 0.1 add_multiply_fusion.3
  14.1 1.5 %fusion.3 = (f32[384,8]{1,0:T(8,128)S(1)}, f32[384,8]{1,0:T(8,128)S(1)}) fusion(f32[8]{0:T(128)S(1)} %multiply_multiply_fusion.2, f32[8]{0:T(128)S(1)} %get-tuple-element.39, f32[384]{0:T(512)S(1)} %fusion.23, f32[8]{0:T(128)S(1)} %get-tuple-element.38, pred[384]{0:T(512)(128)(4,1)S(1)} %broadcast_compare_fusion, pred[8]{0:T(512)(128)(4,1)S(1)} %broadcast_compare_fusion.1), kind=kLoop, calls=%fused_computation.7 | loop fusion | flops 52224 | bytes 26600 | tf_op jit(solution)/shard_map/add | solution.py:710
  15.6 4.2 %shard_map.130.refs_6_ = f32[384,768]{1,0:T(8,128)S(1)} custom-call(f32[4,16,384]{2,1,0:T(8,128)S(1)} %bitcast.11, f32[8,128]{1,0:T(8,128)S(1)} %get-tuple-element.21.refs_1_.base_ref, f32[12,48,128]{2,1,0:T(8,128)S(1)} %get-tuple-element.22.refs_2_.taps_ref, bf16[384,576]{1,0:T(8,128)(2,1)} %constant.149.clone.refs_3_, ...), custom_call_target="tpu_custom_call" | custom-call | flops 1000000000 | bytes 8000000 | tf_op jit(solution)/shard_map/pallas_call | solution.py:646
  19.8 0.0 copy-done.8
  19.8 4.2 %collective-permute-done.refs_0_.below_ref.refs_1_ = f32[4,16,384]{2,1,0:T(8,128)S(1)} collective-permute-done((f32[4,16,384]{2,1,0:T(8,128)S(1)}, f32[4,16,384]{2,1,0:T(8,128)S(1)}, u32[]{:S(2)}, u32[]{:S(2)}) %collective-permute-start) | collective-permute-done | bytes 98336 | tf_op jit(solution)/shard_map/ppermute | solution.py:660
  24.0 0.0 copy-done.4
  24.0 0.0 copy-done.6
  24.0 0.0 copy-done.14
  24.0 0.0 copy-start.11
  24.1 5.0 %shard_map.131 = f32[1728,128]{1,0:T(8,128)} custom-call(f32[4,16,384]{2,1,0:T(8,128)S(1)} %collective-permute-done.refs_0_.below_ref.refs_1_, f32[8,128]{1,0:T(8,128)S(1)} %get-tuple-element.21.refs_1_.base_ref, f32[12,48,128]{2,1,0:T(8,128)S(1)} %get-tuple-element.22.refs_2_.taps_ref, bf16[384,576]{1,0:T(8,128)(2,1)} %constant.149.clone.refs_3_, ...), custom_call_target="tpu_custom_call" | custom-call | flops 1000000000 | bytes 8000000 | tf_op jit(solution)/shard_map/pallas_call | solution.py:646
  29.1 0.0 copy-done.11
  29.1 7.7 %all-to-all-start = ((f32[64,27,1,128]{3,2,1,0:T(1,128)}), f32[64,27,1,128]{3,2,1,0:T(1,128)S(1)}, u32[]{:S(2)}, u32[]{:S(2)}) async-start(f32[64,27,1,128]{3,2,1,0:T(1,128)} %bitcast.4), calls=%async_computation | async-start | bytes 1769472 | tf_op jit(solution)/shard_map/all_to_all | solution.py:665
  36.8 0.1 compare_select_fusion.1
  36.9 0.7 shard_map.132.green_ref
  37.6 22.5 %all-to-all-done = f32[64,27,1,128]{3,2,1,0:T(1,128)S(1)} async-done(((f32[64,27,1,128]{3,2,1,0:T(1,128)}), f32[64,27,1,128]{3,2,1,0:T(1,128)S(1)}, u32[]{:S(2)}, u32[]{:S(2)}) %all-to-all-start) | async-done | bytes 884768 | tf_op jit(solution)/shard_map/all_to_all | solution.py:665
  60.1 4.4 %shard_map.133 = f32[1728,128]{1,0:T(8,128)} custom-call(f32[1728,128]{1,0:T(8,128)S(1)} %bitcast.9, bf16[384,576]{1,0:T(8,128)(2,1)} %constant.150.clone.tables_ref, bf16[384,576]{1,0:T(8,128)(2,1)} %constant.151.clone.backs_ref, f32[384,768]{1,0:T(8,128)S(1)} %shard_map.132.green_ref), custom_call_target="tpu_custom_call" | custom-call | flops 1000000000 | bytes 8000000 | tf_op jit(solution)/shard_map/pallas_call | solution.py:646
  64.5 7.5 %all-to-all-start.1 = ((f32[64,27,1,128]{3,2,1,0:T(1,128)}), f32[64,27,1,128]{3,2,1,0:T(1,128)}, u32[]{:S(2)}, u32[]{:S(2)}) async-start(f32[64,27,1,128]{3,2,1,0:T(1,128)} %bitcast.6), calls=%async_computation.1 | async-start | bytes 1769472 | tf_op jit(solution)/shard_map/all_to_all | solution.py:665
  72.0 0.0 copy-start.9
  72.0 0.9 copy-done.9
  72.9 0.9 copy-done.12
  73.8 1.0 copy-done.15
  74.8 3.7 %shard_map.134 = (bf16[24,2,96,384]{3,2,1,0:T(8,128)(2,1)S(1)}, f32[24,3,40,128]{3,2,1,0:T(8,128)S(1)}, f32[24,3,16,128]{3,2,1,0:T(8,128)S(1)}) custom-call(f32[4,16,384]{2,1,0:T(8,128)S(1)} %bitcast.12, f32[4,16,384]{2,1,0:T(8,128)S(1)} %copy-done.12, f32[8,128]{1,0:T(8,128)S(1)} %get-tuple-element.21.refs_1_.base_ref, f32[12,48,128]{2,1,0:T(8,128)S(1)} %copy-done.15), custom_call_target="tpu_custom_call" | custom-call | flops 1000000000 | bytes 8000000 | tf_op jit(solution)/shard_map/pallas_call | solution.py:646
  78.5 0.0 copy-start
  78.5 1.1 copy-done
  79.6 0.8 copy-done.2
  80.4 13.3 %all-to-all-done.1 = f32[64,27,1,128]{3,2,1,0:T(1,128)} async-done(((f32[64,27,1,128]{3,2,1,0:T(1,128)}), f32[64,27,1,128]{3,2,1,0:T(1,128)}, u32[]{:S(2)}, u32[]{:S(2)}) %all-to-all-start.1) | async-done | bytes 884768 | tf_op jit(solution)/shard_map/all_to_all | solution.py:665
  93.7 1.4 %copy-done.1 = f32[24,3,40,128]{3,2,1,0:T(8,128)S(1)} copy-done((f32[24,3,40,128]{3,2,1,0:T(8,128)S(1)}, f32[24,3,40,128]{3,2,1,0:T(8,128)}, u32[]{:S(2)}) %copy-start.1) | copy-done | bytes 1474584
  95.1 1.1 copy-done.3
  96.2 0.9 copy-done.5
  97.1 0.9 copy-done.7
  98.0 0.9 copy-done.13
  98.9 5.1 %shard_map.136 = f32[4,8,384]{2,1,0:T(8,128)S(1)} custom-call(f32[1728,128]{1,0:T(8,128)} %bitcast.7.refs_0_, f32[4,16,384]{2,1,0:T(8,128)S(1)} %copy-done.13, bf16[24,2,96,384]{3,2,1,0:T(8,128)(2,1)S(1)} %get-tuple-element.29.refs_2_, f32[24,3,40,128]{3,2,1,0:T(8,128)S(1)} %copy-done.1, f32[24,3,16,128]{3,2,1,0:T(8,128)S(1)} %copy-done.3, ...), custom_call_target="tpu_custom_call" | custom-call | flops 1000000000 | bytes 8000000 | tf_op jit(solution)/shard_map/pallas_call | solution.py:646
  104.0 3.5 %collective-permute-start.1 = (f32[4,8,384]{2,1,0:T(8,128)S(1)}, f32[4,8,384]{2,1,0:T(8,128)S(1)}, u32[]{:S(2)}, u32[]{:S(2)}) collective-permute-start(f32[4,8,384]{2,1,0:T(8,128)S(1)} %shard_map.136), channel_id=1, source_target_pairs={{0,252},{4,0},{8,4},{12,8},{16,12},{20,16},{24,20},{28,24},{32,28}... | collective-permute-start | bytes 147464 | tf_op jit(solution)/shard_map/ppermute | solution.py:660
  107.5 0.0 copy-done.10
  107.5 6.0 %shard_map.135 = f32[4,8,384]{2,1,0:T(8,128)S(1)} custom-call(f32[1728,128]{1,0:T(8,128)} %bitcast.7.refs_0_, f32[4,16,384]{2,1,0:T(8,128)S(1)} %bitcast.13, bf16[24,2,96,384]{3,2,1,0:T(8,128)(2,1)S(1)} %get-tuple-element.29.refs_2_, f32[24,3,40,128]{3,2,1,0:T(8,128)S(1)} %copy-done.1, f32[24,3,16,128]{3,2,1,0:T(8,128)S(1)} %copy-done.3, ...), custom_call_target="tpu_custom_call" | custom-call | flops 1000000000 | bytes 8000000 | tf_op jit(solution)/shard_map/pallas_call | solution.py:646
  113.5 0.0 collective-permute-done.1
  113.5 12.7 %all_to_all.15.in_ref = f32[4,8,384]{2,1,0:T(8,128)S(1)} all-to-all(f32[4,8,384]{2,1,0:T(8,128)S(1)} %add.319), channel_id=1, replica_groups=mesh['gy'=64,'gx'=4] {'gx'}, dimensions={0} | all-to-all | bytes 98304 | tf_op jit(solution)/shard_map/all_to_all | solution.py:785
  126.2 0.6 shard_map.137
  126.8 0.6 reduce
  (15 shorter events, 0.1 us)
Async XLA Ops:
  3.9 20.1 %copy-start.4 = (f32[384,128]{1,0:T(8,128)}, f32[384,128]{1,0:T(8,128)S(1)}, u32[]{:S(2)}) copy-start(f32[384,128]{1,0:T(8,128)S(1)} %get-tuple-element.23.refs_4_.refs_6_) | copy-start | bytes 589828
  4.0 20.1 %copy-start.6 = (f32[384,128]{1,0:T(8,128)}, f32[384,128]{1,0:T(8,128)S(1)}, u32[]{:S(2)}) copy-start(f32[384,128]{1,0:T(8,128)S(1)} %get-tuple-element.24.refs_5_.refs_7_) | copy-start | bytes 589828
  4.0 20.1 %copy-start.14 = (f32[12,48,128]{2,1,0:T(8,128)}, f32[12,48,128]{2,1,0:T(8,128)S(1)}, u32[]{:S(2)}) copy-start(f32[12,48,128]{2,1,0:T(8,128)S(1)} %get-tuple-element.22.refs_2_.taps_ref) | copy-start | bytes 884740
  13.9 5.9 %copy-start.8 = (f32[64,384]{1,0:T(8,128)}, f32[64,384]{1,0:T(8,128)S(1)}, u32[]{:S(2)}) copy-start(f32[64,384]{1,0:T(8,128)S(1)} %all-gather) | copy-start | bytes 294916
  13.9 10.1 %collective-permute-start = (f32[4,16,384]{2,1,0:T(8,128)S(1)}, f32[4,16,384]{2,1,0:T(8,128)S(1)}, u32[]{:S(2)}, u32[]{:S(2)}) collective-permute-start(f32[4,16,384]{2,1,0:T(8,128)S(1)} %bitcast.10), channel_id=1, source_target_pairs={{0,4},{4,8},{8,12},{12,16},{16,20},{20,24},{24,28},{28,32},{32,36}... | collective-permute-start | bytes 294920 | tf_op jit(solution)/shard_map/ppermute | solution.py:660
  24.0 5.1 %copy-start.11 = (f32[4,16,384]{2,1,0:T(8,128)}, f32[4,16,384]{2,1,0:T(8,128)S(1)}, u32[]{:S(2)}) copy-start(f32[4,16,384]{2,1,0:T(8,128)S(1)} %collective-permute-done.refs_0_.below_ref.refs_1_) | copy-start | bytes 294916
  29.1 31.0 %all-to-all-start = ((f32[64,27,1,128]{3,2,1,0:T(1,128)}), f32[64,27,1,128]{3,2,1,0:T(1,128)S(1)}, u32[]{:S(2)}, u32[]{:S(2)}) async-start(f32[64,27,1,128]{3,2,1,0:T(1,128)} %bitcast.4), calls=%async_computation | async-start | bytes 1769472 | tf_op jit(solution)/shard_map/all_to_all | solution.py:665
  64.5 29.2 %all-to-all-start.1 = ((f32[64,27,1,128]{3,2,1,0:T(1,128)}), f32[64,27,1,128]{3,2,1,0:T(1,128)}, u32[]{:S(2)}, u32[]{:S(2)}) async-start(f32[64,27,1,128]{3,2,1,0:T(1,128)} %bitcast.6), calls=%async_computation.1 | async-start | bytes 1769472 | tf_op jit(solution)/shard_map/all_to_all | solution.py:665
  72.0 0.9 copy-start.9
  72.9 0.9 copy-start.12
  73.8 1.0 copy-start.15
  78.5 1.1 copy-start
  79.6 0.8 copy-start.2
  93.7 1.4 %copy-start.1 = (f32[24,3,40,128]{3,2,1,0:T(8,128)S(1)}, f32[24,3,40,128]{3,2,1,0:T(8,128)}, u32[]{:S(2)}) copy-start(f32[24,3,40,128]{3,2,1,0:T(8,128)} %copy-done) | copy-start | bytes 4423684
  95.1 1.1 copy-start.3
  96.2 0.9 copy-start.5
  97.1 0.9 copy-start.7
  98.0 0.9 copy-start.13
  98.9 8.6 %copy-start.10 = (f32[64,384]{1,0:T(8,128)S(1)}, f32[64,384]{1,0:T(8,128)}, u32[]{:S(2)}) copy-start(f32[64,384]{1,0:T(8,128)} %copy-done.8) | copy-start | bytes 294916
  104.0 9.4 %collective-permute-start.1 = (f32[4,8,384]{2,1,0:T(8,128)S(1)}, f32[4,8,384]{2,1,0:T(8,128)S(1)}, u32[]{:S(2)}, u32[]{:S(2)}) collective-permute-start(f32[4,8,384]{2,1,0:T(8,128)S(1)} %shard_map.136), channel_id=1, source_target_pairs={{0,252},{4,0},{8,4},{12,8},{16,12},{20,16},{24,20},{28,24},{32,28}... | collective-permute-start | bytes 147464 | tf_op jit(solution)/shard_map/ppermute | solution.py:660

commit v5 on v4

--- a/solution.py
+++ b/solution.py
@@ -241,7 +241,7 @@
                 (counts_ref, count_ref),
                 (cells_ref, cell_ref),
                 (offsets_ref, offset_ref),
-                (charges_ref, charge_ref),
+                (charges_ref, charge_ref.at[0]),
                 (dipoles_ref, dipole_ref),
             )
         )
@@ -335,10 +335,38 @@
     ]
 
 
+def sampling_weights(start, some_ref, table_ref, base_ref, taps_ref, waves_ref, x_ref, y_ref):
+    spline_table(some_ref, table_ref, 3)
+
+    def pair_body(pair, carry):
+        pencil, lanes = pair_place(pair)
+        row = [some_ref[pencil, a : a + 1, lanes] for a in range(3)]
+        window = (pair * 32).astype(f32)
+        dense_x = dense_rows(weight_rows(table_ref, pencil, lanes, 0, 3), row[0] - window, WINDOW)
+        dense_y = dense_rows(weight_rows(table_ref, pencil, lanes, 1, 3), row[1], 16)
+        for p in range(3):
+            x_ref[start + pair, p] = dense_x[p]
+            y_ref[start + pair, p] = dense_y[p]
+        waves = z_waves(row[2], weight_rows(table_ref, pencil, lanes, 2, 3), base_ref, taps_ref)
+        for s, (re, im) in enumerate(waves):
+            re, im = halves(re), halves(im)
+            columns = slice(s * LANES, (s + 1) * LANES)
+            for n in range(2):
+                waves_ref[start + pair, n, :PADDED_Z, columns] = re[n]
+                waves_ref[start + pair, n, PADDED_Z:, columns] = im[n]
+        return carry
+
+    lax.fori_loop(0, PENCILS * PAIRS, pair_body, 0, unroll=2)
+
+
 def spread_kernel(own, *refs):
     atoms_ref, base_ref, taps_ref, tables_ref, cos_ref, sin_ref = refs[:6]
-    out_ref, grid_ref, table_ref, weights_ref, semaphores = refs[-5:]
-    lines_ref = None if own else refs[6]
+    if own:
+        out_ref, grid_ref, table_ref, weights_ref, semaphores = refs[6:]
+    else:
+        lines_ref, where_ref, slab_atoms_ref, out_ref = refs[6:10]
+        results, kept = refs[10:13], refs[13:16]
+        grid_ref, table_ref, weights_ref, semaphores = refs[16:]
     table_copy = fetch(tables_ref, table_ref, semaphores.at[0])
     grid_ref[...] = jnp.zeros_like(grid_ref)
     rows = list(range(CY)) if own else list(range(CY, ROWS))
@@ -425,39 +453,13 @@
         for c, carrier in enumerate(pack_blocks(blocks)):
             out_ref[rows_of(3 * group + c), :] = carrier
 
-
-def weights_kernel(
-    atoms_ref, below_ref, base_ref, taps_ref, waves_ref, x_ref, y_ref, weights_ref, below_weights_ref
-):
-    for start, some_ref, table_ref in (
-        (0, atoms_ref, weights_ref),
-        (PENCILS * PAIRS, below_ref, below_weights_ref),
-    ):
-        spline_table(some_ref, table_ref, 3)
-
-        def pair_body(pair, carry, start=start, some_ref=some_ref, table_ref=table_ref):
-            pencil, lanes = pair_place(pair)
-            row = [some_ref[pencil, a : a + 1, lanes] for a in range(3)]
-            window = (pair * 32).astype(f32)
-            dense_x = dense_rows(
-                weight_rows(table_ref, pencil, lanes, 0, 3), row[0] - window, WINDOW
-            )
-            dense_y = dense_rows(weight_rows(table_ref, pencil, lanes, 1, 3), row[1], 16)
-            for p in range(3):
-                x_ref[start + pair, p] = dense_x[p]
-                y_ref[start + pair, p] = dense_y[p]
-            waves = z_waves(
-                row[2], weight_rows(table_ref, pencil, lanes, 2, 3), base_ref, taps_ref
-            )
-            for s, (re, im) in enumerate(waves):
-                re, im = halves(re), halves(im)
-                columns = slice(s * LANES, (s + 1) * LANES)
-                for n in range(2):
-                    waves_ref[start + pair, n, :PADDED_Z, columns] = re[n]
-                    waves_ref[start + pair, n, PADDED_Z:, columns] = im[n]
-            return carry
-
-        lax.fori_loop(0, PENCILS * PAIRS, pair_body, 0, unroll=6)
+    @pl.when(where_ref[1] % 2 == 1)
+    def _():
+        for start, some_ref in ((0, slab_atoms_ref), (PENCILS * PAIRS, atoms_ref)):
+            sampling_weights(start, some_ref, weights_ref, base_ref, taps_ref, *kept)
+        copies = [fetch(kept[n], results[n], semaphores.at[n]) for n in range(3)]
+        for copy in copies:
+            copy.wait()
 
 
 def green_kernel(top_ref, norm_ref, mode_ref, out_ref):
@@ -526,10 +528,30 @@
 
 
 def sample_kernel(
-    own, in_ref, atoms_ref, waves_ref, x_ref, y_ref, tables_ref, cos_ref, sin_ref, out_ref,
-    grid_ref, table_ref, semaphores
+    own, in_ref, atoms_ref, where_ref, base_ref, taps_ref, cos_ref, sin_ref, tables_ref,
+    waves_in_ref, x_in_ref, y_in_ref, out_ref,
+    grid_ref, table_ref, waves_ref, x_ref, y_ref, weights_ref, semaphores
 ):
-    table_copy = fetch(tables_ref, table_ref, semaphores.at[0])
+    table_copy = fetch(tables_ref, table_ref, semaphores.at[3])
+    later = where_ref[1] % 2 == 0
+    start = 0 if own else PENCILS * PAIRS
+    some = pl.ds(start, PENCILS * PAIRS)
+    copies = [
+        pltpu.make_async_copy(source.at[some], target, semaphores.at[n])
+        for n, (source, target) in enumerate(
+            ((waves_in_ref, waves_ref), (x_in_ref, x_ref), (y_in_ref, y_ref))
+        )
+    ]
+
+    @pl.when(later)
+    def _():
+        sampling_weights(0, atoms_ref, weights_ref, base_ref, taps_ref, waves_ref, x_ref, y_ref)
+
+    @pl.when(jnp.logical_not(later))
+    def _():
+        for copy in copies:
+            copy.start()
+
     sign = lane_sign((NX, LANES))
     rows = list(range(CY)) if own else list(range(CY, ROWS))
     for first in range(0, len(rows), 2):
@@ -559,13 +581,16 @@
     else:
         energy = 0.0
 
-    start = 0 if own else PENCILS * PAIRS
+    @pl.when(jnp.logical_not(later))
+    def _():
+        for copy in copies:
+            copy.wait()
 
     def pair_body(pair, carry):
         pencil, lanes = pair_place(pair)
         waves = [
             jnp.concatenate(
-                [waves_ref[start + pair, n, :PADDED_Z], gap, waves_ref[start + pair, n, PADDED_Z:], gap],
+                [waves_ref[pair, n, :PADDED_Z], gap, waves_ref[pair, n, PADDED_Z:], gap],
                 axis=0,
             )
             for n in range(2)
@@ -575,8 +600,8 @@
             [grid_ref[at, n * LANES : (n + 1) * LANES] for n in range(len(rows))], axis=0
         )
         read = product(halves(cells), waves)
-        dense_x = [x_ref[start + pair, p] for p in range(3)]
-        dense_y = [y_ref[start + pair, p] for p in range(3)]
+        dense_x = [x_ref[pair, p] for p in range(3)]
+        dense_y = [y_ref[pair, p] for p in range(3)]
         lined = {}
         for order_y, order_z in ((0, 0), (1, 0), (2, 0), (0, 1), (1, 1), (0, 2)):
             lined[order_y, order_z] = sum(
@@ -613,12 +638,14 @@
     lax.fori_loop(0, PENCILS * PAIRS, pair_body, 0, unroll=6)
 
 
-def finish_kernel(in_ref, charge_ref, dipole_ref, position_ref, energy_ref):
+def finish_kernel(in_ref, charge_ref, dipole_ref, position_ref, energy_ref, row_ref, semaphore):
     total = (in_ref[0] + in_ref[1]) + (in_ref[2] + in_ref[3])
-    charge_ref[...] = total[0:1]
+    row_ref[...] = total[0:1]
+    copy = fetch(row_ref.at[0], charge_ref, semaphore)
     dipole_ref[...] = total[1:4]
     position_ref[...] = total[4:7]
     energy_ref[...] = total[7:8, 0:1]
+    copy.wait()
 
 
 def spline_modulus(angles):
@@ -635,6 +662,11 @@
 
 SPACES = {"v": pltpu.VMEM, "h": pltpu.HBM, "s": pltpu.SMEM}
 WORK = {"flops": 1_000_000_000, "bytes_accessed": 8_000_000}
+
+
+def out_place(shape):
+    pinned = isinstance(shape, type(pltpu.HBM((8, LANES), f32)))
+    return pl.BlockSpec(memory_space=pltpu.HBM if pinned else pltpu.VMEM)
 
 
 def call(kernel, inputs, out_shape, scratch=()):
@@ -647,8 +679,9 @@
             kernel,
             out_shape=out_shape,
             in_specs=[pl.BlockSpec(memory_space=SPACES[one]) for one in inputs],
+            out_specs=jax.tree.map(out_place, out_shape),
             scratch_shapes=list(scratch),
-            compiler_params=pltpu.CompilerParams(vmem_limit_bytes=20 * 1024 * 1024),
+            compiler_params=pltpu.CompilerParams(vmem_limit_bytes=28 * 1024 * 1024),
             cost_estimate=pl.CostEstimate(transcendentals=0, **WORK),
         )(*placed)
 
@@ -669,9 +702,9 @@
 def on_device(cell_index, offsets, charges, dipoles, block_count, shear_cells):
     pencil_index = lax.axis_index("gx")
     slab_index = lax.axis_index("gy")
-    shear_step = shear_cells[0]
     x_forward, x_inverse, y_forward, y_inverse = wave_tables()
     shape = jax.ShapeDtypeStruct
+    where = jnp.stack([slab_index, pencil_index])
 
     mine, base, taps, cos_t, sin_t = call(
         prepare_kernel,
@@ -692,16 +725,48 @@
             pltpu.SemaphoreType.DMA((5,)),
         ],
     )(
-        jnp.stack([slab_index, pencil_index]),
+        where,
         shear_cells,
         block_count,
         cell_index,
         offsets,
-        charges[None],
+        charges,
         dipoles,
     )
     atoms = lax.all_gather(mine, "gx", axis=0, tiled=False)
     below_atoms = next_slab(atoms)
+
+    packed = shape((SLABS * CARRIERS, LANES), f32)
+    table_space = pltpu.VMEM((NX, 6 * QUARTER), bf16)
+    two = pltpu.SemaphoreType.DMA((2,))
+    pairs = 2 * PENCILS * PAIRS
+    held = [
+        ((2, 2 * PADDED_Z, 3 * LANES), bf16),
+        ((3, WINDOW, LANES), f32),
+        ((3, 16, LANES), f32),
+    ]
+    weights_space = pltpu.VMEM((PENCILS, 18, 8, ATOM_DEV), f32)
+    four = pltpu.SemaphoreType.DMA((4,))
+    own_lines = call(
+        lambda *refs: spread_kernel(True, *refs),
+        "vvvhvv",
+        shape((NX, CY * LANES), f32),
+        [pltpu.VMEM((NX + 8, 2 * CY * LANES), f32), table_space, weights_space, two],
+    )(atoms, base, taps, x_forward, cos_t, sin_t)
+    lines, *weights = call(
+        lambda *refs: spread_kernel(False, *refs),
+        "vvvhvvvsv",
+        (packed, *(pltpu.HBM((pairs, *dims), kind) for dims, kind in held)),
+        [
+            *(pltpu.VMEM((pairs, *dims), kind) for dims, kind in held),
+            pltpu.VMEM((NX + 8, 2 * (ROWS - CY) * LANES), f32),
+            table_space,
+            weights_space,
+            four,
+        ],
+    )(below_atoms, base, taps, x_forward, cos_t, sin_t, own_lines, where, atoms)
+    lines, shear_cells = lax.optimization_barrier((lines, shear_cells))
+    shear_step = shear_cells[0]
 
     own_x = folded(mode_of(jnp.arange(8, dtype=jnp.int32) * SLABS + slab_index), NX)[None, :]
     own_y = folded(mode_of(jnp.arange(NY, dtype=jnp.int32)), NY)[:, None]
@@ -725,43 +790,6 @@
     mode_norm = jnp.where(kept, norm_z, 1.0)
     mode = jnp.stack([mode_top, mode_norm])
 
-    packed = shape((SLABS * CARRIERS, LANES), f32)
-    table_space = pltpu.VMEM((NX, 6 * QUARTER), bf16)
-    two = pltpu.SemaphoreType.DMA((2,))
-    own_lines = call(
-        lambda *refs: spread_kernel(True, *refs),
-        "vvvhvv",
-        shape((NX, CY * LANES), f32),
-        [
-            pltpu.VMEM((NX + 8, 2 * CY * LANES), f32),
-            table_space,
-            pltpu.VMEM((PENCILS, 12, 8, ATOM_DEV), f32),
-            two,
-        ],
-    )(atoms, base, taps, x_forward, cos_t, sin_t)
-    lines = call(
-        lambda *refs: spread_kernel(False, *refs),
-        "vvvhvvv",
-        packed,
-        [
-            pltpu.VMEM((NX + 8, 2 * (ROWS - CY) * LANES), f32),
-            table_space,
-            pltpu.VMEM((PENCILS, 12, 8, ATOM_DEV), f32),
-            two,
-        ],
-    )(below_atoms, base, taps, x_forward, cos_t, sin_t, own_lines)
-    lines, atoms, below_atoms, top = lax.optimization_barrier((lines, atoms, below_atoms, top))
-    pairs = 2 * PENCILS * PAIRS
-    waves, dense_x, dense_y = call(
-        weights_kernel,
-        "vvvv",
-        (
-            shape((pairs, 2, 2 * PADDED_Z, 3 * LANES), bf16),
-            shape((pairs, 3, WINDOW, LANES), f32),
-            shape((pairs, 3, 16, LANES), f32),
-        ),
-        [pltpu.VMEM((PENCILS, 18, 8, ATOM_DEV), f32)] * 2,
-    )(atoms, below_atoms, base, taps)
     green = call(green_kernel, "vvv", shape((NY, PART_X * LANES), f32))(top, norm, mode)
     lines = swap_slabs(lines)
     filtered = call(filter_kernel, "vhhv", packed, [table_space, table_space, two])(
@@ -769,31 +797,38 @@
     )
     filtered = swap_slabs(filtered)
     shares_shape = shape((PENCILS, 8, ATOM_DEV), f32)
+    sample_spaces = [
+        table_space,
+        *(pltpu.VMEM((pairs // 2, *dims), kind) for dims, kind in held),
+        weights_space,
+        four,
+    ]
     below_shares = call(
         lambda *refs: sample_kernel(False, *refs),
-        "vvvvvhvv",
+        "vvsvvvvhhhh",
         shares_shape,
-        [pltpu.VMEM((NX + 8, (ROWS - CY) * LANES), f32), table_space, two],
-    )(filtered, below_atoms, waves, dense_x, dense_y, x_inverse, cos_t, sin_t)
+        [pltpu.VMEM((NX + 8, (ROWS - CY) * LANES), f32), *sample_spaces],
+    )(filtered, below_atoms, where, base, taps, cos_t, sin_t, x_inverse, *weights)
     below_shares = next_slab(below_shares, back=True)
     shares = call(
         lambda *refs: sample_kernel(True, *refs),
-        "vvvvvhvv",
+        "vvsvvvvhhhh",
         shares_shape,
-        [pltpu.VMEM((NX + 8, CY * LANES), f32), table_space, two],
-    )(filtered, atoms, waves, dense_x, dense_y, x_inverse, cos_t, sin_t)
+        [pltpu.VMEM((NX + 8, CY * LANES), f32), *sample_spaces],
+    )(filtered, atoms, where, base, taps, cos_t, sin_t, x_inverse, *weights)
     shares = lax.all_to_all(shares + below_shares, "gx", split_axis=0, concat_axis=0, tiled=True)
     charge_grad, dipole_grad, position_grad, energy = call(
         finish_kernel,
         "v",
         (
-            shape((1, ATOM_DEV), f32),
+            pltpu.HBM((ATOM_DEV,), f32),
             shape((3, ATOM_DEV), f32),
             shape((3, ATOM_DEV), f32),
             shape((1, 1), f32),
         ),
+        [pltpu.VMEM((1, ATOM_DEV), f32), pltpu.SemaphoreType.DMA],
     )(shares)
-    return charge_grad[0], dipole_grad, position_grad, energy[0]
+    return charge_grad, dipole_grad, position_grad, energy[0]
 
 
 def solution(mesh):

time: 128 us -> 117 us (0.914)
  blocking collectives: 22.6 us -> 47.6 us
  waiting for transfers between devices: 40.1 us -> 24.6 us
  local copies, waits for them, and re-layouts: 11.1 us -> 0 us
  starting transfers between devices: 18.7 us -> 8.9 us
  Pallas kernels: 31 us -> 32.3 us
    all_to_all x0 -> x1, blocking collectives: none -> 28.7 us  [swap_slabs(): lines = lax.all_to_all(lines, 'gy', split_axis=0, concat_axis=0, tiled=True)]
    all_to_all x2 -> x1, waiting for transfers between devices: 35.9 us -> 18.5 us  [swap_slabs(): lines = lax.all_to_all(lines, 'gy', split_axis=0, concat_axis=0, tiled=True)]
    unnamed x32 -> x0, local copies, waits for them, and re-layouts: 9.9 us -> none
    all_to_all x2 -> x1, starting transfers between devices: 15.2 us -> 6.43 us  [swap_slabs(): lines = lax.all_to_all(lines, 'gy', split_axis=0, concat_axis=0, tiled=True)]
    all_to_all x1, blocking collectives: 12.7 us -> 9 us  [on_device(): lax.all_to_all(shares + below_shares, 'gx', split_axis=0, concat_axis=0,...]
    ppermute x2, waiting for transfers between devices: 4.21 us -> 6.03 us  [next_slab(): lax.ppermute(value, 'gy', [(i, (i + step) % SLABS) for i in range(SLABS)])]
    pallas_call x9 -> x8, Pallas kernels: 31 us -> 32.3 us  [run(): pl.pallas_call(kernel, out_shape=out_shape, in_specs=[pl.BlockSpec(memory...]
  transfers between devices with their start and end apart: 4 -> 3, of which waited for: 3 -> 2; matrix products, arithmetic and copies ran while one was open for 1% -> 2% of each run, Pallas kernels for 11% -> 9%
where the time goes in v5:
time: 117 us
  blocking collectives  47.6 us (41%)
  Pallas kernels  32.3 us (28%)
  waiting for transfers between devices  24.6 us (21%)
  starting transfers between devices  8.9 us (8%)
  other arithmetic  1.85 us (2%)
  between operations  1.56 us (1%)
    pallas_call x8, Pallas kernels, run(): pl.pallas_call(kernel, out_shape=out_shape, in_specs=[pl.BlockSpec(memory...  32.3 us
    all_to_all x1, blocking collectives, swap_slabs(): lines = lax.all_to_all(lines, 'gy', split_axis=0, concat_axis=0, tiled=True)  28.7 us
    all_to_all x1, waiting for transfers between devices, swap_slabs(): lines = lax.all_to_all(lines, 'gy', split_axis=0, concat_axis=0, tiled=True)  18.5 us
    all_gather x1, blocking collectives, on_device(): atoms = lax.all_gather(mine, 'gx', axis=0, tiled=False)  9.91 us
    all_to_all x1, blocking collectives, on_device(): lax.all_to_all(shares + below_shares, 'gx', split_axis=0, concat_axis=0,...  9 us
    all_to_all x1, starting transfers between devices, swap_slabs(): lines = lax.all_to_all(lines, 'gy', split_axis=0, concat_axis=0, tiled=True)  6.43 us
    ppermute x2, waiting for transfers between devices, next_slab(): lax.ppermute(value, 'gy', [(i, (i + step) % SLABS) for i in range(SLABS)])  6.03 us
    ppermute x2, starting transfers between devices, next_slab(): lax.ppermute(value, 'gy', [(i, (i + step) % SLABS) for i in range(SLABS)])  2.47 us
  transfers between devices with their start and end apart: 3, of which 2 were waited for; matrix products, arithmetic and copies ran while one was open for 2% of the time, Pallas kernels for 9%

profile of v5, /device:TPU:1, one launch (start us, length us, event | category | flops | bytes accessed | tf_op | source)
XLA Modules:
  0.0 116.7 jit_solution(16707923263808104265)
XLA Ops:
  1.3 0.1 pad_add_fusion.where_ref.refs_7_.refs_2_
  1.4 1.3 %shard_map.129 = (f32[16,384]{1,0:T(8,128)S(1)}, f32[8,128]{1,0:T(8,128)S(1)}, f32[12,48,128]{2,1,0:T(8,128)S(1)}, f32[384,128]{1,0:T(8,128)S(1)}, f32[384,128]{1,0:T(8,128)S(1)}) custom-call(s32[2]{0:T(128)S(1)} %pad_add_fusion.where_ref.refs_7_.refs_2_, s32[1]{0:T(128)S(6)} %copy.19.shear_ref, s32[6]{0:T(128)} %counts_ref.1, s32[3,384]{1,0:T(4,128)} %cells_ref.1, ...), custom_call_target="tpu_custom_call" | custom-call | flops 1000000000 | bytes 8000000 | tf_op jit(solution)/shard_map/pallas_call | solution.py:678
  2.7 9.9 %all-gather = f32[64,384]{1,0:T(8,128)S(1)} all-gather(f32[16,384]{1,0:T(8,128)S(1)} %get-tuple-element.19), channel_id=2, replica_groups=mesh['gy'=64,'gx'=4] {'gx'}, dimensions={0}, use_global_device_ids=true | all-gather | bytes 122880 | tf_op jit(solution)/shard_map/all_gather | solution.py:736
  12.6 0.0 collective-permute-start
  12.6 4.1 %shard_map.130.refs_6_ = f32[384,768]{1,0:T(8,128)S(1)} custom-call(f32[4,16,384]{2,1,0:T(8,128)S(1)} %bitcast.14, f32[8,128]{1,0:T(8,128)S(1)} %get-tuple-element.20.refs_1_.refs_3_, f32[12,48,128]{2,1,0:T(8,128)S(1)} %get-tuple-element.21.refs_2_.refs_4_, bf16[384,576]{1,0:T(8,128)(2,1)} %constant.149.clone.refs_3_, ...), custom_call_target="tpu_custom_call" | custom-call | flops 1000000000 | bytes 8000000 | tf_op jit(solution)/shard_map/pallas_call | solution.py:678
  16.7 6.0 %collective-permute-done.refs_0_.refs_1_ = f32[4,16,384]{2,1,0:T(8,128)S(1)} collective-permute-done((f32[4,16,384]{2,1,0:T(8,128)S(1)}, f32[4,16,384]{2,1,0:T(8,128)S(1)}, u32[]{:S(2)}, u32[]{:S(2)}) %collective-permute-start) | collective-permute-done | bytes 98336 | tf_op jit(solution)/shard_map/ppermute | solution.py:693
  22.8 11.6 %shard_map.131 = (f32[1728,128]{1,0:T(8,128)}, bf16[24,2,96,384]{3,2,1,0:T(8,128)(2,1)}, f32[24,3,40,128]{3,2,1,0:T(8,128)}, f32[24,3,16,128]{3,2,1,0:T(8,128)}) custom-call(f32[4,16,384]{2,1,0:T(8,128)S(1)} %collective-permute-done.refs_0_.refs_1_, f32[8,128]{1,0:T(8,128)S(1)} %get-tuple-element.20.refs_1_.refs_3_, ...), custom_call_target="tpu_custom_call" | custom-call | flops 1000000000 | bytes 8000000 | tf_op jit(solution)/shard_map/pallas_call | solution.py:678
  34.4 6.4 %all-to-all-start = ((f32[64,27,1,128]{3,2,1,0:T(1,128)}), f32[64,27,1,128]{3,2,1,0:T(1,128)S(1)}, u32[]{:S(2)}, u32[]{:S(2)}) async-start(f32[64,27,1,128]{3,2,1,0:T(1,128)} %bitcast.3), calls=%async_computation | async-start | bytes 1769472 | tf_op jit(solution)/shard_map/all_to_all | solution.py:698
  40.9 0.1 add_multiply_fusion.3
  41.0 0.1 compare_select_fusion.1
  41.1 1.5 %fusion.3 = (f32[384,8]{1,0:T(8,128)S(1)}, f32[384,8]{1,0:T(8,128)S(1)}) fusion(f32[8]{0:T(128)S(1)} %multiply_multiply_fusion.2, f32[8]{0:T(128)S(1)} %get-tuple-element.37, f32[384]{0:T(512)S(1)} %fusion.23, f32[8]{0:T(128)S(1)} %get-tuple-element.36, pred[384]{0:T(512)(128)(4,1)S(1)} %broadcast_compare_fusion, pred[8]{0:T(512)(128)(4,1)S(1)} %broadcast_compare_fusion.1), kind=kLoop, calls=%fused_computation.7 | loop fusion | flops 52224 | bytes 26600 | tf_op jit(solution)/shard_map/add | solution.py:775
  42.6 0.7 shard_map.132.green_ref
  43.3 18.5 %all-to-all-done = f32[64,27,1,128]{3,2,1,0:T(1,128)S(1)} async-done(((f32[64,27,1,128]{3,2,1,0:T(1,128)}), f32[64,27,1,128]{3,2,1,0:T(1,128)S(1)}, u32[]{:S(2)}, u32[]{:S(2)}) %all-to-all-start) | async-done | bytes 884768 | tf_op jit(solution)/shard_map/all_to_all | solution.py:698
  61.8 3.5 %shard_map.133 = f32[1728,128]{1,0:T(8,128)S(1)} custom-call(f32[1728,128]{1,0:T(8,128)S(1)} %bitcast.11, bf16[384,576]{1,0:T(8,128)(2,1)} %constant.150.clone.tables_ref, bf16[384,576]{1,0:T(8,128)(2,1)} %constant.151.clone.backs_ref, f32[384,768]{1,0:T(8,128)S(1)} %shard_map.132.green_ref), custom_call_target="tpu_custom_call" | custom-call | flops 1000000000 | bytes 8000000 | tf_op jit(solution)/shard_map/pallas_call | solution.py:678
  65.3 28.7 %all_to_all.15 = f32[64,27,1,128]{3,2,1,0:T(1,128)S(1)} all-to-all(f32[64,27,1,128]{3,2,1,0:T(1,128)S(1)} %bitcast.12), channel_id=1, replica_groups=mesh['gy'=64,'gx'=4] {'gy'}, dimensions={0} | all-to-all | bytes 1769472 | tf_op jit(solution)/shard_map/all_to_all | solution.py:698
  94.0 4.5 %shard_map.135 = f32[4,8,384]{2,1,0:T(8,128)S(1)} custom-call(f32[1728,128]{1,0:T(8,128)S(1)} %bitcast.9, f32[4,16,384]{2,1,0:T(8,128)S(1)} %collective-permute-done.refs_0_.refs_1_, s32[2]{0:T(128)S(1)} %pad_add_fusion.where_ref.refs_7_.refs_2_, f32[8,128]{1,0:T(8,128)S(1)} %get-tuple-element.20.refs_1_.refs_3_, ...), custom_call_target="tpu_custom_call" | custom-call | flops 1000000000 | bytes 8000000 | tf_op jit(solution)/shard_map/pallas_call | solution.py:678
  98.5 2.5 %collective-permute-start.1 = (f32[4,8,384]{2,1,0:T(8,128)S(1)}, f32[4,8,384]{2,1,0:T(8,128)S(1)}, u32[]{:S(2)}, u32[]{:S(2)}) collective-permute-start(f32[4,8,384]{2,1,0:T(8,128)S(1)} %shard_map.135), channel_id=1, source_target_pairs={{0,252},{4,0},{8,4},{12,8},{16,12},{20,16},{24,20},{28,24},{32,28}... | collective-permute-start | bytes 147464 | tf_op jit(solution)/shard_map/ppermute | solution.py:693
  101.0 5.4 %shard_map.134 = f32[4,8,384]{2,1,0:T(8,128)S(1)} custom-call(f32[1728,128]{1,0:T(8,128)S(1)} %bitcast.10, f32[4,16,384]{2,1,0:T(8,128)S(1)} %bitcast.16, s32[2]{0:T(128)S(1)} %pad_add_fusion.where_ref.refs_7_.refs_2_, f32[8,128]{1,0:T(8,128)S(1)} %get-tuple-element.20.refs_1_.refs_3_, f32[12,48,128]{2,1,0:T(8,128)S(1)} %get-tuple-element.21.refs_2_.refs_4_, ...), custom_call_target="tpu_custom_call" | custom-call | flops 1000000000 | bytes 8000000 | tf_op jit(solution)/shard_map/pallas_call | solution.py:678
  106.4 0.0 collective-permute-done.1
  106.4 9.0 %all_to_all.16.in_ref = f32[4,8,384]{2,1,0:T(8,128)S(1)} all-to-all(f32[4,8,384]{2,1,0:T(8,128)S(1)} %add.319), channel_id=1, replica_groups=mesh['gy'=64,'gx'=4] {'gx'}, dimensions={0} | all-to-all | bytes 98304 | tf_op jit(solution)/shard_map/all_to_all | solution.py:819
  115.4 1.2 %shard_map.136 = (f32[384]{0:T(512)}, f32[3,384]{1,0:T(4,128)}, f32[3,384]{1,0:T(4,128)}, f32[1,1]{1,0:T(1,128)}) custom-call(f32[4,8,384]{2,1,0:T(8,128)S(1)} %all_to_all.16.in_ref), custom_call_target="tpu_custom_call" | custom-call | flops 1000000000 | bytes 8000000 | tf_op jit(solution)/shard_map/pallas_call | solution.py:678
  (6 shorter events, 0.1 us)
Async XLA Ops:
  12.6 10.1 %collective-permute-start = (f32[4,16,384]{2,1,0:T(8,128)S(1)}, f32[4,16,384]{2,1,0:T(8,128)S(1)}, u32[]{:S(2)}, u32[]{:S(2)}) collective-permute-start(f32[4,16,384]{2,1,0:T(8,128)S(1)} %bitcast.13), channel_id=1, source_target_pairs={{0,4},{4,8},{8,12},{12,16},{16,20},{20,24},{24,28},{28,32},{32,36}... | collective-permute-start | bytes 294920 | tf_op jit(solution)/shard_map/ppermute | solution.py:693
  34.4 27.4 %all-to-all-start = ((f32[64,27,1,128]{3,2,1,0:T(1,128)}), f32[64,27,1,128]{3,2,1,0:T(1,128)S(1)}, u32[]{:S(2)}, u32[]{:S(2)}) async-start(f32[64,27,1,128]{3,2,1,0:T(1,128)} %bitcast.3), calls=%async_computation | async-start | bytes 1769472 | tf_op jit(solution)/shard_map/all_to_all | solution.py:698
  98.5 7.9 %collective-permute-start.1 = (f32[4,8,384]{2,1,0:T(8,128)S(1)}, f32[4,8,384]{2,1,0:T(8,128)S(1)}, u32[]{:S(2)}, u32[]{:S(2)}) collective-permute-start(f32[4,8,384]{2,1,0:T(8,128)S(1)} %shard_map.135), channel_id=1, source_target_pairs={{0,252},{4,0},{8,4},{12,8},{16,12},{20,16},{24,20},{28,24},{32,28}... | collective-permute-start | bytes 147464 | tf_op jit(solution)/shard_map/ppermute | solution.py:693

commit v6 on v5

--- a/solution.py
+++ b/solution.py
@@ -22,7 +22,8 @@
 ATOM_DEV = 384
 PAIRS = 3
 WINDOW = 40
-ROWS = 11
+WIDE = 48
+EXTENDED = NX + WIDE
 HALF = 64
 LANES = 128
 PADDED_Z = 48
@@ -256,8 +257,7 @@
         taps_ref[t] = jnp.where(row < PART_Z, cos_t, 0.0)
         taps_ref[6 + t] = jnp.where(row < PART_Z, sin_t, 0.0)
     column = lax.broadcasted_iota(jnp.int32, (1, LANES), 1)
-    above = jnp.where(slab == 0, SLABS - 1, slab - 1) * CY
-    rows = jnp.where(column < CY, slab * CY, above) + jnp.minimum(column, ROWS)
+    rows = slab * CY + jnp.minimum(column, CY)
     index = lax.broadcasted_iota(jnp.int32, (NX, LANES), 0)
     residue = (
         (index >= QUARTER).astype(jnp.int32)
@@ -310,6 +310,15 @@
     return pencil, pl.ds(pl.multiple_of(pair % PAIRS * LANES, LANES), LANES)
 
 
+def pair_window(pair, own, where_ref):
+    if own:
+        return pl.multiple_of(pair * 32, 8), WINDOW, (pair * 32).astype(f32)
+    place = pair * 32 + where_ref[2]
+    place = jnp.where(place >= NX, place - NX, place)
+    first = place // 8 * 8
+    return pl.multiple_of(first, 8), WIDE, (pair * 32 - (place - first)).astype(f32)
+
+
 def z_waves(cell_z, weights, base_ref, taps_ref):
     turn = base_ref[...] * cell_z
     turn = turn - 360.0 * jnp.floor(turn * (1.0 / 360.0))
@@ -335,17 +344,19 @@
     ]
 
 
-def sampling_weights(start, some_ref, table_ref, base_ref, taps_ref, waves_ref, x_ref, y_ref):
+def sampling_weights(
+    start, own, where_ref, some_ref, table_ref, base_ref, taps_ref, waves_ref, x_ref, y_ref
+):
     spline_table(some_ref, table_ref, 3)
 
     def pair_body(pair, carry):
         pencil, lanes = pair_place(pair)
         row = [some_ref[pencil, a : a + 1, lanes] for a in range(3)]
-        window = (pair * 32).astype(f32)
-        dense_x = dense_rows(weight_rows(table_ref, pencil, lanes, 0, 3), row[0] - window, WINDOW)
+        _, window, origin = pair_window(pair, own, where_ref)
+        dense_x = dense_rows(weight_rows(table_ref, pencil, lanes, 0, 3), row[0] - origin, window)
         dense_y = dense_rows(weight_rows(table_ref, pencil, lanes, 1, 3), row[1], 16)
         for p in range(3):
-            x_ref[start + pair, p] = dense_x[p]
+            x_ref[start + pair, p, :window] = dense_x[p]
             y_ref[start + pair, p] = dense_y[p]
         waves = z_waves(row[2], weight_rows(table_ref, pencil, lanes, 2, 3), base_ref, taps_ref)
         for s, (re, im) in enumerate(waves):
@@ -360,17 +371,18 @@
 
 
 def spread_kernel(own, *refs):
-    atoms_ref, base_ref, taps_ref, tables_ref, cos_ref, sin_ref = refs[:6]
+    atoms_ref, where_ref, base_ref, taps_ref = refs[:4]
     if own:
-        out_ref, grid_ref, table_ref, weights_ref, semaphores = refs[6:]
+        grid_ref, weights_ref = refs[4:]
+        grid_ref[...] = jnp.zeros_like(grid_ref)
     else:
-        lines_ref, where_ref, slab_atoms_ref, out_ref = refs[6:10]
+        slab_grid_ref, tables_ref, cos_ref, sin_ref, slab_atoms_ref, out_ref = refs[4:10]
         results, kept = refs[10:13], refs[13:16]
         grid_ref, table_ref, weights_ref, semaphores = refs[16:]
-    table_copy = fetch(tables_ref, table_ref, semaphores.at[0])
-    grid_ref[...] = jnp.zeros_like(grid_ref)
-    rows = list(range(CY)) if own else list(range(CY, ROWS))
-    part = len(rows) * LANES
+        table_copy = fetch(tables_ref, table_ref, semaphores.at[0])
+        grid_ref[...] = slab_grid_ref[...]
+    rows = list(range(CY)) if own else list(range(CY, 2 * CY - 1))
+    part = CY * LANES
     gap = jnp.zeros((HALF - PADDED_Z, LANES), bf16)
     spline_table(atoms_ref, weights_ref, 2)
 
@@ -378,9 +390,9 @@
         pencil, lanes = pair_place(pair)
         row = [atoms_ref[pencil, a : a + 1, lanes] for a in range(10)]
         charge, dip_x, dip_y, dip_z = row[6:10]
-        window = pair * 32
+        first_row, window, origin = pair_window(pair, own, where_ref)
         dense_x = dense_rows(
-            weight_rows(weights_ref, pencil, lanes, 0, 2), row[0] - window.astype(f32), WINDOW
+            weight_rows(weights_ref, pencil, lanes, 0, 2), row[0] - origin, window
         )
         dense_y = dense_rows(weight_rows(weights_ref, pencil, lanes, 1, 2), row[1], 16)
         value, first = weight_rows(weights_ref, pencil, lanes, 2, 2)
@@ -413,20 +425,22 @@
         added = lax.dot_general(
             left, right, (((1,), (1,)), ((), ())), preferred_element_type=f32
         )
-        at = pl.ds(pl.multiple_of(window, 8), WINDOW)
+        at = pl.ds(first_row, window)
         for n in range(len(rows)):
-            piece = added[n * WINDOW : (n + 1) * WINDOW]
+            piece = added[n * window : (n + 1) * window]
             grid_ref[at, n * LANES : (n + 1) * LANES] += piece[:, :LANES]
             grid_ref[at, part + n * LANES : part + (n + 1) * LANES] += piece[:, LANES:]
         return carry
 
     lax.fori_loop(0, PENCILS * PAIRS, pair_body, 0, unroll=6)
-    grid_ref[0:8] += grid_ref[NX : NX + 8]
+    if own:
+        return
+    grid_ref[0:WIDE] += grid_ref[NX:EXTENDED]
     table_copy.wait()
     sign = lane_sign((NX, LANES))
     totals = []
-    for first in range(0, len(rows), 2):
-        lanes = slice(first * LANES, min(first + 2, len(rows)) * LANES)
+    for first in range(0, CY, 2):
+        lanes = slice(first * LANES, (first + 2) * LANES)
         below = slice(part + lanes.start, part + lanes.stop)
         line = jnp.concatenate(
             forward_line(
@@ -434,17 +448,9 @@
             ),
             axis=0,
         )
-        for n, r in enumerate(rows[first : first + 2]):
+        for n, y in enumerate((first, first + 1)):
             one = line[:, n * LANES : (n + 1) * LANES]
-            total = one * cos_ref[:, r : r + 1] + turned(one, sign) * sin_ref[:, r : r + 1]
-            y = first + n
-            if own:
-                out_ref[:, y * LANES : (y + 1) * LANES] = total
-            else:
-                totals.append(total + lines_ref[:, y * LANES : (y + 1) * LANES])
-    if own:
-        return
-    totals.append(lines_ref[:, (CY - 1) * LANES :])
+            totals.append(one * cos_ref[:, y : y + 1] + turned(one, sign) * sin_ref[:, y : y + 1])
     for group in range(GROUPS):
         blocks = []
         for block in range(4 * group, 4 * group + 4):
@@ -456,7 +462,9 @@
     @pl.when(where_ref[1] % 2 == 1)
     def _():
         for start, some_ref in ((0, slab_atoms_ref), (PENCILS * PAIRS, atoms_ref)):
-            sampling_weights(start, some_ref, weights_ref, base_ref, taps_ref, *kept)
+            sampling_weights(
+                start, start == 0, where_ref, some_ref, weights_ref, base_ref, taps_ref, *kept
+            )
         copies = [fetch(kept[n], results[n], semaphores.at[n]) for n in range(3)]
         for copy in copies:
             copy.wait()
@@ -527,12 +535,15 @@
     out_ref[rows_of(0), :] = jnp.where(lane == PART_Z, share, out_ref[rows_of(0), :])
 
 
-def sample_kernel(
-    own, in_ref, atoms_ref, where_ref, base_ref, taps_ref, cos_ref, sin_ref, tables_ref,
-    waves_in_ref, x_in_ref, y_in_ref, out_ref,
-    grid_ref, table_ref, waves_ref, x_ref, y_ref, weights_ref, semaphores
-):
-    table_copy = fetch(tables_ref, table_ref, semaphores.at[3])
+def sample_kernel(own, *refs):
+    atoms_ref, where_ref, base_ref, taps_ref, waves_in_ref, x_in_ref, y_in_ref = refs[:7]
+    if own:
+        grid_ref, out_ref = refs[7:9]
+    else:
+        in_ref, cos_ref, sin_ref, tables_ref, out_ref, grid_ref, table_ref = refs[7:14]
+    waves_ref, x_ref, y_ref, weights_ref, semaphores = refs[-5:]
+    if not own:
+        table_copy = fetch(tables_ref, table_ref, semaphores.at[3])
     later = where_ref[1] % 2 == 0
     start = 0 if own else PENCILS * PAIRS
     some = pl.ds(start, PENCILS * PAIRS)
@@ -545,41 +556,40 @@
 
     @pl.when(later)
     def _():
-        sampling_weights(0, atoms_ref, weights_ref, base_ref, taps_ref, waves_ref, x_ref, y_ref)
+        sampling_weights(
+            0, own, where_ref, atoms_ref, weights_ref, base_ref, taps_ref, waves_ref, x_ref, y_ref
+        )
 
     @pl.when(jnp.logical_not(later))
     def _():
         for copy in copies:
             copy.start()
 
-    sign = lane_sign((NX, LANES))
-    rows = list(range(CY)) if own else list(range(CY, ROWS))
-    for first in range(0, len(rows), 2):
-        modes, swapped = [], []
-        for y in range(first, min(first + 2, len(rows))):
-            line = jnp.concatenate([block_at(in_ref, j, y) for j in range(PART_X)], axis=0)
-            other = turned(line, sign)
-            r = rows[y]
-            cos_r, sin_r = cos_ref[:, r : r + 1], sin_ref[:, r : r + 1]
-            modes.append(line * cos_r - other * sin_r)
-            swapped.append(other * cos_r + line * sin_r)
-        swapped = jnp.concatenate(swapped, axis=1)
-        stacked = modes
-        modes = jnp.concatenate(modes, axis=1)
-        if first == 0:
-            table_copy.wait()
-        cells = jnp.concatenate(
-            inverse_line(table_ref, quarters_of(modes), quarters_of(swapped)), axis=0
-        )
-        lanes = slice(first * LANES, (first + len(stacked)) * LANES)
-        grid_ref[:NX, lanes] = cells
-        grid_ref[NX:, lanes] = cells[:8]
-    gap = jnp.zeros((HALF - PADDED_Z, 3 * LANES), bf16)
-    if own:
+    rows = list(range(CY)) if own else list(range(CY, 2 * CY - 1))
+    energy = 0.0
+    if not own:
+        sign = lane_sign((NX, LANES))
+        for first in range(0, CY, 2):
+            modes, swapped = [], []
+            for y in range(first, first + 2):
+                line = jnp.concatenate([block_at(in_ref, j, y) for j in range(PART_X)], axis=0)
+                other = turned(line, sign)
+                cos_y, sin_y = cos_ref[:, y : y + 1], sin_ref[:, y : y + 1]
+                modes.append(line * cos_y - other * sin_y)
+                swapped.append(other * cos_y + line * sin_y)
+            swapped = jnp.concatenate(swapped, axis=1)
+            modes = jnp.concatenate(modes, axis=1)
+            if first == 0:
+                table_copy.wait()
+            cells = jnp.concatenate(
+                inverse_line(table_ref, quarters_of(modes), quarters_of(swapped)), axis=0
+            )
+            lanes = slice(first * LANES, (first + 2) * LANES)
+            grid_ref[:NX, lanes] = cells
+            grid_ref[NX:, lanes] = cells[:WIDE]
         lane = lax.broadcasted_iota(jnp.int32, (SLABS, LANES), 1)
         energy = jnp.sum(jnp.where(lane == PART_Z, in_ref[rows_of(0), :], 0.0))
-    else:
-        energy = 0.0
+    gap = jnp.zeros((HALF - PADDED_Z, 3 * LANES), bf16)
 
     @pl.when(jnp.logical_not(later))
     def _():
@@ -595,18 +605,19 @@
             )
             for n in range(2)
         ]
-        at = pl.ds(pl.multiple_of(pair * 32, 8), WINDOW)
+        first_row, window, _ = pair_window(pair, own, where_ref)
+        at = pl.ds(first_row, window)
         cells = jnp.concatenate(
             [grid_ref[at, n * LANES : (n + 1) * LANES] for n in range(len(rows))], axis=0
         )
         read = product(halves(cells), waves)
-        dense_x = [x_ref[pair, p] for p in range(3)]
+        dense_x = [x_ref[pair, p, :window] for p in range(3)]
         dense_y = [y_ref[pair, p] for p in range(3)]
         lined = {}
         for order_y, order_z in ((0, 0), (1, 0), (2, 0), (0, 1), (1, 1), (0, 2)):
             lined[order_y, order_z] = sum(
                 dense_y[order_y][r : r + 1]
-                * read[n * WINDOW : (n + 1) * WINDOW, order_z * LANES : (order_z + 1) * LANES]
+                * read[n * window : (n + 1) * window, order_z * LANES : (order_z + 1) * LANES]
                 for n, r in enumerate(rows)
             )
 
@@ -704,7 +715,8 @@
     slab_index = lax.axis_index("gy")
     x_forward, x_inverse, y_forward, y_inverse = wave_tables()
     shape = jax.ShapeDtypeStruct
-    where = jnp.stack([slab_index, pencil_index])
+    shift = jnp.where(slab_index == 0, shear_cells[0], 0)
+    where = jnp.stack([slab_index, pencil_index, shift])
 
     mine, base, taps, cos_t, sin_t = call(
         prepare_kernel,
@@ -742,29 +754,29 @@
     pairs = 2 * PENCILS * PAIRS
     held = [
         ((2, 2 * PADDED_Z, 3 * LANES), bf16),
-        ((3, WINDOW, LANES), f32),
+        ((3, WIDE, LANES), f32),
         ((3, 16, LANES), f32),
     ]
     weights_space = pltpu.VMEM((PENCILS, 18, 8, ATOM_DEV), f32)
     four = pltpu.SemaphoreType.DMA((4,))
-    own_lines = call(
+    slab_grid = call(
         lambda *refs: spread_kernel(True, *refs),
-        "vvvhvv",
-        shape((NX, CY * LANES), f32),
-        [pltpu.VMEM((NX + 8, 2 * CY * LANES), f32), table_space, weights_space, two],
-    )(atoms, base, taps, x_forward, cos_t, sin_t)
+        "vsvv",
+        shape((EXTENDED, 2 * CY * LANES), f32),
+        [weights_space],
+    )(atoms, where, base, taps)
     lines, *weights = call(
         lambda *refs: spread_kernel(False, *refs),
-        "vvvhvvvsv",
+        "vsvvvhvvv",
         (packed, *(pltpu.HBM((pairs, *dims), kind) for dims, kind in held)),
         [
             *(pltpu.VMEM((pairs, *dims), kind) for dims, kind in held),
-            pltpu.VMEM((NX + 8, 2 * (ROWS - CY) * LANES), f32),
+            pltpu.VMEM((EXTENDED, 2 * CY * LANES), f32),
             table_space,
             weights_space,
             four,
         ],
-    )(below_atoms, base, taps, x_forward, cos_t, sin_t, own_lines, where, atoms)
+    )(below_atoms, where, base, taps, slab_grid, x_forward, cos_t, sin_t, atoms)
     lines, shear_cells = lax.optimization_barrier((lines, shear_cells))
     shear_step = shear_cells[0]
 
@@ -798,24 +810,20 @@
     filtered = swap_slabs(filtered)
     shares_shape = shape((PENCILS, 8, ATOM_DEV), f32)
     sample_spaces = [
-        table_space,
         *(pltpu.VMEM((pairs // 2, *dims), kind) for dims, kind in held),
         weights_space,
         four,
     ]
-    below_shares = call(
+    below_shares, potential = call(
         lambda *refs: sample_kernel(False, *refs),
-        "vvsvvvvhhhh",
-        shares_shape,
-        [pltpu.VMEM((NX + 8, (ROWS - CY) * LANES), f32), *sample_spaces],
-    )(filtered, below_atoms, where, base, taps, cos_t, sin_t, x_inverse, *weights)
+        "vsvvhhhvvvh",
+        (shares_shape, shape((EXTENDED, CY * LANES), f32)),
+        [table_space, *sample_spaces],
+    )(below_atoms, where, base, taps, *weights, filtered, cos_t, sin_t, x_inverse)
     below_shares = next_slab(below_shares, back=True)
     shares = call(
-        lambda *refs: sample_kernel(True, *refs),
-        "vvsvvvvhhhh",
-        shares_shape,
-        [pltpu.VMEM((NX + 8, CY * LANES), f32), *sample_spaces],
-    )(filtered, atoms, where, base, taps, cos_t, sin_t, x_inverse, *weights)
+        lambda *refs: sample_kernel(True, *refs), "vsvvhhhv", shares_shape, sample_spaces
+    )(atoms, where, base, taps, *weights, potential)
     shares = lax.all_to_all(shares + below_shares, "gx", split_axis=0, concat_axis=0, tiled=True)
     charge_grad, dipole_grad, position_grad, energy = call(
         finish_kernel,

time: 117 us -> 117 us (level)
  transfers between devices with their start and end apart: 3 -> 3, of which waited for: 2 -> 2; matrix products, arithmetic and copies ran while one was open for 2% -> 2% of each run, Pallas kernels for 9% -> 7%
where the time goes in v6:
time: 117 us
  blocking collectives  47.2 us (40%)
  Pallas kernels  31.9 us (27%)
  waiting for transfers between devices  25.2 us (22%)
  starting transfers between devices  8.95 us (8%)
  other arithmetic  1.84 us (2%)
  between operations  1.55 us (1%)
    pallas_call x8, Pallas kernels, run(): pl.pallas_call(kernel, out_shape=out_shape, in_specs=[pl.BlockSpec(memory...  31.9 us
    all_to_all x1, blocking collectives, swap_slabs(): lines = lax.all_to_all(lines, 'gy', split_axis=0, concat_axis=0, tiled=True)  28.5 us
    all_to_all x1, waiting for transfers between devices, swap_slabs(): lines = lax.all_to_all(lines, 'gy', split_axis=0, concat_axis=0, tiled=True)  18.4 us
    all_gather x1, blocking collectives, on_device(): atoms = lax.all_gather(mine, 'gx', axis=0, tiled=False)  9.91 us
    all_to_all x1, blocking collectives, on_device(): lax.all_to_all(shares + below_shares, 'gx', split_axis=0, concat_axis=0,...  8.83 us
    ppermute x2, waiting for transfers between devices, next_slab(): lax.ppermute(value, 'gy', [(i, (i + step) % SLABS) for i in range(SLABS)])  6.78 us
    all_to_all x1, starting transfers between devices, swap_slabs(): lines = lax.all_to_all(lines, 'gy', split_axis=0, concat_axis=0, tiled=True)  6.44 us
    ppermute x2, starting transfers between devices, next_slab(): lax.ppermute(value, 'gy', [(i, (i + step) % SLABS) for i in range(SLABS)])  2.51 us
  transfers between devices with their start and end apart: 3, of which 2 were waited for; matrix products, arithmetic and copies ran while one was open for 2% of the time, Pallas kernels for 7%

profile of v6, /device:TPU:1, one launch (start us, length us, event | category | flops | bytes accessed | tf_op | source)
XLA Modules:
  0.0 116.7 jit_solution(5698371079964260487)
XLA Ops:
  1.3 0.1 pad_add_fusion.where_ref.refs_1_
  1.4 1.3 %shard_map.129 = (f32[16,384]{1,0:T(8,128)S(1)}, f32[8,128]{1,0:T(8,128)S(1)}, f32[12,48,128]{2,1,0:T(8,128)S(1)}, f32[384,128]{1,0:T(8,128)S(1)}, f32[384,128]{1,0:T(8,128)S(1)}) custom-call(s32[3]{0:T(128)S(1)} %pad_add_fusion.where_ref.refs_1_, s32[1]{0:T(128)} %copy.19.shear_ref, s32[6]{0:T(128)} %counts_ref.1, s32[3,384]{1,0:T(4,128)} %cells_ref.1, ...), custom_call_target="tpu_custom_call" | custom-call | flops 1000000000 | bytes 8000000 | tf_op jit(solution)/shard_map/pallas_call | solution.py:689
  2.7 9.9 %all-gather = f32[64,384]{1,0:T(8,128)S(1)} all-gather(f32[16,384]{1,0:T(8,128)S(1)} %get-tuple-element.21), channel_id=2, replica_groups=mesh['gy'=64,'gx'=4] {'gx'}, dimensions={0}, use_global_device_ids=true | all-gather | bytes 122880 | tf_op jit(solution)/shard_map/all_gather | solution.py:748
  12.6 0.0 collective-permute-start
  12.6 3.4 %shard_map.130.refs_4_ = f32[432,1536]{1,0:T(8,128)S(1)} custom-call(f32[4,16,384]{2,1,0:T(8,128)S(1)} %bitcast.16, s32[3]{0:T(128)S(1)} %pad_add_fusion.where_ref.refs_1_, f32[8,128]{1,0:T(8,128)S(1)} %get-tuple-element.22.refs_2_, f32[12,48,128]{2,1,0:T(8,128)S(1)} %get-tuple-element.23.refs_3_), custom_call_target="tpu_custom_call" | custom-call | flops 1000000000 | bytes 8000000 | tf_op jit(solution)/shard_map/pallas_call | solution.py:689
  16.0 6.8 %collective-permute-done.refs_0_ = f32[4,16,384]{2,1,0:T(8,128)S(1)} collective-permute-done((f32[4,16,384]{2,1,0:T(8,128)S(1)}, f32[4,16,384]{2,1,0:T(8,128)S(1)}, u32[]{:S(2)}, u32[]{:S(2)}) %collective-permute-start) | collective-permute-done | bytes 98336 | tf_op jit(solution)/shard_map/ppermute | solution.py:704
  22.8 12.3 %shard_map.131 = (f32[1728,128]{1,0:T(8,128)}, bf16[24,2,96,384]{3,2,1,0:T(8,128)(2,1)}, f32[24,3,48,128]{3,2,1,0:T(8,128)}, f32[24,3,16,128]{3,2,1,0:T(8,128)}) custom-call(f32[4,16,384]{2,1,0:T(8,128)S(1)} %collective-permute-done.refs_0_, s32[3]{0:T(128)S(1)} %pad_add_fusion.where_ref.refs_1_, f32[8,128]{1,0:T(8,128)S(1)} %get-tuple-element.22.refs_2_, ...), custom_call_target="tpu_custom_call" | custom-call | flops 1000000000 | bytes 8000000 | tf_op jit(solution)/shard_map/pallas_call | solution.py:689
  35.0 6.4 %all-to-all-start = ((f32[64,27,1,128]{3,2,1,0:T(1,128)}), f32[64,27,1,128]{3,2,1,0:T(1,128)S(1)}, u32[]{:S(2)}, u32[]{:S(2)}) async-start(f32[64,27,1,128]{3,2,1,0:T(1,128)} %bitcast.5), calls=%async_computation | async-start | bytes 1769472 | tf_op jit(solution)/shard_map/all_to_all | solution.py:709
  41.6 0.1 add_multiply_fusion.3
  41.7 0.1 compare_select_fusion.1
  41.8 1.5 %fusion.3 = (f32[384,8]{1,0:T(8,128)S(1)}, f32[384,8]{1,0:T(8,128)S(1)}) fusion(f32[8]{0:T(128)S(1)} %multiply_multiply_fusion.2, f32[8]{0:T(128)S(1)} %get-tuple-element.41, f32[384]{0:T(512)S(1)} %fusion.23, f32[8]{0:T(128)S(1)} %get-tuple-element.40, pred[384]{0:T(512)(128)(4,1)S(1)} %broadcast_compare_fusion, pred[8]{0:T(512)(128)(4,1)S(1)} %broadcast_compare_fusion.1), kind=kLoop, calls=%fused_computation.7 | loop fusion | flops 52224 | bytes 26600 | tf_op jit(solution)/shard_map/add | solution.py:787
  43.3 0.7 shard_map.132.green_ref
  43.9 18.4 %all-to-all-done = f32[64,27,1,128]{3,2,1,0:T(1,128)S(1)} async-done(((f32[64,27,1,128]{3,2,1,0:T(1,128)}), f32[64,27,1,128]{3,2,1,0:T(1,128)S(1)}, u32[]{:S(2)}, u32[]{:S(2)}) %all-to-all-start) | async-done | bytes 884768 | tf_op jit(solution)/shard_map/all_to_all | solution.py:709
  62.4 3.5 %shard_map.133 = f32[1728,128]{1,0:T(8,128)S(1)} custom-call(f32[1728,128]{1,0:T(8,128)S(1)} %bitcast.12, bf16[384,576]{1,0:T(8,128)(2,1)} %constant.151.clone.tables_ref, bf16[384,576]{1,0:T(8,128)(2,1)} %constant.152.clone.backs_ref, f32[384,768]{1,0:T(8,128)S(1)} %shard_map.132.green_ref), custom_call_target="tpu_custom_call" | custom-call | flops 1000000000 | bytes 8000000 | tf_op jit(solution)/shard_map/pallas_call | solution.py:689
  65.8 28.5 %all_to_all.15 = f32[64,27,1,128]{3,2,1,0:T(1,128)S(1)} all-to-all(f32[64,27,1,128]{3,2,1,0:T(1,128)S(1)} %bitcast.13), channel_id=1, replica_groups=mesh['gy'=64,'gx'=4] {'gy'}, dimensions={0} | all-to-all | bytes 1769472 | tf_op jit(solution)/shard_map/all_to_all | solution.py:709
  94.3 5.4 %shard_map.134 = (f32[4,8,384]{2,1,0:T(8,128)S(1)}, f32[432,768]{1,0:T(8,128)S(1)}) custom-call(f32[4,16,384]{2,1,0:T(8,128)S(1)} %collective-permute-done.refs_0_, s32[3]{0:T(128)S(1)} %pad_add_fusion.where_ref.refs_1_, f32[8,128]{1,0:T(8,128)S(1)} %get-tuple-element.22.refs_2_, f32[12,48,128]{2,1,0:T(8,128)S(1)} %get-tuple-element.23.refs_3_, ...), custom_call_target="tpu_custom_call" | custom-call | flops 1000000000 | bytes 8000000 | tf_op jit(solution)/shard_map/pallas_call | solution.py:689
  99.7 2.5 %collective-permute-start.1 = (f32[4,8,384]{2,1,0:T(8,128)S(1)}, f32[4,8,384]{2,1,0:T(8,128)S(1)}, u32[]{:S(2)}, u32[]{:S(2)}) collective-permute-start(f32[4,8,384]{2,1,0:T(8,128)S(1)} %get-tuple-element.33), channel_id=1, source_target_pairs={{0,252},{4,0},{8,4},{12,8},{16,12},{20,16},{24,20},{28,24},{32,28}... | collective-permute-start | bytes 147464 | tf_op jit(solution)/shard_map/ppermute | solution.py:704
  102.2 4.3 %shard_map.135 = f32[4,8,384]{2,1,0:T(8,128)S(1)} custom-call(f32[4,16,384]{2,1,0:T(8,128)S(1)} %bitcast.18, s32[3]{0:T(128)S(1)} %pad_add_fusion.where_ref.refs_1_, f32[8,128]{1,0:T(8,128)S(1)} %get-tuple-element.22.refs_2_, f32[12,48,128]{2,1,0:T(8,128)S(1)} %get-tuple-element.23.refs_3_, bf16[24,2,96,384]{3,2,1,0:T(8,128)(2,1)} %get-tuple-element.26.refs_4_, ...), custom_call_target="tpu_custom_call" | custom-call | flops 1000000000 | bytes 8000000 | tf_op jit(solution)/shard_map/pallas_call | solution.py:689
  106.5 0.0 collective-permute-done.1
  106.5 8.8 %all_to_all.16.in_ref = f32[4,8,384]{2,1,0:T(8,128)S(1)} all-to-all(f32[4,8,384]{2,1,0:T(8,128)S(1)} %add.319), channel_id=1, replica_groups=mesh['gy'=64,'gx'=4] {'gx'}, dimensions={0} | all-to-all | bytes 98304 | tf_op jit(solution)/shard_map/all_to_all | solution.py:827
  115.3 1.2 %shard_map.136 = (f32[384]{0:T(512)}, f32[3,384]{1,0:T(4,128)}, f32[3,384]{1,0:T(4,128)}, f32[1,1]{1,0:T(1,128)}) custom-call(f32[4,8,384]{2,1,0:T(8,128)S(1)} %all_to_all.16.in_ref), custom_call_target="tpu_custom_call" | custom-call | flops 1000000000 | bytes 8000000 | tf_op jit(solution)/shard_map/pallas_call | solution.py:689
  (6 shorter events, 0.1 us)
Async XLA Ops:
  12.6 10.1 %collective-permute-start = (f32[4,16,384]{2,1,0:T(8,128)S(1)}, f32[4,16,384]{2,1,0:T(8,128)S(1)}, u32[]{:S(2)}, u32[]{:S(2)}) collective-permute-start(f32[4,16,384]{2,1,0:T(8,128)S(1)} %bitcast.15), channel_id=1, source_target_pairs={{0,4},{4,8},{8,12},{12,16},{16,20},{20,24},{24,28},{28,32},{32,36}... | collective-permute-start | bytes 294920 | tf_op jit(solution)/shard_map/ppermute | solution.py:704
  35.0 27.3 %all-to-all-start = ((f32[64,27,1,128]{3,2,1,0:T(1,128)}), f32[64,27,1,128]{3,2,1,0:T(1,128)S(1)}, u32[]{:S(2)}, u32[]{:S(2)}) async-start(f32[64,27,1,128]{3,2,1,0:T(1,128)} %bitcast.5), calls=%async_computation | async-start | bytes 1769472 | tf_op jit(solution)/shard_map/all_to_all | solution.py:709
  99.7 6.8 %collective-permute-start.1 = (f32[4,8,384]{2,1,0:T(8,128)S(1)}, f32[4,8,384]{2,1,0:T(8,128)S(1)}, u32[]{:S(2)}, u32[]{:S(2)}) collective-permute-start(f32[4,8,384]{2,1,0:T(8,128)S(1)} %get-tuple-element.33), channel_id=1, source_target_pairs={{0,252},{4,0},{8,4},{12,8},{16,12},{20,16},{24,20},{28,24},{32,28}... | collective-permute-start | bytes 147464 | tf_op jit(solution)/shard_map/ppermute | solution.py:704

commit v7 on v6

--- a/solution.py
+++ b/solution.py
@@ -368,6 +368,16 @@
         return carry
 
     lax.fori_loop(0, PENCILS * PAIRS, pair_body, 0, unroll=2)
+
+
+def keep_weights(atoms, where_ref, weights_ref, base_ref, taps_ref, kept, results, semaphores):
+    for start, some_ref in zip((0, PENCILS * PAIRS), atoms):
+        sampling_weights(
+            start, start == 0, where_ref, some_ref, weights_ref, base_ref, taps_ref, *kept
+        )
+    copies = [fetch(kept[n], results[n], semaphores.at[n]) for n in range(3)]
+    for copy in copies:
+        copy.wait()
 
 
 def spread_kernel(own, *refs):
@@ -461,13 +471,23 @@
 
     @pl.when(where_ref[1] % 2 == 1)
     def _():
-        for start, some_ref in ((0, slab_atoms_ref), (PENCILS * PAIRS, atoms_ref)):
-            sampling_weights(
-                start, start == 0, where_ref, some_ref, weights_ref, base_ref, taps_ref, *kept
-            )
-        copies = [fetch(kept[n], results[n], semaphores.at[n]) for n in range(3)]
-        for copy in copies:
-            copy.wait()
+        keep_weights(
+            (slab_atoms_ref, atoms_ref), where_ref, weights_ref, base_ref, taps_ref,
+            kept, results, semaphores
+        )
+
+
+def weights_kernel(
+    atoms_ref, below_ref, where_ref, base_ref, taps_ref, waves_in_ref, x_in_ref, y_in_ref, *refs
+):
+    results, kept, weights_ref, semaphores = refs[:3], refs[3:6], refs[6], refs[7]
+
+    @pl.when(where_ref[1] % 2 == 0)
+    def _():
+        keep_weights(
+            (atoms_ref, below_ref), where_ref, weights_ref, base_ref, taps_ref,
+            kept, results, semaphores
+        )
 
 
 def green_kernel(top_ref, norm_ref, mode_ref, out_ref):
@@ -536,33 +556,26 @@
 
 
 def sample_kernel(own, *refs):
-    atoms_ref, where_ref, base_ref, taps_ref, waves_in_ref, x_in_ref, y_in_ref = refs[:7]
+    atoms_ref, where_ref, waves_in_ref, x_in_ref, y_in_ref = refs[:5]
     if own:
-        grid_ref, out_ref = refs[7:9]
+        grid_ref, out_ref = refs[5:7]
     else:
-        in_ref, cos_ref, sin_ref, tables_ref, out_ref, grid_ref, table_ref = refs[7:14]
-    waves_ref, x_ref, y_ref, weights_ref, semaphores = refs[-5:]
+        in_ref, cos_ref, sin_ref, tables_ref, out_ref, grid_ref, table_ref = refs[5:12]
+    waves_ref, x_ref, y_ref, semaphores = refs[-4:]
     if not own:
-        table_copy = fetch(tables_ref, table_ref, semaphores.at[3])
-    later = where_ref[1] % 2 == 0
+        table_copy = fetch(tables_ref, table_ref, semaphores.at[3, 0])
     start = 0 if own else PENCILS * PAIRS
-    some = pl.ds(start, PENCILS * PAIRS)
-    copies = [
-        pltpu.make_async_copy(source.at[some], target, semaphores.at[n])
-        for n, (source, target) in enumerate(
-            ((waves_in_ref, waves_ref), (x_in_ref, x_ref), (y_in_ref, y_ref))
-        )
-    ]
-
-    @pl.when(later)
-    def _():
-        sampling_weights(
-            0, own, where_ref, atoms_ref, weights_ref, base_ref, taps_ref, waves_ref, x_ref, y_ref
-        )
-
-    @pl.when(jnp.logical_not(later))
-    def _():
-        for copy in copies:
+
+    def pair_copies(pair):
+        return [
+            pltpu.make_async_copy(source.at[start + pair], target.at[pair], semaphores.at[n, pair])
+            for n, (source, target) in enumerate(
+                ((waves_in_ref, waves_ref), (x_in_ref, x_ref), (y_in_ref, y_ref))
+            )
+        ]
+
+    for pair in range(PENCILS * PAIRS):
+        for copy in pair_copies(pair):
             copy.start()
 
     rows = list(range(CY)) if own else list(range(CY, 2 * CY - 1))
@@ -591,13 +604,10 @@
         energy = jnp.sum(jnp.where(lane == PART_Z, in_ref[rows_of(0), :], 0.0))
     gap = jnp.zeros((HALF - PADDED_Z, 3 * LANES), bf16)
 
-    @pl.when(jnp.logical_not(later))
-    def _():
-        for copy in copies:
-            copy.wait()
-
     def pair_body(pair, carry):
         pencil, lanes = pair_place(pair)
+        for copy in pair_copies(pair):
+            copy.wait()
         waves = [
             jnp.concatenate(
                 [waves_ref[pair, n, :PADDED_Z], gap, waves_ref[pair, n, PADDED_Z:], gap],
@@ -680,7 +690,7 @@
     return pl.BlockSpec(memory_space=pltpu.HBM if pinned else pltpu.VMEM)
 
 
-def call(kernel, inputs, out_shape, scratch=()):
+def call(kernel, inputs, out_shape, scratch=(), aliases=()):
     def run(*operands):
         placed = [
             pltpu.with_memory_space_constraint(one, pltpu.HBM) if where == "h" else one
@@ -692,6 +702,7 @@
             in_specs=[pl.BlockSpec(memory_space=SPACES[one]) for one in inputs],
             out_specs=jax.tree.map(out_place, out_shape),
             scratch_shapes=list(scratch),
+            input_output_aliases=dict(aliases),
             compiler_params=pltpu.CompilerParams(vmem_limit_bytes=28 * 1024 * 1024),
             cost_estimate=pl.CostEstimate(transcendentals=0, **WORK),
         )(*placed)
@@ -807,23 +818,30 @@
     filtered = call(filter_kernel, "vhhv", packed, [table_space, table_space, two])(
         lines, y_forward, y_inverse, green
     )
+    filtered, atoms, below_atoms = lax.optimization_barrier((filtered, atoms, below_atoms))
+    weights = call(
+        weights_kernel,
+        "vvsvvhhh",
+        tuple(pltpu.HBM((pairs, *dims), kind) for dims, kind in held),
+        [*(pltpu.VMEM((pairs, *dims), kind) for dims, kind in held), weights_space, four],
+        ((5, 0), (6, 1), (7, 2)),
+    )(atoms, below_atoms, where, base, taps, *weights)
     filtered = swap_slabs(filtered)
     shares_shape = shape((PENCILS, 8, ATOM_DEV), f32)
     sample_spaces = [
         *(pltpu.VMEM((pairs // 2, *dims), kind) for dims, kind in held),
-        weights_space,
-        four,
+        pltpu.SemaphoreType.DMA((4, pairs // 2)),
     ]
     below_shares, potential = call(
         lambda *refs: sample_kernel(False, *refs),
-        "vsvvhhhvvvh",
+        "vshhhvvvh",
         (shares_shape, shape((EXTENDED, CY * LANES), f32)),
         [table_space, *sample_spaces],
-    )(below_atoms, where, base, taps, *weights, filtered, cos_t, sin_t, x_inverse)
+    )(below_atoms, where, *weights, filtered, cos_t, sin_t, x_inverse)
     below_shares = next_slab(below_shares, back=True)
     shares = call(
-        lambda *refs: sample_kernel(True, *refs), "vsvvhhhv", shares_shape, sample_spaces
-    )(atoms, where, base, taps, *weights, potential)
+        lambda *refs: sample_kernel(True, *refs), "vshhhv", shares_shape, sample_spaces
+    )(atoms, where, *weights, potential)
     shares = lax.all_to_all(shares + below_shares, "gx", split_axis=0, concat_axis=0, tiled=True)
     charge_grad, dipole_grad, position_grad, energy = call(
         finish_kernel,

time: 117 us -> 122 us (1.043)
  blocking collectives: 47.2 us -> 18.8 us
  waiting for transfers between devices: 25.2 us -> 47.3 us
  starting transfers between devices: 8.95 us -> 14.8 us
  Pallas kernels: 31.9 us -> 37.3 us
    all_to_all x1 -> x0, blocking collectives: 28.5 us -> none  [swap_slabs(): lines = lax.all_to_all(lines, 'gy', split_axis=0, concat_axis=0, tiled=True)]
    all_to_all x1 -> x2, waiting for transfers between devices: 18.4 us -> 40.6 us  [swap_slabs(): lines = lax.all_to_all(lines, 'gy', split_axis=0, concat_axis=0, tiled=True)]
    all_to_all x1 -> x2, starting transfers between devices: 6.44 us -> 12.3 us  [swap_slabs(): lines = lax.all_to_all(lines, 'gy', split_axis=0, concat_axis=0, tiled=True)]
    pallas_call x8 -> x9, Pallas kernels: 31.9 us -> 37.3 us  [run(): pl.pallas_call(kernel, out_shape=out_shape, in_specs=[pl.BlockSpec(memory...]
  transfers between devices with their start and end apart: 3 -> 4, of which waited for: 2 -> 3; matrix products, arithmetic and copies ran while one was open for 2% -> 1% of each run, Pallas kernels for 7% -> 9%
where the time goes in v7:
time: 122 us
  waiting for transfers between devices  47.3 us (39%)
  Pallas kernels  37.3 us (31%)
  blocking collectives  18.8 us (15%)
  starting transfers between devices  14.8 us (12%)
  other arithmetic  1.85 us (2%)
  between operations  1.56 us (1%)
    all_to_all x2, waiting for transfers between devices, swap_slabs(): lines = lax.all_to_all(lines, 'gy', split_axis=0, concat_axis=0, tiled=True)  40.6 us
    pallas_call x9, Pallas kernels, run(): pl.pallas_call(kernel, out_shape=out_shape, in_specs=[pl.BlockSpec(memory...  37.3 us
    all_to_all x2, starting transfers between devices, swap_slabs(): lines = lax.all_to_all(lines, 'gy', split_axis=0, concat_axis=0, tiled=True)  12.3 us
    all_gather x1, blocking collectives, on_device(): atoms = lax.all_gather(mine, 'gx', axis=0, tiled=False)  9.91 us
    all_to_all x1, blocking collectives, on_device(): lax.all_to_all(shares + below_shares, 'gx', split_axis=0, concat_axis=0,...  8.87 us
    ppermute x2, waiting for transfers between devices, next_slab(): lax.ppermute(value, 'gy', [(i, (i + step) % SLABS) for i in range(SLABS)])  6.78 us
    ppermute x2, starting transfers between devices, next_slab(): lax.ppermute(value, 'gy', [(i, (i + step) % SLABS) for i in range(SLABS)])  2.55 us
  transfers between devices with their start and end apart: 4, of which 3 were waited for; matrix products, arithmetic and copies ran while one was open for 1% of the time, Pallas kernels for 9%

profile of v7, /device:TPU:1, one launch (start us, length us, event | category | flops | bytes accessed | tf_op | source)
XLA Modules:
  0.0 121.6 jit_solution(3188290511878570060)
XLA Ops:
  1.3 0.1 pad_add_fusion.where_ref.refs_1_
  1.4 1.3 %shard_map.129 = (f32[16,384]{1,0:T(8,128)S(1)}, f32[8,128]{1,0:T(8,128)S(1)}, f32[12,48,128]{2,1,0:T(8,128)S(1)}, f32[384,128]{1,0:T(8,128)S(1)}, f32[384,128]{1,0:T(8,128)S(1)}) custom-call(s32[3]{0:T(128)S(1)} %pad_add_fusion.where_ref.refs_1_, s32[1]{0:T(128)} %copy.25.shear_ref, s32[6]{0:T(128)} %counts_ref.1, s32[3,384]{1,0:T(4,128)} %cells_ref.1, ...), custom_call_target="tpu_custom_call" | custom-call | flops 1000000000 | bytes 8000000 | tf_op jit(solution)/shard_map/pallas_call | solution.py:699
  2.7 9.9 %all-gather = f32[64,384]{1,0:T(8,128)S(1)} all-gather(f32[16,384]{1,0:T(8,128)S(1)} %get-tuple-element.27), channel_id=2, replica_groups=mesh['gy'=64,'gx'=4] {'gx'}, dimensions={0}, use_global_device_ids=true | all-gather | bytes 122880 | tf_op jit(solution)/shard_map/all_gather | solution.py:759
  12.6 0.0 collective-permute-start
  12.6 3.4 %shard_map.130.refs_4_ = f32[432,1536]{1,0:T(8,128)S(1)} custom-call(f32[4,16,384]{2,1,0:T(8,128)S(1)} %bitcast.15, s32[3]{0:T(128)S(1)} %pad_add_fusion.where_ref.refs_1_, f32[8,128]{1,0:T(8,128)S(1)} %get-tuple-element.28.refs_2_.base_ref, f32[12,48,128]{2,1,0:T(8,128)S(1)} %get-tuple-element.29.refs_3_.taps_ref), custom_call_target="tpu_custom_call" | custom-call | flops 1000000000 | bytes 8000000 | tf_op jit(solution)/shard_map/pallas_call | solution.py:699
  16.0 6.8 %collective-permute-done.refs_0_.below_ref = f32[4,16,384]{2,1,0:T(8,128)S(1)} collective-permute-done((f32[4,16,384]{2,1,0:T(8,128)S(1)}, f32[4,16,384]{2,1,0:T(8,128)S(1)}, u32[]{:S(2)}, u32[]{:S(2)}) %collective-permute-start) | collective-permute-done | bytes 98336 | tf_op jit(solution)/shard_map/ppermute | solution.py:715
  22.8 12.3 %shard_map.131 = (f32[1728,128]{1,0:T(8,128)}, bf16[24,2,96,384]{3,2,1,0:T(8,128)(2,1)}, f32[24,3,48,128]{3,2,1,0:T(8,128)}, f32[24,3,16,128]{3,2,1,0:T(8,128)}) custom-call(f32[4,16,384]{2,1,0:T(8,128)S(1)} %collective-permute-done.refs_0_.below_ref, s32[3]{0:T(128)S(1)} %pad_add_fusion.where_ref.refs_1_, f32[8,128]{1,0:T(8,128)S(1)} %get-tuple-element.28.refs_2_.base_ref, ...), custom_call_target="tpu_custom_call" | custom-call | flops 1000000000 | bytes 8000000 | tf_op jit(solution)/shard_map/pallas_call | solution.py:699
  35.0 6.4 %all-to-all-start = ((f32[64,27,1,128]{3,2,1,0:T(1,128)}), f32[64,27,1,128]{3,2,1,0:T(1,128)S(1)}, u32[]{:S(2)}, u32[]{:S(2)}) async-start(f32[64,27,1,128]{3,2,1,0:T(1,128)} %bitcast.5), calls=%async_computation | async-start | bytes 1769472 | tf_op jit(solution)/shard_map/all_to_all | solution.py:720
  41.6 0.1 add_multiply_fusion.3
  41.7 0.1 compare_select_fusion.1
  41.8 1.5 %fusion.3 = (f32[384,8]{1,0:T(8,128)S(1)}, f32[384,8]{1,0:T(8,128)S(1)}) fusion(f32[8]{0:T(128)S(1)} %multiply_multiply_fusion.2, f32[8]{0:T(128)S(1)} %get-tuple-element.53, f32[384]{0:T(512)S(1)} %fusion.23, f32[8]{0:T(128)S(1)} %get-tuple-element.52, pred[384]{0:T(512)(128)(4,1)S(1)} %broadcast_compare_fusion, pred[8]{0:T(512)(128)(4,1)S(1)} %broadcast_compare_fusion.1), kind=kLoop, calls=%fused_computation.7 | loop fusion | flops 52224 | bytes 26600 | tf_op jit(solution)/shard_map/add | solution.py:798
  43.3 0.7 shard_map.132.green_ref
  44.0 18.4 %all-to-all-done = f32[64,27,1,128]{3,2,1,0:T(1,128)S(1)} async-done(((f32[64,27,1,128]{3,2,1,0:T(1,128)}), f32[64,27,1,128]{3,2,1,0:T(1,128)S(1)}, u32[]{:S(2)}, u32[]{:S(2)}) %all-to-all-start) | async-done | bytes 884768 | tf_op jit(solution)/shard_map/all_to_all | solution.py:720
  62.3 4.4 %shard_map.133 = f32[1728,128]{1,0:T(8,128)} custom-call(f32[1728,128]{1,0:T(8,128)S(1)} %bitcast.12, bf16[384,576]{1,0:T(8,128)(2,1)} %constant.151.clone.tables_ref, bf16[384,576]{1,0:T(8,128)(2,1)} %constant.152.clone.backs_ref, f32[384,768]{1,0:T(8,128)S(1)} %shard_map.132.green_ref), custom_call_target="tpu_custom_call" | custom-call | flops 1000000000 | bytes 8000000 | tf_op jit(solution)/shard_map/pallas_call | solution.py:699
  66.8 5.8 %all-to-all-start.1 = ((f32[64,27,1,128]{3,2,1,0:T(1,128)}), f32[64,27,1,128]{3,2,1,0:T(1,128)S(1)}, u32[]{:S(2)}, u32[]{:S(2)}) async-start(f32[64,27,1,128]{3,2,1,0:T(1,128)} %bitcast.8), calls=%async_computation.1 | async-start | bytes 1769472 | tf_op jit(solution)/shard_map/all_to_all | solution.py:720
  72.6 0.6 shard_map.134
  73.2 22.2 %all-to-all-done.1 = f32[64,27,1,128]{3,2,1,0:T(1,128)S(1)} async-done(((f32[64,27,1,128]{3,2,1,0:T(1,128)}), f32[64,27,1,128]{3,2,1,0:T(1,128)S(1)}, u32[]{:S(2)}, u32[]{:S(2)}) %all-to-all-start.1) | async-done | bytes 884768 | tf_op jit(solution)/shard_map/all_to_all | solution.py:720
  95.4 7.7 %shard_map.135 = (f32[4,8,384]{2,1,0:T(8,128)S(1)}, f32[432,768]{1,0:T(8,128)S(1)}) custom-call(f32[4,16,384]{2,1,0:T(8,128)S(1)} %collective-permute-done.refs_0_.below_ref, s32[3]{0:T(128)S(1)} %pad_add_fusion.where_ref.refs_1_, bf16[24,2,96,384]{3,2,1,0:T(8,128)(2,1)} %get-tuple-element.40.refs_2_, f32[24,3,48,128]{3,2,1,0:T(8,128)} %get-tuple-element.41.refs_3_, ...), custom_call_target="tpu_custom_call" | custom-call | flops 1000000000 | bytes 8000000 | tf_op jit(solution)/shard_map/pallas_call | solution.py:699
  103.1 2.5 %collective-permute-start.1 = (f32[4,8,384]{2,1,0:T(8,128)S(1)}, f32[4,8,384]{2,1,0:T(8,128)S(1)}, u32[]{:S(2)}, u32[]{:S(2)}) collective-permute-start(f32[4,8,384]{2,1,0:T(8,128)S(1)} %get-tuple-element.45), channel_id=1, source_target_pairs={{0,252},{4,0},{8,4},{12,8},{16,12},{20,16},{24,20},{28,24},{32,28}... | collective-permute-start | bytes 147464 | tf_op jit(solution)/shard_map/ppermute | solution.py:715
  105.6 5.8 %shard_map.136 = f32[4,8,384]{2,1,0:T(8,128)S(1)} custom-call(f32[4,16,384]{2,1,0:T(8,128)S(1)} %bitcast.18, s32[3]{0:T(128)S(1)} %pad_add_fusion.where_ref.refs_1_, bf16[24,2,96,384]{3,2,1,0:T(8,128)(2,1)} %get-tuple-element.40.refs_2_, f32[24,3,48,128]{3,2,1,0:T(8,128)} %get-tuple-element.41.refs_3_, f32[24,3,16,128]{3,2,1,0:T(8,128)} %get-tuple-element.42.refs_4_, ...), custom_call_target="tpu_custom_call" | custom-call | flops 1000000000 | bytes 8000000 | tf_op jit(solution)/shard_map/pallas_call | solution.py:699
  111.4 0.0 collective-permute-done.1
  111.4 8.9 %all_to_all.15.in_ref = f32[4,8,384]{2,1,0:T(8,128)S(1)} all-to-all(f32[4,8,384]{2,1,0:T(8,128)S(1)} %add.319), channel_id=1, replica_groups=mesh['gy'=64,'gx'=4] {'gx'}, dimensions={0} | all-to-all | bytes 98304 | tf_op jit(solution)/shard_map/all_to_all | solution.py:845
  120.3 1.2 shard_map.137
  (6 shorter events, 0.1 us)
Async XLA Ops:
  12.6 10.1 %collective-permute-start = (f32[4,16,384]{2,1,0:T(8,128)S(1)}, f32[4,16,384]{2,1,0:T(8,128)S(1)}, u32[]{:S(2)}, u32[]{:S(2)}) collective-permute-start(f32[4,16,384]{2,1,0:T(8,128)S(1)} %bitcast.14), channel_id=1, source_target_pairs={{0,4},{4,8},{8,12},{12,16},{16,20},{20,24},{24,28},{28,32},{32,36}... | collective-permute-start | bytes 294920 | tf_op jit(solution)/shard_map/ppermute | solution.py:715
  35.0 27.3 %all-to-all-start = ((f32[64,27,1,128]{3,2,1,0:T(1,128)}), f32[64,27,1,128]{3,2,1,0:T(1,128)S(1)}, u32[]{:S(2)}, u32[]{:S(2)}) async-start(f32[64,27,1,128]{3,2,1,0:T(1,128)} %bitcast.5), calls=%async_computation | async-start | bytes 1769472 | tf_op jit(solution)/shard_map/all_to_all | solution.py:720
  66.8 28.6 %all-to-all-start.1 = ((f32[64,27,1,128]{3,2,1,0:T(1,128)}), f32[64,27,1,128]{3,2,1,0:T(1,128)S(1)}, u32[]{:S(2)}, u32[]{:S(2)}) async-start(f32[64,27,1,128]{3,2,1,0:T(1,128)} %bitcast.8), calls=%async_computation.1 | async-start | bytes 1769472 | tf_op jit(solution)/shard_map/all_to_all | solution.py:720
  103.1 8.3 %collective-permute-start.1 = (f32[4,8,384]{2,1,0:T(8,128)S(1)}, f32[4,8,384]{2,1,0:T(8,128)S(1)}, u32[]{:S(2)}, u32[]{:S(2)}) collective-permute-start(f32[4,8,384]{2,1,0:T(8,128)S(1)} %get-tuple-element.45), channel_id=1, source_target_pairs={{0,252},{4,0},{8,4},{12,8},{16,12},{20,16},{24,20},{28,24},{32,28}... | collective-permute-start | bytes 147464 | tf_op jit(solution)/shard_map/ppermute | solution.py:715

commit v8 on v6

--- a/solution.py
+++ b/solution.py
@@ -376,11 +376,10 @@
         grid_ref, weights_ref = refs[4:]
         grid_ref[...] = jnp.zeros_like(grid_ref)
     else:
-        slab_grid_ref, tables_ref, cos_ref, sin_ref, slab_atoms_ref, out_ref = refs[4:10]
-        results, kept = refs[10:13], refs[13:16]
-        grid_ref, table_ref, weights_ref, semaphores = refs[16:]
+        _, tables_ref, cos_ref, sin_ref, slab_atoms_ref, grid_ref, out_ref = refs[4:11]
+        results, kept = refs[11:14], refs[14:17]
+        table_ref, weights_ref, semaphores = refs[17:]
         table_copy = fetch(tables_ref, table_ref, semaphores.at[0])
-        grid_ref[...] = slab_grid_ref[...]
     rows = list(range(CY)) if own else list(range(CY, 2 * CY - 1))
     part = CY * LANES
     gap = jnp.zeros((HALF - PADDED_Z, LANES), bf16)
@@ -536,34 +535,40 @@
 
 
 def sample_kernel(own, *refs):
-    atoms_ref, where_ref, base_ref, taps_ref, waves_in_ref, x_in_ref, y_in_ref = refs[:7]
     if own:
-        grid_ref, out_ref = refs[7:9]
+        atoms_ref, where_ref, waves_ref, x_ref, y_ref, grid_ref, out_ref = refs
     else:
-        in_ref, cos_ref, sin_ref, tables_ref, out_ref, grid_ref, table_ref = refs[7:14]
-    waves_ref, x_ref, y_ref, weights_ref, semaphores = refs[-5:]
-    if not own:
-        table_copy = fetch(tables_ref, table_ref, semaphores.at[3])
-    later = where_ref[1] % 2 == 0
-    start = 0 if own else PENCILS * PAIRS
-    some = pl.ds(start, PENCILS * PAIRS)
-    copies = [
-        pltpu.make_async_copy(source.at[some], target, semaphores.at[n])
-        for n, (source, target) in enumerate(
-            ((waves_in_ref, waves_ref), (x_in_ref, x_ref), (y_in_ref, y_ref))
-        )
-    ]
-
-    @pl.when(later)
-    def _():
-        sampling_weights(
-            0, own, where_ref, atoms_ref, weights_ref, base_ref, taps_ref, waves_ref, x_ref, y_ref
-        )
-
-    @pl.when(jnp.logical_not(later))
-    def _():
-        for copy in copies:
-            copy.start()
+        atoms_ref, where_ref, base_ref, taps_ref = refs[:4]
+        kept = refs[4:7]
+        in_ref, cos_ref, sin_ref, tables_ref, slab_atoms_ref, out_ref, grid_ref = refs[7:14]
+        slab_weights, below_weights = refs[14:17], refs[17:20]
+        waves_ref, x_ref, y_ref = below_weights
+        table_ref, weights_ref, semaphores = refs[20:]
+        table_copy = fetch(tables_ref, table_ref, semaphores.at[6])
+        later = where_ref[1] % 2 == 0
+        pairs = PENCILS * PAIRS
+        copies = [
+            pltpu.make_async_copy(source.at[pl.ds(start, pairs)], target, semaphores.at[n])
+            for n, (source, start, target) in enumerate(
+                [(kept[n], pairs, below_weights[n]) for n in range(3)]
+                + [(kept[n], 0, slab_weights[n]) for n in range(3)]
+            )
+        ]
+
+        @pl.when(later)
+        def _():
+            for slab, some_ref, targets in (
+                (False, atoms_ref, below_weights),
+                (True, slab_atoms_ref, slab_weights),
+            ):
+                sampling_weights(
+                    0, slab, where_ref, some_ref, weights_ref, base_ref, taps_ref, *targets
+                )
+
+        @pl.when(jnp.logical_not(later))
+        def _():
+            for copy in copies:
+                copy.start()
 
     rows = list(range(CY)) if own else list(range(CY, 2 * CY - 1))
     energy = 0.0
@@ -591,10 +596,12 @@
         energy = jnp.sum(jnp.where(lane == PART_Z, in_ref[rows_of(0), :], 0.0))
     gap = jnp.zeros((HALF - PADDED_Z, 3 * LANES), bf16)
 
-    @pl.when(jnp.logical_not(later))
-    def _():
-        for copy in copies:
-            copy.wait()
+    if not own:
+
+        @pl.when(jnp.logical_not(later))
+        def _():
+            for copy in copies[:3]:
+                copy.wait()
 
     def pair_body(pair, carry):
         pencil, lanes = pair_place(pair)
@@ -647,6 +654,12 @@
         return carry
 
     lax.fori_loop(0, PENCILS * PAIRS, pair_body, 0, unroll=6)
+    if not own:
+
+        @pl.when(jnp.logical_not(later))
+        def _():
+            for copy in copies[3:]:
+                copy.wait()
 
 
 def finish_kernel(in_ref, charge_ref, dipole_ref, position_ref, energy_ref, row_ref, semaphore):
@@ -680,7 +693,7 @@
     return pl.BlockSpec(memory_space=pltpu.HBM if pinned else pltpu.VMEM)
 
 
-def call(kernel, inputs, out_shape, scratch=()):
+def call(kernel, inputs, out_shape, scratch=(), aliases=()):
     def run(*operands):
         placed = [
             pltpu.with_memory_space_constraint(one, pltpu.HBM) if where == "h" else one
@@ -692,6 +705,7 @@
             in_specs=[pl.BlockSpec(memory_space=SPACES[one]) for one in inputs],
             out_specs=jax.tree.map(out_place, out_shape),
             scratch_shapes=list(scratch),
+            input_output_aliases=dict(aliases),
             compiler_params=pltpu.CompilerParams(vmem_limit_bytes=28 * 1024 * 1024),
             cost_estimate=pl.CostEstimate(transcendentals=0, **WORK),
         )(*placed)
@@ -759,23 +773,24 @@
     ]
     weights_space = pltpu.VMEM((PENCILS, 18, 8, ATOM_DEV), f32)
     four = pltpu.SemaphoreType.DMA((4,))
+    grid_shape = shape((EXTENDED, 2 * CY * LANES), f32)
     slab_grid = call(
         lambda *refs: spread_kernel(True, *refs),
         "vsvv",
-        shape((EXTENDED, 2 * CY * LANES), f32),
+        grid_shape,
         [weights_space],
     )(atoms, where, base, taps)
-    lines, *weights = call(
+    _, lines, *weights = call(
         lambda *refs: spread_kernel(False, *refs),
         "vsvvvhvvv",
-        (packed, *(pltpu.HBM((pairs, *dims), kind) for dims, kind in held)),
+        (grid_shape, packed, *(pltpu.HBM((pairs, *dims), kind) for dims, kind in held)),
         [
             *(pltpu.VMEM((pairs, *dims), kind) for dims, kind in held),
-            pltpu.VMEM((EXTENDED, 2 * CY * LANES), f32),
             table_space,
             weights_space,
             four,
         ],
+        ((4, 0),),
     )(below_atoms, where, base, taps, slab_grid, x_forward, cos_t, sin_t, atoms)
     lines, shear_cells = lax.optimization_barrier((lines, shear_cells))
     shear_step = shear_cells[0]
@@ -809,21 +824,25 @@
     )
     filtered = swap_slabs(filtered)
     shares_shape = shape((PENCILS, 8, ATOM_DEV), f32)
-    sample_spaces = [
-        *(pltpu.VMEM((pairs // 2, *dims), kind) for dims, kind in held),
-        weights_space,
-        four,
-    ]
-    below_shares, potential = call(
+    below_shares, potential, *weights = call(
         lambda *refs: sample_kernel(False, *refs),
-        "vsvvhhhvvvh",
-        (shares_shape, shape((EXTENDED, CY * LANES), f32)),
-        [table_space, *sample_spaces],
-    )(below_atoms, where, base, taps, *weights, filtered, cos_t, sin_t, x_inverse)
+        "vsvvhhhvvvhv",
+        (
+            shares_shape,
+            shape((EXTENDED, CY * LANES), f32),
+            *(shape((pairs // 2, *dims), kind) for dims, kind in held),
+        ),
+        [
+            *(pltpu.VMEM((pairs // 2, *dims), kind) for dims, kind in held),
+            table_space,
+            weights_space,
+            pltpu.SemaphoreType.DMA((7,)),
+        ],
+    )(below_atoms, where, base, taps, *weights, filtered, cos_t, sin_t, x_inverse, atoms)
     below_shares = next_slab(below_shares, back=True)
-    shares = call(
-        lambda *refs: sample_kernel(True, *refs), "vsvvhhhv", shares_shape, sample_spaces
-    )(atoms, where, base, taps, *weights, potential)
+    shares = call(lambda *refs: sample_kernel(True, *refs), "vsvvvv", shares_shape)(
+        atoms, where, *weights, potential
+    )
     shares = lax.all_to_all(shares + below_shares, "gx", split_axis=0, concat_axis=0, tiled=True)
     charge_grad, dipole_grad, position_grad, energy = call(
         finish_kernel,

time: 117 us -> 116 us (level)
  Pallas kernels: 31.9 us -> 30.1 us
    pallas_call x8, Pallas kernels: 31.9 us -> 30.1 us  [run(): pl.pallas_call(kernel, out_shape=out_shape, in_specs=[pl.BlockSpec(memory...]
  transfers between devices with their start and end apart: 3 -> 3, of which waited for: 2 -> 2; matrix products, arithmetic and copies ran while one was open for 2% -> 2% of each run, Pallas kernels for 7% -> 6%
where the time goes in v8:
time: 116 us; the launch traced here: 115 us
  blocking collectives  47.6 us (41%)
  Pallas kernels  30.1 us (26%)
  waiting for transfers between devices  25.2 us (22%)
  starting transfers between devices  8.94 us (8%)
  other arithmetic  1.84 us (2%)
  between operations  1.55 us (1%)
    pallas_call x8, Pallas kernels, run(): pl.pallas_call(kernel, out_shape=out_shape, in_specs=[pl.BlockSpec(memory...  30.1 us
    all_to_all x1, blocking collectives, swap_slabs(): lines = lax.all_to_all(lines, 'gy', split_axis=0, concat_axis=0, tiled=True)  28.5 us
    all_to_all x1, waiting for transfers between devices, swap_slabs(): lines = lax.all_to_all(lines, 'gy', split_axis=0, concat_axis=0, tiled=True)  18.4 us
    all_gather x1, blocking collectives, on_device(): atoms = lax.all_gather(mine, 'gx', axis=0, tiled=False)  9.91 us
    all_to_all x1, blocking collectives, on_device(): lax.all_to_all(shares + below_shares, 'gx', split_axis=0, concat_axis=0,...  9.2 us
    ppermute x2, waiting for transfers between devices, next_slab(): lax.ppermute(value, 'gy', [(i, (i + step) % SLABS) for i in range(SLABS)])  6.78 us
    all_to_all x1, starting transfers between devices, swap_slabs(): lines = lax.all_to_all(lines, 'gy', split_axis=0, concat_axis=0, tiled=True)  6.43 us
    ppermute x2, starting transfers between devices, next_slab(): lax.ppermute(value, 'gy', [(i, (i + step) % SLABS) for i in range(SLABS)])  2.51 us
  transfers between devices with their start and end apart: 3, of which 2 were waited for; matrix products, arithmetic and copies ran while one was open for 2% of the time, Pallas kernels for 6%

profile of v8, /device:TPU:1, one launch (start us, length us, event | category | flops | bytes accessed | tf_op | source)
XLA Modules:
  0.0 115.3 jit_solution(2780148548259832240)
XLA Ops:
  1.3 0.1 pad_add_fusion.where_ref.refs_1_
  1.4 1.3 %shard_map.129 = (f32[16,384]{1,0:T(8,128)S(1)}, f32[8,128]{1,0:T(8,128)S(1)}, f32[12,48,128]{2,1,0:T(8,128)S(1)}, f32[384,128]{1,0:T(8,128)S(1)}, f32[384,128]{1,0:T(8,128)S(1)}) custom-call(s32[3]{0:T(128)S(1)} %pad_add_fusion.where_ref.refs_1_, s32[1]{0:T(128)} %copy.21.shear_ref, s32[6]{0:T(128)} %counts_ref.1, s32[3,384]{1,0:T(4,128)} %cells_ref.1, ...), custom_call_target="tpu_custom_call" | custom-call | flops 1000000000 | bytes 8000000 | tf_op jit(solution)/shard_map/pallas_call | solution.py:702
  2.7 9.9 %all-gather = f32[64,384]{1,0:T(8,128)S(1)} all-gather(f32[16,384]{1,0:T(8,128)S(1)} %get-tuple-element.24), channel_id=2, replica_groups=mesh['gy'=64,'gx'=4] {'gx'}, dimensions={0}, use_global_device_ids=true | all-gather | bytes 122880 | tf_op jit(solution)/shard_map/all_gather | solution.py:762
  12.6 0.0 collective-permute-start
  12.6 3.4 %shard_map.130.refs_4_ = f32[432,1536]{1,0:T(8,128)S(1)} custom-call(f32[4,16,384]{2,1,0:T(8,128)S(1)} %bitcast.16, s32[3]{0:T(128)S(1)} %pad_add_fusion.where_ref.refs_1_, f32[8,128]{1,0:T(8,128)S(1)} %get-tuple-element.25.refs_2_, f32[12,48,128]{2,1,0:T(8,128)S(1)} %get-tuple-element.26.refs_3_), custom_call_target="tpu_custom_call" | custom-call | flops 1000000000 | bytes 8000000 | tf_op jit(solution)/shard_map/pallas_call | solution.py:702
  16.0 6.8 %collective-permute-done.refs_0_ = f32[4,16,384]{2,1,0:T(8,128)S(1)} collective-permute-done((f32[4,16,384]{2,1,0:T(8,128)S(1)}, f32[4,16,384]{2,1,0:T(8,128)S(1)}, u32[]{:S(2)}, u32[]{:S(2)}) %collective-permute-start) | collective-permute-done | bytes 98336 | tf_op jit(solution)/shard_map/ppermute | solution.py:718
  22.8 12.2 %shard_map.131 = (f32[432,1536]{1,0:T(8,128)S(1)}, f32[1728,128]{1,0:T(8,128)}, bf16[24,2,96,384]{3,2,1,0:T(8,128)(2,1)}, f32[24,3,48,128]{3,2,1,0:T(8,128)}, f32[24,3,16,128]{3,2,1,0:T(8,128)}) custom-call(f32[4,16,384]{2,1,0:T(8,128)S(1)} %collective-permute-done.refs_0_, s32[3]{0:T(128)S(1)} %pad_add_fusion.where_ref.refs_1_, ...), custom_call_target="tpu_custom_call", output_to_operand_aliasing={{0}: (4, {})} | custom-call | flops 1000000000 | bytes 8000000 | tf_op jit(solution)/shard_map/pallas_call | solution.py:702
  35.0 6.4 %all-to-all-start = ((f32[64,27,1,128]{3,2,1,0:T(1,128)}), f32[64,27,1,128]{3,2,1,0:T(1,128)S(1)}, u32[]{:S(2)}, u32[]{:S(2)}) async-start(f32[64,27,1,128]{3,2,1,0:T(1,128)} %bitcast.5), calls=%async_computation | async-start | bytes 1769472 | tf_op jit(solution)/shard_map/all_to_all | solution.py:723
  41.5 0.1 add_multiply_fusion.3
  41.6 0.1 compare_select_fusion.1
  41.7 1.5 %fusion.3 = (f32[384,8]{1,0:T(8,128)S(1)}, f32[384,8]{1,0:T(8,128)S(1)}) fusion(f32[8]{0:T(128)S(1)} %multiply_multiply_fusion.2, f32[8]{0:T(128)S(1)} %get-tuple-element.47, f32[384]{0:T(512)S(1)} %fusion.23, f32[8]{0:T(128)S(1)} %get-tuple-element.46, pred[384]{0:T(512)(128)(4,1)S(1)} %broadcast_compare_fusion, pred[8]{0:T(512)(128)(4,1)S(1)} %broadcast_compare_fusion.1), kind=kLoop, calls=%fused_computation.7 | loop fusion | flops 52224 | bytes 26600 | tf_op jit(solution)/shard_map/add | solution.py:802
  43.2 0.7 shard_map.132.green_ref
  43.9 18.4 %all-to-all-done = f32[64,27,1,128]{3,2,1,0:T(1,128)S(1)} async-done(((f32[64,27,1,128]{3,2,1,0:T(1,128)}), f32[64,27,1,128]{3,2,1,0:T(1,128)S(1)}, u32[]{:S(2)}, u32[]{:S(2)}) %all-to-all-start) | async-done | bytes 884768 | tf_op jit(solution)/shard_map/all_to_all | solution.py:723
  62.3 3.5 %shard_map.133 = f32[1728,128]{1,0:T(8,128)S(1)} custom-call(f32[1728,128]{1,0:T(8,128)S(1)} %bitcast.12, bf16[384,576]{1,0:T(8,128)(2,1)} %constant.151.clone.tables_ref, bf16[384,576]{1,0:T(8,128)(2,1)} %constant.152.clone.backs_ref, f32[384,768]{1,0:T(8,128)S(1)} %shard_map.132.green_ref), custom_call_target="tpu_custom_call" | custom-call | flops 1000000000 | bytes 8000000 | tf_op jit(solution)/shard_map/pallas_call | solution.py:702
  65.8 28.5 %all_to_all.15 = f32[64,27,1,128]{3,2,1,0:T(1,128)S(1)} all-to-all(f32[64,27,1,128]{3,2,1,0:T(1,128)S(1)} %bitcast.13), channel_id=1, replica_groups=mesh['gy'=64,'gx'=4] {'gy'}, dimensions={0} | all-to-all | bytes 1769472 | tf_op jit(solution)/shard_map/all_to_all | solution.py:723
  94.3 5.4 %shard_map.134 = (f32[4,8,384]{2,1,0:T(8,128)S(1)}, f32[432,768]{1,0:T(8,128)S(1)}, bf16[12,2,96,384]{3,2,1,0:T(8,128)(2,1)S(1)}, f32[12,3,48,128]{3,2,1,0:T(8,128)S(1)}, f32[12,3,16,128]{3,2,1,0:T(8,128)S(1)}) custom-call(f32[4,16,384]{2,1,0:T(8,128)S(1)} %collective-permute-done.refs_0_, s32[3]{0:T(128)S(1)} %pad_add_fusion.where_ref.refs_1_, ...), custom_call_target="tpu_custom_call" | custom-call | flops 1000000000 | bytes 8000000 | tf_op jit(solution)/shard_map/pallas_call | solution.py:702
  99.7 2.5 %collective-permute-start.1 = (f32[4,8,384]{2,1,0:T(8,128)S(1)}, f32[4,8,384]{2,1,0:T(8,128)S(1)}, u32[]{:S(2)}, u32[]{:S(2)}) collective-permute-start(f32[4,8,384]{2,1,0:T(8,128)S(1)} %get-tuple-element.39), channel_id=1, source_target_pairs={{0,252},{4,0},{8,4},{12,8},{16,12},{20,16},{24,20},{28,24},{32,28}... | collective-permute-start | bytes 147464 | tf_op jit(solution)/shard_map/ppermute | solution.py:718
  102.2 2.5 %shard_map.135 = f32[4,8,384]{2,1,0:T(8,128)S(1)} custom-call(f32[4,16,384]{2,1,0:T(8,128)S(1)} %bitcast.19, s32[3]{0:T(128)S(1)} %pad_add_fusion.where_ref.refs_1_, bf16[12,2,96,384]{3,2,1,0:T(8,128)(2,1)S(1)} %get-tuple-element.35.refs_2_, f32[12,3,48,128]{3,2,1,0:T(8,128)S(1)} %get-tuple-element.36.refs_3_, ...), custom_call_target="tpu_custom_call" | custom-call | flops 1000000000 | bytes 8000000 | tf_op jit(solution)/shard_map/pallas_call | solution.py:702
  104.7 0.0 collective-permute-done.1
  104.7 9.2 %all_to_all.16.in_ref = f32[4,8,384]{2,1,0:T(8,128)S(1)} all-to-all(f32[4,8,384]{2,1,0:T(8,128)S(1)} %add.319), channel_id=1, replica_groups=mesh['gy'=64,'gx'=4] {'gx'}, dimensions={0} | all-to-all | bytes 98304 | tf_op jit(solution)/shard_map/all_to_all | solution.py:846
  113.9 1.2 %shard_map.136 = (f32[384]{0:T(512)}, f32[3,384]{1,0:T(4,128)}, f32[3,384]{1,0:T(4,128)}, f32[1,1]{1,0:T(1,128)}) custom-call(f32[4,8,384]{2,1,0:T(8,128)S(1)} %all_to_all.16.in_ref), custom_call_target="tpu_custom_call" | custom-call | flops 1000000000 | bytes 8000000 | tf_op jit(solution)/shard_map/pallas_call | solution.py:702
  (6 shorter events, 0.1 us)
Async XLA Ops:
  12.6 10.1 %collective-permute-start = (f32[4,16,384]{2,1,0:T(8,128)S(1)}, f32[4,16,384]{2,1,0:T(8,128)S(1)}, u32[]{:S(2)}, u32[]{:S(2)}) collective-permute-start(f32[4,16,384]{2,1,0:T(8,128)S(1)} %bitcast.15), channel_id=1, source_target_pairs={{0,4},{4,8},{8,12},{12,16},{16,20},{20,24},{24,28},{28,32},{32,36}... | collective-permute-start | bytes 294920 | tf_op jit(solution)/shard_map/ppermute | solution.py:718
  35.0 27.3 %all-to-all-start = ((f32[64,27,1,128]{3,2,1,0:T(1,128)}), f32[64,27,1,128]{3,2,1,0:T(1,128)S(1)}, u32[]{:S(2)}, u32[]{:S(2)}) async-start(f32[64,27,1,128]{3,2,1,0:T(1,128)} %bitcast.5), calls=%async_computation | async-start | bytes 1769472 | tf_op jit(solution)/shard_map/all_to_all | solution.py:723
  99.7 5.0 %collective-permute-start.1 = (f32[4,8,384]{2,1,0:T(8,128)S(1)}, f32[4,8,384]{2,1,0:T(8,128)S(1)}, u32[]{:S(2)}, u32[]{:S(2)}) collective-permute-start(f32[4,8,384]{2,1,0:T(8,128)S(1)} %get-tuple-element.39), channel_id=1, source_target_pairs={{0,252},{4,0},{8,4},{12,8},{16,12},{20,16},{24,20},{28,24},{32,28}... | collective-permute-start | bytes 147464 | tf_op jit(solution)/shard_map/ppermute | solution.py:718

commit v9 on v8

--- a/solution.py
+++ b/solution.py
@@ -259,13 +259,7 @@
     column = lax.broadcasted_iota(jnp.int32, (1, LANES), 1)
     rows = slab * CY + jnp.minimum(column, CY)
     index = lax.broadcasted_iota(jnp.int32, (NX, LANES), 0)
-    residue = (
-        (index >= QUARTER).astype(jnp.int32)
-        + (index >= 2 * QUARTER).astype(jnp.int32)
-        + (index >= 3 * QUARTER).astype(jnp.int32)
-    )
-    mode_x = 4 * (index - QUARTER * residue) + residue
-    folds = jnp.where(mode_x < NX // 2, mode_x, mode_x - NX)
+    folds = folded_mode(index)
     ticks = folds * (shear_ref[0] * rows)
     whole = jnp.floor(ticks.astype(f32) * (1.0 / (NX * NY))).astype(jnp.int32)
     rest = ticks - whole * (NX * NY)
@@ -377,8 +371,8 @@
         grid_ref[...] = jnp.zeros_like(grid_ref)
     else:
         _, tables_ref, cos_ref, sin_ref, slab_atoms_ref, grid_ref, out_ref = refs[4:11]
-        results, kept = refs[11:14], refs[14:17]
-        table_ref, weights_ref, semaphores = refs[17:]
+        results, green_out_ref, kept = refs[11:14], refs[14], refs[15:18]
+        green_ref, table_ref, weights_ref, semaphores = refs[18:]
         table_copy = fetch(tables_ref, table_ref, semaphores.at[0])
     rows = list(range(CY)) if own else list(range(CY, 2 * CY - 1))
     part = CY * LANES
@@ -460,29 +454,80 @@
 
     @pl.when(where_ref[1] % 2 == 1)
     def _():
+        make_green(where_ref, green_ref)
+        green_copy = fetch(green_ref, green_out_ref, semaphores.at[3])
         for start, some_ref in ((0, slab_atoms_ref), (PENCILS * PAIRS, atoms_ref)):
             sampling_weights(
                 start, start == 0, where_ref, some_ref, weights_ref, base_ref, taps_ref, *kept
             )
         copies = [fetch(kept[n], results[n], semaphores.at[n]) for n in range(3)]
-        for copy in copies:
+        for copy in [green_copy, *copies]:
             copy.wait()
 
 
-def green_kernel(top_ref, norm_ref, mode_ref, out_ref):
+def spline_modulus(turns):
+    cosine, _ = unit_phase(turns)
+    return (64.0 + 52.0 * cosine + 4.0 * cosine * cosine) * (1.0 / 120.0)
+
+
+def folded_mode(row):
+    residue = (
+        (row >= QUARTER).astype(jnp.int32)
+        + (row >= 2 * QUARTER).astype(jnp.int32)
+        + (row >= 3 * QUARTER).astype(jnp.int32)
+    )
+    mode = 4 * (row - QUARTER * residue) + residue
+    return jnp.where(mode < NX // 2, mode, mode - NX)
+
+
+def make_green(where_ref, out_ref):
+    slab, pencil, shear = where_ref[0], where_ref[1], where_ref[3].astype(f32)
+    decay = (math.pi / screening) ** 2
+    column = lax.broadcasted_iota(jnp.int32, (1, LANES), 1)
+    own_x = folded_mode(jnp.minimum(column, PART_X) * SLABS + slab)
+    own_y = folded_mode(lax.broadcasted_iota(jnp.int32, (NY, LANES), 0))
+    float_x = own_x.astype(f32)
+    wave_y = own_y.astype(f32) + float_x * shear * (1.0 / NX)
+    part_x, part_y = float_x * (1.0 / NX), wave_y * (1.0 / NY)
+    norm = part_x * part_x + part_y * part_y
+    moduli = spline_modulus(part_x) * spline_modulus(part_y)
+    top = jnp.exp(-decay * norm) / (math.pi * moduli * moduli)
+    top = jnp.where((own_x == -(NX // 2)) | (own_y == -(NY // 2)), 0.0, top)
+    lane = jnp.where(column < HALF, column, column - HALF)
+    mode = pencil * PART_Z + lane
+    part_z = mode.astype(f32) * (1.0 / NZ)
+    modulus = spline_modulus(part_z)
+    norm_z = part_z * part_z
+    twice = jnp.where(mode == 0, 1.0, 2.0) * (1.0 / (NX * NY * NZ))
+    mode_top = jnp.where(
+        lane < PART_Z, twice * jnp.exp(-decay * norm_z) / (modulus * modulus), 0.0
+    )
+    mode_norm = jnp.where(lane < PART_Z, norm_z, 1.0)
     for j in range(PART_X):
-        square = norm_ref[:, j : j + 1] + mode_ref[1:2, :]
-        green = top_ref[:, j : j + 1] * mode_ref[0:1, :] / jnp.where(square == 0.0, 1.0, square)
+        square = norm[:, j : j + 1] + mode_norm
+        green = top[:, j : j + 1] * mode_top / jnp.where(square == 0.0, 1.0, square)
         out_ref[:, j * LANES : (j + 1) * LANES] = jnp.where(square == 0.0, 0.0, green)
 
 
+def green_kernel(where_ref, _, result_ref, green_ref, semaphore):
+    @pl.when(where_ref[1] % 2 == 0)
+    def _():
+        make_green(where_ref, green_ref)
+        fetch(green_ref, result_ref, semaphore).wait()
+
+
 def filter_kernel(
-    in_ref, tables_ref, backs_ref, green_ref, out_ref, table_ref, back_ref, semaphores
+    in_ref, tables_ref, backs_ref, greens_ref, out_ref, table_ref, back_ref, green_ref, semaphores
 ):
     copies = [
         fetch(tables_ref, table_ref, semaphores.at[0]),
         fetch(backs_ref, back_ref, semaphores.at[1]),
     ]
+    for first in range(0, PART_X, 2):
+        lanes = pl.ds(first * LANES, 2 * LANES)
+        copies.append(
+            fetch(greens_ref.at[:, lanes], green_ref.at[:, lanes], semaphores.at[2 + first // 2])
+        )
     sign = lane_sign((NY, LANES))
     energy = jnp.zeros((8, LANES), f32)
     blocks = []
@@ -503,6 +548,7 @@
             forward_line(table_ref, quarters_of(lines), quarters_of(swapped)), axis=0
         )
         modes = []
+        copies[2 + first // 2].wait()
         for n in range(2):
             j = first + n
             one = spectrum[:, n * LANES : (n + 1) * LANES]
@@ -672,18 +718,6 @@
     copy.wait()
 
 
-def spline_modulus(angles):
-    return (66.0 + 52.0 * jnp.cos(angles) + 2.0 * jnp.cos(2.0 * angles)) / 120.0
-
-
-def mode_of(row):
-    return 4 * (row % QUARTER) + row // QUARTER
-
-
-def folded(index, size):
-    return (index + size // 2) % size - size // 2
-
-
 SPACES = {"v": pltpu.VMEM, "h": pltpu.HBM, "s": pltpu.SMEM}
 WORK = {"flops": 1_000_000_000, "bytes_accessed": 8_000_000}
 
@@ -730,7 +764,7 @@
     x_forward, x_inverse, y_forward, y_inverse = wave_tables()
     shape = jax.ShapeDtypeStruct
     shift = jnp.where(slab_index == 0, shear_cells[0], 0)
-    where = jnp.stack([slab_index, pencil_index, shift])
+    where = jnp.stack([slab_index, pencil_index, shift, shear_cells[0]])
 
     mine, base, taps, cos_t, sin_t = call(
         prepare_kernel,
@@ -764,7 +798,6 @@
 
     packed = shape((SLABS * CARRIERS, LANES), f32)
     table_space = pltpu.VMEM((NX, 6 * QUARTER), bf16)
-    two = pltpu.SemaphoreType.DMA((2,))
     pairs = 2 * PENCILS * PAIRS
     held = [
         ((2, 2 * PADDED_Z, 3 * LANES), bf16),
@@ -780,46 +813,37 @@
         grid_shape,
         [weights_space],
     )(atoms, where, base, taps)
-    _, lines, *weights = call(
+    green_shape = pltpu.HBM((NY, PART_X * LANES), f32)
+    green_space = pltpu.VMEM((NY, PART_X * LANES), f32)
+    _, lines, *weights, green = call(
         lambda *refs: spread_kernel(False, *refs),
         "vsvvvhvvv",
-        (grid_shape, packed, *(pltpu.HBM((pairs, *dims), kind) for dims, kind in held)),
+        (
+            grid_shape,
+            packed,
+            *(pltpu.HBM((pairs, *dims), kind) for dims, kind in held),
+            green_shape,
+        ),
         [
             *(pltpu.VMEM((pairs, *dims), kind) for dims, kind in held),
+            green_space,
             table_space,
             weights_space,
             four,
         ],
         ((4, 0),),
     )(below_atoms, where, base, taps, slab_grid, x_forward, cos_t, sin_t, atoms)
-    lines, shear_cells = lax.optimization_barrier((lines, shear_cells))
-    shear_step = shear_cells[0]
-
-    own_x = folded(mode_of(jnp.arange(8, dtype=jnp.int32) * SLABS + slab_index), NX)[None, :]
-    own_y = folded(mode_of(jnp.arange(NY, dtype=jnp.int32)), NY)[:, None]
-    float_x = own_x.astype(f32)
-    wave_y = own_y.astype(f32) + float_x * shear_step.astype(f32) / NX
-    norm = (float_x / NX) ** 2 + (wave_y / NY) ** 2
-    moduli = spline_modulus(2.0 * math.pi * float_x / NX) * spline_modulus(
-        2.0 * math.pi * wave_y / NY
-    )
-    decay = (math.pi / screening) ** 2
-    top = jnp.exp(-decay * norm) / (math.pi * moduli * moduli)
-    top = jnp.where((own_x == -(NX // 2)) | (own_y == -(NY // 2)), 0.0, top)
-    lane = jnp.arange(LANES, dtype=jnp.int32) % HALF
-    mode_z = pencil_index * PART_Z + lane
-    kept = lane < PART_Z
-    float_z = mode_z.astype(f32)
-    norm_z = (float_z / NZ) ** 2
-    modulus_z = spline_modulus(2.0 * math.pi * float_z / NZ)
-    twice = jnp.where(mode_z == 0, 1.0, 2.0) / (NX * NY * NZ)
-    mode_top = jnp.where(kept, twice * jnp.exp(-decay * norm_z) / (modulus_z * modulus_z), 0.0)
-    mode_norm = jnp.where(kept, norm_z, 1.0)
-    mode = jnp.stack([mode_top, mode_norm])
-
-    green = call(green_kernel, "vvv", shape((NY, PART_X * LANES), f32))(top, norm, mode)
+    lines, where = lax.optimization_barrier((lines, where))
+    green = call(
+        green_kernel, "sh", green_shape, [green_space, pltpu.SemaphoreType.DMA], ((1, 0),)
+    )(where, green)
     lines = swap_slabs(lines)
-    filtered = call(filter_kernel, "vhhv", packed, [table_space, table_space, two])(
+    filtered = call(
+        filter_kernel,
+        "vhhh",
+        packed,
+        [table_space, table_space, green_space, pltpu.SemaphoreType.DMA((5,))],
+    )(
         lines, y_forward, y_inverse, green
     )
     filtered = swap_slabs(filtered)

time: 116 us -> 115 us (level)
  other arithmetic: 1.84 us -> 0.09 us
  Pallas kernels: 30.1 us -> 31.5 us
  blocking collectives: 47.6 us -> 46.2 us
    add x1 -> x0, other arithmetic: 1.49 us -> none  [on_device(): norm = (float_x / NX) ** 2 + (wave_y / NY) ** 2]
    pallas_call x8, Pallas kernels: 30.1 us -> 31.5 us  [run(): pl.pallas_call(kernel, out_shape=out_shape, in_specs=[pl.BlockSpec(memory...]
  transfers between devices with their start and end apart: 3 -> 3, of which waited for: 2 -> 2; matrix products, arithmetic and copies ran while one was open for 2% -> 0% of each run, Pallas kernels for 6% -> 6%
where the time goes in v9:
time: 115 us; the launch traced here: 114 us
  blocking collectives  46.2 us (40%)
  Pallas kernels  31.5 us (27%)
  waiting for transfers between devices  26.1 us (23%)
  starting transfers between devices  9.01 us (8%)
  between operations  1.52 us (1%)
    pallas_call x8, Pallas kernels, run(): pl.pallas_call(kernel, out_shape=out_shape, in_specs=[pl.BlockSpec(memory...  31.5 us
    all_to_all x1, blocking collectives, swap_slabs(): lines = lax.all_to_all(lines, 'gy', split_axis=0, concat_axis=0, tiled=True)  27.5 us
    all_to_all x1, waiting for transfers between devices, swap_slabs(): lines = lax.all_to_all(lines, 'gy', split_axis=0, concat_axis=0, tiled=True)  19.3 us
    all_gather x1, blocking collectives, on_device(): atoms = lax.all_gather(mine, 'gx', axis=0, tiled=False)  9.91 us
    all_to_all x1, blocking collectives, on_device(): lax.all_to_all(shares + below_shares, 'gx', split_axis=0, concat_axis=0,...  8.8 us
    ppermute x2, waiting for transfers between devices, next_slab(): lax.ppermute(value, 'gy', [(i, (i + step) % SLABS) for i in range(SLABS)])  6.78 us
    all_to_all x1, starting transfers between devices, swap_slabs(): lines = lax.all_to_all(lines, 'gy', split_axis=0, concat_axis=0, tiled=True)  6.26 us
    ppermute x2, starting transfers between devices, next_slab(): lax.ppermute(value, 'gy', [(i, (i + step) % SLABS) for i in range(SLABS)])  2.75 us
  transfers between devices with their start and end apart: 3, of which 2 were waited for; matrix products, arithmetic and copies ran while one was open for 0% of the time, Pallas kernels for 6%

profile of v9, /device:TPU:1, one launch (start us, length us, event | category | flops | bytes accessed | tf_op | source)
XLA Modules:
  0.0 114.4 jit_solution(8770103046866664753)
XLA Ops:
  1.3 0.1 pad_add_fusion.where_ref.refs_1_
  1.4 1.3 %shard_map.129 = (f32[16,384]{1,0:T(8,128)S(1)}, f32[8,128]{1,0:T(8,128)S(1)}, f32[12,48,128]{2,1,0:T(8,128)S(1)}, f32[384,128]{1,0:T(8,128)S(1)}, f32[384,128]{1,0:T(8,128)S(1)}) custom-call(s32[4]{0:T(128)S(1)} %pad_add_fusion.where_ref.refs_1_, s32[1]{0:T(128)} %copy.20.shear_ref, s32[6]{0:T(128)} %counts_ref.1, s32[3,384]{1,0:T(4,128)} %cells_ref.1, ...), custom_call_target="tpu_custom_call" | custom-call | flops 1000000000 | bytes 8000000 | tf_op jit(solution)/shard_map/pallas_call | solution.py:736
  2.7 9.9 %all-gather = f32[64,384]{1,0:T(8,128)S(1)} all-gather(f32[16,384]{1,0:T(8,128)S(1)} %get-tuple-element.25), channel_id=2, replica_groups=mesh['gy'=64,'gx'=4] {'gx'}, dimensions={0}, use_global_device_ids=true | all-gather | bytes 122880 | tf_op jit(solution)/shard_map/all_gather | solution.py:796
  12.6 0.0 collective-permute-start
  12.6 3.4 %shard_map.130.refs_4_ = f32[432,1536]{1,0:T(8,128)S(1)} custom-call(f32[4,16,384]{2,1,0:T(8,128)S(1)} %bitcast.15, s32[4]{0:T(128)S(1)} %pad_add_fusion.where_ref.refs_1_, f32[8,128]{1,0:T(8,128)S(1)} %get-tuple-element.26.refs_2_, f32[12,48,128]{2,1,0:T(8,128)S(1)} %get-tuple-element.27.refs_3_), custom_call_target="tpu_custom_call" | custom-call | flops 1000000000 | bytes 8000000 | tf_op jit(solution)/shard_map/pallas_call | solution.py:736
  16.0 6.8 %collective-permute-done.refs_0_ = f32[4,16,384]{2,1,0:T(8,128)S(1)} collective-permute-done((f32[4,16,384]{2,1,0:T(8,128)S(1)}, f32[4,16,384]{2,1,0:T(8,128)S(1)}, u32[]{:S(2)}, u32[]{:S(2)}) %collective-permute-start) | collective-permute-done | bytes 98336 | tf_op jit(solution)/shard_map/ppermute | solution.py:752
  22.8 13.2 %shard_map.131 = (f32[432,1536]{1,0:T(8,128)S(1)}, f32[1728,128]{1,0:T(8,128)}, bf16[24,2,96,384]{3,2,1,0:T(8,128)(2,1)}, f32[24,3,48,128]{3,2,1,0:T(8,128)}, f3...) custom-call(f32[4,16,384]{2,1,0:T(8,128)S(1)} %collective-permute-done.refs_0_, ...), custom_call_target="tpu_custom_call", output_to_operand_aliasing={{0}: (4, {})} | custom-call | flops 1000000000 | bytes 8000000 | tf_op jit(solution)/shard_map/pallas_call | solution.py:736
  36.0 6.3 %all-to-all-start = ((f32[64,27,1,128]{3,2,1,0:T(1,128)}), f32[64,27,1,128]{3,2,1,0:T(1,128)S(1)}, u32[]{:S(2)}, u32[]{:S(2)}) async-start(f32[64,27,1,128]{3,2,1,0:T(1,128)} %bitcast.5), calls=%async_computation | async-start | bytes 1769472 | tf_op jit(solution)/shard_map/all_to_all | solution.py:757
  42.3 0.7 shard_map.132.greens_ref
  43.0 19.3 %all-to-all-done = f32[64,27,1,128]{3,2,1,0:T(1,128)S(1)} async-done(((f32[64,27,1,128]{3,2,1,0:T(1,128)}), f32[64,27,1,128]{3,2,1,0:T(1,128)S(1)}, u32[]{:S(2)}, u32[]{:S(2)}) %all-to-all-start) | async-done | bytes 884768 | tf_op jit(solution)/shard_map/all_to_all | solution.py:757
  62.3 3.7 %shard_map.133 = f32[1728,128]{1,0:T(8,128)S(1)} custom-call(f32[1728,128]{1,0:T(8,128)S(1)} %bitcast.11, bf16[384,576]{1,0:T(8,128)(2,1)} %constant.20.clone.tables_ref, bf16[384,576]{1,0:T(8,128)(2,1)} %constant.21.clone.backs_ref, f32[384,768]{1,0:T(8,128)} %shard_map.132.greens_ref), custom_call_target="tpu_custom_call" | custom-call | flops 1000000000 | bytes 8000000 | tf_op jit(solution)/shard_map/pallas_call | solution.py:736
  66.1 27.5 %all_to_all.15 = f32[64,27,1,128]{3,2,1,0:T(1,128)S(1)} all-to-all(f32[64,27,1,128]{3,2,1,0:T(1,128)S(1)} %bitcast.12), channel_id=1, replica_groups=mesh['gy'=64,'gx'=4] {'gy'}, dimensions={0} | all-to-all | bytes 1769472 | tf_op jit(solution)/shard_map/all_to_all | solution.py:757
  93.6 5.4 %shard_map.134 = (f32[4,8,384]{2,1,0:T(8,128)S(1)}, f32[432,768]{1,0:T(8,128)S(1)}, bf16[12,2,96,384]{3,2,1,0:T(8,128)(2,1)S(1)}, f32[12,3,48,128]{3,2,1,0:T(8,128)S(1)}, f32[12,3,16,128]{3,2,1,0:T(8,128)S(1)}) custom-call(f32[4,16,384]{2,1,0:T(8,128)S(1)} %collective-permute-done.refs_0_, s32[4]{0:T(128)S(1)} %pad_add_fusion.where_ref.refs_1_, ...), custom_call_target="tpu_custom_call" | custom-call | flops 1000000000 | bytes 8000000 | tf_op jit(solution)/shard_map/pallas_call | solution.py:736
  99.0 2.8 %collective-permute-start.1 = (f32[4,8,384]{2,1,0:T(8,128)S(1)}, f32[4,8,384]{2,1,0:T(8,128)S(1)}, u32[]{:S(2)}, u32[]{:S(2)}) collective-permute-start(f32[4,8,384]{2,1,0:T(8,128)S(1)} %get-tuple-element.41), channel_id=1, source_target_pairs={{0,252},{4,0},{8,4},{12,8},{16,12},{20,16},{24,20},{28,24},{32,28}... | collective-permute-start | bytes 147464 | tf_op jit(solution)/shard_map/ppermute | solution.py:752
  101.7 2.5 %shard_map.135 = f32[4,8,384]{2,1,0:T(8,128)S(1)} custom-call(f32[4,16,384]{2,1,0:T(8,128)S(1)} %bitcast.18, s32[4]{0:T(128)S(1)} %pad_add_fusion.where_ref.refs_1_, bf16[12,2,96,384]{3,2,1,0:T(8,128)(2,1)S(1)} %get-tuple-element.37.refs_2_, f32[12,3,48,128]{3,2,1,0:T(8,128)S(1)} %get-tuple-element.38.refs_3_, ...), custom_call_target="tpu_custom_call" | custom-call | flops 1000000000 | bytes 8000000 | tf_op jit(solution)/shard_map/pallas_call | solution.py:736
  104.2 0.0 collective-permute-done.1
  104.2 8.8 %all_to_all.16.in_ref = f32[4,8,384]{2,1,0:T(8,128)S(1)} all-to-all(f32[4,8,384]{2,1,0:T(8,128)S(1)} %add.3), channel_id=1, replica_groups=mesh['gy'=64,'gx'=4] {'gx'}, dimensions={0} | all-to-all | bytes 98304 | tf_op jit(solution)/shard_map/all_to_all | solution.py:870
  113.0 1.2 %shard_map.136 = (f32[384]{0:T(512)}, f32[3,384]{1,0:T(4,128)}, f32[3,384]{1,0:T(4,128)}, f32[1,1]{1,0:T(1,128)}) custom-call(f32[4,8,384]{2,1,0:T(8,128)S(1)} %all_to_all.16.in_ref), custom_call_target="tpu_custom_call" | custom-call | flops 1000000000 | bytes 8000000 | tf_op jit(solution)/shard_map/pallas_call | solution.py:736
  (1 shorter events, 0.0 us)
Async XLA Ops:
  12.6 10.1 %collective-permute-start = (f32[4,16,384]{2,1,0:T(8,128)S(1)}, f32[4,16,384]{2,1,0:T(8,128)S(1)}, u32[]{:S(2)}, u32[]{:S(2)}) collective-permute-start(f32[4,16,384]{2,1,0:T(8,128)S(1)} %bitcast.14), channel_id=1, source_target_pairs={{0,4},{4,8},{8,12},{12,16},{16,20},{20,24},{24,28},{28,32},{32,36}... | collective-permute-start | bytes 294920 | tf_op jit(solution)/shard_map/ppermute | solution.py:752
  36.0 26.3 %all-to-all-start = ((f32[64,27,1,128]{3,2,1,0:T(1,128)}), f32[64,27,1,128]{3,2,1,0:T(1,128)S(1)}, u32[]{:S(2)}, u32[]{:S(2)}) async-start(f32[64,27,1,128]{3,2,1,0:T(1,128)} %bitcast.5), calls=%async_computation | async-start | bytes 1769472 | tf_op jit(solution)/shard_map/all_to_all | solution.py:757
  99.0 5.2 %collective-permute-start.1 = (f32[4,8,384]{2,1,0:T(8,128)S(1)}, f32[4,8,384]{2,1,0:T(8,128)S(1)}, u32[]{:S(2)}, u32[]{:S(2)}) collective-permute-start(f32[4,8,384]{2,1,0:T(8,128)S(1)} %get-tuple-element.41), channel_id=1, source_target_pairs={{0,252},{4,0},{8,4},{12,8},{16,12},{20,16},{24,20},{28,24},{32,28}... | collective-permute-start | bytes 147464 | tf_op jit(solution)/shard_map/ppermute | solution.py:752

commit v10 on v9

--- a/solution.py
+++ b/solution.py
@@ -112,6 +112,25 @@
     return cos_out, sin_out
 
 
+class Twist:
+    def __init__(self, cos_ref, sin_ref):
+        whole = (NX, LANES)
+        self.cos = jnp.broadcast_to(cos_ref[:, 0:1], whole)
+        self.sin = jnp.broadcast_to(sin_ref[:, 0:1], whole)
+        self.cos_step = jnp.broadcast_to(cos_ref[:, CY : CY + 1], whole)
+        self.sin_step = jnp.broadcast_to(sin_ref[:, CY : CY + 1], whole)
+        self.row = 0
+
+    def at(self, row):
+        while self.row < row:
+            self.cos, self.sin = (
+                self.cos * self.cos_step - self.sin * self.sin_step,
+                self.sin * self.cos_step + self.cos * self.sin_step,
+            )
+            self.row += 1
+        return self.cos, self.sin
+
+
 def halves(value):
     high = value.astype(bf16)
     return high, (value - high.astype(f32)).astype(bf16)
@@ -257,7 +276,7 @@
         taps_ref[t] = jnp.where(row < PART_Z, cos_t, 0.0)
         taps_ref[6 + t] = jnp.where(row < PART_Z, sin_t, 0.0)
     column = lax.broadcasted_iota(jnp.int32, (1, LANES), 1)
-    rows = slab * CY + jnp.minimum(column, CY)
+    rows = jnp.where(column < CY, slab * CY + column, 1)
     index = lax.broadcasted_iota(jnp.int32, (NX, LANES), 0)
     folds = folded_mode(index)
     ticks = folds * (shear_ref[0] * rows)
@@ -425,12 +444,13 @@
             grid_ref[at, part + n * LANES : part + (n + 1) * LANES] += piece[:, LANES:]
         return carry
 
-    lax.fori_loop(0, PENCILS * PAIRS, pair_body, 0, unroll=6)
+    lax.fori_loop(0, PENCILS * PAIRS, pair_body, 0, unroll=12)
     if own:
         return
     grid_ref[0:WIDE] += grid_ref[NX:EXTENDED]
     table_copy.wait()
     sign = lane_sign((NX, LANES))
+    twist = Twist(cos_ref, sin_ref)
     totals = []
     for first in range(0, CY, 2):
         lanes = slice(first * LANES, (first + 2) * LANES)
@@ -443,7 +463,8 @@
         )
         for n, y in enumerate((first, first + 1)):
             one = line[:, n * LANES : (n + 1) * LANES]
-            totals.append(one * cos_ref[:, y : y + 1] + turned(one, sign) * sin_ref[:, y : y + 1])
+            cos_y, sin_y = twist.at(y)
+            totals.append(one * cos_y + turned(one, sign) * sin_y)
     for group in range(GROUPS):
         blocks = []
         for block in range(4 * group, 4 * group + 4):
@@ -620,12 +641,13 @@
     energy = 0.0
     if not own:
         sign = lane_sign((NX, LANES))
+        twist = Twist(cos_ref, sin_ref)
         for first in range(0, CY, 2):
             modes, swapped = [], []
             for y in range(first, first + 2):
                 line = jnp.concatenate([block_at(in_ref, j, y) for j in range(PART_X)], axis=0)
                 other = turned(line, sign)
-                cos_y, sin_y = cos_ref[:, y : y + 1], sin_ref[:, y : y + 1]
+                cos_y, sin_y = twist.at(y)
                 modes.append(line * cos_y - other * sin_y)
                 swapped.append(other * cos_y + line * sin_y)
             swapped = jnp.concatenate(swapped, axis=1)
@@ -696,10 +718,11 @@
             charge * s001 + dip_x * s101 + dip_y * s011 + dip_z * sampled(0, 0, 2),
             jnp.full(live.shape, energy, f32),
         ]
-        out_ref[pencil, :, lanes] = jnp.concatenate(out, axis=0)
+        ahead = lax.rem(pencil - where_ref[1] + PENCILS, PENCILS)
+        out_ref[ahead, :, lanes] = jnp.concatenate(out, axis=0)
         return carry
 
-    lax.fori_loop(0, PENCILS * PAIRS, pair_body, 0, unroll=6)
+    lax.fori_loop(0, PENCILS * PAIRS, pair_body, 0, unroll=12)
     if not own:
 
         @pl.when(jnp.logical_not(later))
@@ -708,8 +731,11 @@
                 copy.wait()
 
 
-def finish_kernel(in_ref, charge_ref, dipole_ref, position_ref, energy_ref, row_ref, semaphore):
-    total = (in_ref[0] + in_ref[1]) + (in_ref[2] + in_ref[3])
+def finish_kernel(
+    own_ref, one_ref, two_ref, three_ref, charge_ref, dipole_ref, position_ref, energy_ref,
+    row_ref, semaphore
+):
+    total = (own_ref[...] + one_ref[...]) + (two_ref[...] + three_ref[...])
     row_ref[...] = total[0:1]
     copy = fetch(row_ref.at[0], charge_ref, semaphore)
     dipole_ref[...] = total[1:4]
@@ -867,10 +893,14 @@
     shares = call(lambda *refs: sample_kernel(True, *refs), "vsvvvv", shares_shape)(
         atoms, where, *weights, potential
     )
-    shares = lax.all_to_all(shares + below_shares, "gx", split_axis=0, concat_axis=0, tiled=True)
+    shares = shares + below_shares
+    arrived = [
+        lax.ppermute(shares[ahead], "gx", [(i, (i + ahead) % PENCILS) for i in range(PENCILS)])
+        for ahead in range(1, PENCILS)
+    ]
     charge_grad, dipole_grad, position_grad, energy = call(
         finish_kernel,
-        "v",
+        "vvvv",
         (
             pltpu.HBM((ATOM_DEV,), f32),
             shape((3, ATOM_DEV), f32),
@@ -878,7 +908,7 @@
             shape((1, 1), f32),
         ),
         [pltpu.VMEM((1, ATOM_DEV), f32), pltpu.SemaphoreType.DMA],
-    )(shares)
+    )(shares[0], *arrived)
     return charge_grad, dipole_grad, position_grad, energy[0]
 
 

time: 115 us -> 112 us (0.974)
  blocking collectives: 46.2 us -> 37.4 us
  starting transfers between devices: 9.01 us -> 15.1 us
  Pallas kernels: 31.5 us -> 30.2 us
    all_to_all x1 -> x0, blocking collectives: 8.8 us -> none  [on_device(): lax.all_to_all(shares + below_shares, 'gx', split_axis=0, concat_axis=0,...]
    ppermute x0 -> x3, starting transfers between devices: none -> 6.12 us  [on_device(): lax.ppermute(shares[ahead], 'gx', [(i, (i + ahead) % PENCILS) for i in ra...]
    pallas_call x8, Pallas kernels: 31.5 us -> 30.2 us  [run(): pl.pallas_call(kernel, out_shape=out_shape, in_specs=[pl.BlockSpec(memory...]
  transfers between devices with their start and end apart: 3 -> 6, of which waited for: 2 -> 3; matrix products, arithmetic and copies ran while one was open for 0% -> 0% of each run, Pallas kernels for 6% -> 6%
where the time goes in v10:
time: 112 us; the launch traced here: 111 us
  blocking collectives  37.4 us (33%)
  Pallas kernels  30.2 us (27%)
  waiting for transfers between devices  27 us (24%)
  starting transfers between devices  15.1 us (13%)
  between operations  1.54 us (1%)
    pallas_call x8, Pallas kernels, run(): pl.pallas_call(kernel, out_shape=out_shape, in_specs=[pl.BlockSpec(memory...  30.2 us
    all_to_all x1, blocking collectives, swap_slabs(): lines = lax.all_to_all(lines, 'gy', split_axis=0, concat_axis=0, tiled=True)  27.5 us
    all_to_all x1, waiting for transfers between devices, swap_slabs(): lines = lax.all_to_all(lines, 'gy', split_axis=0, concat_axis=0, tiled=True)  19.3 us
    all_gather x1, blocking collectives, on_device(): atoms = lax.all_gather(mine, 'gx', axis=0, tiled=False)  9.91 us
    ppermute x2, waiting for transfers between devices, next_slab(): lax.ppermute(value, 'gy', [(i, (i + step) % SLABS) for i in range(SLABS)])  6.93 us
    all_to_all x1, starting transfers between devices, swap_slabs(): lines = lax.all_to_all(lines, 'gy', split_axis=0, concat_axis=0, tiled=True)  6.23 us
    ppermute x3, starting transfers between devices, on_device(): lax.ppermute(shares[ahead], 'gx', [(i, (i + ahead) % PENCILS) for i in ra...  6.12 us
    ppermute x2, starting transfers between devices, next_slab(): lax.ppermute(value, 'gy', [(i, (i + step) % SLABS) for i in range(SLABS)])  2.77 us
  transfers between devices with their start and end apart: 6, of which 3 were waited for; matrix products, arithmetic and copies ran while one was open for 0% of the time, Pallas kernels for 6%

profile of v10, /device:TPU:1, one launch (start us, length us, event | category | flops | bytes accessed | tf_op | source)
XLA Modules:
  0.0 111.4 jit_solution(1537109252462202835)
XLA Ops:
  1.3 0.1 pad_add_fusion.where_ref.refs_1_
  1.4 1.3 %shard_map.129 = (f32[16,384]{1,0:T(8,128)S(1)}, f32[8,128]{1,0:T(8,128)S(1)}, f32[12,48,128]{2,1,0:T(8,128)S(1)}, f32[384,128]{1,0:T(8,128)S(1)}, f32[384,128]{1,0:T(8,128)S(1)}) custom-call(s32[4]{0:T(128)S(1)} %pad_add_fusion.where_ref.refs_1_, s32[1]{0:T(128)} %copy.20.shear_ref, s32[6]{0:T(128)} %counts_ref.1, s32[3,384]{1,0:T(4,128)} %cells_ref.1, ...), custom_call_target="tpu_custom_call" | custom-call | flops 1000000000 | bytes 8000000 | tf_op jit(solution)/shard_map/pallas_call | solution.py:762
  2.7 9.9 %all-gather = f32[64,384]{1,0:T(8,128)S(1)} all-gather(f32[16,384]{1,0:T(8,128)S(1)} %get-tuple-element.25), channel_id=2, replica_groups=mesh['gy'=64,'gx'=4] {'gx'}, dimensions={0}, use_global_device_ids=true | all-gather | bytes 122880 | tf_op jit(solution)/shard_map/all_gather | solution.py:822
  12.6 0.0 collective-permute-start
  12.6 3.2 %shard_map.130.refs_4_ = f32[432,1536]{1,0:T(8,128)S(1)} custom-call(f32[4,16,384]{2,1,0:T(8,128)S(1)} %bitcast.23, s32[4]{0:T(128)S(1)} %pad_add_fusion.where_ref.refs_1_, f32[8,128]{1,0:T(8,128)S(1)} %get-tuple-element.26.refs_2_, f32[12,48,128]{2,1,0:T(8,128)S(1)} %get-tuple-element.27.refs_3_), custom_call_target="tpu_custom_call" | custom-call | flops 1000000000 | bytes 8000000 | tf_op jit(solution)/shard_map/pallas_call | solution.py:762
  15.8 6.9 %collective-permute-done.refs_0_ = f32[4,16,384]{2,1,0:T(8,128)S(1)} collective-permute-done((f32[4,16,384]{2,1,0:T(8,128)S(1)}, f32[4,16,384]{2,1,0:T(8,128)S(1)}, u32[]{:S(2)}, u32[]{:S(2)}) %collective-permute-start) | collective-permute-done | bytes 98336 | tf_op jit(solution)/shard_map/ppermute | solution.py:778
  22.8 13.2 %shard_map.131 = (f32[432,1536]{1,0:T(8,128)S(1)}, f32[1728,128]{1,0:T(8,128)}, bf16[24,2,96,384]{3,2,1,0:T(8,128)(2,1)}, f32[24,3,48,128]{3,2,1,0:T(8,128)}, f3...) custom-call(f32[4,16,384]{2,1,0:T(8,128)S(1)} %collective-permute-done.refs_0_, ...), custom_call_target="tpu_custom_call", output_to_operand_aliasing={{0}: (4, {})} | custom-call | flops 1000000000 | bytes 8000000 | tf_op jit(solution)/shard_map/pallas_call | solution.py:762
  35.9 6.2 %all-to-all-start = ((f32[64,27,1,128]{3,2,1,0:T(1,128)}), f32[64,27,1,128]{3,2,1,0:T(1,128)S(1)}, u32[]{:S(2)}, u32[]{:S(2)}) async-start(f32[64,27,1,128]{3,2,1,0:T(1,128)} %bitcast.5), calls=%async_computation | async-start | bytes 1769472 | tf_op jit(solution)/shard_map/all_to_all | solution.py:783
  42.2 0.7 shard_map.132.greens_ref
  42.9 19.3 %all-to-all-done = f32[64,27,1,128]{3,2,1,0:T(1,128)S(1)} async-done(((f32[64,27,1,128]{3,2,1,0:T(1,128)}), f32[64,27,1,128]{3,2,1,0:T(1,128)S(1)}, u32[]{:S(2)}, u32[]{:S(2)}) %all-to-all-start) | async-done | bytes 884768 | tf_op jit(solution)/shard_map/all_to_all | solution.py:783
  62.2 3.7 %shard_map.133 = f32[1728,128]{1,0:T(8,128)S(1)} custom-call(f32[1728,128]{1,0:T(8,128)S(1)} %bitcast.19, bf16[384,576]{1,0:T(8,128)(2,1)} %constant.20.clone.tables_ref, bf16[384,576]{1,0:T(8,128)(2,1)} %constant.21.clone.backs_ref, f32[384,768]{1,0:T(8,128)} %shard_map.132.greens_ref), custom_call_target="tpu_custom_call" | custom-call | flops 1000000000 | bytes 8000000 | tf_op jit(solution)/shard_map/pallas_call | solution.py:762
  65.9 27.5 %all_to_all.10 = f32[64,27,1,128]{3,2,1,0:T(1,128)S(1)} all-to-all(f32[64,27,1,128]{3,2,1,0:T(1,128)S(1)} %bitcast.20), channel_id=1, replica_groups=mesh['gy'=64,'gx'=4] {'gy'}, dimensions={0} | all-to-all | bytes 1769472 | tf_op jit(solution)/shard_map/all_to_all | solution.py:783
  93.5 4.6 %shard_map.134 = (f32[4,8,384]{2,1,0:T(8,128)S(1)}, f32[432,768]{1,0:T(8,128)S(1)}, bf16[12,2,96,384]{3,2,1,0:T(8,128)(2,1)S(1)}, f32[12,3,48,128]{3,2,1,0:T(8,128)S(1)}, f32[12,3,16,128]{3,2,1,0:T(8,128)S(1)}) custom-call(f32[4,16,384]{2,1,0:T(8,128)S(1)} %collective-permute-done.refs_0_, s32[4]{0:T(128)S(1)} %pad_add_fusion.where_ref.refs_1_, ...), custom_call_target="tpu_custom_call" | custom-call | flops 1000000000 | bytes 8000000 | tf_op jit(solution)/shard_map/pallas_call | solution.py:762
  98.0 2.8 %collective-permute-start.1 = (f32[4,8,384]{2,1,0:T(8,128)S(1)}, f32[4,8,384]{2,1,0:T(8,128)S(1)}, u32[]{:S(2)}, u32[]{:S(2)}) collective-permute-start(f32[4,8,384]{2,1,0:T(8,128)S(1)} %get-tuple-element.41), channel_id=1, source_target_pairs={{0,252},{4,0},{8,4},{12,8},{16,12},{20,16},{24,20},{28,24},{32,28}... | collective-permute-start | bytes 147464 | tf_op jit(solution)/shard_map/ppermute | solution.py:778
  100.8 2.3 %shard_map.135 = f32[4,8,384]{2,1,0:T(8,128)S(1)} custom-call(f32[4,16,384]{2,1,0:T(8,128)S(1)} %bitcast.26, s32[4]{0:T(128)S(1)} %pad_add_fusion.where_ref.refs_1_, bf16[12,2,96,384]{3,2,1,0:T(8,128)(2,1)S(1)} %get-tuple-element.37.refs_2_, f32[12,3,48,128]{3,2,1,0:T(8,128)S(1)} %get-tuple-element.38.refs_3_, ...), custom_call_target="tpu_custom_call" | custom-call | flops 1000000000 | bytes 8000000 | tf_op jit(solution)/shard_map/pallas_call | solution.py:762
  103.1 0.0 collective-permute-done.1
  103.1 0.1 collective-permute-start.4
  103.2 2.6 %collective-permute-start.3 = (f32[8,384]{1,0:T(8,128)S(1)}, f32[8,384]{1,0:T(8,128)S(1)}, u32[]{:S(2)}, u32[]{:S(2)}) collective-permute-start(f32[8,384]{1,0:T(8,128)S(1)} %get-tuple-element.47), channel_id=1, source_target_pairs={{0,2},{1,3},{2,0},{3,1},{4,6},{5,7},{6,4},{7,5},{8,10},{9,11},{10,... | collective-permute-start | bytes 36872 | tf_op jit(solution)/shard_map/ppermute | solution.py:898
  105.8 3.4 %collective-permute-start.2 = (f32[8,384]{1,0:T(8,128)S(1)}, f32[8,384]{1,0:T(8,128)S(1)}, u32[]{:S(2)}, u32[]{:S(2)}) collective-permute-start(f32[8,384]{1,0:T(8,128)S(1)} %get-tuple-element.48), channel_id=1, source_target_pairs={{0,1},{1,2},{2,3},{3,0},{4,5},{5,6},{6,7},{7,4},{8,9},{9,10},{10,1... | collective-permute-start | bytes 36872 | tf_op jit(solution)/shard_map/ppermute | solution.py:898
  109.3 0.0 collective-permute-done.4.three_ref
  109.3 0.0 collective-permute-done.3.two_ref
  109.3 0.8 collective-permute-done.2.one_ref
  110.1 1.2 %shard_map.136 = (f32[384]{0:T(512)}, f32[3,384]{1,0:T(4,128)}, f32[3,384]{1,0:T(4,128)}, f32[1,1]{1,0:T(1,128)}) custom-call(f32[8,384]{1,0:T(8,128)S(1)} %get-tuple-element.49.own_ref, f32[8,384]{1,0:T(8,128)S(1)} %collective-permute-done.2.one_ref, f32[8,384]{1,0:T(8,128)S(1)} %collective-permute-done.3.two_ref, f32[8,384]{1,0:T(8,128)S(1)} %collective-permute-done.4.three_ref), custom_call_target="tpu_custom_call" | custom-call | flops 1000000000 | bytes 8000000 | tf_op jit(solution)/shard_map/pallas_call | solution.py:762
  (2 shorter events, 0.0 us)
Async XLA Ops:
  12.6 10.1 %collective-permute-start = (f32[4,16,384]{2,1,0:T(8,128)S(1)}, f32[4,16,384]{2,1,0:T(8,128)S(1)}, u32[]{:S(2)}, u32[]{:S(2)}) collective-permute-start(f32[4,16,384]{2,1,0:T(8,128)S(1)} %bitcast.22), channel_id=1, source_target_pairs={{0,4},{4,8},{8,12},{12,16},{16,20},{20,24},{24,28},{28,32},{32,36}... | collective-permute-start | bytes 294920 | tf_op jit(solution)/shard_map/ppermute | solution.py:778
  35.9 26.2 %all-to-all-start = ((f32[64,27,1,128]{3,2,1,0:T(1,128)}), f32[64,27,1,128]{3,2,1,0:T(1,128)S(1)}, u32[]{:S(2)}, u32[]{:S(2)}) async-start(f32[64,27,1,128]{3,2,1,0:T(1,128)} %bitcast.5), calls=%async_computation | async-start | bytes 1769472 | tf_op jit(solution)/shard_map/all_to_all | solution.py:783
  98.0 5.1 %collective-permute-start.1 = (f32[4,8,384]{2,1,0:T(8,128)S(1)}, f32[4,8,384]{2,1,0:T(8,128)S(1)}, u32[]{:S(2)}, u32[]{:S(2)}) collective-permute-start(f32[4,8,384]{2,1,0:T(8,128)S(1)} %get-tuple-element.41), channel_id=1, source_target_pairs={{0,252},{4,0},{8,4},{12,8},{16,12},{20,16},{24,20},{28,24},{32,28}... | collective-permute-start | bytes 147464 | tf_op jit(solution)/shard_map/ppermute | solution.py:778
  103.1 6.1 %collective-permute-start.4 = (f32[8,384]{1,0:T(8,128)S(1)}, f32[8,384]{1,0:T(8,128)S(1)}, u32[]{:S(2)}, u32[]{:S(2)}) collective-permute-start(f32[8,384]{1,0:T(8,128)S(1)} %get-tuple-element.46), channel_id=1, source_target_pairs={{0,3},{1,0},{2,1},{3,2},{4,7},{5,4},{6,5},{7,6},{8,11},{9,8},{10,9... | collective-permute-start | bytes 36872 | tf_op jit(solution)/shard_map/ppermute | solution.py:898
  103.2 6.0 %collective-permute-start.3 = (f32[8,384]{1,0:T(8,128)S(1)}, f32[8,384]{1,0:T(8,128)S(1)}, u32[]{:S(2)}, u32[]{:S(2)}) collective-permute-start(f32[8,384]{1,0:T(8,128)S(1)} %get-tuple-element.47), channel_id=1, source_target_pairs={{0,2},{1,3},{2,0},{3,1},{4,6},{5,7},{6,4},{7,5},{8,10},{9,11},{10,... | collective-permute-start | bytes 36872 | tf_op jit(solution)/shard_map/ppermute | solution.py:898
  105.8 4.3 %collective-permute-start.2 = (f32[8,384]{1,0:T(8,128)S(1)}, f32[8,384]{1,0:T(8,128)S(1)}, u32[]{:S(2)}, u32[]{:S(2)}) collective-permute-start(f32[8,384]{1,0:T(8,128)S(1)} %get-tuple-element.48), channel_id=1, source_target_pairs={{0,1},{1,2},{2,3},{3,0},{4,5},{5,6},{6,7},{7,4},{8,9},{9,10},{10,1... | collective-permute-start | bytes 36872 | tf_op jit(solution)/shard_map/ppermute | solution.py:898

commit v11 on v10

--- a/solution.py
+++ b/solution.py
@@ -271,10 +271,10 @@
     row = lax.broadcasted_iota(jnp.int32, (PADDED_Z, LANES), 0)
     mode = (row + first).astype(f32)
     base_ref[...] = mode[:8]
-    for t in range(6):
-        cos_t, sin_t = unit_phase(mode * float(t) * (1.0 / NZ))
+    for t in range(3):
+        cos_t, sin_t = unit_phase(mode * (t + 0.5) * (1.0 / NZ))
         taps_ref[t] = jnp.where(row < PART_Z, cos_t, 0.0)
-        taps_ref[6 + t] = jnp.where(row < PART_Z, sin_t, 0.0)
+        taps_ref[3 + t] = jnp.where(row < PART_Z, sin_t, 0.0)
     column = lax.broadcasted_iota(jnp.int32, (1, LANES), 1)
     rows = jnp.where(column < CY, slab * CY + column, 1)
     index = lax.broadcasted_iota(jnp.int32, (NX, LANES), 0)
@@ -333,21 +333,29 @@
 
 
 def z_waves(cell_z, weights, base_ref, taps_ref):
-    turn = base_ref[...] * cell_z
+    centre = cell_z + 2.5
+    turn = base_ref[...] * centre
     turn = turn - 360.0 * jnp.floor(turn * (1.0 / 360.0))
     cos_k, sin_k = unit_phase(turn * (1.0 / 360.0))
-    turn = 8.0 * cell_z
+    turn = 8.0 * centre
     turn = turn - 360.0 * jnp.floor(turn * (1.0 / 360.0))
     cos_8, sin_8 = unit_phase(jnp.broadcast_to(turn * (1.0 / 360.0), cos_k.shape))
+    folded = [
+        (
+            [weight[2 - t] + weight[3 + t] for t in range(3)],
+            [weight[3 + t] - weight[2 - t] for t in range(3)],
+        )
+        for weight in weights
+    ]
     pieces = [[] for _ in weights]
     pieces_im = [[] for _ in weights]
     for q in range(PADDED_Z // 8):
         span = slice(q * 8, q * 8 + 8)
-        cos_t = [taps_ref[t, span, :] for t in range(6)]
-        sin_t = [taps_ref[6 + t, span, :] for t in range(6)]
-        for s, weight in enumerate(weights):
-            real = weight[0] * cos_t[0] + sum(weight[t] * cos_t[t] for t in range(1, 6))
-            imag = sum(weight[t] * sin_t[t] for t in range(1, 6))
+        cos_t = [taps_ref[t, span, :] for t in range(3)]
+        sin_t = [taps_ref[3 + t, span, :] for t in range(3)]
+        for s, (even, odd) in enumerate(folded):
+            real = even[0] * cos_t[0] + even[1] * cos_t[1] + even[2] * cos_t[2]
+            imag = odd[0] * sin_t[0] + odd[1] * sin_t[1] + odd[2] * sin_t[2]
             pieces[s].append(real * cos_k - imag * sin_k)
             pieces_im[s].append(-(real * sin_k + imag * cos_k))
         cos_k, sin_k = cos_k * cos_8 - sin_k * sin_8, sin_k * cos_8 + cos_k * sin_8
@@ -732,16 +740,13 @@
 
 
 def finish_kernel(
-    own_ref, one_ref, two_ref, three_ref, charge_ref, dipole_ref, position_ref, energy_ref,
-    row_ref, semaphore
+    own_ref, one_ref, two_ref, three_ref, charge_ref, dipole_ref, position_ref, energy_ref
 ):
     total = (own_ref[...] + one_ref[...]) + (two_ref[...] + three_ref[...])
-    row_ref[...] = total[0:1]
-    copy = fetch(row_ref.at[0], charge_ref, semaphore)
+    charge_ref[...] = total[0]
     dipole_ref[...] = total[1:4]
     position_ref[...] = total[4:7]
     energy_ref[...] = total[7:8, 0:1]
-    copy.wait()
 
 
 SPACES = {"v": pltpu.VMEM, "h": pltpu.HBM, "s": pltpu.SMEM}
@@ -798,7 +803,7 @@
         (
             shape((16, ATOM_DEV), f32),
             shape((8, LANES), f32),
-            shape((12, PADDED_Z, LANES), f32),
+            shape((6, PADDED_Z, LANES), f32),
             shape((NX, LANES), f32),
             shape((NX, LANES), f32),
         ),
@@ -902,12 +907,11 @@
         finish_kernel,
         "vvvv",
         (
-            pltpu.HBM((ATOM_DEV,), f32),
+            shape((ATOM_DEV,), f32),
             shape((3, ATOM_DEV), f32),
             shape((3, ATOM_DEV), f32),
             shape((1, 1), f32),
         ),
-        [pltpu.VMEM((1, ATOM_DEV), f32), pltpu.SemaphoreType.DMA],
     )(shares[0], *arrived)
     return charge_grad, dipole_grad, position_grad, energy[0]
 

time: 112 us -> 111 us (level)
  Pallas kernels: 30.2 us -> 28.7 us
    pallas_call x8, Pallas kernels: 30.2 us -> 28.7 us  [run(): pl.pallas_call(kernel, out_shape=out_shape, in_specs=[pl.BlockSpec(memory...]
  transfers between devices with their start and end apart: 6 -> 6, of which waited for: 3 -> 3; matrix products, arithmetic and copies ran while one was open for 0% -> 0% of each run, Pallas kernels for 6% -> 5%
where the time goes in v11:
time: 111 us
  blocking collectives  37.7 us (34%)
  Pallas kernels  28.7 us (26%)
  waiting for transfers between devices  27.8 us (25%)
  starting transfers between devices  15.2 us (14%)
  between operations  1.38 us (1%)
    pallas_call x8, Pallas kernels, run(): pl.pallas_call(kernel, out_shape=out_shape, in_specs=[pl.BlockSpec(memory...  28.7 us
    all_to_all x1, blocking collectives, swap_slabs(): lines = lax.all_to_all(lines, 'gy', split_axis=0, concat_axis=0, tiled=True)  27.8 us
    all_to_all x1, waiting for transfers between devices, swap_slabs(): lines = lax.all_to_all(lines, 'gy', split_axis=0, concat_axis=0, tiled=True)  19.8 us
    all_gather x1, blocking collectives, on_device(): atoms = lax.all_gather(mine, 'gx', axis=0, tiled=False)  9.91 us
    ppermute x2, waiting for transfers between devices, next_slab(): lax.ppermute(value, 'gy', [(i, (i + step) % SLABS) for i in range(SLABS)])  7.14 us
    all_to_all x1, starting transfers between devices, swap_slabs(): lines = lax.all_to_all(lines, 'gy', split_axis=0, concat_axis=0, tiled=True)  6.24 us
    ppermute x3, starting transfers between devices, on_device(): lax.ppermute(shares[ahead], 'gx', [(i, (i + ahead) % PENCILS) for i in ra...  6.21 us
    ppermute x2, starting transfers between devices, next_slab(): lax.ppermute(value, 'gy', [(i, (i + step) % SLABS) for i in range(SLABS)])  2.73 us
  transfers between devices with their start and end apart: 6, of which 3 were waited for; matrix products, arithmetic and copies ran while one was open for 0% of the time, Pallas kernels for 5%

profile of v11, /device:TPU:1, one launch (start us, length us, event | category | flops | bytes accessed | tf_op | source)
XLA Modules:
  0.0 110.8 jit_solution(15759307366804489538)
XLA Ops:
  1.3 0.1 pad_add_fusion.where_ref.refs_1_
  1.4 1.3 %shard_map.129 = (f32[16,384]{1,0:T(8,128)S(1)}, f32[8,128]{1,0:T(8,128)S(1)}, f32[6,48,128]{2,1,0:T(8,128)S(1)}, f32[384,128]{1,0:T(8,128)S(1)}, f32[384,128]{1,0:T(8,128)S(1)}) custom-call(s32[4]{0:T(128)S(1)} %pad_add_fusion.where_ref.refs_1_, s32[1]{0:T(128)} %copy.20.shear_ref, s32[6]{0:T(128)} %counts_ref.1, s32[3,384]{1,0:T(4,128)} %cells_ref.1, ...), custom_call_target="tpu_custom_call" | custom-call | flops 1000000000 | bytes 8000000 | tf_op jit(solution)/shard_map/pallas_call | solution.py:767
  2.7 9.9 %all-gather = f32[64,384]{1,0:T(8,128)S(1)} all-gather(f32[16,384]{1,0:T(8,128)S(1)} %get-tuple-element.25), channel_id=2, replica_groups=mesh['gy'=64,'gx'=4] {'gx'}, dimensions={0}, use_global_device_ids=true | all-gather | bytes 122880 | tf_op jit(solution)/shard_map/all_gather | solution.py:827
  12.6 0.0 collective-permute-start
  12.6 3.0 %shard_map.130.refs_4_ = f32[432,1536]{1,0:T(8,128)S(1)} custom-call(f32[4,16,384]{2,1,0:T(8,128)S(1)} %bitcast.23, s32[4]{0:T(128)S(1)} %pad_add_fusion.where_ref.refs_1_, f32[8,128]{1,0:T(8,128)S(1)} %get-tuple-element.26.refs_2_, f32[6,48,128]{2,1,0:T(8,128)S(1)} %get-tuple-element.27.refs_3_), custom_call_target="tpu_custom_call" | custom-call | flops 1000000000 | bytes 8000000 | tf_op jit(solution)/shard_map/pallas_call | solution.py:767
  15.6 7.1 %collective-permute-done.refs_0_ = f32[4,16,384]{2,1,0:T(8,128)S(1)} collective-permute-done((f32[4,16,384]{2,1,0:T(8,128)S(1)}, f32[4,16,384]{2,1,0:T(8,128)S(1)}, u32[]{:S(2)}, u32[]{:S(2)}) %collective-permute-start) | collective-permute-done | bytes 98336 | tf_op jit(solution)/shard_map/ppermute | solution.py:783
  22.8 12.4 %shard_map.131 = (f32[432,1536]{1,0:T(8,128)S(1)}, f32[1728,128]{1,0:T(8,128)}, bf16[24,2,96,384]{3,2,1,0:T(8,128)(2,1)}, f32[24,3,48,128]{3,2,1,0:T(8,128)}, f3...) custom-call(f32[4,16,384]{2,1,0:T(8,128)S(1)} %collective-permute-done.refs_0_, ...), custom_call_target="tpu_custom_call", output_to_operand_aliasing={{0}: (4, {})} | custom-call | flops 1000000000 | bytes 8000000 | tf_op jit(solution)/shard_map/pallas_call | solution.py:767
  35.2 6.2 %all-to-all-start = ((f32[64,27,1,128]{3,2,1,0:T(1,128)}), f32[64,27,1,128]{3,2,1,0:T(1,128)S(1)}, u32[]{:S(2)}, u32[]{:S(2)}) async-start(f32[64,27,1,128]{3,2,1,0:T(1,128)} %bitcast.5), calls=%async_computation | async-start | bytes 1769472 | tf_op jit(solution)/shard_map/all_to_all | solution.py:788
  41.5 0.7 shard_map.132.greens_ref
  42.2 19.8 %all-to-all-done = f32[64,27,1,128]{3,2,1,0:T(1,128)S(1)} async-done(((f32[64,27,1,128]{3,2,1,0:T(1,128)}), f32[64,27,1,128]{3,2,1,0:T(1,128)S(1)}, u32[]{:S(2)}, u32[]{:S(2)}) %all-to-all-start) | async-done | bytes 884768 | tf_op jit(solution)/shard_map/all_to_all | solution.py:788
  62.0 3.7 %shard_map.133 = f32[1728,128]{1,0:T(8,128)S(1)} custom-call(f32[1728,128]{1,0:T(8,128)S(1)} %bitcast.20, bf16[384,576]{1,0:T(8,128)(2,1)} %constant.20.clone.tables_ref, bf16[384,576]{1,0:T(8,128)(2,1)} %constant.21.clone.backs_ref, f32[384,768]{1,0:T(8,128)} %shard_map.132.greens_ref), custom_call_target="tpu_custom_call" | custom-call | flops 1000000000 | bytes 8000000 | tf_op jit(solution)/shard_map/pallas_call | solution.py:767
  65.7 27.8 %all_to_all.10 = f32[64,27,1,128]{3,2,1,0:T(1,128)S(1)} all-to-all(f32[64,27,1,128]{3,2,1,0:T(1,128)S(1)} %bitcast.21), channel_id=1, replica_groups=mesh['gy'=64,'gx'=4] {'gy'}, dimensions={0} | all-to-all | bytes 1769472 | tf_op jit(solution)/shard_map/all_to_all | solution.py:788
  93.5 4.6 %shard_map.134 = (f32[4,8,384]{2,1,0:T(8,128)S(1)}, f32[432,768]{1,0:T(8,128)S(1)}, bf16[12,2,96,384]{3,2,1,0:T(8,128)(2,1)S(1)}, f32[12,3,48,128]{3,2,1,0:T(8,128)S(1)}, f32[12,3,16,128]{3,2,1,0:T(8,128)S(1)}) custom-call(f32[4,16,384]{2,1,0:T(8,128)S(1)} %collective-permute-done.refs_0_, s32[4]{0:T(128)S(1)} %pad_add_fusion.where_ref.refs_1_, ...), custom_call_target="tpu_custom_call" | custom-call | flops 1000000000 | bytes 8000000 | tf_op jit(solution)/shard_map/pallas_call | solution.py:767
  98.1 2.7 %collective-permute-start.1 = (f32[4,8,384]{2,1,0:T(8,128)S(1)}, f32[4,8,384]{2,1,0:T(8,128)S(1)}, u32[]{:S(2)}, u32[]{:S(2)}) collective-permute-start(f32[4,8,384]{2,1,0:T(8,128)S(1)} %get-tuple-element.41), channel_id=1, source_target_pairs={{0,252},{4,0},{8,4},{12,8},{16,12},{20,16},{24,20},{28,24},{32,28}... | collective-permute-start | bytes 147464 | tf_op jit(solution)/shard_map/ppermute | solution.py:783
  100.8 2.3 %shard_map.135 = f32[4,8,384]{2,1,0:T(8,128)S(1)} custom-call(f32[4,16,384]{2,1,0:T(8,128)S(1)} %bitcast.26, s32[4]{0:T(128)S(1)} %pad_add_fusion.where_ref.refs_1_, bf16[12,2,96,384]{3,2,1,0:T(8,128)(2,1)S(1)} %get-tuple-element.37.refs_2_, f32[12,3,48,128]{3,2,1,0:T(8,128)S(1)} %get-tuple-element.38.refs_3_, ...), custom_call_target="tpu_custom_call" | custom-call | flops 1000000000 | bytes 8000000 | tf_op jit(solution)/shard_map/pallas_call | solution.py:767
  103.1 0.0 collective-permute-done.1
  103.2 0.1 collective-permute-start.4
  103.3 2.7 %collective-permute-start.3 = (f32[8,384]{1,0:T(8,128)S(1)}, f32[8,384]{1,0:T(8,128)S(1)}, u32[]{:S(2)}, u32[]{:S(2)}) collective-permute-start(f32[8,384]{1,0:T(8,128)S(1)} %get-tuple-element.47), channel_id=1, source_target_pairs={{0,2},{1,3},{2,0},{3,1},{4,6},{5,7},{6,4},{7,5},{8,10},{9,11},{10,... | collective-permute-start | bytes 36872 | tf_op jit(solution)/shard_map/ppermute | solution.py:903
  106.0 3.4 %collective-permute-start.2 = (f32[8,384]{1,0:T(8,128)S(1)}, f32[8,384]{1,0:T(8,128)S(1)}, u32[]{:S(2)}, u32[]{:S(2)}) collective-permute-start(f32[8,384]{1,0:T(8,128)S(1)} %get-tuple-element.48), channel_id=1, source_target_pairs={{0,1},{1,2},{2,3},{3,0},{4,5},{5,6},{6,7},{7,4},{8,9},{9,10},{10,1... | collective-permute-start | bytes 36872 | tf_op jit(solution)/shard_map/ppermute | solution.py:903
  109.4 0.0 collective-permute-done.4.three_ref
  109.4 0.0 collective-permute-done.3.two_ref
  109.4 0.8 collective-permute-done.2.one_ref
  110.2 0.6 shard_map.136
  (2 shorter events, 0.0 us)
Async XLA Ops:
  12.6 10.1 %collective-permute-start = (f32[4,16,384]{2,1,0:T(8,128)S(1)}, f32[4,16,384]{2,1,0:T(8,128)S(1)}, u32[]{:S(2)}, u32[]{:S(2)}) collective-permute-start(f32[4,16,384]{2,1,0:T(8,128)S(1)} %bitcast.22), channel_id=1, source_target_pairs={{0,4},{4,8},{8,12},{12,16},{16,20},{20,24},{24,28},{28,32},{32,36}... | collective-permute-start | bytes 294920 | tf_op jit(solution)/shard_map/ppermute | solution.py:783
  35.2 26.8 %all-to-all-start = ((f32[64,27,1,128]{3,2,1,0:T(1,128)}), f32[64,27,1,128]{3,2,1,0:T(1,128)S(1)}, u32[]{:S(2)}, u32[]{:S(2)}) async-start(f32[64,27,1,128]{3,2,1,0:T(1,128)} %bitcast.5), calls=%async_computation | async-start | bytes 1769472 | tf_op jit(solution)/shard_map/all_to_all | solution.py:788
  98.1 5.0 %collective-permute-start.1 = (f32[4,8,384]{2,1,0:T(8,128)S(1)}, f32[4,8,384]{2,1,0:T(8,128)S(1)}, u32[]{:S(2)}, u32[]{:S(2)}) collective-permute-start(f32[4,8,384]{2,1,0:T(8,128)S(1)} %get-tuple-element.41), channel_id=1, source_target_pairs={{0,252},{4,0},{8,4},{12,8},{16,12},{20,16},{24,20},{28,24},{32,28}... | collective-permute-start | bytes 147464 | tf_op jit(solution)/shard_map/ppermute | solution.py:783
  103.2 6.2 %collective-permute-start.4 = (f32[8,384]{1,0:T(8,128)S(1)}, f32[8,384]{1,0:T(8,128)S(1)}, u32[]{:S(2)}, u32[]{:S(2)}) collective-permute-start(f32[8,384]{1,0:T(8,128)S(1)} %get-tuple-element.46), channel_id=1, source_target_pairs={{0,3},{1,0},{2,1},{3,2},{4,7},{5,4},{6,5},{7,6},{8,11},{9,8},{10,9... | collective-permute-start | bytes 36872 | tf_op jit(solution)/shard_map/ppermute | solution.py:903
  103.3 6.1 %collective-permute-start.3 = (f32[8,384]{1,0:T(8,128)S(1)}, f32[8,384]{1,0:T(8,128)S(1)}, u32[]{:S(2)}, u32[]{:S(2)}) collective-permute-start(f32[8,384]{1,0:T(8,128)S(1)} %get-tuple-element.47), channel_id=1, source_target_pairs={{0,2},{1,3},{2,0},{3,1},{4,6},{5,7},{6,4},{7,5},{8,10},{9,11},{10,... | collective-permute-start | bytes 36872 | tf_op jit(solution)/shard_map/ppermute | solution.py:903
  106.0 4.3 %collective-permute-start.2 = (f32[8,384]{1,0:T(8,128)S(1)}, f32[8,384]{1,0:T(8,128)S(1)}, u32[]{:S(2)}, u32[]{:S(2)}) collective-permute-start(f32[8,384]{1,0:T(8,128)S(1)} %get-tuple-element.48), channel_id=1, source_target_pairs={{0,1},{1,2},{2,3},{3,0},{4,5},{5,6},{6,7},{7,4},{8,9},{9,10},{10,1... | collective-permute-start | bytes 36872 | tf_op jit(solution)/shard_map/ppermute | solution.py:903

commit v12 on v11

--- a/solution.py
+++ b/solution.py
@@ -397,10 +397,9 @@
         grid_ref, weights_ref = refs[4:]
         grid_ref[...] = jnp.zeros_like(grid_ref)
     else:
-        _, tables_ref, cos_ref, sin_ref, slab_atoms_ref, grid_ref, out_ref = refs[4:11]
-        results, green_out_ref, kept = refs[11:14], refs[14], refs[15:18]
-        green_ref, table_ref, weights_ref, semaphores = refs[18:]
-        table_copy = fetch(tables_ref, table_ref, semaphores.at[0])
+        _, tables_ref, cos_ref, sin_ref, grid_ref, out_ref = refs[4:10]
+        table_ref, weights_ref, semaphore = refs[10:]
+        table_copy = fetch(tables_ref, table_ref, semaphore)
     rows = list(range(CY)) if own else list(range(CY, 2 * CY - 1))
     part = CY * LANES
     gap = jnp.zeros((HALF - PADDED_Z, LANES), bf16)
@@ -481,18 +480,6 @@
         for c, carrier in enumerate(pack_blocks(blocks)):
             out_ref[rows_of(3 * group + c), :] = carrier
 
-    @pl.when(where_ref[1] % 2 == 1)
-    def _():
-        make_green(where_ref, green_ref)
-        green_copy = fetch(green_ref, green_out_ref, semaphores.at[3])
-        for start, some_ref in ((0, slab_atoms_ref), (PENCILS * PAIRS, atoms_ref)):
-            sampling_weights(
-                start, start == 0, where_ref, some_ref, weights_ref, base_ref, taps_ref, *kept
-            )
-        copies = [fetch(kept[n], results[n], semaphores.at[n]) for n in range(3)]
-        for copy in [green_copy, *copies]:
-            copy.wait()
-
 
 def spline_modulus(turns):
     cosine, _ = unit_phase(turns)
@@ -538,11 +525,22 @@
         out_ref[:, j * LANES : (j + 1) * LANES] = jnp.where(square == 0.0, 0.0, green)
 
 
-def green_kernel(where_ref, _, result_ref, green_ref, semaphore):
-    @pl.when(where_ref[1] % 2 == 0)
-    def _():
-        make_green(where_ref, green_ref)
-        fetch(green_ref, result_ref, semaphore).wait()
+def weights_kernel(where_ref, atoms_ref, below_ref, base_ref, taps_ref, *refs):
+    results, green_out_ref, kept, green_ref, weights_ref, semaphores = (
+        refs[:3], refs[3], refs[4:7], *refs[7:]
+    )
+    make_green(where_ref, green_ref)
+    copies = [fetch(green_ref, green_out_ref, semaphores.at[6])]
+    pairs = PENCILS * PAIRS
+    for own, some_ref in ((True, atoms_ref), (False, below_ref)):
+        start = 0 if own else pairs
+        sampling_weights(start, own, where_ref, some_ref, weights_ref, base_ref, taps_ref, *kept)
+        some = pl.ds(start, pairs)
+        for n in range(3):
+            semaphore = semaphores.at[n if own else 3 + n]
+            copies.append(fetch(kept[n].at[some], results[n].at[some], semaphore))
+    for copy in copies:
+        copy.wait()
 
 
 def filter_kernel(
@@ -613,38 +611,21 @@
     if own:
         atoms_ref, where_ref, waves_ref, x_ref, y_ref, grid_ref, out_ref = refs
     else:
-        atoms_ref, where_ref, base_ref, taps_ref = refs[:4]
-        kept = refs[4:7]
-        in_ref, cos_ref, sin_ref, tables_ref, slab_atoms_ref, out_ref, grid_ref = refs[7:14]
-        slab_weights, below_weights = refs[14:17], refs[17:20]
+        atoms_ref, where_ref = refs[:2]
+        kept = refs[2:5]
+        in_ref, cos_ref, sin_ref, tables_ref, out_ref, grid_ref = refs[5:11]
+        slab_weights, below_weights = refs[11:14], refs[14:17]
         waves_ref, x_ref, y_ref = below_weights
-        table_ref, weights_ref, semaphores = refs[20:]
+        table_ref, semaphores = refs[17:]
         table_copy = fetch(tables_ref, table_ref, semaphores.at[6])
-        later = where_ref[1] % 2 == 0
         pairs = PENCILS * PAIRS
         copies = [
-            pltpu.make_async_copy(source.at[pl.ds(start, pairs)], target, semaphores.at[n])
+            fetch(source.at[pl.ds(start, pairs)], target, semaphores.at[n])
             for n, (source, start, target) in enumerate(
                 [(kept[n], pairs, below_weights[n]) for n in range(3)]
                 + [(kept[n], 0, slab_weights[n]) for n in range(3)]
             )
         ]
-
-        @pl.when(later)
-        def _():
-            for slab, some_ref, targets in (
-                (False, atoms_ref, below_weights),
-                (True, slab_atoms_ref, slab_weights),
-            ):
-                sampling_weights(
-                    0, slab, where_ref, some_ref, weights_ref, base_ref, taps_ref, *targets
-                )
-
-        @pl.when(jnp.logical_not(later))
-        def _():
-            for copy in copies:
-                copy.start()
-
     rows = list(range(CY)) if own else list(range(CY, 2 * CY - 1))
     energy = 0.0
     if not own:
@@ -673,11 +654,8 @@
     gap = jnp.zeros((HALF - PADDED_Z, 3 * LANES), bf16)
 
     if not own:
-
-        @pl.when(jnp.logical_not(later))
-        def _():
-            for copy in copies[:3]:
-                copy.wait()
+        for copy in copies[:3]:
+            copy.wait()
 
     def pair_body(pair, carry):
         pencil, lanes = pair_place(pair)
@@ -732,11 +710,8 @@
 
     lax.fori_loop(0, PENCILS * PAIRS, pair_body, 0, unroll=12)
     if not own:
-
-        @pl.when(jnp.logical_not(later))
-        def _():
-            for copy in copies[3:]:
-                copy.wait()
+        for copy in copies[3:]:
+            copy.wait()
 
 
 def finish_kernel(
@@ -836,7 +811,6 @@
         ((3, 16, LANES), f32),
     ]
     weights_space = pltpu.VMEM((PENCILS, 18, 8, ATOM_DEV), f32)
-    four = pltpu.SemaphoreType.DMA((4,))
     grid_shape = shape((EXTENDED, 2 * CY * LANES), f32)
     slab_grid = call(
         lambda *refs: spread_kernel(True, *refs),
@@ -846,28 +820,27 @@
     )(atoms, where, base, taps)
     green_shape = pltpu.HBM((NY, PART_X * LANES), f32)
     green_space = pltpu.VMEM((NY, PART_X * LANES), f32)
-    _, lines, *weights, green = call(
+    _, lines = call(
         lambda *refs: spread_kernel(False, *refs),
-        "vsvvvhvvv",
-        (
-            grid_shape,
-            packed,
-            *(pltpu.HBM((pairs, *dims), kind) for dims, kind in held),
-            green_shape,
-        ),
+        "vsvvvhvv",
+        (grid_shape, packed),
+        [table_space, weights_space, pltpu.SemaphoreType.DMA],
+        ((4, 0),),
+    )(below_atoms, where, base, taps, slab_grid, x_forward, cos_t, sin_t)
+    lines, where, atoms, below_atoms = lax.optimization_barrier(
+        (lines, where, atoms, below_atoms)
+    )
+    *weights, green = call(
+        weights_kernel,
+        "svvvv",
+        (*(pltpu.HBM((pairs, *dims), kind) for dims, kind in held), green_shape),
         [
             *(pltpu.VMEM((pairs, *dims), kind) for dims, kind in held),
             green_space,
-            table_space,
             weights_space,
-            four,
+            pltpu.SemaphoreType.DMA((7,)),
         ],
-        ((4, 0),),
-    )(below_atoms, where, base, taps, slab_grid, x_forward, cos_t, sin_t, atoms)
-    lines, where = lax.optimization_barrier((lines, where))
-    green = call(
-        green_kernel, "sh", green_shape, [green_space, pltpu.SemaphoreType.DMA], ((1, 0),)
-    )(where, green)
+    )(where, atoms, below_atoms, base, taps)
     lines = swap_slabs(lines)
     filtered = call(
         filter_kernel,
@@ -881,7 +854,7 @@
     shares_shape = shape((PENCILS, 8, ATOM_DEV), f32)
     below_shares, potential, *weights = call(
         lambda *refs: sample_kernel(False, *refs),
-        "vsvvhhhvvvhv",
+        "vshhhvvvh",
         (
             shares_shape,
             shape((EXTENDED, CY * LANES), f32),
@@ -890,10 +863,9 @@
         [
             *(pltpu.VMEM((pairs // 2, *dims), kind) for dims, kind in held),
             table_space,
-            weights_space,
             pltpu.SemaphoreType.DMA((7,)),
         ],
-    )(below_atoms, where, base, taps, *weights, filtered, cos_t, sin_t, x_inverse, atoms)
+    )(below_atoms, where, *weights, filtered, cos_t, sin_t, x_inverse)
     below_shares = next_slab(below_shares, back=True)
     shares = call(lambda *refs: sample_kernel(True, *refs), "vsvvvv", shares_shape)(
         atoms, where, *weights, potential

time: 111 us -> 112 us (level); the launches traced: 111 us -> 110 us
  waiting for transfers between devices: 27.8 us -> 23.9 us
  starting transfers between devices: 15.2 us -> 17.6 us
    all_to_all x1, waiting for transfers between devices: 19.8 us -> 15.9 us  [swap_slabs(): lines = lax.all_to_all(lines, 'gy', split_axis=0, concat_axis=0, tiled=True)]
    ppermute x3, starting transfers between devices: 6.21 us -> 7.63 us  [on_device(): lax.ppermute(shares[ahead], 'gx', [(i, (i + ahead) % PENCILS) for i in ra...]
  transfers between devices with their start and end apart: 6 -> 6, of which waited for: 3 -> 4; matrix products, arithmetic and copies ran while one was open for 0% -> 0% of each run, Pallas kernels for 5% -> 11%
where the time goes in v12:
time: 112 us; the launch traced here: 110 us
  blocking collectives  38.7 us (35%)
  Pallas kernels  27.8 us (25%)
  waiting for transfers between devices  23.9 us (21%)
  starting transfers between devices  17.6 us (16%)
  between operations  1.38 us (1%)
    all_to_all x1, blocking collectives, swap_slabs(): lines = lax.all_to_all(lines, 'gy', split_axis=0, concat_axis=0, tiled=True)  28.8 us
    pallas_call x8, Pallas kernels, run(): pl.pallas_call(kernel, out_shape=out_shape, in_specs=[pl.BlockSpec(memory...  27.8 us
    all_to_all x1, waiting for transfers between devices, swap_slabs(): lines = lax.all_to_all(lines, 'gy', split_axis=0, concat_axis=0, tiled=True)  15.9 us
    all_gather x1, blocking collectives, on_device(): atoms = lax.all_gather(mine, 'gx', axis=0, tiled=False)  9.91 us
    ppermute x3, starting transfers between devices, on_device(): lax.ppermute(shares[ahead], 'gx', [(i, (i + ahead) % PENCILS) for i in ra...  7.63 us
    ppermute x2, waiting for transfers between devices, next_slab(): lax.ppermute(value, 'gy', [(i, (i + step) % SLABS) for i in range(SLABS)])  7.13 us
    all_to_all x1, starting transfers between devices, swap_slabs(): lines = lax.all_to_all(lines, 'gy', split_axis=0, concat_axis=0, tiled=True)  6.43 us
    ppermute x2, starting transfers between devices, next_slab(): lax.ppermute(value, 'gy', [(i, (i + step) % SLABS) for i in range(SLABS)])  3.54 us
  transfers between devices with their start and end apart: 6, of which 4 were waited for; matrix products, arithmetic and copies ran while one was open for 0% of the time, Pallas kernels for 11%

profile of v12, /device:TPU:1, one launch (start us, length us, event | category | flops | bytes accessed | tf_op | source)
XLA Modules:
  0.0 109.5 jit_solution(15399839210873688314)
XLA Ops:
  1.3 0.1 pad_add_fusion.where_ref.refs_1_
  1.4 1.3 %shard_map.129 = (f32[16,384]{1,0:T(8,128)S(1)}, f32[8,128]{1,0:T(8,128)S(1)}, f32[6,48,128]{2,1,0:T(8,128)S(1)}, f32[384,128]{1,0:T(8,128)S(1)}, f32[384,128]{1,0:T(8,128)S(1)}) custom-call(s32[4]{0:T(128)S(1)} %pad_add_fusion.where_ref.refs_1_, s32[1]{0:T(128)} %copy.18.shear_ref, s32[6]{0:T(128)} %counts_ref.1, s32[3,384]{1,0:T(4,128)} %cells_ref.1, ...), custom_call_target="tpu_custom_call" | custom-call | flops 1000000000 | bytes 8000000 | tf_op jit(solution)/shard_map/pallas_call | solution.py:742
  2.7 9.9 %all-gather = f32[64,384]{1,0:T(8,128)S(1)} all-gather(f32[16,384]{1,0:T(8,128)S(1)} %get-tuple-element.27), channel_id=2, replica_groups=mesh['gy'=64,'gx'=4] {'gx'}, dimensions={0}, use_global_device_ids=true | all-gather | bytes 122880 | tf_op jit(solution)/shard_map/all_gather | solution.py:802
  12.6 0.0 collective-permute-start
  12.6 3.0 %shard_map.130.refs_4_ = f32[432,1536]{1,0:T(8,128)S(1)} custom-call(f32[4,16,384]{2,1,0:T(8,128)S(1)} %bitcast.23, s32[4]{0:T(128)S(1)} %pad_add_fusion.where_ref.refs_1_, f32[8,128]{1,0:T(8,128)S(1)} %get-tuple-element.28.refs_2_.base_ref, f32[6,48,128]{2,1,0:T(8,128)S(1)} %get-tuple-element.29.refs_3_.taps_ref), custom_call_target="tpu_custom_call" | custom-call | flops 1000000000 | bytes 8000000 | tf_op jit(solution)/shard_map/pallas_call | solution.py:742
  15.6 7.1 %collective-permute-done.refs_0_.below_ref = f32[4,16,384]{2,1,0:T(8,128)S(1)} collective-permute-done((f32[4,16,384]{2,1,0:T(8,128)S(1)}, f32[4,16,384]{2,1,0:T(8,128)S(1)}, u32[]{:S(2)}, u32[]{:S(2)}) %collective-permute-start) | collective-permute-done | bytes 98336 | tf_op jit(solution)/shard_map/ppermute | solution.py:758
  22.8 5.5 %shard_map.131 = (f32[432,1536]{1,0:T(8,128)S(1)}, f32[1728,128]{1,0:T(8,128)}) custom-call(f32[4,16,384]{2,1,0:T(8,128)S(1)} %collective-permute-done.refs_0_.below_ref, s32[4]{0:T(128)S(1)} %pad_add_fusion.where_ref.refs_1_, f32[8,128]{1,0:T(8,128)S(1)} %get-tuple-element.28.refs_2_.base_ref, ...), custom_call_target="tpu_custom_call", output_to_operand_aliasing={{0}: (4, {})} | custom-call | flops 1000000000 | bytes 8000000 | tf_op jit(solution)/shard_map/pallas_call | solution.py:742
  28.3 6.4 %all-to-all-start = ((f32[64,27,1,128]{3,2,1,0:T(1,128)}), f32[64,27,1,128]{3,2,1,0:T(1,128)S(1)}, u32[]{:S(2)}, u32[]{:S(2)}) async-start(f32[64,27,1,128]{3,2,1,0:T(1,128)} %bitcast.5), calls=%async_computation | async-start | bytes 1769472 | tf_op jit(solution)/shard_map/all_to_all | solution.py:763
  34.7 6.6 %shard_map.132 = (bf16[24,2,96,384]{3,2,1,0:T(8,128)(2,1)}, f32[24,3,48,128]{3,2,1,0:T(8,128)}, f32[24,3,16,128]{3,2,1,0:T(8,128)}, f32[384,768]{1,0:T(8,128)}) custom-call(s32[4]{0:T(128)S(1)} %pad_add_fusion.where_ref.refs_1_, f32[4,16,384]{2,1,0:T(8,128)S(1)} %bitcast.24, f32[4,16,384]{2,1,0:T(8,128)S(1)} %collective-permute-done.refs_0_.below_ref, ...), custom_call_target="tpu_custom_call" | custom-call | flops 1000000000 | bytes 8000000 | tf_op jit(solution)/shard_map/pallas_call | solution.py:742
  41.4 15.9 %all-to-all-done = f32[64,27,1,128]{3,2,1,0:T(1,128)S(1)} async-done(((f32[64,27,1,128]{3,2,1,0:T(1,128)}), f32[64,27,1,128]{3,2,1,0:T(1,128)S(1)}, u32[]{:S(2)}, u32[]{:S(2)}) %all-to-all-start) | async-done | bytes 884768 | tf_op jit(solution)/shard_map/all_to_all | solution.py:763
  57.3 3.7 %shard_map.133 = f32[1728,128]{1,0:T(8,128)S(1)} custom-call(f32[1728,128]{1,0:T(8,128)S(1)} %bitcast.19, bf16[384,576]{1,0:T(8,128)(2,1)} %constant.20.clone.tables_ref, bf16[384,576]{1,0:T(8,128)(2,1)} %constant.21.clone.backs_ref, f32[384,768]{1,0:T(8,128)} %get-tuple-element.40.greens_ref), custom_call_target="tpu_custom_call" | custom-call | flops 1000000000 | bytes 8000000 | tf_op jit(solution)/shard_map/pallas_call | solution.py:742
  61.1 28.8 %all_to_all.10 = f32[64,27,1,128]{3,2,1,0:T(1,128)S(1)} all-to-all(f32[64,27,1,128]{3,2,1,0:T(1,128)S(1)} %bitcast.20), channel_id=1, replica_groups=mesh['gy'=64,'gx'=4] {'gy'}, dimensions={0} | all-to-all | bytes 1769472 | tf_op jit(solution)/shard_map/all_to_all | solution.py:763
  89.9 4.7 %shard_map.134 = (f32[4,8,384]{2,1,0:T(8,128)S(1)}, f32[432,768]{1,0:T(8,128)S(1)}, bf16[12,2,96,384]{3,2,1,0:T(8,128)(2,1)S(1)}, f32[12,3,48,128]{3,2,1,0:T(8,128)S(1)}, f32[12,3,16,128]{3,2,1,0:T(8,128)S(1)}) custom-call(f32[4,16,384]{2,1,0:T(8,128)S(1)} %collective-permute-done.refs_0_.below_ref, s32[4]{0:T(128)S(1)} %pad_add_fusion.where_ref.refs_1_, ...), custom_call_target="tpu_custom_call" | custom-call | flops 1000000000 | bytes 8000000 | tf_op jit(solution)/shard_map/pallas_call | solution.py:742
  94.6 3.5 %collective-permute-start.1 = (f32[4,8,384]{2,1,0:T(8,128)S(1)}, f32[4,8,384]{2,1,0:T(8,128)S(1)}, u32[]{:S(2)}, u32[]{:S(2)}) collective-permute-start(f32[4,8,384]{2,1,0:T(8,128)S(1)} %get-tuple-element.45), channel_id=1, source_target_pairs={{0,252},{4,0},{8,4},{12,8},{16,12},{20,16},{24,20},{28,24},{32,28}... | collective-permute-start | bytes 147464 | tf_op jit(solution)/shard_map/ppermute | solution.py:758
  98.1 2.3 %shard_map.135 = f32[4,8,384]{2,1,0:T(8,128)S(1)} custom-call(f32[4,16,384]{2,1,0:T(8,128)S(1)} %bitcast.25, s32[4]{0:T(128)S(1)} %pad_add_fusion.where_ref.refs_1_, bf16[12,2,96,384]{3,2,1,0:T(8,128)(2,1)S(1)} %get-tuple-element.41.refs_2_, f32[12,3,48,128]{3,2,1,0:T(8,128)S(1)} %get-tuple-element.42.refs_3_, ...), custom_call_target="tpu_custom_call" | custom-call | flops 1000000000 | bytes 8000000 | tf_op jit(solution)/shard_map/pallas_call | solution.py:742
  100.4 0.0 collective-permute-done.1
  100.4 4.4 %collective-permute-start.4 = (f32[8,384]{1,0:T(8,128)S(1)}, f32[8,384]{1,0:T(8,128)S(1)}, u32[]{:S(2)}, u32[]{:S(2)}) collective-permute-start(f32[8,384]{1,0:T(8,128)S(1)} %get-tuple-element.50), channel_id=1, source_target_pairs={{0,3},{1,0},{2,1},{3,2},{4,7},{5,4},{6,5},{7,6},{8,11},{9,8},{10,9... | collective-permute-start | bytes 36872 | tf_op jit(solution)/shard_map/ppermute | solution.py:875
  104.8 2.6 %collective-permute-start.3 = (f32[8,384]{1,0:T(8,128)S(1)}, f32[8,384]{1,0:T(8,128)S(1)}, u32[]{:S(2)}, u32[]{:S(2)}) collective-permute-start(f32[8,384]{1,0:T(8,128)S(1)} %get-tuple-element.51), channel_id=1, source_target_pairs={{0,2},{1,3},{2,0},{3,1},{4,6},{5,7},{6,4},{7,5},{8,10},{9,11},{10,... | collective-permute-start | bytes 36872 | tf_op jit(solution)/shard_map/ppermute | solution.py:875
  107.5 0.6 collective-permute-start.2
  108.1 0.7 collective-permute-done.4.three_ref
  108.7 0.2 collective-permute-done.3.two_ref
  108.9 0.0 collective-permute-done.2.one_ref
  108.9 0.6 shard_map.136
  (2 shorter events, 0.0 us)
Async XLA Ops:
  12.6 10.1 %collective-permute-start = (f32[4,16,384]{2,1,0:T(8,128)S(1)}, f32[4,16,384]{2,1,0:T(8,128)S(1)}, u32[]{:S(2)}, u32[]{:S(2)}) collective-permute-start(f32[4,16,384]{2,1,0:T(8,128)S(1)} %bitcast.22), channel_id=1, source_target_pairs={{0,4},{4,8},{8,12},{12,16},{16,20},{20,24},{24,28},{28,32},{32,36}... | collective-permute-start | bytes 294920 | tf_op jit(solution)/shard_map/ppermute | solution.py:758
  28.3 29.0 %all-to-all-start = ((f32[64,27,1,128]{3,2,1,0:T(1,128)}), f32[64,27,1,128]{3,2,1,0:T(1,128)S(1)}, u32[]{:S(2)}, u32[]{:S(2)}) async-start(f32[64,27,1,128]{3,2,1,0:T(1,128)} %bitcast.5), calls=%async_computation | async-start | bytes 1769472 | tf_op jit(solution)/shard_map/all_to_all | solution.py:763
  94.6 5.8 %collective-permute-start.1 = (f32[4,8,384]{2,1,0:T(8,128)S(1)}, f32[4,8,384]{2,1,0:T(8,128)S(1)}, u32[]{:S(2)}, u32[]{:S(2)}) collective-permute-start(f32[4,8,384]{2,1,0:T(8,128)S(1)} %get-tuple-element.45), channel_id=1, source_target_pairs={{0,252},{4,0},{8,4},{12,8},{16,12},{20,16},{24,20},{28,24},{32,28}... | collective-permute-start | bytes 147464 | tf_op jit(solution)/shard_map/ppermute | solution.py:758
  100.4 8.3 %collective-permute-start.4 = (f32[8,384]{1,0:T(8,128)S(1)}, f32[8,384]{1,0:T(8,128)S(1)}, u32[]{:S(2)}, u32[]{:S(2)}) collective-permute-start(f32[8,384]{1,0:T(8,128)S(1)} %get-tuple-element.50), channel_id=1, source_target_pairs={{0,3},{1,0},{2,1},{3,2},{4,7},{5,4},{6,5},{7,6},{8,11},{9,8},{10,9... | collective-permute-start | bytes 36872 | tf_op jit(solution)/shard_map/ppermute | solution.py:875
  104.8 4.1 %collective-permute-start.3 = (f32[8,384]{1,0:T(8,128)S(1)}, f32[8,384]{1,0:T(8,128)S(1)}, u32[]{:S(2)}, u32[]{:S(2)}) collective-permute-start(f32[8,384]{1,0:T(8,128)S(1)} %get-tuple-element.51), channel_id=1, source_target_pairs={{0,2},{1,3},{2,0},{3,1},{4,6},{5,7},{6,4},{7,5},{8,10},{9,11},{10,... | collective-permute-start | bytes 36872 | tf_op jit(solution)/shard_map/ppermute | solution.py:875
  107.5 1.4 %collective-permute-start.2 = (f32[8,384]{1,0:T(8,128)S(1)}, f32[8,384]{1,0:T(8,128)S(1)}, u32[]{:S(2)}, u32[]{:S(2)}) collective-permute-start(f32[8,384]{1,0:T(8,128)S(1)} %get-tuple-element.52), channel_id=1, source_target_pairs={{0,1},{1,2},{2,3},{3,0},{4,5},{5,6},{6,7},{7,4},{8,9},{9,10},{10,1... | collective-permute-start | bytes 36872 | tf_op jit(solution)/shard_map/ppermute | solution.py:875

commit v13 on v12

--- a/solution.py
+++ b/solution.py
@@ -525,12 +525,16 @@
         out_ref[:, j * LANES : (j + 1) * LANES] = jnp.where(square == 0.0, 0.0, green)
 
 
-def weights_kernel(where_ref, atoms_ref, below_ref, base_ref, taps_ref, *refs):
-    results, green_out_ref, kept, green_ref, weights_ref, semaphores = (
-        refs[:3], refs[3], refs[4:7], *refs[7:]
-    )
+def weights_kernel(
+    where_ref, atoms_ref, below_ref, base_ref, taps_ref, tables_ref, backs_ref, *refs
+):
+    results, (green_ref, table_ref, back_ref), kept = refs[:3], refs[3:6], refs[6:9]
+    weights_ref, semaphores = refs[9:]
+    copies = [
+        fetch(tables_ref, table_ref, semaphores.at[6]),
+        fetch(backs_ref, back_ref, semaphores.at[7]),
+    ]
     make_green(where_ref, green_ref)
-    copies = [fetch(green_ref, green_out_ref, semaphores.at[6])]
     pairs = PENCILS * PAIRS
     for own, some_ref in ((True, atoms_ref), (False, below_ref)):
         start = 0 if own else pairs
@@ -543,18 +547,7 @@
         copy.wait()
 
 
-def filter_kernel(
-    in_ref, tables_ref, backs_ref, greens_ref, out_ref, table_ref, back_ref, green_ref, semaphores
-):
-    copies = [
-        fetch(tables_ref, table_ref, semaphores.at[0]),
-        fetch(backs_ref, back_ref, semaphores.at[1]),
-    ]
-    for first in range(0, PART_X, 2):
-        lanes = pl.ds(first * LANES, 2 * LANES)
-        copies.append(
-            fetch(greens_ref.at[:, lanes], green_ref.at[:, lanes], semaphores.at[2 + first // 2])
-        )
+def filter_kernel(in_ref, table_ref, back_ref, green_ref, out_ref):
     sign = lane_sign((NY, LANES))
     energy = jnp.zeros((8, LANES), f32)
     blocks = []
@@ -569,13 +562,10 @@
             )
         swapped = jnp.concatenate([turned(one, sign) for one in lines], axis=1)
         lines = jnp.concatenate(lines, axis=1)
-        if first == 0:
-            copies[0].wait()
         spectrum = jnp.concatenate(
             forward_line(table_ref, quarters_of(lines), quarters_of(swapped)), axis=0
         )
         modes = []
-        copies[2 + first // 2].wait()
         for n in range(2):
             j = first + n
             one = spectrum[:, n * LANES : (n + 1) * LANES]
@@ -585,8 +575,6 @@
             modes.append(scaled)
         swapped = jnp.concatenate([turned(one, sign) for one in modes], axis=1)
         modes = jnp.concatenate(modes, axis=1)
-        if first == 0:
-            copies[1].wait()
         parts = inverse_line(back_ref, quarters_of(modes), quarters_of(swapped))
         for n in range(2):
             for y in range(CY):
@@ -818,8 +806,8 @@
         grid_shape,
         [weights_space],
     )(atoms, where, base, taps)
-    green_shape = pltpu.HBM((NY, PART_X * LANES), f32)
-    green_space = pltpu.VMEM((NY, PART_X * LANES), f32)
+    green_shape = shape((NY, PART_X * LANES), f32)
+    table_shape = shape((NX, 6 * QUARTER), bf16)
     _, lines = call(
         lambda *refs: spread_kernel(False, *refs),
         "vsvvvhvv",
@@ -830,26 +818,23 @@
     lines, where, atoms, below_atoms = lax.optimization_barrier(
         (lines, where, atoms, below_atoms)
     )
-    *weights, green = call(
+    *weights, green, table, back = call(
         weights_kernel,
-        "svvvv",
-        (*(pltpu.HBM((pairs, *dims), kind) for dims, kind in held), green_shape),
+        "svvvvhh",
+        (
+            *(pltpu.HBM((pairs, *dims), kind) for dims, kind in held),
+            green_shape,
+            table_shape,
+            table_shape,
+        ),
         [
             *(pltpu.VMEM((pairs, *dims), kind) for dims, kind in held),
-            green_space,
             weights_space,
-            pltpu.SemaphoreType.DMA((7,)),
+            pltpu.SemaphoreType.DMA((8,)),
         ],
-    )(where, atoms, below_atoms, base, taps)
+    )(where, atoms, below_atoms, base, taps, y_forward, y_inverse)
     lines = swap_slabs(lines)
-    filtered = call(
-        filter_kernel,
-        "vhhh",
-        packed,
-        [table_space, table_space, green_space, pltpu.SemaphoreType.DMA((5,))],
-    )(
-        lines, y_forward, y_inverse, green
-    )
+    filtered = call(filter_kernel, "vvvv", packed)(lines, table, back, green)
     filtered = swap_slabs(filtered)
     shares_shape = shape((PENCILS, 8, ATOM_DEV), f32)
     below_shares, potential, *weights = call(

time: 112 us -> 110 us (0.982)
  waiting for transfers between devices: 23.9 us -> 22 us
  local copies, waits for them, and re-layouts: 0.01 us -> 1.81 us
  Pallas kernels: 27.8 us -> 26.5 us
    all_to_all x1, waiting for transfers between devices: 15.9 us -> 14.1 us  [swap_slabs(): lines = lax.all_to_all(lines, 'gy', split_axis=0, concat_axis=0, tiled=True)]
    unnamed x0 -> x10, local copies, waits for them, and re-layouts: none -> 1.81 us
    pallas_call x8, Pallas kernels: 27.8 us -> 26.5 us  [run(): pl.pallas_call(kernel, out_shape=out_shape, in_specs=[pl.BlockSpec(memory...]
where the time goes in v13:
time: 110 us; the launch traced here: 108 us
  blocking collectives  38.7 us (35%)
  Pallas kernels  26.5 us (24%)
  waiting for transfers between devices  22 us (20%)
  starting transfers between devices  17.6 us (16%)
  local copies, waits for them, and re-layouts  1.81 us (2%)
  between operations  1.4 us (1%)
    all_to_all x1, blocking collectives, swap_slabs(): lines = lax.all_to_all(lines, 'gy', split_axis=0, concat_axis=0, tiled=True)  28.8 us
    pallas_call x8, Pallas kernels, run(): pl.pallas_call(kernel, out_shape=out_shape, in_specs=[pl.BlockSpec(memory...  26.5 us
    all_to_all x1, waiting for transfers between devices, swap_slabs(): lines = lax.all_to_all(lines, 'gy', split_axis=0, concat_axis=0, tiled=True)  14.1 us
    all_gather x1, blocking collectives, on_device(): atoms = lax.all_gather(mine, 'gx', axis=0, tiled=False)  9.91 us
    ppermute x3, starting transfers between devices, on_device(): lax.ppermute(shares[ahead], 'gx', [(i, (i + ahead) % PENCILS) for i in ra...  7.62 us
    ppermute x2, waiting for transfers between devices, next_slab(): lax.ppermute(value, 'gy', [(i, (i + step) % SLABS) for i in range(SLABS)])  7.1 us
    all_to_all x1, starting transfers between devices, swap_slabs(): lines = lax.all_to_all(lines, 'gy', split_axis=0, concat_axis=0, tiled=True)  6.44 us
    ppermute x2, starting transfers between devices, next_slab(): lax.ppermute(value, 'gy', [(i, (i + step) % SLABS) for i in range(SLABS)])  3.55 us
  transfers between devices with their start and end apart: 6, of which 4 were waited for; matrix products, arithmetic and copies ran while one was open for 0% of the time, Pallas kernels for 11%

profile of v13, /device:TPU:1, one launch (start us, length us, event | category | flops | bytes accessed | tf_op | source)
XLA Modules:
  0.0 108.2 jit_solution(11116979556758588516)
XLA Ops:
  1.3 0.1 pad_add_fusion.where_ref.refs_1_
  1.4 1.3 %shard_map.129 = (f32[16,384]{1,0:T(8,128)S(1)}, f32[8,128]{1,0:T(8,128)S(1)}, f32[6,48,128]{2,1,0:T(8,128)S(1)}, f32[384,128]{1,0:T(8,128)S(1)}, f32[384,128]{1,0:T(8,128)S(1)}) custom-call(s32[4]{0:T(128)S(1)} %pad_add_fusion.where_ref.refs_1_, s32[1]{0:T(128)} %copy.18.shear_ref, s32[6]{0:T(128)} %counts_ref.1, s32[3,384]{1,0:T(4,128)} %cells_ref.1, ...), custom_call_target="tpu_custom_call" | custom-call | flops 1000000000 | bytes 8000000 | tf_op jit(solution)/shard_map/pallas_call | solution.py:730
  2.7 0.0 copy-start.3
  2.7 9.9 %all-gather = f32[64,384]{1,0:T(8,128)S(1)} all-gather(f32[16,384]{1,0:T(8,128)S(1)} %get-tuple-element.29), channel_id=2, replica_groups=mesh['gy'=64,'gx'=4] {'gx'}, dimensions={0}, use_global_device_ids=true | all-gather | bytes 122880 | tf_op jit(solution)/shard_map/all_gather | solution.py:790
  12.6 0.0 copy-start
  12.6 0.0 collective-permute-start
  12.6 3.0 %shard_map.130.refs_4_ = f32[432,1536]{1,0:T(8,128)S(1)} custom-call(f32[4,16,384]{2,1,0:T(8,128)S(1)} %bitcast.23, s32[4]{0:T(128)S(1)} %pad_add_fusion.where_ref.refs_1_, f32[8,128]{1,0:T(8,128)S(1)} %get-tuple-element.30.refs_2_.base_ref, f32[6,48,128]{2,1,0:T(8,128)S(1)} %get-tuple-element.31.refs_3_.taps_ref), custom_call_target="tpu_custom_call" | custom-call | flops 1000000000 | bytes 8000000 | tf_op jit(solution)/shard_map/pallas_call | solution.py:730
  15.7 0.0 copy-done
  15.7 7.1 %collective-permute-done.refs_0_.below_ref = f32[4,16,384]{2,1,0:T(8,128)S(1)} collective-permute-done((f32[4,16,384]{2,1,0:T(8,128)S(1)}, f32[4,16,384]{2,1,0:T(8,128)S(1)}, u32[]{:S(2)}, u32[]{:S(2)}) %collective-permute-start) | collective-permute-done | bytes 98336 | tf_op jit(solution)/shard_map/ppermute | solution.py:746
  22.8 0.0 copy-done.3
  22.8 5.5 %shard_map.131 = (f32[432,1536]{1,0:T(8,128)S(1)}, f32[1728,128]{1,0:T(8,128)}) custom-call(f32[4,16,384]{2,1,0:T(8,128)S(1)} %collective-permute-done.refs_0_.below_ref, s32[4]{0:T(128)S(1)} %pad_add_fusion.where_ref.refs_1_, f32[8,128]{1,0:T(8,128)S(1)} %get-tuple-element.30.refs_2_.base_ref, ...), custom_call_target="tpu_custom_call", output_to_operand_aliasing={{0}: (4, {})} | custom-call | flops 1000000000 | bytes 8000000 | tf_op jit(solution)/shard_map/pallas_call | solution.py:730
  28.3 6.4 %all-to-all-start = ((f32[64,27,1,128]{3,2,1,0:T(1,128)}), f32[64,27,1,128]{3,2,1,0:T(1,128)S(1)}, u32[]{:S(2)}, u32[]{:S(2)}) async-start(f32[64,27,1,128]{3,2,1,0:T(1,128)} %bitcast.5), calls=%async_computation | async-start | bytes 1769472 | tf_op jit(solution)/shard_map/all_to_all | solution.py:751
  34.8 0.0 copy-start.1
  34.8 0.9 copy-done.1
  35.7 0.0 copy-start.4
  35.7 0.9 copy-done.4
  36.6 6.6 %shard_map.132 = (bf16[24,2,96,384]{3,2,1,0:T(8,128)(2,1)}, f32[24,3,48,128]{3,2,1,0:T(8,128)}, f32[24,3,16,128]{3,2,1,0:T(8,128)}, f32[384,768]{1,0:T(8,128)S(1...) custom-call(s32[4]{0:T(128)S(1)} %pad_add_fusion.where_ref.refs_1_, f32[4,16,384]{2,1,0:T(8,128)S(1)} %bitcast.24, ...), custom_call_target="tpu_custom_call" | custom-call | flops 1000000000 | bytes 8000000 | tf_op jit(solution)/shard_map/pallas_call | solution.py:730
  43.2 14.1 %all-to-all-done = f32[64,27,1,128]{3,2,1,0:T(1,128)S(1)} async-done(((f32[64,27,1,128]{3,2,1,0:T(1,128)}), f32[64,27,1,128]{3,2,1,0:T(1,128)S(1)}, u32[]{:S(2)}, u32[]{:S(2)}) %all-to-all-start) | async-done | bytes 884768 | tf_op jit(solution)/shard_map/all_to_all | solution.py:751
  57.3 2.4 %shard_map.133 = f32[1728,128]{1,0:T(8,128)S(1)} custom-call(f32[1728,128]{1,0:T(8,128)S(1)} %bitcast.19, bf16[384,576]{1,0:T(8,128)(2,1)S(1)} %get-tuple-element.42.table_ref, bf16[384,576]{1,0:T(8,128)(2,1)S(1)} %get-tuple-element.43.back_ref, f32[384,768]{1,0:T(8,128)S(1)} %get-tuple-element.44.green_ref), custom_call_target="tpu_custom_call" | custom-call | flops 1000000000 | bytes 8000000 | tf_op jit(solution)/shard_map/pallas_call | solution.py:730
  59.8 28.8 %all_to_all.10 = f32[64,27,1,128]{3,2,1,0:T(1,128)S(1)} all-to-all(f32[64,27,1,128]{3,2,1,0:T(1,128)S(1)} %bitcast.20), channel_id=1, replica_groups=mesh['gy'=64,'gx'=4] {'gy'}, dimensions={0} | all-to-all | bytes 1769472 | tf_op jit(solution)/shard_map/all_to_all | solution.py:751
  88.6 0.0 copy-start.2
  88.6 4.7 %shard_map.134 = (f32[4,8,384]{2,1,0:T(8,128)S(1)}, f32[432,768]{1,0:T(8,128)S(1)}, bf16[12,2,96,384]{3,2,1,0:T(8,128)(2,1)S(1)}, f32[12,3,48,128]{3,2,1,0:T(8,128)S(1)}, f32[12,3,16,128]{3,2,1,0:T(8,128)S(1)}) custom-call(f32[4,16,384]{2,1,0:T(8,128)S(1)} %collective-permute-done.refs_0_.below_ref, s32[4]{0:T(128)S(1)} %pad_add_fusion.where_ref.refs_1_, ...), custom_call_target="tpu_custom_call" | custom-call | flops 1000000000 | bytes 8000000 | tf_op jit(solution)/shard_map/pallas_call | solution.py:730
  93.2 3.5 %collective-permute-start.1 = (f32[4,8,384]{2,1,0:T(8,128)S(1)}, f32[4,8,384]{2,1,0:T(8,128)S(1)}, u32[]{:S(2)}, u32[]{:S(2)}) collective-permute-start(f32[4,8,384]{2,1,0:T(8,128)S(1)} %get-tuple-element.49), channel_id=1, source_target_pairs={{0,252},{4,0},{8,4},{12,8},{16,12},{20,16},{24,20},{28,24},{32,28}... | collective-permute-start | bytes 147464 | tf_op jit(solution)/shard_map/ppermute | solution.py:746
  96.8 0.0 copy-done.2
  96.8 2.3 %shard_map.135 = f32[4,8,384]{2,1,0:T(8,128)S(1)} custom-call(f32[4,16,384]{2,1,0:T(8,128)S(1)} %bitcast.25, s32[4]{0:T(128)S(1)} %pad_add_fusion.where_ref.refs_1_, bf16[12,2,96,384]{3,2,1,0:T(8,128)(2,1)S(1)} %get-tuple-element.45.refs_2_, f32[12,3,48,128]{3,2,1,0:T(8,128)S(1)} %get-tuple-element.46.refs_3_, ...), custom_call_target="tpu_custom_call" | custom-call | flops 1000000000 | bytes 8000000 | tf_op jit(solution)/shard_map/pallas_call | solution.py:730
  99.1 0.0 collective-permute-done.1
  99.1 4.4 %collective-permute-start.4 = (f32[8,384]{1,0:T(8,128)S(1)}, f32[8,384]{1,0:T(8,128)S(1)}, u32[]{:S(2)}, u32[]{:S(2)}) collective-permute-start(f32[8,384]{1,0:T(8,128)S(1)} %get-tuple-element.54), channel_id=1, source_target_pairs={{0,3},{1,0},{2,1},{3,2},{4,7},{5,4},{6,5},{7,6},{8,11},{9,8},{10,9... | collective-permute-start | bytes 36872 | tf_op jit(solution)/shard_map/ppermute | solution.py:860
  103.5 2.6 %collective-permute-start.3 = (f32[8,384]{1,0:T(8,128)S(1)}, f32[8,384]{1,0:T(8,128)S(1)}, u32[]{:S(2)}, u32[]{:S(2)}) collective-permute-start(f32[8,384]{1,0:T(8,128)S(1)} %get-tuple-element.55), channel_id=1, source_target_pairs={{0,2},{1,3},{2,0},{3,1},{4,6},{5,7},{6,4},{7,5},{8,10},{9,11},{10,... | collective-permute-start | bytes 36872 | tf_op jit(solution)/shard_map/ppermute | solution.py:860
  106.1 0.6 collective-permute-start.2
  106.7 0.6 collective-permute-done.4.three_ref
  107.4 0.2 collective-permute-done.3.two_ref
  107.6 0.0 collective-permute-done.2.one_ref
  107.6 0.6 shard_map.136
  (2 shorter events, 0.0 us)
Async XLA Ops:
  2.7 20.1 %copy-start.3 = (f32[6,48,128]{2,1,0:T(8,128)}, f32[6,48,128]{2,1,0:T(8,128)S(1)}, u32[]{:S(2)}) copy-start(f32[6,48,128]{2,1,0:T(8,128)S(1)} %get-tuple-element.31.refs_3_.taps_ref) | copy-start | bytes 442372
  12.6 3.0 %copy-start = (f32[64,384]{1,0:T(8,128)}, f32[64,384]{1,0:T(8,128)S(1)}, u32[]{:S(2)}) copy-start(f32[64,384]{1,0:T(8,128)S(1)} %all-gather) | copy-start | bytes 294916
  12.6 10.1 %collective-permute-start = (f32[4,16,384]{2,1,0:T(8,128)S(1)}, f32[4,16,384]{2,1,0:T(8,128)S(1)}, u32[]{:S(2)}, u32[]{:S(2)}) collective-permute-start(f32[4,16,384]{2,1,0:T(8,128)S(1)} %bitcast.22), channel_id=1, source_target_pairs={{0,4},{4,8},{8,12},{12,16},{16,20},{20,24},{24,28},{28,32},{32,36}... | collective-permute-start | bytes 294920 | tf_op jit(solution)/shard_map/ppermute | solution.py:746
  28.3 29.0 %all-to-all-start = ((f32[64,27,1,128]{3,2,1,0:T(1,128)}), f32[64,27,1,128]{3,2,1,0:T(1,128)S(1)}, u32[]{:S(2)}, u32[]{:S(2)}) async-start(f32[64,27,1,128]{3,2,1,0:T(1,128)} %bitcast.5), calls=%async_computation | async-start | bytes 1769472 | tf_op jit(solution)/shard_map/all_to_all | solution.py:751
  34.8 0.9 copy-start.1
  35.7 0.9 copy-start.4
  88.6 8.2 %copy-start.2 = (f32[64,384]{1,0:T(8,128)S(1)}, f32[64,384]{1,0:T(8,128)}, u32[]{:S(2)}) copy-start(f32[64,384]{1,0:T(8,128)} %copy-done) | copy-start | bytes 294916
  93.2 5.8 %collective-permute-start.1 = (f32[4,8,384]{2,1,0:T(8,128)S(1)}, f32[4,8,384]{2,1,0:T(8,128)S(1)}, u32[]{:S(2)}, u32[]{:S(2)}) collective-permute-start(f32[4,8,384]{2,1,0:T(8,128)S(1)} %get-tuple-element.49), channel_id=1, source_target_pairs={{0,252},{4,0},{8,4},{12,8},{16,12},{20,16},{24,20},{28,24},{32,28}... | collective-permute-start | bytes 147464 | tf_op jit(solution)/shard_map/ppermute | solution.py:746
  99.1 8.3 %collective-permute-start.4 = (f32[8,384]{1,0:T(8,128)S(1)}, f32[8,384]{1,0:T(8,128)S(1)}, u32[]{:S(2)}, u32[]{:S(2)}) collective-permute-start(f32[8,384]{1,0:T(8,128)S(1)} %get-tuple-element.54), channel_id=1, source_target_pairs={{0,3},{1,0},{2,1},{3,2},{4,7},{5,4},{6,5},{7,6},{8,11},{9,8},{10,9... | collective-permute-start | bytes 36872 | tf_op jit(solution)/shard_map/ppermute | solution.py:860
  103.5 4.1 %collective-permute-start.3 = (f32[8,384]{1,0:T(8,128)S(1)}, f32[8,384]{1,0:T(8,128)S(1)}, u32[]{:S(2)}, u32[]{:S(2)}) collective-permute-start(f32[8,384]{1,0:T(8,128)S(1)} %get-tuple-element.55), channel_id=1, source_target_pairs={{0,2},{1,3},{2,0},{3,1},{4,6},{5,7},{6,4},{7,5},{8,10},{9,11},{10,... | collective-permute-start | bytes 36872 | tf_op jit(solution)/shard_map/ppermute | solution.py:860
  106.1 1.4 %collective-permute-start.2 = (f32[8,384]{1,0:T(8,128)S(1)}, f32[8,384]{1,0:T(8,128)S(1)}, u32[]{:S(2)}, u32[]{:S(2)}) collective-permute-start(f32[8,384]{1,0:T(8,128)S(1)} %get-tuple-element.56), channel_id=1, source_target_pairs={{0,1},{1,2},{2,3},{3,0},{4,5},{5,6},{6,7},{7,4},{8,9},{9,10},{10,1... | collective-permute-start | bytes 36872 | tf_op jit(solution)/shard_map/ppermute | solution.py:860

commit v14 on v13

--- a/solution.py
+++ b/solution.py
@@ -365,21 +365,18 @@
     ]
 
 
-def sampling_weights(
-    start, own, where_ref, some_ref, table_ref, base_ref, taps_ref, waves_ref, x_ref, y_ref
-):
+def sampling_weights(start, some_ref, table_ref, base_ref, taps_ref, waves_ref, rows_ref):
     spline_table(some_ref, table_ref, 3)
 
     def pair_body(pair, carry):
         pencil, lanes = pair_place(pair)
-        row = [some_ref[pencil, a : a + 1, lanes] for a in range(3)]
-        _, window, origin = pair_window(pair, own, where_ref)
-        dense_x = dense_rows(weight_rows(table_ref, pencil, lanes, 0, 3), row[0] - origin, window)
-        dense_y = dense_rows(weight_rows(table_ref, pencil, lanes, 1, 3), row[1], 16)
-        for p in range(3):
-            x_ref[start + pair, p, :window] = dense_x[p]
-            y_ref[start + pair, p] = dense_y[p]
-        waves = z_waves(row[2], weight_rows(table_ref, pencil, lanes, 2, 3), base_ref, taps_ref)
+        for dim in range(2):
+            for o, taps in enumerate(weight_rows(table_ref, pencil, lanes, dim, 3)):
+                for t in range(6):
+                    row = (dim * 3 + o) * 6 + t
+                    rows_ref[start + pair, row : row + 1, :] = taps[t]
+        weights = weight_rows(table_ref, pencil, lanes, 2, 3)
+        waves = z_waves(some_ref[pencil, 2:3, lanes], weights, base_ref, taps_ref)
         for s, (re, im) in enumerate(waves):
             re, im = halves(re), halves(im)
             columns = slice(s * LANES, (s + 1) * LANES)
@@ -528,8 +525,8 @@
 def weights_kernel(
     where_ref, atoms_ref, below_ref, base_ref, taps_ref, tables_ref, backs_ref, *refs
 ):
-    results, (green_ref, table_ref, back_ref), kept = refs[:3], refs[3:6], refs[6:9]
-    weights_ref, semaphores = refs[9:]
+    results, (green_ref, table_ref, back_ref), kept = refs[:2], refs[2:5], refs[5:7]
+    weights_ref, semaphores = refs[7:]
     copies = [
         fetch(tables_ref, table_ref, semaphores.at[6]),
         fetch(backs_ref, back_ref, semaphores.at[7]),
@@ -538,10 +535,10 @@
     pairs = PENCILS * PAIRS
     for own, some_ref in ((True, atoms_ref), (False, below_ref)):
         start = 0 if own else pairs
-        sampling_weights(start, own, where_ref, some_ref, weights_ref, base_ref, taps_ref, *kept)
+        sampling_weights(start, some_ref, weights_ref, base_ref, taps_ref, *kept)
         some = pl.ds(start, pairs)
-        for n in range(3):
-            semaphore = semaphores.at[n if own else 3 + n]
+        for n in range(2):
+            semaphore = semaphores.at[n if own else 2 + n]
             copies.append(fetch(kept[n].at[some], results[n].at[some], semaphore))
     for copy in copies:
         copy.wait()
@@ -597,21 +594,21 @@
 
 def sample_kernel(own, *refs):
     if own:
-        atoms_ref, where_ref, waves_ref, x_ref, y_ref, grid_ref, out_ref = refs
+        atoms_ref, where_ref, waves_ref, rows_ref, grid_ref, out_ref = refs
     else:
         atoms_ref, where_ref = refs[:2]
-        kept = refs[2:5]
-        in_ref, cos_ref, sin_ref, tables_ref, out_ref, grid_ref = refs[5:11]
-        slab_weights, below_weights = refs[11:14], refs[14:17]
-        waves_ref, x_ref, y_ref = below_weights
-        table_ref, semaphores = refs[17:]
+        kept = refs[2:4]
+        in_ref, cos_ref, sin_ref, tables_ref, out_ref, grid_ref = refs[4:10]
+        slab_weights, below_weights = refs[10:12], refs[12:14]
+        waves_ref, rows_ref = below_weights
+        table_ref, semaphores = refs[14:]
         table_copy = fetch(tables_ref, table_ref, semaphores.at[6])
         pairs = PENCILS * PAIRS
         copies = [
             fetch(source.at[pl.ds(start, pairs)], target, semaphores.at[n])
             for n, (source, start, target) in enumerate(
-                [(kept[n], pairs, below_weights[n]) for n in range(3)]
-                + [(kept[n], 0, slab_weights[n]) for n in range(3)]
+                [(kept[n], pairs, below_weights[n]) for n in range(2)]
+                + [(kept[n], 0, slab_weights[n]) for n in range(2)]
             )
         ]
     rows = list(range(CY)) if own else list(range(CY, 2 * CY - 1))
@@ -642,7 +639,7 @@
     gap = jnp.zeros((HALF - PADDED_Z, 3 * LANES), bf16)
 
     if not own:
-        for copy in copies[:3]:
+        for copy in copies[:2]:
             copy.wait()
 
     def pair_body(pair, carry):
@@ -654,14 +651,21 @@
             )
             for n in range(2)
         ]
-        first_row, window, _ = pair_window(pair, own, where_ref)
+        first_row, window, origin = pair_window(pair, own, where_ref)
         at = pl.ds(first_row, window)
         cells = jnp.concatenate(
             [grid_ref[at, n * LANES : (n + 1) * LANES] for n in range(len(rows))], axis=0
         )
         read = product(halves(cells), waves)
-        dense_x = [x_ref[pair, p, :window] for p in range(3)]
-        dense_y = [y_ref[pair, p] for p in range(3)]
+        rows_x, rows_y = [
+            [
+                [rows_ref[pair, row + t : row + t + 1, :] for t in range(6)]
+                for row in range(dim * 18, dim * 18 + 18, 6)
+            ]
+            for dim in range(2)
+        ]
+        dense_x = dense_rows(rows_x, atoms_ref[pencil, 0:1, lanes] - origin, window)
+        dense_y = dense_rows(rows_y, atoms_ref[pencil, 1:2, lanes], 16)
         lined = {}
         for order_y, order_z in ((0, 0), (1, 0), (2, 0), (0, 1), (1, 1), (0, 2)):
             lined[order_y, order_z] = sum(
@@ -698,7 +702,7 @@
 
     lax.fori_loop(0, PENCILS * PAIRS, pair_body, 0, unroll=12)
     if not own:
-        for copy in copies[3:]:
+        for copy in copies[2:]:
             copy.wait()
 
 
@@ -795,8 +799,7 @@
     pairs = 2 * PENCILS * PAIRS
     held = [
         ((2, 2 * PADDED_Z, 3 * LANES), bf16),
-        ((3, WIDE, LANES), f32),
-        ((3, 16, LANES), f32),
+        ((36, LANES), f32),
     ]
     weights_space = pltpu.VMEM((PENCILS, 18, 8, ATOM_DEV), f32)
     grid_shape = shape((EXTENDED, 2 * CY * LANES), f32)
@@ -839,7 +842,7 @@
     shares_shape = shape((PENCILS, 8, ATOM_DEV), f32)
     below_shares, potential, *weights = call(
         lambda *refs: sample_kernel(False, *refs),
-        "vshhhvvvh",
+        "vshhvvvh",
         (
             shares_shape,
             shape((EXTENDED, CY * LANES), f32),
@@ -852,7 +855,7 @@
         ],
     )(below_atoms, where, *weights, filtered, cos_t, sin_t, x_inverse)
     below_shares = next_slab(below_shares, back=True)
-    shares = call(lambda *refs: sample_kernel(True, *refs), "vsvvvv", shares_shape)(
+    shares = call(lambda *refs: sample_kernel(True, *refs), "vsvvv", shares_shape)(
         atoms, where, *weights, potential
     )
     shares = shares + below_shares

time: 110 us -> 110 us (level)
  transfers between devices with their start and end apart: 6 -> 6, of which waited for: 4 -> 4; matrix products, arithmetic and copies ran while one was open for 0% -> 0% of each run, Pallas kernels for 11% -> 10%
where the time goes in v14:
time: 110 us; the launch traced here: 108 us
  blocking collectives  38.7 us (35%)
  Pallas kernels  25.5 us (23%)
  waiting for transfers between devices  23 us (21%)
  starting transfers between devices  17.6 us (16%)
  local copies, waits for them, and re-layouts  1.81 us (2%)
  between operations  1.41 us (1%)
    all_to_all x1, blocking collectives, swap_slabs(): lines = lax.all_to_all(lines, 'gy', split_axis=0, concat_axis=0, tiled=True)  28.8 us
    pallas_call x8, Pallas kernels, run(): pl.pallas_call(kernel, out_shape=out_shape, in_specs=[pl.BlockSpec(memory...  25.5 us
    all_to_all x1, waiting for transfers between devices, swap_slabs(): lines = lax.all_to_all(lines, 'gy', split_axis=0, concat_axis=0, tiled=True)  15.1 us
    all_gather x1, blocking collectives, on_device(): atoms = lax.all_gather(mine, 'gx', axis=0, tiled=False)  9.91 us
    ppermute x3, starting transfers between devices, on_device(): lax.ppermute(shares[ahead], 'gx', [(i, (i + ahead) % PENCILS) for i in ra...  7.62 us
    ppermute x2, waiting for transfers between devices, next_slab(): lax.ppermute(value, 'gy', [(i, (i + step) % SLABS) for i in range(SLABS)])  7.11 us
    all_to_all x1, starting transfers between devices, swap_slabs(): lines = lax.all_to_all(lines, 'gy', split_axis=0, concat_axis=0, tiled=True)  6.44 us
    ppermute x2, starting transfers between devices, next_slab(): lax.ppermute(value, 'gy', [(i, (i + step) % SLABS) for i in range(SLABS)])  3.55 us
  transfers between devices with their start and end apart: 6, of which 4 were waited for; matrix products, arithmetic and copies ran while one was open for 0% of the time, Pallas kernels for 10%

profile of v14, /device:TPU:1, one launch (start us, length us, event | category | flops | bytes accessed | tf_op | source)
XLA Modules:
  0.0 108.1 jit_solution(14415536066601194122)
XLA Ops:
  1.3 0.1 pad_add_fusion.where_ref.refs_1_
  1.4 1.3 %shard_map.129 = (f32[16,384]{1,0:T(8,128)S(1)}, f32[8,128]{1,0:T(8,128)S(1)}, f32[6,48,128]{2,1,0:T(8,128)S(1)}, f32[384,128]{1,0:T(8,128)S(1)}, f32[384,128]{1,0:T(8,128)S(1)}) custom-call(s32[4]{0:T(128)S(1)} %pad_add_fusion.where_ref.refs_1_, s32[1]{0:T(128)} %copy.18.shear_ref, s32[6]{0:T(128)} %counts_ref.1, s32[3,384]{1,0:T(4,128)} %cells_ref.1, ...), custom_call_target="tpu_custom_call" | custom-call | flops 1000000000 | bytes 8000000 | tf_op jit(solution)/shard_map/pallas_call | solution.py:734
  2.7 0.0 copy-start
  2.7 9.9 %all-gather = f32[64,384]{1,0:T(8,128)S(1)} all-gather(f32[16,384]{1,0:T(8,128)S(1)} %get-tuple-element.27), channel_id=2, replica_groups=mesh['gy'=64,'gx'=4] {'gx'}, dimensions={0}, use_global_device_ids=true | all-gather | bytes 122880 | tf_op jit(solution)/shard_map/all_gather | solution.py:794
  12.6 0.0 copy-start.2
  12.6 0.0 collective-permute-start
  12.6 3.0 %shard_map.130.refs_4_ = f32[432,1536]{1,0:T(8,128)S(1)} custom-call(f32[4,16,384]{2,1,0:T(8,128)S(1)} %bitcast.23, s32[4]{0:T(128)S(1)} %pad_add_fusion.where_ref.refs_1_, f32[8,128]{1,0:T(8,128)S(1)} %get-tuple-element.28.refs_2_.base_ref, f32[6,48,128]{2,1,0:T(8,128)S(1)} %get-tuple-element.29.refs_3_.taps_ref), custom_call_target="tpu_custom_call" | custom-call | flops 1000000000 | bytes 8000000 | tf_op jit(solution)/shard_map/pallas_call | solution.py:734
  15.7 7.1 %collective-permute-done.refs_0_.below_ref = f32[4,16,384]{2,1,0:T(8,128)S(1)} collective-permute-done((f32[4,16,384]{2,1,0:T(8,128)S(1)}, f32[4,16,384]{2,1,0:T(8,128)S(1)}, u32[]{:S(2)}, u32[]{:S(2)}) %collective-permute-start) | collective-permute-done | bytes 98336 | tf_op jit(solution)/shard_map/ppermute | solution.py:750
  22.8 5.5 %shard_map.131 = (f32[432,1536]{1,0:T(8,128)S(1)}, f32[1728,128]{1,0:T(8,128)}) custom-call(f32[4,16,384]{2,1,0:T(8,128)S(1)} %collective-permute-done.refs_0_.below_ref, s32[4]{0:T(128)S(1)} %pad_add_fusion.where_ref.refs_1_, f32[8,128]{1,0:T(8,128)S(1)} %get-tuple-element.28.refs_2_.base_ref, ...), custom_call_target="tpu_custom_call", output_to_operand_aliasing={{0}: (4, {})} | custom-call | flops 1000000000 | bytes 8000000 | tf_op jit(solution)/shard_map/pallas_call | solution.py:734
  28.3 0.0 copy-done
  28.3 0.0 copy-done.2
  28.3 6.4 %all-to-all-start = ((f32[64,27,1,128]{3,2,1,0:T(1,128)}), f32[64,27,1,128]{3,2,1,0:T(1,128)S(1)}, u32[]{:S(2)}, u32[]{:S(2)}) async-start(f32[64,27,1,128]{3,2,1,0:T(1,128)} %bitcast.5), calls=%async_computation | async-start | bytes 1769472 | tf_op jit(solution)/shard_map/all_to_all | solution.py:755
  34.8 0.0 copy-start.1
  34.8 0.9 copy-done.1
  35.7 0.0 copy-start.3
  35.7 0.9 copy-done.3
  36.6 5.7 %shard_map.132 = (bf16[24,2,96,384]{3,2,1,0:T(8,128)(2,1)}, f32[24,36,128]{2,1,0:T(8,128)}, f32[384,768]{1,0:T(8,128)S(1)}, bf16[384,576]{1,0:T(8,128)(2,1)S(1)}, bf16[384,576]{1,0:T(8,128)(2,1)S(1)}) custom-call(s32[4]{0:T(128)S(1)} %pad_add_fusion.where_ref.refs_1_, f32[4,16,384]{2,1,0:T(8,128)S(1)} %bitcast.24, ...), custom_call_target="tpu_custom_call" | custom-call | flops 1000000000 | bytes 8000000 | tf_op jit(solution)/shard_map/pallas_call | solution.py:734
  42.3 15.1 %all-to-all-done = f32[64,27,1,128]{3,2,1,0:T(1,128)S(1)} async-done(((f32[64,27,1,128]{3,2,1,0:T(1,128)}), f32[64,27,1,128]{3,2,1,0:T(1,128)S(1)}, u32[]{:S(2)}, u32[]{:S(2)}) %all-to-all-start) | async-done | bytes 884768 | tf_op jit(solution)/shard_map/all_to_all | solution.py:755
  57.4 2.4 %shard_map.133 = f32[1728,128]{1,0:T(8,128)S(1)} custom-call(f32[1728,128]{1,0:T(8,128)S(1)} %bitcast.20, bf16[384,576]{1,0:T(8,128)(2,1)S(1)} %get-tuple-element.39.table_ref, bf16[384,576]{1,0:T(8,128)(2,1)S(1)} %get-tuple-element.40.back_ref, f32[384,768]{1,0:T(8,128)S(1)} %get-tuple-element.41.green_ref), custom_call_target="tpu_custom_call" | custom-call | flops 1000000000 | bytes 8000000 | tf_op jit(solution)/shard_map/pallas_call | solution.py:734
  59.8 28.8 %all_to_all.10 = f32[64,27,1,128]{3,2,1,0:T(1,128)S(1)} all-to-all(f32[64,27,1,128]{3,2,1,0:T(1,128)S(1)} %bitcast.21), channel_id=1, replica_groups=mesh['gy'=64,'gx'=4] {'gy'}, dimensions={0} | all-to-all | bytes 1769472 | tf_op jit(solution)/shard_map/all_to_all | solution.py:755
  88.6 0.0 copy-start.4
  88.6 4.6 %shard_map.134 = (f32[4,8,384]{2,1,0:T(8,128)S(1)}, f32[432,768]{1,0:T(8,128)S(1)}, bf16[12,2,96,384]{3,2,1,0:T(8,128)(2,1)S(1)}, f32[12,36,128]{2,1,0:T(8,128)S(1)}) custom-call(f32[4,16,384]{2,1,0:T(8,128)S(1)} %collective-permute-done.refs_0_.below_ref, s32[4]{0:T(128)S(1)} %pad_add_fusion.where_ref.refs_1_, ...), custom_call_target="tpu_custom_call" | custom-call | flops 1000000000 | bytes 8000000 | tf_op jit(solution)/shard_map/pallas_call | solution.py:734
  93.2 3.5 %collective-permute-start.1 = (f32[4,8,384]{2,1,0:T(8,128)S(1)}, f32[4,8,384]{2,1,0:T(8,128)S(1)}, u32[]{:S(2)}, u32[]{:S(2)}) collective-permute-start(f32[4,8,384]{2,1,0:T(8,128)S(1)} %get-tuple-element.45), channel_id=1, source_target_pairs={{0,252},{4,0},{8,4},{12,8},{16,12},{20,16},{24,20},{28,24},{32,28}... | collective-permute-start | bytes 147464 | tf_op jit(solution)/shard_map/ppermute | solution.py:750
  96.7 0.0 copy-done.4
  96.7 2.3 %shard_map.135 = f32[4,8,384]{2,1,0:T(8,128)S(1)} custom-call(f32[4,16,384]{2,1,0:T(8,128)S(1)} %bitcast.25, s32[4]{0:T(128)S(1)} %pad_add_fusion.where_ref.refs_1_, bf16[12,2,96,384]{3,2,1,0:T(8,128)(2,1)S(1)} %get-tuple-element.42.refs_2_, f32[12,36,128]{2,1,0:T(8,128)S(1)} %get-tuple-element.43.refs_3_, f32[432,768]{1,0:T(8,128)S(1)} %get-tuple-element.44.refs_4_), custom_call_target="tpu_custom_call" | custom-call | flops 1000000000 | bytes 8000000 | tf_op jit(solution)/shard_map/pallas_call | solution.py:734
  99.0 0.0 collective-permute-done.1
  99.1 4.4 %collective-permute-start.4 = (f32[8,384]{1,0:T(8,128)S(1)}, f32[8,384]{1,0:T(8,128)S(1)}, u32[]{:S(2)}, u32[]{:S(2)}) collective-permute-start(f32[8,384]{1,0:T(8,128)S(1)} %get-tuple-element.50), channel_id=1, source_target_pairs={{0,3},{1,0},{2,1},{3,2},{4,7},{5,4},{6,5},{7,6},{8,11},{9,8},{10,9... | collective-permute-start | bytes 36872 | tf_op jit(solution)/shard_map/ppermute | solution.py:863
  103.5 2.6 %collective-permute-start.3 = (f32[8,384]{1,0:T(8,128)S(1)}, f32[8,384]{1,0:T(8,128)S(1)}, u32[]{:S(2)}, u32[]{:S(2)}) collective-permute-start(f32[8,384]{1,0:T(8,128)S(1)} %get-tuple-element.51), channel_id=1, source_target_pairs={{0,2},{1,3},{2,0},{3,1},{4,6},{5,7},{6,4},{7,5},{8,10},{9,11},{10,... | collective-permute-start | bytes 36872 | tf_op jit(solution)/shard_map/ppermute | solution.py:863
  106.1 0.6 collective-permute-start.2
  106.7 0.6 collective-permute-done.4.three_ref
  107.3 0.2 collective-permute-done.3.two_ref
  107.5 0.0 collective-permute-done.2.one_ref
  107.5 0.6 shard_map.136
  (2 shorter events, 0.0 us)
Async XLA Ops:
  2.7 25.6 %copy-start = (f32[6,48,128]{2,1,0:T(8,128)}, f32[6,48,128]{2,1,0:T(8,128)S(1)}, u32[]{:S(2)}) copy-start(f32[6,48,128]{2,1,0:T(8,128)S(1)} %get-tuple-element.29.refs_3_.taps_ref) | copy-start | bytes 442372
  12.6 15.7 %copy-start.2 = (f32[64,384]{1,0:T(8,128)}, f32[64,384]{1,0:T(8,128)S(1)}, u32[]{:S(2)}) copy-start(f32[64,384]{1,0:T(8,128)S(1)} %all-gather) | copy-start | bytes 294916
  12.6 10.1 %collective-permute-start = (f32[4,16,384]{2,1,0:T(8,128)S(1)}, f32[4,16,384]{2,1,0:T(8,128)S(1)}, u32[]{:S(2)}, u32[]{:S(2)}) collective-permute-start(f32[4,16,384]{2,1,0:T(8,128)S(1)} %bitcast.22), channel_id=1, source_target_pairs={{0,4},{4,8},{8,12},{12,16},{16,20},{20,24},{24,28},{28,32},{32,36}... | collective-permute-start | bytes 294920 | tf_op jit(solution)/shard_map/ppermute | solution.py:750
  28.3 29.0 %all-to-all-start = ((f32[64,27,1,128]{3,2,1,0:T(1,128)}), f32[64,27,1,128]{3,2,1,0:T(1,128)S(1)}, u32[]{:S(2)}, u32[]{:S(2)}) async-start(f32[64,27,1,128]{3,2,1,0:T(1,128)} %bitcast.5), calls=%async_computation | async-start | bytes 1769472 | tf_op jit(solution)/shard_map/all_to_all | solution.py:755
  34.8 0.9 copy-start.1
  35.7 0.9 copy-start.3
  88.6 8.2 %copy-start.4 = (f32[64,384]{1,0:T(8,128)S(1)}, f32[64,384]{1,0:T(8,128)}, u32[]{:S(2)}) copy-start(f32[64,384]{1,0:T(8,128)} %copy-done.2) | copy-start | bytes 294916
  93.2 5.9 %collective-permute-start.1 = (f32[4,8,384]{2,1,0:T(8,128)S(1)}, f32[4,8,384]{2,1,0:T(8,128)S(1)}, u32[]{:S(2)}, u32[]{:S(2)}) collective-permute-start(f32[4,8,384]{2,1,0:T(8,128)S(1)} %get-tuple-element.45), channel_id=1, source_target_pairs={{0,252},{4,0},{8,4},{12,8},{16,12},{20,16},{24,20},{28,24},{32,28}... | collective-permute-start | bytes 147464 | tf_op jit(solution)/shard_map/ppermute | solution.py:750
  99.1 8.3 %collective-permute-start.4 = (f32[8,384]{1,0:T(8,128)S(1)}, f32[8,384]{1,0:T(8,128)S(1)}, u32[]{:S(2)}, u32[]{:S(2)}) collective-permute-start(f32[8,384]{1,0:T(8,128)S(1)} %get-tuple-element.50), channel_id=1, source_target_pairs={{0,3},{1,0},{2,1},{3,2},{4,7},{5,4},{6,5},{7,6},{8,11},{9,8},{10,9... | collective-permute-start | bytes 36872 | tf_op jit(solution)/shard_map/ppermute | solution.py:863
  103.5 4.1 %collective-permute-start.3 = (f32[8,384]{1,0:T(8,128)S(1)}, f32[8,384]{1,0:T(8,128)S(1)}, u32[]{:S(2)}, u32[]{:S(2)}) collective-permute-start(f32[8,384]{1,0:T(8,128)S(1)} %get-tuple-element.51), channel_id=1, source_target_pairs={{0,2},{1,3},{2,0},{3,1},{4,6},{5,7},{6,4},{7,5},{8,10},{9,11},{10,... | collective-permute-start | bytes 36872 | tf_op jit(solution)/shard_map/ppermute | solution.py:863
  106.1 1.4 %collective-permute-start.2 = (f32[8,384]{1,0:T(8,128)S(1)}, f32[8,384]{1,0:T(8,128)S(1)}, u32[]{:S(2)}, u32[]{:S(2)}) collective-permute-start(f32[8,384]{1,0:T(8,128)S(1)} %get-tuple-element.52), channel_id=1, source_target_pairs={{0,1},{1,2},{2,3},{3,0},{4,5},{5,6},{6,7},{7,4},{8,9},{9,10},{10,1... | collective-permute-start | bytes 36872 | tf_op jit(solution)/shard_map/ppermute | solution.py:863

commit v15 on v14

--- a/solution.py
+++ b/solution.py
@@ -605,7 +605,7 @@
         table_copy = fetch(tables_ref, table_ref, semaphores.at[6])
         pairs = PENCILS * PAIRS
         copies = [
-            fetch(source.at[pl.ds(start, pairs)], target, semaphores.at[n])
+            pltpu.make_async_copy(source.at[pl.ds(start, pairs)], target, semaphores.at[n])
             for n, (source, start, target) in enumerate(
                 [(kept[n], pairs, below_weights[n]) for n in range(2)]
                 + [(kept[n], 0, slab_weights[n]) for n in range(2)]
@@ -628,6 +628,8 @@
             modes = jnp.concatenate(modes, axis=1)
             if first == 0:
                 table_copy.wait()
+                for copy in copies:
+                    copy.start()
             cells = jnp.concatenate(
                 inverse_line(table_ref, quarters_of(modes), quarters_of(swapped)), axis=0
             )

time: 110 us -> 111 us (level)
  no operation moved by 1% of the time
where the time goes in v15:
time: 111 us; the launch traced here: 109 us
  blocking collectives  38.7 us (35%)
  Pallas kernels  26.2 us (24%)
  waiting for transfers between devices  23 us (21%)
  starting transfers between devices  17.6 us (16%)
  local copies, waits for them, and re-layouts  1.81 us (2%)
  between operations  1.41 us (1%)
    all_to_all x1, blocking collectives, swap_slabs(): lines = lax.all_to_all(lines, 'gy', split_axis=0, concat_axis=0, tiled=True)  28.8 us
    pallas_call x8, Pallas kernels, run(): pl.pallas_call(kernel, out_shape=out_shape, in_specs=[pl.BlockSpec(memory...  26.2 us
    all_to_all x1, waiting for transfers between devices, swap_slabs(): lines = lax.all_to_all(lines, 'gy', split_axis=0, concat_axis=0, tiled=True)  15.1 us
    all_gather x1, blocking collectives, on_device(): atoms = lax.all_gather(mine, 'gx', axis=0, tiled=False)  9.91 us
    ppermute x3, starting transfers between devices, on_device(): lax.ppermute(shares[ahead], 'gx', [(i, (i + ahead) % PENCILS) for i in ra...  7.61 us
    ppermute x2, waiting for transfers between devices, next_slab(): lax.ppermute(value, 'gy', [(i, (i + step) % SLABS) for i in range(SLABS)])  7.11 us
    all_to_all x1, starting transfers between devices, swap_slabs(): lines = lax.all_to_all(lines, 'gy', split_axis=0, concat_axis=0, tiled=True)  6.44 us
    ppermute x2, starting transfers between devices, next_slab(): lax.ppermute(value, 'gy', [(i, (i + step) % SLABS) for i in range(SLABS)])  3.56 us
  transfers between devices with their start and end apart: 6, of which 4 were waited for; matrix products, arithmetic and copies ran while one was open for 0% of the time, Pallas kernels for 10%

profile of v15, /device:TPU:1, one launch (start us, length us, event | category | flops | bytes accessed | tf_op | source)
XLA Modules:
  0.0 108.8 jit_solution(13403747494462894011)
XLA Ops:
  1.3 0.1 pad_add_fusion.where_ref.refs_1_
  1.4 1.3 %shard_map.129 = (f32[16,384]{1,0:T(8,128)S(1)}, f32[8,128]{1,0:T(8,128)S(1)}, f32[6,48,128]{2,1,0:T(8,128)S(1)}, f32[384,128]{1,0:T(8,128)S(1)}, f32[384,128]{1,0:T(8,128)S(1)}) custom-call(s32[4]{0:T(128)S(1)} %pad_add_fusion.where_ref.refs_1_, s32[1]{0:T(128)} %copy.18.shear_ref, s32[6]{0:T(128)} %counts_ref.1, s32[3,384]{1,0:T(4,128)} %cells_ref.1, ...), custom_call_target="tpu_custom_call" | custom-call | flops 1000000000 | bytes 8000000 | tf_op jit(solution)/shard_map/pallas_call | solution.py:736
  2.7 0.0 copy-start
  2.7 9.9 %all-gather = f32[64,384]{1,0:T(8,128)S(1)} all-gather(f32[16,384]{1,0:T(8,128)S(1)} %get-tuple-element.27), channel_id=2, replica_groups=mesh['gy'=64,'gx'=4] {'gx'}, dimensions={0}, use_global_device_ids=true | all-gather | bytes 122880 | tf_op jit(solution)/shard_map/all_gather | solution.py:796
  12.6 0.0 copy-start.2
  12.6 0.0 collective-permute-start
  12.6 3.0 %shard_map.130.refs_4_ = f32[432,1536]{1,0:T(8,128)S(1)} custom-call(f32[4,16,384]{2,1,0:T(8,128)S(1)} %bitcast.23, s32[4]{0:T(128)S(1)} %pad_add_fusion.where_ref.refs_1_, f32[8,128]{1,0:T(8,128)S(1)} %get-tuple-element.28.refs_2_.base_ref, f32[6,48,128]{2,1,0:T(8,128)S(1)} %get-tuple-element.29.refs_3_.taps_ref), custom_call_target="tpu_custom_call" | custom-call | flops 1000000000 | bytes 8000000 | tf_op jit(solution)/shard_map/pallas_call | solution.py:736
  15.7 7.1 %collective-permute-done.refs_0_.below_ref = f32[4,16,384]{2,1,0:T(8,128)S(1)} collective-permute-done((f32[4,16,384]{2,1,0:T(8,128)S(1)}, f32[4,16,384]{2,1,0:T(8,128)S(1)}, u32[]{:S(2)}, u32[]{:S(2)}) %collective-permute-start) | collective-permute-done | bytes 98336 | tf_op jit(solution)/shard_map/ppermute | solution.py:752
  22.8 5.5 %shard_map.131 = (f32[432,1536]{1,0:T(8,128)S(1)}, f32[1728,128]{1,0:T(8,128)}) custom-call(f32[4,16,384]{2,1,0:T(8,128)S(1)} %collective-permute-done.refs_0_.below_ref, s32[4]{0:T(128)S(1)} %pad_add_fusion.where_ref.refs_1_, f32[8,128]{1,0:T(8,128)S(1)} %get-tuple-element.28.refs_2_.base_ref, ...), custom_call_target="tpu_custom_call", output_to_operand_aliasing={{0}: (4, {})} | custom-call | flops 1000000000 | bytes 8000000 | tf_op jit(solution)/shard_map/pallas_call | solution.py:736
  28.3 0.0 copy-done
  28.3 0.0 copy-done.2
  28.3 6.4 %all-to-all-start = ((f32[64,27,1,128]{3,2,1,0:T(1,128)}), f32[64,27,1,128]{3,2,1,0:T(1,128)S(1)}, u32[]{:S(2)}, u32[]{:S(2)}) async-start(f32[64,27,1,128]{3,2,1,0:T(1,128)} %bitcast.5), calls=%async_computation | async-start | bytes 1769472 | tf_op jit(solution)/shard_map/all_to_all | solution.py:757
  34.8 0.0 copy-start.1
  34.8 0.9 copy-done.1
  35.7 0.0 copy-start.3
  35.7 0.9 copy-done.3
  36.6 5.7 %shard_map.132 = (bf16[24,2,96,384]{3,2,1,0:T(8,128)(2,1)}, f32[24,36,128]{2,1,0:T(8,128)}, f32[384,768]{1,0:T(8,128)S(1)}, bf16[384,576]{1,0:T(8,128)(2,1)S(1)}, bf16[384,576]{1,0:T(8,128)(2,1)S(1)}) custom-call(s32[4]{0:T(128)S(1)} %pad_add_fusion.where_ref.refs_1_, f32[4,16,384]{2,1,0:T(8,128)S(1)} %bitcast.24, ...), custom_call_target="tpu_custom_call" | custom-call | flops 1000000000 | bytes 8000000 | tf_op jit(solution)/shard_map/pallas_call | solution.py:736
  42.3 15.1 %all-to-all-done = f32[64,27,1,128]{3,2,1,0:T(1,128)S(1)} async-done(((f32[64,27,1,128]{3,2,1,0:T(1,128)}), f32[64,27,1,128]{3,2,1,0:T(1,128)S(1)}, u32[]{:S(2)}, u32[]{:S(2)}) %all-to-all-start) | async-done | bytes 884768 | tf_op jit(solution)/shard_map/all_to_all | solution.py:757
  57.4 2.4 %shard_map.133 = f32[1728,128]{1,0:T(8,128)S(1)} custom-call(f32[1728,128]{1,0:T(8,128)S(1)} %bitcast.20, bf16[384,576]{1,0:T(8,128)(2,1)S(1)} %get-tuple-element.39.table_ref, bf16[384,576]{1,0:T(8,128)(2,1)S(1)} %get-tuple-element.40.back_ref, f32[384,768]{1,0:T(8,128)S(1)} %get-tuple-element.41.green_ref), custom_call_target="tpu_custom_call" | custom-call | flops 1000000000 | bytes 8000000 | tf_op jit(solution)/shard_map/pallas_call | solution.py:736
  59.8 28.8 %all_to_all.10 = f32[64,27,1,128]{3,2,1,0:T(1,128)S(1)} all-to-all(f32[64,27,1,128]{3,2,1,0:T(1,128)S(1)} %bitcast.21), channel_id=1, replica_groups=mesh['gy'=64,'gx'=4] {'gy'}, dimensions={0} | all-to-all | bytes 1769472 | tf_op jit(solution)/shard_map/all_to_all | solution.py:757
  88.6 0.0 copy-start.4
  88.6 5.3 %shard_map.134 = (f32[4,8,384]{2,1,0:T(8,128)S(1)}, f32[432,768]{1,0:T(8,128)S(1)}, bf16[12,2,96,384]{3,2,1,0:T(8,128)(2,1)S(1)}, f32[12,36,128]{2,1,0:T(8,128)S(1)}) custom-call(f32[4,16,384]{2,1,0:T(8,128)S(1)} %collective-permute-done.refs_0_.below_ref, s32[4]{0:T(128)S(1)} %pad_add_fusion.where_ref.refs_1_, ...), custom_call_target="tpu_custom_call" | custom-call | flops 1000000000 | bytes 8000000 | tf_op jit(solution)/shard_map/pallas_call | solution.py:736
  93.9 3.6 %collective-permute-start.1 = (f32[4,8,384]{2,1,0:T(8,128)S(1)}, f32[4,8,384]{2,1,0:T(8,128)S(1)}, u32[]{:S(2)}, u32[]{:S(2)}) collective-permute-start(f32[4,8,384]{2,1,0:T(8,128)S(1)} %get-tuple-element.45), channel_id=1, source_target_pairs={{0,252},{4,0},{8,4},{12,8},{16,12},{20,16},{24,20},{28,24},{32,28}... | collective-permute-start | bytes 147464 | tf_op jit(solution)/shard_map/ppermute | solution.py:752
  97.4 0.0 copy-done.4
  97.4 2.3 %shard_map.135 = f32[4,8,384]{2,1,0:T(8,128)S(1)} custom-call(f32[4,16,384]{2,1,0:T(8,128)S(1)} %bitcast.25, s32[4]{0:T(128)S(1)} %pad_add_fusion.where_ref.refs_1_, bf16[12,2,96,384]{3,2,1,0:T(8,128)(2,1)S(1)} %get-tuple-element.42.refs_2_, f32[12,36,128]{2,1,0:T(8,128)S(1)} %get-tuple-element.43.refs_3_, f32[432,768]{1,0:T(8,128)S(1)} %get-tuple-element.44.refs_4_), custom_call_target="tpu_custom_call" | custom-call | flops 1000000000 | bytes 8000000 | tf_op jit(solution)/shard_map/pallas_call | solution.py:736
  99.7 0.0 collective-permute-done.1
  99.8 4.4 %collective-permute-start.4 = (f32[8,384]{1,0:T(8,128)S(1)}, f32[8,384]{1,0:T(8,128)S(1)}, u32[]{:S(2)}, u32[]{:S(2)}) collective-permute-start(f32[8,384]{1,0:T(8,128)S(1)} %get-tuple-element.50), channel_id=1, source_target_pairs={{0,3},{1,0},{2,1},{3,2},{4,7},{5,4},{6,5},{7,6},{8,11},{9,8},{10,9... | collective-permute-start | bytes 36872 | tf_op jit(solution)/shard_map/ppermute | solution.py:865
  104.1 2.6 %collective-permute-start.3 = (f32[8,384]{1,0:T(8,128)S(1)}, f32[8,384]{1,0:T(8,128)S(1)}, u32[]{:S(2)}, u32[]{:S(2)}) collective-permute-start(f32[8,384]{1,0:T(8,128)S(1)} %get-tuple-element.51), channel_id=1, source_target_pairs={{0,2},{1,3},{2,0},{3,1},{4,6},{5,7},{6,4},{7,5},{8,10},{9,11},{10,... | collective-permute-start | bytes 36872 | tf_op jit(solution)/shard_map/ppermute | solution.py:865
  106.8 0.6 collective-permute-start.2
  107.4 0.6 collective-permute-done.4.three_ref
  108.0 0.2 collective-permute-done.3.two_ref
  108.2 0.0 collective-permute-done.2.one_ref
  108.2 0.6 shard_map.136
  (2 shorter events, 0.0 us)
Async XLA Ops:
  2.7 25.6 %copy-start = (f32[6,48,128]{2,1,0:T(8,128)}, f32[6,48,128]{2,1,0:T(8,128)S(1)}, u32[]{:S(2)}) copy-start(f32[6,48,128]{2,1,0:T(8,128)S(1)} %get-tuple-element.29.refs_3_.taps_ref) | copy-start | bytes 442372
  12.6 15.7 %copy-start.2 = (f32[64,384]{1,0:T(8,128)}, f32[64,384]{1,0:T(8,128)S(1)}, u32[]{:S(2)}) copy-start(f32[64,384]{1,0:T(8,128)S(1)} %all-gather) | copy-start | bytes 294916
  12.6 10.1 %collective-permute-start = (f32[4,16,384]{2,1,0:T(8,128)S(1)}, f32[4,16,384]{2,1,0:T(8,128)S(1)}, u32[]{:S(2)}, u32[]{:S(2)}) collective-permute-start(f32[4,16,384]{2,1,0:T(8,128)S(1)} %bitcast.22), channel_id=1, source_target_pairs={{0,4},{4,8},{8,12},{12,16},{16,20},{20,24},{24,28},{28,32},{32,36}... | collective-permute-start | bytes 294920 | tf_op jit(solution)/shard_map/ppermute | solution.py:752
  28.3 29.0 %all-to-all-start = ((f32[64,27,1,128]{3,2,1,0:T(1,128)}), f32[64,27,1,128]{3,2,1,0:T(1,128)S(1)}, u32[]{:S(2)}, u32[]{:S(2)}) async-start(f32[64,27,1,128]{3,2,1,0:T(1,128)} %bitcast.5), calls=%async_computation | async-start | bytes 1769472 | tf_op jit(solution)/shard_map/all_to_all | solution.py:757
  34.8 0.9 copy-start.1
  35.7 0.9 copy-start.3
  88.6 8.9 %copy-start.4 = (f32[64,384]{1,0:T(8,128)S(1)}, f32[64,384]{1,0:T(8,128)}, u32[]{:S(2)}) copy-start(f32[64,384]{1,0:T(8,128)} %copy-done.2) | copy-start | bytes 294916
  93.9 5.9 %collective-permute-start.1 = (f32[4,8,384]{2,1,0:T(8,128)S(1)}, f32[4,8,384]{2,1,0:T(8,128)S(1)}, u32[]{:S(2)}, u32[]{:S(2)}) collective-permute-start(f32[4,8,384]{2,1,0:T(8,128)S(1)} %get-tuple-element.45), channel_id=1, source_target_pairs={{0,252},{4,0},{8,4},{12,8},{16,12},{20,16},{24,20},{28,24},{32,28}... | collective-permute-start | bytes 147464 | tf_op jit(solution)/shard_map/ppermute | solution.py:752
  99.8 8.3 %collective-permute-start.4 = (f32[8,384]{1,0:T(8,128)S(1)}, f32[8,384]{1,0:T(8,128)S(1)}, u32[]{:S(2)}, u32[]{:S(2)}) collective-permute-start(f32[8,384]{1,0:T(8,128)S(1)} %get-tuple-element.50), channel_id=1, source_target_pairs={{0,3},{1,0},{2,1},{3,2},{4,7},{5,4},{6,5},{7,6},{8,11},{9,8},{10,9... | collective-permute-start | bytes 36872 | tf_op jit(solution)/shard_map/ppermute | solution.py:865
  104.1 4.1 %collective-permute-start.3 = (f32[8,384]{1,0:T(8,128)S(1)}, f32[8,384]{1,0:T(8,128)S(1)}, u32[]{:S(2)}, u32[]{:S(2)}) collective-permute-start(f32[8,384]{1,0:T(8,128)S(1)} %get-tuple-element.51), channel_id=1, source_target_pairs={{0,2},{1,3},{2,0},{3,1},{4,6},{5,7},{6,4},{7,5},{8,10},{9,11},{10,... | collective-permute-start | bytes 36872 | tf_op jit(solution)/shard_map/ppermute | solution.py:865
  106.8 1.4 %collective-permute-start.2 = (f32[8,384]{1,0:T(8,128)S(1)}, f32[8,384]{1,0:T(8,128)S(1)}, u32[]{:S(2)}, u32[]{:S(2)}) collective-permute-start(f32[8,384]{1,0:T(8,128)S(1)} %get-tuple-element.52), channel_id=1, source_target_pairs={{0,1},{1,2},{2,3},{3,0},{4,5},{5,6},{6,7},{7,4},{8,9},{9,10},{10,1... | collective-permute-start | bytes 36872 | tf_op jit(solution)/shard_map/ppermute | solution.py:865
